TPU v7x, 512 devices: a whole 4x4x16 slice. The times are simulated.
512 devices in a mesh: mode: 8 (over z_hi, x), space: 64 (over y, z_lo, core).
Axes of the slice: x: 4, y: 4, z: 16 (z_hi: 2, z_lo: 8; z = z_hi * 8 + z_lo), core: 2. Of those that a mesh axis runs over, the one named last changes fastest.
Arguments:
- load_modes: float32 [96, 3, 64, 4, 128], P('mode', None, 'space'), may hold values from -8 to 8
- first_guess: float32 [96, 3, 64, 4, 128], P('mode', None, 'space'), may hold values from -4 to 4
- kl_fields: float32 [8, 64, 4, 128], P(None, 'space'), may hold values from -3 to 3
- region_labels: int32 [64, 4, 128], P('space'), may hold values from 0 to 2
- partner: int32 [96, 8], replicated, may hold values from 0 to 95, as said below
- variable: int32 [96, 8], replicated, may hold values from 0 to 7
- weight: float32 [96, 8], replicated, may hold values from 0.2 to 1
Outputs:
- solution_modes: float32 [96, 3, 64, 4, 128], P('mode', None, 'space')
Inputs may be any that keep to these rules, and one draw needn't show every extreme that they name: partner[i, l] is never i.
All inputs are finite; a program needn't handle non-finite values.
Results may differ from a plain program's by a relative error of at most 0.00011.
Values sent between devices are 32-bit elements; how exact they have to be, the bound alone decides.
No kernel may reach another device: no remote copies, remote signals or barrier semaphores. Data moves between devices by JAX's collectives and lax.ppermute only.
A program may use at most 64 MiB of HBM per device.

v0:
```python
import jax
import jax.numpy as jnp
from jax import lax
from jax.sharding import PartitionSpec as P

CG_STEPS = 3
SWEEPS = 2


def padded_2(value, sides, width):
    for axis, dim in sides:
        count, length = (lax.axis_size(axis), value.shape[dim])
        up = [(i, (i + 1) % count) for i in range(count - 1)]
        down = [(j, i) for i, j in up]
        last = lax.slice_in_dim(value, length - width, length, axis=dim)
        initial = lax.slice_in_dim(value, 0, width, axis=dim)
        before = lax.ppermute(last, axis, up)
        after = lax.ppermute(initial, axis, down)
        value = jnp.concatenate([before, value, after], axis=dim)
    return value


def trailing(array, index):
    return array[tuple([slice(None)] * (array.ndim - 3) + list(index))]


def neighbour(array, dimension, offset_side):
    index = [slice(1, -1), slice(1, -1), slice(1, -1)]
    length = array.shape[array.ndim - 3 + dimension]
    index[dimension] = slice(offset_side, length - 2 + offset_side)
    return trailing(array, index)


def stiffness(field, coefficient):
    lead_field = field.ndim - 3
    field = jnp.pad(field, [(0, 0)] * lead_field + [(0, 0), (1, 1), (1, 1)])
    lead_coef = coefficient.ndim - 3
    coefficient = jnp.pad(coefficient, [(0, 0)] * lead_coef + [(0, 0), (1, 1), (1, 1)])
    inner = [slice(1, -1), slice(1, -1), slice(1, -1)]
    centre_val = trailing(field, inner)
    centre_mod = trailing(coefficient, inner)
    running = None
    for dimension in range(3):
        weighting = (
            jnp.where(jnp.arange(3) == dimension, 2.0, 1.0).astype(jnp.float32).reshape(3, 1, 1, 1)
        )
        for offset_side in (0, 2):
            face_mod = 0.5 * (centre_mod + neighbour(coefficient, dimension, offset_side))
            change = centre_val - neighbour(field, dimension, offset_side)
            term = weighting * jnp.expand_dims(face_mod, -4) * change
            running = term if running is None else running + term
    return running


def coefficients(region_labels, kl_fields):
    mean_coef = jnp.where(region_labels == 0, 1.3, jnp.where(region_labels == 1, 1.0, 0.6)).astype(
        jnp.float32
    )
    copper = (region_labels == 1).astype(jnp.float32)
    return (mean_coef, kl_fields * copper[None])


def expand(values):
    return values[:, None, None, None, None]


def local_sum(first, second):
    return jnp.sum(first * second, axis=(1, 2, 3, 4))


def apply_mean(field, mean_padded):
    grown = padded_2(field, (("space", 2),), 1)
    return stiffness(grown, mean_padded)


def squares(residual):
    return lax.psum(local_sum(residual, residual), "space")


def build_links(weights_rows, same_mode, same_variable):
    return jnp.einsum(
        "il,ilj,ilk->ijk",
        weights_rows,
        same_mode.astype(jnp.float32),
        same_variable.astype(jnp.float32),
        precision=lax.Precision.HIGHEST,
    )


def conjugate(right_side, estimate, padded, mean_padded):
    residual = right_side - stiffness(padded, mean_padded)
    direction = residual
    norm_now = squares(residual)
    for step_index in range(CG_STEPS):
        image = apply_mean(direction, mean_padded)
        curve = lax.psum(local_sum(direction, image), "space")
        step_size = norm_now / curve
        estimate = estimate + expand(step_size) * direction
        residual = residual - expand(step_size) * image
        if step_index + 1 < CG_STEPS:
            norm_next = squares(residual)
            direction = residual + expand(norm_next / norm_now) * direction
            norm_now = norm_next
    return estimate


def shards(load_modes, first_guess, kl_fields, region_labels, partner, variable, weight):
    mode_dev = load_modes.shape[0]
    mode_count = mode_dev * lax.axis_size("mode")
    variables = kl_fields.shape[0]
    offset = lax.axis_index("mode") * mode_dev
    mean_coef, varying = coefficients(region_labels, kl_fields)
    stacked = jnp.concatenate([mean_coef[None], varying], 0)
    padded_coef = padded_2(stacked, (("space", 1),), 1)
    mean_padded = padded_coef[0]
    vary_padded = padded_coef[1:]
    mode_ids = jnp.arange(mode_count, dtype=jnp.int32)
    variable_ids = jnp.arange(variables, dtype=jnp.int32)
    iterate = first_guess
    for sweep_index in range(SWEEPS):
        padded = padded_2(iterate, (("space", 2),), 1)
        rows_partner = lax.dynamic_slice_in_dim(partner, offset, mode_dev, 0)
        rows_variable = lax.dynamic_slice_in_dim(variable, offset, mode_dev, 0)
        rows_weight = lax.dynamic_slice_in_dim(weight, offset, mode_dev, 0)
        links = build_links(
            rows_weight,
            rows_partner[:, :, None] == mode_ids[None, None, :],
            rows_variable[:, :, None] == variable_ids[None, None, :],
        )
        mixed = jnp.einsum(
            "ijk,jcxyz->kicxyz",
            links,
            lax.all_gather(iterate, "mode", axis=0, tiled=True),
            precision=lax.Precision.HIGHEST,
        )
        mixed_padded = padded_2(mixed, (("space", 3),), 1)
        coupling = jnp.sum(stiffness(mixed_padded, vary_padded[:, None]), axis=0)
        right_side = load_modes - coupling
        iterate = conjugate(right_side, iterate, padded, mean_padded)
    return iterate


def solution(mesh):
    return jax.shard_map(
        shards,
        mesh=mesh,
        in_specs=(
            P("mode", None, "space", None, None),
            P("mode", None, "space", None, None),
            P(None, "space", None, None),
            P("space", None, None),
            P(),
            P(),
            P(),
        ),
        out_specs=P("mode", None, "space", None, None),
        check_vma=False,
    )
```

profile of v0, /device:TPU:1, one launch (start us, length us, event | category | flops | bytes accessed | tf_op | source)
XLA Modules:
  0.0 2339.3 jit_solution(2110789107130429243)
XLA Ops:
  0.0 0.7 fusion.133
  0.7 0.7 broadcast_multiply_fusion.6
  1.4 4.9 collective-permute-start
  6.4 5.1 collective-permute-start.1
  11.5 0.8 constant_dynamic-slice_fusion.1
  12.7 65.5 %all_gather.6 = f32[96,3,1,4,128]{4,3,2,1,0:T(4,128)S(1)} all-gather(f32[12,3,1,4,128]{4,3,2,1,0:T(4,128)} %param.8), channel_id=1, replica_groups=mesh['mode'=8,'space'=64] {'mode'}, dimensions={0}, use_global_device_ids=true | all-gather | bytes 663552 | tf_op jit(solution)/shard_map/all_gather | solution.py:133
  78.4 0.6 convolution_bitcast_fusion.1
  79.0 4.9 collective-permute-start.2
  83.9 1.9 collective-permute-start.3
  85.8 3.6 collective-permute-start.4
  89.5 1.9 collective-permute-start.5
  92.1 3.8 collective-permute-done.5
  95.9 1.2 select_maximum_fusion.18
  97.1 1.9 select_maximum_fusion.2
  99.0 0.7 fusion.17
  99.9 1.9 collective-permute-start.6
  101.9 2.4 collective-permute-start.7
  104.3 4.4 collective-permute-done.7
  108.7 0.3 select_maximum_fusion.16
  109.0 0.4 multiply_reduce_fusion.8
  109.4 206.6 %all-reduce.13 = (f32[12]{0:T(128)S(1)}, f32[12]{0:T(128)S(1)}) all-reduce(f32[12]{0:T(128)S(1)} %get-tuple-element.8, f32[12]{0:T(128)S(1)} %get-tuple-element.7), channel_id=1, replica_groups=mesh['mode'=8,'space'=64] {'space'}, use_global_device_ids=true, to_apply=%region_2.3 | all-reduce | flops 24 | bytes 192 | tf_op jit(solution)/shard_map/psum | solution.py:77
  316.2 216.1 %psum.86 = f32[12]{0:T(128)S(1)} all-reduce(f32[12]{0:T(128)S(1)} %get-tuple-element.20), channel_id=1, replica_groups=mesh['mode'=8,'space'=64] {'space'}, use_global_device_ids=true, to_apply=%region_6.7 | all-reduce | flops 12 | bytes 96 | tf_op jit(solution)/shard_map/psum | solution.py:77
  532.4 1.9 collective-permute-start.8
  534.4 2.4 collective-permute-start.9
  536.8 3.2 collective-permute-done.9
  540.0 0.3 select_maximum_fusion.14
  540.4 0.3 multiply_reduce_fusion.6
  540.7 207.7 %psum.87 = f32[12]{0:T(128)S(1)} all-reduce(f32[12]{0:T(128)S(1)} %get-tuple-element.18), channel_id=1, replica_groups=mesh['mode'=8,'space'=64] {'space'}, use_global_device_ids=true, to_apply=%region_8.9 | all-reduce | flops 12 | bytes 96 | tf_op jit(solution)/shard_map/psum | solution.py:96
  748.6 212.9 %psum.88 = f32[12]{0:T(128)S(1)} all-reduce(f32[12]{0:T(128)S(1)} %multiply_reduce_fusion.5), channel_id=1, replica_groups=mesh['mode'=8,'space'=64] {'space'}, use_global_device_ids=true, to_apply=%region_10.11 | all-reduce | flops 12 | bytes 96 | tf_op jit(solution)/shard_map/psum | solution.py:77
  961.6 1.9 collective-permute-start.10
  963.5 2.4 collective-permute-start.11
  966.0 3.2 collective-permute-done.11
  969.2 0.3 select_maximum_fusion.12
  969.5 0.3 fusion.96
  969.8 208.1 %psum.89 = f32[12]{0:T(128)S(1)} all-reduce(f32[12]{0:T(128)S(1)} %fusion.96), channel_id=1, replica_groups=mesh['mode'=8,'space'=64] {'space'}, use_global_device_ids=true, to_apply=%region_12.13 | all-reduce | flops 12 | bytes 96 | tf_op jit(solution)/shard_map/psum | solution.py:96
  1178.0 62.5 %all_gather.7 = f32[96,3,1,4,128]{4,3,2,1,0:T(4,128)S(1)} all-gather(f32[12,3,1,4,128]{4,3,2,1,0:T(4,128)S(1)} %bitcast.102), channel_id=1, replica_groups=mesh['mode'=8,'space'=64] {'mode'}, dimensions={0}, use_global_device_ids=true | all-gather | bytes 663552 | tf_op jit(solution)/shard_map/all_gather | solution.py:133
  1240.6 0.7 convolution_bitcast_fusion
  1241.2 4.5 collective-permute-start.12
  1245.8 7.8 collective-permute-start.13
  1253.6 1.9 collective-permute-start.14
  1255.5 2.4 collective-permute-start.15
  1257.9 3.2 collective-permute-done.15
  1261.5 1.9 select_maximum_fusion
  1263.4 0.7 fusion.8
  1264.3 1.9 collective-permute-start.16
  1266.2 2.4 collective-permute-start.17
  1268.7 3.2 collective-permute-done.17
  1272.2 0.4 multiply_reduce_fusion.3
  1272.6 207.7 %all-reduce.12 = (f32[12]{0:T(128)S(1)}, f32[12]{0:T(128)S(1)}) all-reduce(f32[12]{0:T(128)S(1)} %get-tuple-element.6, f32[12]{0:T(128)S(1)} %get-tuple-element.5), channel_id=1, replica_groups=mesh['mode'=8,'space'=64] {'space'}, use_global_device_ids=true, to_apply=%region_15.16 | all-reduce | flops 24 | bytes 192 | tf_op jit(solution)/shard_map/psum | solution.py:77
  1480.5 212.9 %psum.92 = f32[12]{0:T(128)S(1)} all-reduce(f32[12]{0:T(128)S(1)} %get-tuple-element.15), channel_id=1, replica_groups=mesh['mode'=8,'space'=64] {'space'}, use_global_device_ids=true, to_apply=%region_19.20 | all-reduce | flops 12 | bytes 96 | tf_op jit(solution)/shard_map/psum | solution.py:77
  1693.5 1.9 collective-permute-start.18
  1695.4 2.4 collective-permute-start.19
  1697.8 3.2 collective-permute-done.19
  1701.1 0.3 select_maximum_fusion.6
  1701.4 0.3 multiply_reduce_fusion.1
  1701.7 207.7 %psum.93 = f32[12]{0:T(128)S(1)} all-reduce(f32[12]{0:T(128)S(1)} %get-tuple-element.13), channel_id=1, replica_groups=mesh['mode'=8,'space'=64] {'space'}, use_global_device_ids=true, to_apply=%region_21.22 | all-reduce | flops 12 | bytes 96 | tf_op jit(solution)/shard_map/psum | solution.py:96
  1909.7 212.9 %psum.94 = f32[12]{0:T(128)S(1)} all-reduce(f32[12]{0:T(128)S(1)} %multiply_reduce_fusion), channel_id=1, replica_groups=mesh['mode'=8,'space'=64] {'space'}, use_global_device_ids=true, to_apply=%region_23.24 | all-reduce | flops 12 | bytes 96 | tf_op jit(solution)/shard_map/psum | solution.py:77
  2122.6 1.9 collective-permute-start.20
  2124.6 2.4 collective-permute-start.21
  2127.0 3.2 collective-permute-done.21
  2130.2 0.3 select_maximum_fusion.4
  2130.6 0.3 fusion.97
  2130.9 207.7 %psum.95 = f32[12]{0:T(128)S(1)} all-reduce(f32[12]{0:T(128)S(1)} %fusion.97), channel_id=1, replica_groups=mesh['mode'=8,'space'=64] {'space'}, use_global_device_ids=true, to_apply=%region_25.26 | all-reduce | flops 12 | bytes 96 | tf_op jit(solution)/shard_map/psum | solution.py:96
  2338.6 0.7 add_bitcast_fusion
  (68 shorter events, 3.8 us)
Async XLA Ops:
  0.0 12.5 copy-start
  1.4 88.1 %collective-permute-start = (f32[9,1,4,128]{3,2,1,0:T(4,128)S(1)}, f32[9,1,4,128]{3,2,1,0:T(4,128)S(1)}, u32[]{:S(2)}, u32[]{:S(2)}) collective-permute-start(f32[9,1,4,128]{3,2,1,0:T(4,128)S(1)} %pad_maximum_fusion.1), channel_id=1, source_target_pairs={{0,1},{1,2},{2,3},{3,4},{4,5},{5,6},{6,7},{7,8},{8,9},{9,10},{10,1... | collective-permute-start | bytes 55304 | tf_op jit(solution)/shard_map/ppermute | solution.py:17
  6.4 85.1 %collective-permute-start.1 = (f32[9,1,4,128]{3,2,1,0:T(4,128)S(1)}, f32[9,1,4,128]{3,2,1,0:T(4,128)S(1)}, u32[]{:S(2)}, u32[]{:S(2)}) collective-permute-start(f32[9,1,4,128]{3,2,1,0:T(4,128)S(1)} %pad_maximum_fusion.1), channel_id=1, source_target_pairs={{1,0},{2,1},{3,2},{4,3},{5,4},{6,5},{7,6},{8,7},{9,8},{10,9},{11,1... | collective-permute-start | bytes 55304 | tf_op jit(solution)/shard_map/ppermute | solution.py:18
  79.0 18.1 collective-permute-start.2
  83.9 13.2 collective-permute-start.3
  85.8 6.2 collective-permute-start.4
  89.5 6.4 collective-permute-start.5
  97.1 2.6 copy-start.1
  97.1 2.6 copy-start.2
  99.9 4.3 collective-permute-start.6
  101.9 6.8 collective-permute-start.7
  532.4 4.3 collective-permute-start.8
  534.4 5.7 collective-permute-start.9
  961.6 4.3 collective-permute-start.10
  963.5 5.7 collective-permute-start.11
  1241.2 20.3 collective-permute-start.12
  1245.8 15.7 collective-permute-start.13
  1253.6 4.3 collective-permute-start.14
  1255.5 5.7 collective-permute-start.15
  1264.3 4.3 collective-permute-start.16
  1266.2 5.7 collective-permute-start.17
  1693.5 4.3 collective-permute-start.18
  1695.4 5.7 collective-permute-start.19
  2122.6 4.3 collective-permute-start.20
  2124.6 5.7 collective-permute-start.21
where the time goes:
time: 2340 us
  blocking collectives  2230 us (95%)
  starting transfers between devices  65.1 us (3%)
  waiting for transfers between devices  27.8 us (1%)
    psum x6, blocking collectives, squares(): return lax.psum(local_sum(residual, residual), 'space')  1270 us
    psum x4, blocking collectives, conjugate(): curve = lax.psum(local_sum(direction, image), 'space')  831 us
    all_gather x2, blocking collectives, shards(): lax.all_gather(iterate, 'mode', axis=0, tiled=True)  128 us
  transfers between devices with their start and end apart: 22, of which 8 were waited for; matrix products, arithmetic and copies ran while one was open for 0% of the time, Pallas kernels for 0%

commit v1 on v0

v1 whole, which is shorter than its diff:
```python
import functools

import jax
import jax.numpy as jnp
from jax import lax
from jax.experimental import pallas as pl
from jax.experimental.pallas import tpu as pltpu
from jax.sharding import Mesh
from jax.sharding import PartitionSpec as P

AXES = ("zh", "x", "y", "zl", "c")
GROUPS = ("c", "x")
DEPTH = ("zh", "zl")
NG, NM, NL, NK = 8, 12, 8, 8
NY, NZ, SHIFT = 4, 128, 4.0
QUAD = 4
TRI = NM // QUAD
ROWS = 3 * TRI
SLAB = NY * ROWS
F32 = jnp.float32


def flat(zh, x, y, zl, c):
    return (((zh * 4 + x) * 4 + y) * 8 + zl) * 2 + c


def moves():
    pairs = []
    for zh in range(2):
        for x in range(4):
            for y in range(4):
                for zl in range(8):
                    for c in range(2):
                        s = y * 16 + zl * 2 + c
                        z = s // 4
                        pairs.append((flat(zh, x, y, zl, c), flat(z // 8, x, s % 4, z % 8, zh)))
    return pairs


def slab_steps(step):
    def place(s):
        z = s // 4
        return ((z // 8) * 4 + s % 4) * 8 + z % 8

    return [(place(s), place(s + step)) for s in range(64) if 0 <= s + step < 64]


def depth_steps(step):
    return [(z, z + step) for z in range(16) if 0 <= z + step < 16]


def call(kernel, outs, scratch=()):
    return pl.pallas_call(
        kernel,
        out_shape=[jax.ShapeDtypeStruct(s, F32) for s in outs],
        scratch_shapes=[pltpu.VMEM(s, F32) for s in scratch],
    )


def faces(e, other):
    return 0.5 * (e + other)


def coupling_kernel(nk, *refs):
    first = nk > NK
    if first:
        (u, load, e0, em, ep, partner, variable, weight, out, us, mx, fx, fy, fz) = refs
    else:
        (u, e0, em, ep, partner, variable, weight, out, us, mx, fx, fy, fz) = refs
    for g in range(NG):
        for yc in range(NY * 3):
            us[yc, g * NM : (g + 1) * NM, :] = u[g, yc * NM : (yc + 1) * NM, :]
    lane = lax.broadcasted_iota(jnp.int32, (16, NG * NM), 1)
    pr, vr, wr = partner[...], variable[...], weight[...]
    links = NL + 1 if first else NL
    hit = [jnp.where(lane == pr[:, l : l + 1], wr[:, l : l + 1], 0.0) for l in range(links)]
    blocks = []
    for k in range(nk):
        acc = None
        for l in range(links):
            if (k == NK) != (l == NL):
                continue
            term = hit[l] if l == NL else jnp.where(vr[:, l : l + 1] == k, hit[l], 0.0)
            acc = term if acc is None else acc + term
        blocks.append(acc)
    mix = jnp.concatenate(blocks, axis=0)
    for yc in range(NY * 3):
        mx[yc] = lax.dot_general(
            mix,
            us[yc],
            (((1,), (0,)), ((), ())),
            precision=lax.Precision.HIGHEST,
            preferred_element_type=F32,
        )
    e = e0[...]
    zlane = lax.broadcasted_iota(jnp.int32, e.shape, 1)
    row = lax.broadcasted_iota(jnp.int32, e.shape, 0)
    zup = jnp.where(zlane == NZ - 1, 0.0, pltpu.roll(e, NZ - 1, 1))
    zdn = jnp.where(zlane == 0, 0.0, pltpu.roll(e, 1, 1))
    count = e.shape[0]
    yup = jnp.where(row % NY == NY - 1, 0.0, pltpu.roll(e, count - 1, 0))
    ydn = jnp.where(row % NY == 0, 0.0, pltpu.roll(e, 1, 0))
    fx[0] = faces(e, ep[...])
    fx[1] = faces(e, em[...])
    fy[0] = faces(e, yup)
    fy[1] = faces(e, ydn)
    fzu, fzd = faces(e, zup), faces(e, zdn)
    base = fx[0] + fx[1] + fy[0] + fy[1] + fzu + fzd
    fz[0] = jnp.where(zlane == NZ - 1, 0.0, fzu)
    fz[1] = jnp.where(zlane == 0, 0.0, fzd)
    fz[2] = base + fx[0] + fx[1]
    fz[3] = base + fy[0] + fy[1]
    fz[4] = base + fzu + fzd
    for y in range(NY):
        for c in range(3):
            own = up = down = None
            for k in range(nk):
                r = slice(k * NY + y, k * NY + y + 1)
                rows = slice(k * 16, k * 16 + 16)
                m = mx[y * 3 + c, rows, :]
                t = fz[2 + c, r, :] * m
                side = None
                if y + 1 < NY:
                    side = fy[0, r, :] * mx[(y + 1) * 3 + c, rows, :]
                if y > 0:
                    less = fy[1, r, :] * mx[(y - 1) * 3 + c, rows, :]
                    side = less if side is None else side + less
                t = t - (2.0 * side if c == 1 else side)
                side = fz[0, r, :] * pltpu.roll(m, NZ - 1, 1) + fz[1, r, :] * pltpu.roll(m, 1, 1)
                t = t - (2.0 * side if c == 2 else side)
                p, q = fx[0, r, :] * m, fx[1, r, :] * m
                own, up, down = (t, p, q) if own is None else (own + t, up + p, down + q)
            if c == 0:
                up, down = 2.0 * up, 2.0 * down
            yc = y * 3 + c
            own = load[yc * NM : (yc + 1) * NM, :] - own[:NM] if first else -own[:NM]
            for kind, val in enumerate((own, up, down)):
                at = (kind * NY + y) * ROWS + c * TRI
                for d in range(QUAD):
                    out[d, at : at + TRI, :] = val[d * TRI : (d + 1) * TRI]
    tail = e[NK * NY : NK * NY + NY] if first else jnp.zeros((NY, NZ), F32)
    for d in range(QUAD):
        out[d, 3 * SLAB : 3 * SLAB + NY, :] = tail


def edges_kernel(first, *refs):
    if first:
        q, own, up, down = refs
    else:
        q, rest, own, up, down = refs
    rs = []
    for s in range(QUAD):
        r = q[s, 0:SLAB, :]
        if not first:
            r = r + rest[s]
        if s > 0:
            r = r + q[s - 1, SLAB : 2 * SLAB, :]
        if s + 1 < QUAD:
            r = r + q[s + 1, 2 * SLAB : 3 * SLAB, :]
        own[s] = r
        rs.append(r)
    for j in range(3):
        up[j * SLAB : (j + 1) * SLAB, :] = rs[j + 1]
        down[j * SLAB : (j + 1) * SLAB, :] = rs[j]
    up[3 * SLAB : 4 * SLAB, :] = q[3, SLAB : 2 * SLAB, :]
    down[3 * SLAB : 4 * SLAB, :] = q[0, 2 * SLAB : 3 * SLAB, :]
    if first:
        for j in range(3):
            at = 4 * SLAB + j * NY
            up[at : at + NY, :] = q[j + 1, 3 * SLAB : 3 * SLAB + NY, :]
            down[at : at + NY, :] = q[j, 3 * SLAB : 3 * SLAB + NY, :]
        up[4 * SLAB + 12 :, :] = jnp.zeros((4, NZ), F32)
        down[4 * SLAB + 12 :, :] = jnp.zeros((4, NZ), F32)


def powers_kernel(first, *refs):
    if first:
        q, own, low, high, v0, v1, v2, v3, mom, ec, w0, w1, w2, dg = refs
        for j in range(3):
            at = 4 * SLAB + j * NY
            ec[j * NY : (j + 1) * NY, :] = low[at : at + NY, :]
            ec[(7 + j) * NY : (8 + j) * NY, :] = high[at : at + NY, :]
        for s in range(QUAD):
            ec[(3 + s) * NY : (4 + s) * NY, :] = q[s, 3 * SLAB : 3 * SLAB + NY, :]
    else:
        q, own, low, high, ec, v0, v1, v2, v3, mom, w0, w1, w2, dg = refs

    def rows(ref, at, y):
        return ref[at + y * ROWS : at + (y + 1) * ROWS, :]

    rid = lax.broadcasted_iota(jnp.int32, (ROWS, NZ), 0)
    wx = jnp.where(rid < TRI, 2.0, 1.0)
    wy = jnp.where((rid >= TRI) & (rid < 2 * TRI), 2.0, 1.0)
    wz = jnp.where(rid >= 2 * TRI, 2.0, 1.0)
    lane1 = lax.broadcasted_iota(jnp.int32, (1, NZ), 1)
    em = [[ec[p * NY + y : p * NY + y + 1, :] for y in range(NY)] for p in range(10)]
    zero = jnp.zeros((1, NZ), F32)

    def inside(p, y, val):
        return val if 3 <= p <= 6 else jnp.where(em[p][y] > 0.0, val, 0.0)

    for y in range(NY):
        for p in range(3):
            lo = rows(low, p * SLAB, y)
            hi = rows(high, p * SLAB, y)
            if p == 2:
                lo = lo + rows(q.at[0], 2 * SLAB, y)
            if p == 0:
                hi = hi + rows(q.at[QUAD - 1], SLAB, y)
            w0[p * NY + y] = inside(p, y, lo)
            w0[(7 + p) * NY + y] = inside(7 + p, y, hi)
        for s in range(QUAD):
            r = rows(own.at[s], 0, y)
            if s == 0:
                r = r + rows(low, 3 * SLAB, y)
            if s == QUAD - 1:
                r = r + rows(high, 3 * SLAB, y)
            w0[(3 + s) * NY + y] = r
            v0[s * NY + y] = r

    def face(p, y):
        e = em[p][y]
        xu, xd = faces(e, em[p + 1][y]), faces(e, em[p - 1][y])
        yu = faces(e, em[p][y + 1] if y + 1 < NY else zero)
        yd = faces(e, em[p][y - 1] if y > 0 else zero)
        zu = faces(e, jnp.where(lane1 == NZ - 1, 0.0, pltpu.roll(e, NZ - 1, 1)))
        zd = faces(e, jnp.where(lane1 == 0, 0.0, pltpu.roll(e, 1, 1)))
        return xu, xd, yu, yd, zu, zd

    coef = {}
    for p in range(1, 9):
        for y in range(NY):
            xu, xd, yu, yd, zu, zd = face(p, y)
            dg[p * NY + y] = wx * (xu + xd) + wy * (yu + yd) + wz * (zu + zd) - SHIFT
            coef[p, y] = (
                xu, xd, yu, yd,
                jnp.where(lane1 == NZ - 1, 0.0, zu),
                jnp.where(lane1 == 0, 0.0, zd),
            )

    def apply(src, p, y):
        xu, xd, yu, yd, zu, zd = coef[p, y]
        m = src[p * NY + y]
        t = dg[p * NY + y] * m
        t = t - wx * (xu * src[(p + 1) * NY + y] + xd * src[(p - 1) * NY + y])
        side = None
        if y + 1 < NY:
            side = yu * src[p * NY + y + 1]
        if y > 0:
            less = yd * src[p * NY + y - 1]
            side = less if side is None else side + less
        t = t - wy * side
        t = t - wz * (zu * pltpu.roll(m, NZ - 1, 1) + zd * pltpu.roll(m, 1, 1))
        return inside(p, y, t)

    for p in range(1, 9):
        for y in range(NY):
            t = apply(w0, p, y)
            w1[p * NY + y] = t
            if 3 <= p <= 6:
                v1[(p - 3) * NY + y] = t
    for p in range(2, 8):
        for y in range(NY):
            t = apply(w1, p, y)
            w2[p * NY + y] = t
            if 3 <= p <= 6:
                v2[(p - 3) * NY + y] = t
    sums = [None] * 6
    for p in range(3, 7):
        for y in range(NY):
            a, b, d = w0[p * NY + y], w1[p * NY + y], w2[p * NY + y]
            t = apply(w2, p, y)
            v3[(p - 3) * NY + y] = t
            for j, val in enumerate((a * a, a * b, b * b, b * d, d * d, d * t)):
                sums[j] = val if sums[j] is None else sums[j] + val
    lane = lax.broadcasted_iota(jnp.int32, (ROWS, NZ), 1)
    spot = lane - 8 * (rid % TRI)
    packed = jnp.zeros((ROWS, NZ), F32)
    for j in range(6):
        packed = jnp.where(spot == j, jnp.sum(sums[j], axis=1, keepdims=True), packed)
    mom[...] = jnp.broadcast_to(jnp.sum(packed, axis=0, keepdims=True), mom.shape)


def step_coefficients(mom):
    def inner(a, b):
        total = None
        for i, s in enumerate(a):
            for j, t in enumerate(b):
                term = s * t * mom[i + j]
                total = term if total is None else total + term
        return total

    def image(a):
        q = [SHIFT * s for s in a] + [None]
        for i, s in enumerate(a):
            q[i + 1] = s if q[i + 1] is None else q[i + 1] + s
        return q

    one = jnp.ones_like(mom[0])
    x, r, p = [], [one], [one]
    rr = mom[0]
    for step in range(3):
        q = image(p)
        alpha = rr / inner(p, q)
        x = [x[i] + alpha * s if i < len(x) else alpha * s for i, s in enumerate(p)]
        r = [r[i] - alpha * s if i < len(r) else -alpha * s for i, s in enumerate(q)]
        if step < 2:
            new = inner(r, r)
            beta = new / rr
            p = [s + beta * p[i] if i < len(p) else s for i, s in enumerate(r)]
            rr = new
    return x, r


def update_kernel(first, *refs):
    if first:
        mom, v0, v1, v2, v3, out, rest = refs
    else:
        mom, v0, v1, v2, before, out = refs
    total = jnp.sum(mom[...], axis=0, keepdims=True)
    rid = lax.broadcasted_iota(jnp.int32, (ROWS, NZ), 0)
    lane = lax.broadcasted_iota(jnp.int32, (ROWS, NZ), 1)
    spot = lane - 8 * (rid % TRI)
    picked = [jnp.sum(jnp.where(spot == j, total, 0.0), axis=1, keepdims=True) for j in range(6)]
    x, r = step_coefficients(picked)
    x = [jnp.broadcast_to(s, (ROWS, NZ)) for s in x]
    r = [jnp.broadcast_to(s, (ROWS, NZ)) for s in r]
    for s in range(QUAD):
        for y in range(NY):
            at = s * NY + y
            rows = slice(y * ROWS, (y + 1) * ROWS)
            a, b, d = v0[at], v1[at], v2[at]
            change = x[0] * a + x[1] * b + x[2] * d
            if first:
                rest[s, rows, :] = r[0] * a + r[1] * b + r[2] * d + r[3] * v3[at]
            else:
                change = change + before[s, rows, :]
            out[s, rows, :] = change


def spread_kernel(q, out):
    for y in range(NY):
        for c in range(3):
            for d in range(QUAD):
                at = y * ROWS + c * TRI
                piece = q[d, at : at + TRI, :]
                to = (y * 3 + c) * NM + d * TRI
                for g in range(NG):
                    out[g, to : to + TRI, :] = piece


def packed(field):
    return field[:, :, 0].transpose(2, 1, 0, 3).reshape(NY * 3 * NM, NZ)


def shards(load_modes, first_guess, kl_fields, region_labels, partner, variable, weight):
    mean = jnp.where(region_labels == 0, 1.3, jnp.where(region_labels == 1, 1.0, 0.6)).astype(F32)
    varying = jnp.where(region_labels[None] == 1, kl_fields, 0.0)
    moduli = jnp.concatenate([varying, mean[None]], 0).reshape((NK + 1) * NY, NZ)
    there = moves()
    back = [(b, a) for a, b in there]
    guess = lax.ppermute(jnp.concatenate([packed(first_guess), moduli], 0), AXES, there)
    load = lax.ppermute(packed(load_modes), AXES, there)
    e0 = guess[NY * 3 * NM :]
    guess = guess[: NY * 3 * NM]
    em = lax.ppermute(e0, ("zh", "y", "zl"), slab_steps(1))
    ep = lax.ppermute(e0, ("zh", "y", "zl"), slab_steps(-1))

    offset = (lax.axis_index("c") * 4 + lax.axis_index("x")) * NM
    own = offset + jnp.arange(NM, dtype=jnp.int32)[:, None]
    pad = ((0, 16 - NM), (0, 0))
    rows_partner = lax.dynamic_slice_in_dim(partner, offset, NM, 0)
    rows_partner = jnp.pad(jnp.concatenate([rows_partner, own], 1), pad, constant_values=-1)
    rows_variable = jnp.pad(lax.dynamic_slice_in_dim(variable, offset, NM, 0), pad)
    rows_weight = lax.dynamic_slice_in_dim(weight, offset, NM, 0)
    rows_weight = jnp.pad(jnp.concatenate([rows_weight, jnp.ones((NM, 1), F32)], 1), pad)
    links = (rows_partner, rows_variable, rows_weight)

    spread = jnp.broadcast_to(guess[None], (NG,) + guess.shape)
    chunk, cells = (QUAD, SLAB, NZ), (QUAD * NY, ROWS, NZ)
    for sweep in range(2):
        first = sweep == 0
        nk = NK + 1 if first else NK
        gathered = lax.all_to_all(spread, GROUPS, 0, 0, tiled=True)
        fields = (gathered, load, e0, em, ep) if first else (gathered, e0, em, ep)
        face_rows = ((NK + 1) * NY, NZ)
        (sent,) = call(
            functools.partial(coupling_kernel, nk),
            [(QUAD, 3 * SLAB + NY, NZ)],
            [
                (NY * 3, NG * NM, NZ),
                (NY * 3, nk * 16, NZ),
                (2,) + face_rows,
                (2,) + face_rows,
                (5,) + face_rows,
            ],
        )(*fields, *links)
        q = lax.all_to_all(sent, "y", 0, 0, tiled=True)
        edge = (4 * SLAB + 16 if first else 4 * SLAB, NZ)
        chunk_r, up, down = call(functools.partial(edges_kernel, first), [chunk, edge, edge])(
            *((q,) if first else (q, rest))
        )
        low = lax.ppermute(up, DEPTH, depth_steps(1))
        high = lax.ppermute(down, DEPTH, depth_steps(-1))
        scratch = [(10 * NY, ROWS, NZ)] * 4
        outs = [cells] * 4 + [(16, NZ)]
        if first:
            v0, v1, v2, v3, mom, ec = call(
                functools.partial(powers_kernel, True), outs + [(10 * NY, NZ)], scratch
            )(q, chunk_r, low, high)
        else:
            v0, v1, v2, v3, mom = call(functools.partial(powers_kernel, False), outs, scratch)(
                q, chunk_r, low, high, ec
            )
        mom = lax.all_to_all(mom, DEPTH, 0, 0, tiled=True)
        if first:
            change, rest = call(functools.partial(update_kernel, True), [chunk, chunk])(
                mom, v0, v1, v2, v3
            )
        else:
            (change,) = call(functools.partial(update_kernel, False), [chunk])(
                mom, v0, v1, v2, change
            )
        by_slab = lax.all_to_all(change, "y", 0, 0, tiled=True)
        if first:
            (spread,) = call(spread_kernel, [(NG, NY * 3 * NM, NZ)])(by_slab)
    total = lax.ppermute(by_slab, AXES, back)
    total = total.reshape(QUAD, NY, 3, TRI, NZ).transpose(0, 3, 2, 1, 4)
    return first_guess + total.reshape(NM, 3, 1, NY, NZ)


def solution(mesh):
    split = Mesh(mesh.devices.reshape(2, 4, 4, 8, 2), AXES)
    mode, space = ("zh", "x"), ("y", "zl", "c")
    return jax.shard_map(
        shards,
        mesh=split,
        in_specs=(
            P(mode, None, space, None, None),
            P(mode, None, space, None, None),
            P(None, space, None, None),
            P(space, None, None),
            P(),
            P(),
            P(),
        ),
        out_specs=P(mode, None, space, None, None),
        check_vma=False,
    )
```

time: 2340 us -> 220 us (0.09)
  the two profiles are of different devices: /device:TPU:1 before, /device:TPU:16 now
where the time goes in v1:
time: 220 us; the launch traced here: 219 us
  blocking collectives  101 us (46%)
  starting transfers between devices  65.3 us (30%)
  waiting for transfers between devices  24.1 us (11%)
  Pallas kernels  20.2 us (9%)
  local copies, waits for them, and re-layouts  5.87 us (3%)
  other arithmetic  2.84 us (1%)
    all_to_all x2, blocking collectives, shards(): mom = lax.all_to_all(mom, DEPTH, 0, 0, tiled=True)  43.9 us
    ppermute x1, starting transfers between devices, shards(): em = lax.ppermute(e0, ('zh', 'y', 'zl'), slab_steps(1))  23.4 us
    all_to_all x2, blocking collectives, shards(): q = lax.all_to_all(sent, 'y', 0, 0, tiled=True)  22.3 us
    all_to_all x2, blocking collectives, shards(): by_slab = lax.all_to_all(change, 'y', 0, 0, tiled=True)  18.7 us
    all_to_all x1, blocking collectives, shards(): gathered = lax.all_to_all(spread, GROUPS, 0, 0, tiled=True)  15.7 us
    ppermute x1, starting transfers between devices, shards(): lax.ppermute(jnp.concatenate([packed(first_guess), moduli], 0), AXES, there)  15.5 us
    ppermute x1, waiting for transfers between devices, shards(): total = lax.ppermute(by_slab, AXES, back)  12.9 us
    ppermute x2, starting transfers between devices, shards(): low = lax.ppermute(up, DEPTH, depth_steps(1))  8.84 us
  transfers between devices with their start and end apart: 10, of which 7 were waited for; matrix products, arithmetic and copies ran while one was open for 1% of the time, Pallas kernels for 0%

profile of v1, /device:TPU:16, one launch (start us, length us, event | category | flops | bytes accessed | tf_op | source)
XLA Modules:
  0.0 219.1 jit_solution(12228864441544800276)
XLA Ops:
  0.0 0.0 copy-start
  0.0 0.8 fusion
  0.8 0.0 copy-done.12
  0.8 0.7 broadcast_select_fusion
  1.5 0.0 copy-done.2
  1.6 0.0 copy-start.8
  1.6 15.5 %collective-permute-start = (f32[180,128]{1,0:T(8,128)S(1)}, f32[180,128]{1,0:T(8,128)S(1)}, u32[]{:S(2)}, u32[]{:S(2)}) collective-permute-start(f32[180,128]{1,0:T(8,128)S(1)} %pad_maximum_fusion), channel_id=1, source_target_pairs={{0,0},{1,16},{2,32},{3,48},{4,2},{5,18},{6,34},{7,50},{8,4},{9,20}... | collective-permute-start | bytes 276488 | tf_op jit(solution)/shard_map/ppermute | solution.py:362
  17.1 0.0 copy-done.8
  17.1 1.9 collective-permute-start.1
  19.1 0.7 collective-permute-done
  19.8 0.8 broadcast_in_dim.41
  20.7 6.6 %all-to-all-start = ((f32[8,144,128]{2,1,0:T(8,128)}), f32[8,144,128]{2,1,0:T(8,128)S(1)}, u32[]{:S(2)}, u32[]{:S(2)}) async-start(f32[8,144,128]{2,1,0:T(8,128)} %broadcast_in_dim.41), calls=%async_computation | async-start | bytes 1179648 | tf_op jit(solution)/shard_map/all_to_all | solution.py:384
  27.2 0.0 copy-done
  27.3 0.1 constant_dynamic-slice_fusion
  27.3 0.1 copy.42
  27.4 0.6 copy-done.13
  28.0 0.0 copy-done.14
  28.0 0.1 constant_dynamic-slice_fusion.1
  28.1 0.1 copy.40
  28.2 0.6 pad_select_fusion.refs_7_.refs_6_
  28.8 1.9 collective-permute-start.3
  30.7 23.4 %collective-permute-start.2 = (f32[36,128]{1,0:T(8,128)S(1)}, f32[36,128]{1,0:T(8,128)S(1)}, u32[]{:S(2)}, u32[]{:S(2)}) collective-permute-start(f32[36,128]{1,0:T(8,128)S(1)} %slice.9.refs_2_.refs_1_), channel_id=1, source_target_pairs={{0,16},{16,32},{32,48},{48,2},{2,18},{18,34},{34,50},{50,4},{4,20}... | collective-permute-start | bytes 55304 | tf_op jit(solution)/shard_map/ppermute | solution.py:366
  54.2 0.1 pad_add_fusion
  54.2 0.1 copy.41
  54.3 0.6 pad.14.refs_6_.refs_5_
  54.9 0.0 copy-done.3
  54.9 0.6 pad.13.refs_5_.refs_4_
  55.5 0.0 collective-permute-done.1.refs_1_
  55.5 0.0 collective-permute-done.3.refs_4_.refs_3_
  55.6 0.0 copy-start.6
  55.6 0.1 collective-permute-done.2.refs_3_.refs_2_
  55.6 0.0 all-to-all-done.refs_0_
  55.6 0.5 copy-done.11
  56.2 0.0 copy-done.7
  56.2 0.8 copy-done.1
  57.0 3.3 %shard_map.73 = f32[4,112,128]{2,1,0:T(8,128)} custom-call(f32[8,144,128]{2,1,0:T(8,128)} %copy-done.1, f32[144,128]{1,0:T(8,128)} %copy-done.11, f32[36,128]{1,0:T(8,128)} %copy-done.3, f32[36,128]{1,0:T(8,128)} %copy-done.7, f32[36,128]{1,0:T(8,128)} %copy-done.6, s32[16,9]{1,0:T(8,128)} %pad.13.refs_5_.refs_4_, s32[16,8]{1,0:T(8,128)} %pad.14.refs_6_.refs_5_, ...), custom_call_target="tpu_custom_call" | custom-call | tf_op jit(solution)/shard_map/pallas_call | solution.py:387
  60.3 11.4 %all_to_all.52.refs_0_ = f32[4,112,128]{2,1,0:T(8,128)} all-to-all(f32[4,112,128]{2,1,0:T(8,128)} %shard_map.73), channel_id=1, replica_groups=mesh['zh'=2,'x'=4,'y'=4,'zl'=8,'c'=2] {'y'}, dimensions={0} | all-to-all | bytes 458752 | tf_op jit(solution)/shard_map/all_to_all | solution.py:398
  71.8 1.6 shard_map.74
  73.4 6.3 %collective-permute-start.4 = (f32[160,128]{1,0:T(8,128)}, f32[160,128]{1,0:T(8,128)S(1)}, u32[]{:S(2)}, u32[]{:S(2)}) collective-permute-start(f32[160,128]{1,0:T(8,128)} %get-tuple-element.24), channel_id=1, source_target_pairs={{0,2},{2,4},{4,6},{6,8},{8,10},{10,12},{12,14},{14,256},{256,258},... | collective-permute-start | bytes 245768 | tf_op jit(solution)/shard_map/ppermute | solution.py:403
  79.7 1.3 collective-permute-start.5
  81.0 1.1 collective-permute-done.4.refs_2_
  82.1 4.2 %collective-permute-done.5.refs_3_ = f32[160,128]{1,0:T(8,128)S(1)} collective-permute-done((f32[160,128]{1,0:T(8,128)}, f32[160,128]{1,0:T(8,128)S(1)}, u32[]{:S(2)}, u32[]{:S(2)}) %collective-permute-start.5) | collective-permute-done | bytes 81952 | tf_op jit(solution)/shard_map/ppermute | solution.py:404
  86.3 0.6 copy-done.5
  86.9 2.3 %shard_map.75 = (f32[16,9,128]{2,1,0:T(8,128)}, f32[16,9,128]{2,1,0:T(8,128)}, f32[16,9,128]{2,1,0:T(8,128)}, f32[16,9,128]{2,1,0:T(8,128)}, f32[16,128]{1,0:T(8,128)}, /*index=5*/f32[40,128]{1,0:T(8,128)}) custom-call(f32[4,112,128]{2,1,0:T(8,128)} %all_to_all.52.refs_0_, f32[4,36,128]{2,1,0:T(8,128)} %get-tuple-element.23.refs_1_, f32[160,128]{1,0:T(8,128)} %copy-done.4, ...), custom_call_target="tpu_custom_call" | custom-call | tf_op jit(solution)/shard_map/pallas_call | solution.py:408
  89.3 26.1 %all_to_all.53 = f32[16,1,128]{2,1,0:T(1,128)} all-to-all(f32[16,1,128]{2,1,0:T(1,128)} %bitcast.31), channel_id=1, replica_groups=mesh['zh'=2,'x'=4,'y'=4,'zl'=8,'c'=2] {'zh','zl'}, dimensions={0} | all-to-all | bytes 16384 | tf_op jit(solution)/shard_map/all_to_all | solution.py:415
  115.4 2.0 shard_map.76
  117.4 9.7 %all_to_all.54.q = f32[4,36,128]{2,1,0:T(8,128)} all-to-all(f32[4,36,128]{2,1,0:T(8,128)} %get-tuple-element.31.refs_4_), channel_id=1, replica_groups=mesh['zh'=2,'x'=4,'y'=4,'zl'=8,'c'=2] {'y'}, dimensions={0} | all-to-all | bytes 147456 | tf_op jit(solution)/shard_map/all_to_all | solution.py:424
  127.1 1.8 shard_map.77
  128.9 15.7 %all_to_all.55.refs_0_ = f32[8,144,128]{2,1,0:T(8,128)} all-to-all(f32[8,144,128]{2,1,0:T(8,128)} %shard_map.77), channel_id=1, replica_groups=mesh['zh'=2,'x'=4,'y'=4,'zl'=8,'c'=2] {'c','x'}, dimensions={0} | all-to-all | bytes 1179648 | tf_op jit(solution)/shard_map/all_to_all | solution.py:384
  144.6 3.1 %shard_map.78 = f32[4,112,128]{2,1,0:T(8,128)} custom-call(f32[8,144,128]{2,1,0:T(8,128)} %all_to_all.55.refs_0_, f32[36,128]{1,0:T(8,128)} %copy-done.3, f32[36,128]{1,0:T(8,128)} %copy-done.7, f32[36,128]{1,0:T(8,128)} %copy-done.6, s32[16,9]{1,0:T(8,128)} %pad.13.refs_5_.refs_4_, s32[16,8]{1,0:T(8,128)} %pad.14.refs_6_.refs_5_, ...), custom_call_target="tpu_custom_call" | custom-call | tf_op jit(solution)/shard_map/pallas_call | solution.py:387
  147.8 10.9 %all_to_all.56.refs_0_ = f32[4,112,128]{2,1,0:T(8,128)} all-to-all(f32[4,112,128]{2,1,0:T(8,128)} %shard_map.78), channel_id=1, replica_groups=mesh['zh'=2,'x'=4,'y'=4,'zl'=8,'c'=2] {'y'}, dimensions={0} | all-to-all | bytes 458752 | tf_op jit(solution)/shard_map/all_to_all | solution.py:398
  158.7 1.7 shard_map.79
  160.4 2.5 %collective-permute-start.6 = (f32[144,128]{1,0:T(8,128)}, f32[144,128]{1,0:T(8,128)S(1)}, u32[]{:S(2)}, u32[]{:S(2)}) collective-permute-start(f32[144,128]{1,0:T(8,128)} %get-tuple-element.34), channel_id=1, source_target_pairs={{0,2},{2,4},{4,6},{6,8},{8,10},{10,12},{12,14},{14,256},{256,258},... | collective-permute-start | bytes 221192 | tf_op jit(solution)/shard_map/ppermute | solution.py:403
  162.9 1.3 collective-permute-start.7
  164.2 1.0 collective-permute-done.6.refs_2_
  165.2 4.2 %collective-permute-done.7.refs_3_ = f32[144,128]{1,0:T(8,128)S(1)} collective-permute-done((f32[144,128]{1,0:T(8,128)}, f32[144,128]{1,0:T(8,128)S(1)}, u32[]{:S(2)}, u32[]{:S(2)}) %collective-permute-start.7) | collective-permute-done | bytes 73760 | tf_op jit(solution)/shard_map/ppermute | solution.py:404
  169.3 0.6 copy-done.10
  170.0 2.3 %shard_map.80 = (f32[16,9,128]{2,1,0:T(8,128)}, f32[16,9,128]{2,1,0:T(8,128)}, f32[16,9,128]{2,1,0:T(8,128)}, f32[16,9,128]{2,1,0:T(8,128)}, f32[16,128]{1,0:T(8,128)}) custom-call(f32[4,112,128]{2,1,0:T(8,128)} %all_to_all.56.refs_0_, f32[4,36,128]{2,1,0:T(8,128)} %get-tuple-element.33.refs_1_, f32[144,128]{1,0:T(8,128)} %copy-done.9, ...), custom_call_target="tpu_custom_call" | custom-call | tf_op jit(solution)/shard_map/pallas_call | solution.py:412
  172.3 17.8 %all_to_all.57 = f32[16,1,128]{2,1,0:T(1,128)} all-to-all(f32[16,1,128]{2,1,0:T(1,128)} %bitcast.32), channel_id=1, replica_groups=mesh['zh'=2,'x'=4,'y'=4,'zl'=8,'c'=2] {'zh','zl'}, dimensions={0} | all-to-all | bytes 16384 | tf_op jit(solution)/shard_map/all_to_all | solution.py:415
  190.0 1.9 shard_map.81
  192.0 9.0 %all_to_all.58 = f32[4,36,128]{2,1,0:T(8,128)S(1)} all-to-all(f32[4,36,128]{2,1,0:T(8,128)} %shard_map.81), channel_id=1, replica_groups=mesh['zh'=2,'x'=4,'y'=4,'zl'=8,'c'=2] {'y'}, dimensions={0} | all-to-all | bytes 147456 | tf_op jit(solution)/shard_map/all_to_all | solution.py:424
  201.0 4.6 %collective-permute-start.8 = (f32[4,36,128]{2,1,0:T(8,128)S(1)}, f32[4,36,128]{2,1,0:T(8,128)S(1)}, u32[]{:S(2)}, u32[]{:S(2)}) collective-permute-start(f32[4,36,128]{2,1,0:T(8,128)S(1)} %all_to_all.58), channel_id=1, source_target_pairs={{0,0},{16,1},{32,2},{48,3},{2,4},{18,5},{34,6},{50,7},{4,8},{20,9}... | collective-permute-start | bytes 221192 | tf_op jit(solution)/shard_map/ppermute | solution.py:427
  205.6 12.9 %collective-permute-done.8 = f32[4,36,128]{2,1,0:T(8,128)S(1)} collective-permute-done((f32[4,36,128]{2,1,0:T(8,128)S(1)}, f32[4,36,128]{2,1,0:T(8,128)S(1)}, u32[]{:S(2)}, u32[]{:S(2)}) %collective-permute-start.8) | collective-permute-done | bytes 73760 | tf_op jit(solution)/shard_map/ppermute | solution.py:427
  218.5 0.7 bitcast_add_fusion
  (28 shorter events, 0.2 us)
Async XLA Ops:
  0.0 27.2 %copy-start = (f32[96,8]{0,1:T(8,128)S(1)}, f32[96,8]{0,1:T(8,128)}, u32[]{:S(2)}) copy-start(f32[96,8]{0,1:T(8,128)} %param.13) | copy-start | bytes 9220
  0.0 0.8 copy-start.12
  0.0 1.5 copy-start.2
  1.6 15.5 %copy-start.8 = (f32[12,3,1,4,128]{4,3,2,1,0:T(4,128)S(1)}, f32[12,3,1,4,128]{4,3,2,1,0:T(4,128)}, u32[]{:S(2)}) copy-start(f32[12,3,1,4,128]{4,3,2,1,0:T(4,128)} %param.7) | copy-start | bytes 221188
  1.6 18.2 %collective-permute-start = (f32[180,128]{1,0:T(8,128)S(1)}, f32[180,128]{1,0:T(8,128)S(1)}, u32[]{:S(2)}, u32[]{:S(2)}) collective-permute-start(f32[180,128]{1,0:T(8,128)S(1)} %pad_maximum_fusion), channel_id=1, source_target_pairs={{0,0},{1,16},{2,32},{3,48},{4,2},{5,18},{6,34},{7,50},{8,4},{9,20}... | collective-permute-start | bytes 276488 | tf_op jit(solution)/shard_map/ppermute | solution.py:362
  17.1 38.4 %collective-permute-start.1 = (f32[144,128]{1,0:T(8,128)S(1)}, f32[144,128]{1,0:T(8,128)S(1)}, u32[]{:S(2)}, u32[]{:S(2)}) collective-permute-start(f32[144,128]{1,0:T(8,128)S(1)} %reshape.41), channel_id=1, source_target_pairs={{0,0},{1,16},{2,32},{3,48},{4,2},{5,18},{6,34},{7,50},{8,4},{9,20}... | collective-permute-start | bytes 221192 | tf_op jit(solution)/shard_map/ppermute | solution.py:363
  20.7 35.0 %all-to-all-start = ((f32[8,144,128]{2,1,0:T(8,128)}), f32[8,144,128]{2,1,0:T(8,128)S(1)}, u32[]{:S(2)}, u32[]{:S(2)}) async-start(f32[8,144,128]{2,1,0:T(8,128)} %broadcast_in_dim.41), calls=%async_computation | async-start | bytes 1179648 | tf_op jit(solution)/shard_map/all_to_all | solution.py:384
  27.3 0.7 copy-start.13
  27.3 0.7 copy-start.14
  28.8 26.1 %copy-start.3 = (f32[36,128]{1,0:T(8,128)}, f32[36,128]{1,0:T(8,128)S(1)}, u32[]{:S(2)}) copy-start(f32[36,128]{1,0:T(8,128)S(1)} %slice.9.refs_2_.refs_1_) | copy-start | bytes 55300
  28.8 26.8 %collective-permute-start.3 = (f32[36,128]{1,0:T(8,128)S(1)}, f32[36,128]{1,0:T(8,128)S(1)}, u32[]{:S(2)}, u32[]{:S(2)}) collective-permute-start(f32[36,128]{1,0:T(8,128)S(1)} %slice.9.refs_2_.refs_1_), channel_id=1, source_target_pairs={{16,0},{32,16},{48,32},{2,48},{18,2},{34,18},{50,34},{4,50},{20,4}... | collective-permute-start | bytes 55304 | tf_op jit(solution)/shard_map/ppermute | solution.py:367
  30.7 24.9 %collective-permute-start.2 = (f32[36,128]{1,0:T(8,128)S(1)}, f32[36,128]{1,0:T(8,128)S(1)}, u32[]{:S(2)}, u32[]{:S(2)}) collective-permute-start(f32[36,128]{1,0:T(8,128)S(1)} %slice.9.refs_2_.refs_1_), channel_id=1, source_target_pairs={{0,16},{16,32},{32,48},{48,2},{2,18},{18,34},{34,50},{50,4},{4,20}... | collective-permute-start | bytes 55304 | tf_op jit(solution)/shard_map/ppermute | solution.py:366
  55.5 0.6 copy-start.11
  55.6 0.6 copy-start.6
  55.6 0.6 copy-start.7
  56.2 0.8 copy-start.1
  73.4 8.7 %collective-permute-start.4 = (f32[160,128]{1,0:T(8,128)}, f32[160,128]{1,0:T(8,128)S(1)}, u32[]{:S(2)}, u32[]{:S(2)}) collective-permute-start(f32[160,128]{1,0:T(8,128)} %get-tuple-element.24), channel_id=1, source_target_pairs={{0,2},{2,4},{4,6},{6,8},{8,10},{10,12},{12,14},{14,256},{256,258},... | collective-permute-start | bytes 245768 | tf_op jit(solution)/shard_map/ppermute | solution.py:403
  79.7 6.5 %collective-permute-start.5 = (f32[160,128]{1,0:T(8,128)}, f32[160,128]{1,0:T(8,128)S(1)}, u32[]{:S(2)}, u32[]{:S(2)}) collective-permute-start(f32[160,128]{1,0:T(8,128)} %get-tuple-element.25), channel_id=1, source_target_pairs={{2,0},{4,2},{6,4},{8,6},{10,8},{12,10},{14,12},{256,14},{258,256},... | collective-permute-start | bytes 245768 | tf_op jit(solution)/shard_map/ppermute | solution.py:404
  82.1 4.2 %copy-start.4 = (f32[160,128]{1,0:T(8,128)}, f32[160,128]{1,0:T(8,128)S(1)}, u32[]{:S(2)}) copy-start(f32[160,128]{1,0:T(8,128)S(1)} %collective-permute-done.4.refs_2_) | copy-start | bytes 245764
  86.3 0.6 copy-start.5
  160.4 4.8 %collective-permute-start.6 = (f32[144,128]{1,0:T(8,128)}, f32[144,128]{1,0:T(8,128)S(1)}, u32[]{:S(2)}, u32[]{:S(2)}) collective-permute-start(f32[144,128]{1,0:T(8,128)} %get-tuple-element.34), channel_id=1, source_target_pairs={{0,2},{2,4},{4,6},{6,8},{8,10},{10,12},{12,14},{14,256},{256,258},... | collective-permute-start | bytes 221192 | tf_op jit(solution)/shard_map/ppermute | solution.py:403
  162.9 6.5 %collective-permute-start.7 = (f32[144,128]{1,0:T(8,128)}, f32[144,128]{1,0:T(8,128)S(1)}, u32[]{:S(2)}, u32[]{:S(2)}) collective-permute-start(f32[144,128]{1,0:T(8,128)} %get-tuple-element.35), channel_id=1, source_target_pairs={{2,0},{4,2},{6,4},{8,6},{10,8},{12,10},{14,12},{256,14},{258,256},... | collective-permute-start | bytes 221192 | tf_op jit(solution)/shard_map/ppermute | solution.py:404
  165.1 4.2 %copy-start.9 = (f32[144,128]{1,0:T(8,128)}, f32[144,128]{1,0:T(8,128)S(1)}, u32[]{:S(2)}) copy-start(f32[144,128]{1,0:T(8,128)S(1)} %collective-permute-done.6.refs_2_) | copy-start | bytes 221188
  169.3 0.6 copy-start.10
  201.0 17.4 %collective-permute-start.8 = (f32[4,36,128]{2,1,0:T(8,128)S(1)}, f32[4,36,128]{2,1,0:T(8,128)S(1)}, u32[]{:S(2)}, u32[]{:S(2)}) collective-permute-start(f32[4,36,128]{2,1,0:T(8,128)S(1)} %all_to_all.58), channel_id=1, source_target_pairs={{0,0},{16,1},{32,2},{48,3},{2,4},{18,5},{34,6},{50,7},{4,8},{20,9}... | collective-permute-start | bytes 221192 | tf_op jit(solution)/shard_map/ppermute | solution.py:427

commit v2 on v1

--- a/solution.py
+++ b/solution.py
@@ -8,9 +8,10 @@
 from jax.sharding import Mesh
 from jax.sharding import PartitionSpec as P
 
-AXES = ("zh", "x", "y", "zl", "c")
-GROUPS = ("c", "x")
-DEPTH = ("zh", "zl")
+AXES = ("zh", "x", "y", "zp", "zq", "c")
+SLABS = ("y", "zp", "zq", "c")
+CHUNKS = ("y", "zp")
+WITHIN = ("zq", "c")
 NG, NM, NL, NK = 8, 12, 8, 8
 NY, NZ, SHIFT = 4, 128, 4.0
 QUAD = 4
@@ -20,33 +21,8 @@
 F32 = jnp.float32
 
 
-def flat(zh, x, y, zl, c):
-    return (((zh * 4 + x) * 4 + y) * 8 + zl) * 2 + c
-
-
-def moves():
-    pairs = []
-    for zh in range(2):
-        for x in range(4):
-            for y in range(4):
-                for zl in range(8):
-                    for c in range(2):
-                        s = y * 16 + zl * 2 + c
-                        z = s // 4
-                        pairs.append((flat(zh, x, y, zl, c), flat(z // 8, x, s % 4, z % 8, zh)))
-    return pairs
-
-
-def slab_steps(step):
-    def place(s):
-        z = s // 4
-        return ((z // 8) * 4 + s % 4) * 8 + z % 8
-
-    return [(place(s), place(s + step)) for s in range(64) if 0 <= s + step < 64]
-
-
-def depth_steps(step):
-    return [(z, z + step) for z in range(16) if 0 <= z + step < 16]
+def line(count, step):
+    return [(i, i + step) for i in range(count) if 0 <= i + step < count]
 
 
 def call(kernel, outs, scratch=()):
@@ -64,12 +40,13 @@
 def coupling_kernel(nk, *refs):
     first = nk > NK
     if first:
-        (u, load, e0, em, ep, partner, variable, weight, out, us, mx, fx, fy, fz) = refs
+        (near, far, load, e0, em, ep, partner, variable, weight, out, us, mx, fx, fy, fz) = refs
     else:
-        (u, e0, em, ep, partner, variable, weight, out, us, mx, fx, fy, fz) = refs
+        (near, far, e0, em, ep, partner, variable, weight, out, us, mx, fx, fy, fz) = refs
     for g in range(NG):
         for yc in range(NY * 3):
-            us[yc, g * NM : (g + 1) * NM, :] = u[g, yc * NM : (yc + 1) * NM, :]
+            half = near if g < NG // 2 else far
+            us[yc, g * NM : (g + 1) * NM, :] = half[g % (NG // 2), yc * NM : (yc + 1) * NM, :]
     lane = lax.broadcasted_iota(jnp.int32, (16, NG * NM), 1)
     pr, vr, wr = partner[...], variable[...], weight[...]
     links = NL + 1 if first else NL
@@ -338,15 +315,16 @@
             out[s, rows, :] = change
 
 
-def spread_kernel(q, out):
+def merge_kernel(q, out, copies):
     for y in range(NY):
         for c in range(3):
             for d in range(QUAD):
                 at = y * ROWS + c * TRI
                 piece = q[d, at : at + TRI, :]
                 to = (y * 3 + c) * NM + d * TRI
-                for g in range(NG):
-                    out[g, to : to + TRI, :] = piece
+                out[to : to + TRI, :] = piece
+                for g in range(NG // 2):
+                    copies[g, to : to + TRI, :] = piece
 
 
 def packed(field):
@@ -357,32 +335,34 @@
     mean = jnp.where(region_labels == 0, 1.3, jnp.where(region_labels == 1, 1.0, 0.6)).astype(F32)
     varying = jnp.where(region_labels[None] == 1, kl_fields, 0.0)
     moduli = jnp.concatenate([varying, mean[None]], 0).reshape((NK + 1) * NY, NZ)
-    there = moves()
-    back = [(b, a) for a, b in there]
-    guess = lax.ppermute(jnp.concatenate([packed(first_guess), moduli], 0), AXES, there)
-    load = lax.ppermute(packed(load_modes), AXES, there)
-    e0 = guess[NY * 3 * NM :]
-    guess = guess[: NY * 3 * NM]
-    em = lax.ppermute(e0, ("zh", "y", "zl"), slab_steps(1))
-    ep = lax.ppermute(e0, ("zh", "y", "zl"), slab_steps(-1))
-
-    offset = (lax.axis_index("c") * 4 + lax.axis_index("x")) * NM
-    own = offset + jnp.arange(NM, dtype=jnp.int32)[:, None]
+    e0 = moduli
+    em = lax.ppermute(e0, SLABS, line(64, 1))
+    ep = lax.ppermute(e0, SLABS, line(64, -1))
+    load = packed(load_modes)
+    mine = packed(first_guess)
+    copies = jnp.broadcast_to(mine[None], (NG // 2,) + mine.shape)
+
+    half = lax.axis_index("zh") * (NG // 2 * NM)
+    offset = half + lax.axis_index("x") * NM
+    modes = NG * NM
+    own = offset - half + jnp.arange(NM, dtype=jnp.int32)[:, None]
     pad = ((0, 16 - NM), (0, 0))
-    rows_partner = lax.dynamic_slice_in_dim(partner, offset, NM, 0)
+    rows_partner = (lax.dynamic_slice_in_dim(partner, offset, NM, 0) + modes - half) % modes
     rows_partner = jnp.pad(jnp.concatenate([rows_partner, own], 1), pad, constant_values=-1)
     rows_variable = jnp.pad(lax.dynamic_slice_in_dim(variable, offset, NM, 0), pad)
     rows_weight = lax.dynamic_slice_in_dim(weight, offset, NM, 0)
     rows_weight = jnp.pad(jnp.concatenate([rows_weight, jnp.ones((NM, 1), F32)], 1), pad)
     links = (rows_partner, rows_variable, rows_weight)
 
-    spread = jnp.broadcast_to(guess[None], (NG,) + guess.shape)
     chunk, cells = (QUAD, SLAB, NZ), (QUAD * NY, ROWS, NZ)
     for sweep in range(2):
         first = sweep == 0
         nk = NK + 1 if first else NK
-        gathered = lax.all_to_all(spread, GROUPS, 0, 0, tiled=True)
-        fields = (gathered, load, e0, em, ep) if first else (gathered, e0, em, ep)
+        far = lax.ppermute(mine, "zh", [(0, 1), (1, 0)])
+        near = lax.all_to_all(copies, "x", 0, 0, tiled=True)
+        far = jnp.broadcast_to(far[None], (NG // 2,) + far.shape)
+        far = lax.all_to_all(far, "x", 0, 0, tiled=True)
+        fields = (near, far, load, e0, em, ep) if first else (near, far, e0, em, ep)
         face_rows = ((NK + 1) * NY, NZ)
         (sent,) = call(
             functools.partial(coupling_kernel, nk),
@@ -395,13 +375,13 @@
                 (5,) + face_rows,
             ],
         )(*fields, *links)
-        q = lax.all_to_all(sent, "y", 0, 0, tiled=True)
+        q = lax.all_to_all(sent, WITHIN, 0, 0, tiled=True)
         edge = (4 * SLAB + 16 if first else 4 * SLAB, NZ)
         chunk_r, up, down = call(functools.partial(edges_kernel, first), [chunk, edge, edge])(
             *((q,) if first else (q, rest))
         )
-        low = lax.ppermute(up, DEPTH, depth_steps(1))
-        high = lax.ppermute(down, DEPTH, depth_steps(-1))
+        low = lax.ppermute(up, CHUNKS, line(16, 1))
+        high = lax.ppermute(down, CHUNKS, line(16, -1))
         scratch = [(10 * NY, ROWS, NZ)] * 4
         outs = [cells] * 4 + [(16, NZ)]
         if first:
@@ -412,7 +392,7 @@
             v0, v1, v2, v3, mom = call(functools.partial(powers_kernel, False), outs, scratch)(
                 q, chunk_r, low, high, ec
             )
-        mom = lax.all_to_all(mom, DEPTH, 0, 0, tiled=True)
+        mom = lax.all_to_all(mom, CHUNKS, 0, 0, tiled=True)
         if first:
             change, rest = call(functools.partial(update_kernel, True), [chunk, chunk])(
                 mom, v0, v1, v2, v3
@@ -421,17 +401,17 @@
             (change,) = call(functools.partial(update_kernel, False), [chunk])(
                 mom, v0, v1, v2, change
             )
-        by_slab = lax.all_to_all(change, "y", 0, 0, tiled=True)
+        by_slab = lax.all_to_all(change, WITHIN, 0, 0, tiled=True)
         if first:
-            (spread,) = call(spread_kernel, [(NG, NY * 3 * NM, NZ)])(by_slab)
-    total = lax.ppermute(by_slab, AXES, back)
-    total = total.reshape(QUAD, NY, 3, TRI, NZ).transpose(0, 3, 2, 1, 4)
+            rows = (NY * 3 * NM, NZ)
+            mine, copies = call(merge_kernel, [rows, (NG // 2,) + rows])(by_slab)
+    total = by_slab.reshape(QUAD, NY, 3, TRI, NZ).transpose(0, 3, 2, 1, 4)
     return first_guess + total.reshape(NM, 3, 1, NY, NZ)
 
 
 def solution(mesh):
-    split = Mesh(mesh.devices.reshape(2, 4, 4, 8, 2), AXES)
-    mode, space = ("zh", "x"), ("y", "zl", "c")
+    split = Mesh(mesh.devices.reshape(2, 4, 4, 4, 2, 2), AXES)
+    mode, space = ("zh", "x"), SLABS
     return jax.shard_map(
         shards,
         mesh=split,

time: 220 us -> 216 us (0.982)
  the two profiles are of different devices: /device:TPU:16 before, /device:TPU:1 now
where the time goes in v2:
time: 216 us; the launch traced here: 215 us
  blocking collectives  105 us (49%)
  starting transfers between devices  47 us (22%)
  waiting for transfers between devices  32.6 us (15%)
  Pallas kernels  19.9 us (9%)
  local copies, waits for them, and re-layouts  6.58 us (3%)
  other arithmetic  2.85 us (1%)
    all_to_all x2, blocking collectives, shards(): mom = lax.all_to_all(mom, CHUNKS, 0, 0, tiled=True)  51.2 us
    all_to_all x2, blocking collectives, shards(): q = lax.all_to_all(sent, WITHIN, 0, 0, tiled=True)  22.7 us
    all_to_all x2, blocking collectives, shards(): by_slab = lax.all_to_all(change, WITHIN, 0, 0, tiled=True)  21.4 us
    ppermute x2, starting transfers between devices, shards(): far = lax.ppermute(mine, 'zh', [(0, 1), (1, 0)])  17.2 us
    ppermute x2, waiting for transfers between devices, shards(): high = lax.ppermute(down, CHUNKS, line(16, -1))  12.1 us
    ppermute x2, waiting for transfers between devices, shards(): far = lax.ppermute(mine, 'zh', [(0, 1), (1, 0)])  10.2 us
    all_to_all x1, blocking collectives, shards(): far = lax.all_to_all(far, 'x', 0, 0, tiled=True)  10.1 us
    ppermute x1, starting transfers between devices, shards(): ep = lax.ppermute(e0, SLABS, line(64, -1))  8.79 us
  transfers between devices with their start and end apart: 11, of which 7 were waited for; matrix products, arithmetic and copies ran while one was open for 2% of the time, Pallas kernels for 0%

profile of v2, /device:TPU:1, one launch (start us, length us, event | category | flops | bytes accessed | tf_op | source)
XLA Modules:
  0.0 214.7 jit_solution(9550664594455618973)
XLA Ops:
  0.0 0.0 copy-start
  0.0 0.8 fusion
  0.8 0.7 broadcast_select_fusion
  1.5 8.8 %collective-permute-start.2 = (f32[36,128]{1,0:T(8,128)S(1)}, f32[36,128]{1,0:T(8,128)S(1)}, u32[]{:S(2)}, u32[]{:S(2)}) collective-permute-start(f32[36,128]{1,0:T(8,128)S(1)} %reshape.40.refs_3_.refs_2_), channel_id=1, source_target_pairs={{1,0},{2,1},{3,2},{4,3},{5,4},{6,5},{7,6},{8,7},{9,8},{10,9},{11,1... | collective-permute-start | bytes 55304 | tf_op jit(solution)/shard_map/ppermute | solution.py:340
  10.3 1.9 collective-permute-start.1
  12.3 0.0 copy-done.5
  12.3 11.1 %collective-permute-start = (f32[144,128]{1,0:T(8,128)S(1)}, f32[144,128]{1,0:T(8,128)S(1)}, u32[]{:S(2)}, u32[]{:S(2)}) collective-permute-start(f32[144,128]{1,0:T(8,128)S(1)} %broadcast_in_dim.48), channel_id=1, source_target_pairs={{0,256},{256,0},{1,257},{257,1},{2,258},{258,2},{3,259},{259,3},{4... | collective-permute-start | bytes 221192 | tf_op jit(solution)/shard_map/ppermute | solution.py:361
  23.4 0.7 broadcast_in_dim.49
  24.2 4.0 %all-to-all-start = ((f32[4,144,128]{2,1,0:T(8,128)}), f32[4,144,128]{2,1,0:T(8,128)S(1)}, u32[]{:S(2)}, u32[]{:S(2)}) async-start(f32[4,144,128]{2,1,0:T(8,128)} %broadcast_in_dim.49), calls=%async_computation | async-start | bytes 589824 | tf_op jit(solution)/shard_map/all_to_all | solution.py:362
  28.2 0.7 copy-done.15
  28.9 0.0 copy-done.14
  28.9 0.1 constant_dynamic-slice_fusion.1
  29.0 0.1 copy.39
  29.1 0.0 copy-done
  29.1 0.1 constant_dynamic-slice_fusion
  29.2 0.1 copy.41
  29.2 0.0 collective-permute-done
  29.2 6.1 %all-to-all-done.refs_0_ = f32[4,144,128]{2,1,0:T(8,128)S(1)} async-done(((f32[4,144,128]{2,1,0:T(8,128)}), f32[4,144,128]{2,1,0:T(8,128)S(1)}, u32[]{:S(2)}, u32[]{:S(2)}) %all-to-all-start) | async-done | bytes 294944 | tf_op jit(solution)/shard_map/all_to_all | solution.py:362
  35.4 0.8 broadcast_in_dim.50
  36.1 0.1 copy-done.2
  36.2 3.5 %all-to-all-start.1 = ((f32[4,144,128]{2,1,0:T(8,128)}), f32[4,144,128]{2,1,0:T(8,128)S(1)}, u32[]{:S(2)}, u32[]{:S(2)}) async-start(f32[4,144,128]{2,1,0:T(8,128)} %broadcast_in_dim.50), calls=%async_computation.1 | async-start | bytes 589824 | tf_op jit(solution)/shard_map/all_to_all | solution.py:364
  39.7 0.0 copy-start.10
  39.7 0.6 pad_select_fusion.refs_8_.refs_7_
  40.3 0.1 pad_add_fusion
  40.3 0.1 copy.40
  40.4 0.6 pad.14.refs_7_.refs_6_
  41.0 0.6 reshape.39.refs_2_
  41.7 0.6 pad.13.refs_6_.refs_5_
  42.3 0.0 collective-permute-done.2.refs_5_.refs_4_
  42.3 0.0 collective-permute-done.1.refs_4_.refs_3_
  42.3 3.3 %all-to-all-done.1.refs_1_ = f32[4,144,128]{2,1,0:T(8,128)S(1)} async-done(((f32[4,144,128]{2,1,0:T(8,128)}), f32[4,144,128]{2,1,0:T(8,128)S(1)}, u32[]{:S(2)}, u32[]{:S(2)}) %all-to-all-start.1) | async-done | bytes 294944 | tf_op jit(solution)/shard_map/all_to_all | solution.py:364
  45.6 0.7 copy-done.3
  46.3 3.2 %shard_map.73 = f32[4,112,128]{2,1,0:T(8,128)} custom-call(f32[4,144,128]{2,1,0:T(8,128)} %copy-done.2, f32[4,144,128]{2,1,0:T(8,128)} %copy-done.3, f32[144,128]{1,0:T(8,128)} %reshape.39.refs_2_, f32[36,128]{1,0:T(8,128)} %copy-done.5, f32[36,128]{1,0:T(8,128)} %copy-done.9, f32[36,128]{1,0:T(8,128)} %copy-done.8, s32[16,9]{1,0:T(8,128)} %pad.13.refs_6_.refs_5_, ...), custom_call_target="tpu_custom_call" | custom-call | tf_op jit(solution)/shard_map/pallas_call | solution.py:367
  49.6 10.8 %all_to_all.62.refs_0_ = f32[4,112,128]{2,1,0:T(8,128)} all-to-all(f32[4,112,128]{2,1,0:T(8,128)} %shard_map.73), channel_id=1, replica_groups=mesh['zh'=2,'x'=4,'y'=4,'zp'=4,'zq'=2,'c'=2] {'zq','c'}, dimensions={0} | all-to-all | bytes 458752 | tf_op jit(solution)/shard_map/all_to_all | solution.py:378
  60.4 1.7 shard_map.74
  62.0 3.1 %collective-permute-start.3 = (f32[160,128]{1,0:T(8,128)}, f32[160,128]{1,0:T(8,128)S(1)}, u32[]{:S(2)}, u32[]{:S(2)}) collective-permute-start(f32[160,128]{1,0:T(8,128)} %get-tuple-element.26), channel_id=1, source_target_pairs={{0,4},{4,8},{8,12},{12,16},{16,20},{20,24},{24,28},{28,32},{32,36}... | collective-permute-start | bytes 245768 | tf_op jit(solution)/shard_map/ppermute | solution.py:383
  65.1 1.3 collective-permute-start.4
  66.4 0.5 collective-permute-done.3.refs_2_
  66.9 6.8 %collective-permute-done.4.refs_3_ = f32[160,128]{1,0:T(8,128)S(1)} collective-permute-done((f32[160,128]{1,0:T(8,128)}, f32[160,128]{1,0:T(8,128)S(1)}, u32[]{:S(2)}, u32[]{:S(2)}) %collective-permute-start.4) | collective-permute-done | bytes 81952 | tf_op jit(solution)/shard_map/ppermute | solution.py:384
  73.7 0.6 copy-done.7
  74.3 2.3 %shard_map.75 = (f32[16,9,128]{2,1,0:T(8,128)}, f32[16,9,128]{2,1,0:T(8,128)}, f32[16,9,128]{2,1,0:T(8,128)}, f32[16,9,128]{2,1,0:T(8,128)}, f32[16,128]{1,0:T(8,128)}, /*index=5*/f32[40,128]{1,0:T(8,128)}) custom-call(f32[4,112,128]{2,1,0:T(8,128)} %all_to_all.62.refs_0_, f32[4,36,128]{2,1,0:T(8,128)} %get-tuple-element.25.refs_1_, f32[160,128]{1,0:T(8,128)} %copy-done.6, ...), custom_call_target="tpu_custom_call" | custom-call | tf_op jit(solution)/shard_map/pallas_call | solution.py:388
  76.6 26.2 %all_to_all.63 = f32[16,1,128]{2,1,0:T(1,128)} all-to-all(f32[16,1,128]{2,1,0:T(1,128)} %bitcast.31), channel_id=1, replica_groups=mesh['zh'=2,'x'=4,'y'=4,'zp'=4,'zq'=2,'c'=2] {'y','zp'}, dimensions={0} | all-to-all | bytes 16384 | tf_op jit(solution)/shard_map/all_to_all | solution.py:395
  102.8 2.0 shard_map.76
  104.8 11.2 %all_to_all.64.q = f32[4,36,128]{2,1,0:T(8,128)} all-to-all(f32[4,36,128]{2,1,0:T(8,128)} %get-tuple-element.33.refs_4_), channel_id=1, replica_groups=mesh['zh'=2,'x'=4,'y'=4,'zp'=4,'zq'=2,'c'=2] {'zq','c'}, dimensions={0} | all-to-all | bytes 147456 | tf_op jit(solution)/shard_map/all_to_all | solution.py:404
  116.0 1.7 shard_map.77
  117.7 3.6 %all-to-all-start.5 = ((f32[4,144,128]{2,1,0:T(8,128)}), f32[4,144,128]{2,1,0:T(8,128)S(1)}, u32[]{:S(2)}, u32[]{:S(2)}) async-start(f32[4,144,128]{2,1,0:T(8,128)} %get-tuple-element.34), calls=%async_computation.5 | async-start | bytes 589824 | tf_op jit(solution)/shard_map/all_to_all | solution.py:362
  121.3 6.1 %collective-permute-start.5 = (f32[144,128]{1,0:T(8,128)S(1)}, f32[144,128]{1,0:T(8,128)S(1)}, u32[]{:S(2)}, u32[]{:S(2)}) collective-permute-start(f32[144,128]{1,0:T(8,128)S(1)} %copy-done.16), channel_id=1, source_target_pairs={{0,256},{256,0},{1,257},{257,1},{2,258},{258,2},{3,259},{259,3},{4... | collective-permute-start | bytes 221192 | tf_op jit(solution)/shard_map/ppermute | solution.py:361
  127.4 10.2 %collective-permute-done.5 = f32[144,128]{1,0:T(8,128)S(1)} collective-permute-done((f32[144,128]{1,0:T(8,128)S(1)}, f32[144,128]{1,0:T(8,128)S(1)}, u32[]{:S(2)}, u32[]{:S(2)}) %collective-permute-start.5) | collective-permute-done | bytes 73760 | tf_op jit(solution)/shard_map/ppermute | solution.py:361
  137.6 0.0 all-to-all-done.5.refs_0_
  137.6 10.1 %all_to_all.65.refs_1_ = f32[4,144,128]{2,1,0:T(8,128)} all-to-all(f32[4,144,128]{2,1,0:T(8,128)S(1)} %broadcast_in_dim.57), channel_id=1, replica_groups=mesh['zh'=2,'x'=4,'y'=4,'zp'=4,'zq'=2,'c'=2] {'x'}, dimensions={0} | all-to-all | bytes 589824 | tf_op jit(solution)/shard_map/all_to_all | solution.py:364
  147.7 0.0 copy-done.1
  147.7 3.1 %shard_map.78 = f32[4,112,128]{2,1,0:T(8,128)} custom-call(f32[4,144,128]{2,1,0:T(8,128)} %copy-done.1, f32[4,144,128]{2,1,0:T(8,128)} %all_to_all.65.refs_1_, f32[36,128]{1,0:T(8,128)} %copy-done.5, f32[36,128]{1,0:T(8,128)} %copy-done.9, f32[36,128]{1,0:T(8,128)} %copy-done.8, s32[16,9]{1,0:T(8,128)} %pad.13.refs_6_.refs_5_, s32[16,8]{1,0:T(8,128)} %pad.14.refs_7_.refs_6_, ...), custom_call_target="tpu_custom_call" | custom-call | tf_op jit(solution)/shard_map/pallas_call | solution.py:367
  150.8 12.0 %all_to_all.66.refs_0_ = f32[4,112,128]{2,1,0:T(8,128)} all-to-all(f32[4,112,128]{2,1,0:T(8,128)} %shard_map.78), channel_id=1, replica_groups=mesh['zh'=2,'x'=4,'y'=4,'zp'=4,'zq'=2,'c'=2] {'zq','c'}, dimensions={0} | all-to-all | bytes 458752 | tf_op jit(solution)/shard_map/all_to_all | solution.py:378
  162.7 1.7 shard_map.79
  164.4 2.4 %collective-permute-start.6 = (f32[144,128]{1,0:T(8,128)}, f32[144,128]{1,0:T(8,128)S(1)}, u32[]{:S(2)}, u32[]{:S(2)}) collective-permute-start(f32[144,128]{1,0:T(8,128)} %get-tuple-element.38), channel_id=1, source_target_pairs={{0,4},{4,8},{8,12},{12,16},{16,20},{20,24},{24,28},{28,32},{32,36}... | collective-permute-start | bytes 221192 | tf_op jit(solution)/shard_map/ppermute | solution.py:383
  166.9 1.3 collective-permute-start.7
  168.2 0.4 collective-permute-done.6.refs_2_
  168.6 5.3 %collective-permute-done.7.refs_3_ = f32[144,128]{1,0:T(8,128)S(1)} collective-permute-done((f32[144,128]{1,0:T(8,128)}, f32[144,128]{1,0:T(8,128)S(1)}, u32[]{:S(2)}, u32[]{:S(2)}) %collective-permute-start.7) | collective-permute-done | bytes 73760 | tf_op jit(solution)/shard_map/ppermute | solution.py:384
  173.9 0.6 copy-done.12
  174.5 2.3 %shard_map.80 = (f32[16,9,128]{2,1,0:T(8,128)}, f32[16,9,128]{2,1,0:T(8,128)}, f32[16,9,128]{2,1,0:T(8,128)}, f32[16,9,128]{2,1,0:T(8,128)}, f32[16,128]{1,0:T(8,128)}) custom-call(f32[4,112,128]{2,1,0:T(8,128)} %all_to_all.66.refs_0_, f32[4,36,128]{2,1,0:T(8,128)} %get-tuple-element.37.refs_1_, f32[144,128]{1,0:T(8,128)} %copy-done.11, ...), custom_call_target="tpu_custom_call" | custom-call | tf_op jit(solution)/shard_map/pallas_call | solution.py:392
  176.8 25.1 %all_to_all.67 = f32[16,1,128]{2,1,0:T(1,128)} all-to-all(f32[16,1,128]{2,1,0:T(1,128)} %bitcast.32), channel_id=1, replica_groups=mesh['zh'=2,'x'=4,'y'=4,'zp'=4,'zq'=2,'c'=2] {'y','zp'}, dimensions={0} | all-to-all | bytes 16384 | tf_op jit(solution)/shard_map/all_to_all | solution.py:395
  201.9 1.9 shard_map.81
  203.8 10.2 %all_to_all.68 = f32[4,36,128]{2,1,0:T(8,128)S(1)} all-to-all(f32[4,36,128]{2,1,0:T(8,128)} %shard_map.81), channel_id=1, replica_groups=mesh['zh'=2,'x'=4,'y'=4,'zp'=4,'zq'=2,'c'=2] {'zq','c'}, dimensions={0} | all-to-all | bytes 147456 | tf_op jit(solution)/shard_map/all_to_all | solution.py:404
  214.0 0.7 bitcast_add_fusion
  (34 shorter events, 0.2 us)
Async XLA Ops:
  0.0 29.1 %copy-start = (f32[96,8]{0,1:T(8,128)S(1)}, f32[96,8]{0,1:T(8,128)}, u32[]{:S(2)}) copy-start(f32[96,8]{0,1:T(8,128)} %param.13) | copy-start | bytes 9220
  0.0 0.8 copy-start.13
  0.0 12.3 %copy-start.4 = (f32[12,3,1,4,128]{4,3,2,1,0:T(4,128)S(1)}, f32[12,3,1,4,128]{4,3,2,1,0:T(4,128)}, u32[]{:S(2)}) copy-start(f32[12,3,1,4,128]{4,3,2,1,0:T(4,128)} %param.8) | copy-start | bytes 221188
  1.5 10.8 %copy-start.5 = (f32[36,128]{1,0:T(8,128)}, f32[36,128]{1,0:T(8,128)S(1)}, u32[]{:S(2)}) copy-start(f32[36,128]{1,0:T(8,128)S(1)} %reshape.40.refs_3_.refs_2_) | copy-start | bytes 55300
  1.5 40.8 %collective-permute-start.2 = (f32[36,128]{1,0:T(8,128)S(1)}, f32[36,128]{1,0:T(8,128)S(1)}, u32[]{:S(2)}, u32[]{:S(2)}) collective-permute-start(f32[36,128]{1,0:T(8,128)S(1)} %reshape.40.refs_3_.refs_2_), channel_id=1, source_target_pairs={{1,0},{2,1},{3,2},{4,3},{5,4},{6,5},{7,6},{8,7},{9,8},{10,9},{11,1... | collective-permute-start | bytes 55304 | tf_op jit(solution)/shard_map/ppermute | solution.py:340
  10.3 32.0 %collective-permute-start.1 = (f32[36,128]{1,0:T(8,128)S(1)}, f32[36,128]{1,0:T(8,128)S(1)}, u32[]{:S(2)}, u32[]{:S(2)}) collective-permute-start(f32[36,128]{1,0:T(8,128)S(1)} %reshape.40.refs_3_.refs_2_), channel_id=1, source_target_pairs={{0,1},{1,2},{2,3},{3,4},{4,5},{5,6},{6,7},{7,8},{8,9},{9,10},{10,1... | collective-permute-start | bytes 55304 | tf_op jit(solution)/shard_map/ppermute | solution.py:339
  12.3 16.9 %collective-permute-start = (f32[144,128]{1,0:T(8,128)S(1)}, f32[144,128]{1,0:T(8,128)S(1)}, u32[]{:S(2)}, u32[]{:S(2)}) collective-permute-start(f32[144,128]{1,0:T(8,128)S(1)} %broadcast_in_dim.48), channel_id=1, source_target_pairs={{0,256},{256,0},{1,257},{257,1},{2,258},{258,2},{3,259},{259,3},{4... | collective-permute-start | bytes 221192 | tf_op jit(solution)/shard_map/ppermute | solution.py:361
  24.2 11.2 %all-to-all-start = ((f32[4,144,128]{2,1,0:T(8,128)}), f32[4,144,128]{2,1,0:T(8,128)S(1)}, u32[]{:S(2)}, u32[]{:S(2)}) async-start(f32[4,144,128]{2,1,0:T(8,128)} %broadcast_in_dim.49), calls=%async_computation | async-start | bytes 589824 | tf_op jit(solution)/shard_map/all_to_all | solution.py:362
  28.2 0.7 copy-start.15
  28.2 0.7 copy-start.14
  35.4 0.8 copy-start.2
  36.2 9.4 %all-to-all-start.1 = ((f32[4,144,128]{2,1,0:T(8,128)}), f32[4,144,128]{2,1,0:T(8,128)S(1)}, u32[]{:S(2)}, u32[]{:S(2)}) async-start(f32[4,144,128]{2,1,0:T(8,128)} %broadcast_in_dim.50), calls=%async_computation.1 | async-start | bytes 589824 | tf_op jit(solution)/shard_map/all_to_all | solution.py:364
  39.7 1.4 copy-start.10
  42.3 3.3 %copy-start.8 = (f32[36,128]{1,0:T(8,128)}, f32[36,128]{1,0:T(8,128)S(1)}, u32[]{:S(2)}) copy-start(f32[36,128]{1,0:T(8,128)S(1)} %collective-permute-done.2.refs_5_.refs_4_) | copy-start | bytes 55300
  42.3 3.3 %copy-start.9 = (f32[36,128]{1,0:T(8,128)}, f32[36,128]{1,0:T(8,128)S(1)}, u32[]{:S(2)}) copy-start(f32[36,128]{1,0:T(8,128)S(1)} %collective-permute-done.1.refs_4_.refs_3_) | copy-start | bytes 55300
  45.6 0.7 copy-start.3
  62.0 4.9 %collective-permute-start.3 = (f32[160,128]{1,0:T(8,128)}, f32[160,128]{1,0:T(8,128)S(1)}, u32[]{:S(2)}, u32[]{:S(2)}) collective-permute-start(f32[160,128]{1,0:T(8,128)} %get-tuple-element.26), channel_id=1, source_target_pairs={{0,4},{4,8},{8,12},{12,16},{16,20},{20,24},{24,28},{28,32},{32,36}... | collective-permute-start | bytes 245768 | tf_op jit(solution)/shard_map/ppermute | solution.py:383
  65.1 8.5 %collective-permute-start.4 = (f32[160,128]{1,0:T(8,128)}, f32[160,128]{1,0:T(8,128)S(1)}, u32[]{:S(2)}, u32[]{:S(2)}) collective-permute-start(f32[160,128]{1,0:T(8,128)} %get-tuple-element.27), channel_id=1, source_target_pairs={{4,0},{8,4},{12,8},{16,12},{20,16},{24,20},{28,24},{32,28},{36,32}... | collective-permute-start | bytes 245768 | tf_op jit(solution)/shard_map/ppermute | solution.py:384
  66.9 6.8 %copy-start.6 = (f32[160,128]{1,0:T(8,128)}, f32[160,128]{1,0:T(8,128)S(1)}, u32[]{:S(2)}) copy-start(f32[160,128]{1,0:T(8,128)S(1)} %collective-permute-done.3.refs_2_) | copy-start | bytes 245764
  73.7 0.6 copy-start.7
  117.7 3.6 %copy-start.16 = (f32[144,128]{1,0:T(8,128)S(1)}, f32[144,128]{1,0:T(8,128)}, u32[]{:S(2)}) copy-start(f32[144,128]{1,0:T(8,128)} %get-tuple-element.35) | copy-start | bytes 221188
  117.7 19.9 %all-to-all-start.5 = ((f32[4,144,128]{2,1,0:T(8,128)}), f32[4,144,128]{2,1,0:T(8,128)S(1)}, u32[]{:S(2)}, u32[]{:S(2)}) async-start(f32[4,144,128]{2,1,0:T(8,128)} %get-tuple-element.34), calls=%async_computation.5 | async-start | bytes 589824 | tf_op jit(solution)/shard_map/all_to_all | solution.py:362
  121.3 16.3 %collective-permute-start.5 = (f32[144,128]{1,0:T(8,128)S(1)}, f32[144,128]{1,0:T(8,128)S(1)}, u32[]{:S(2)}, u32[]{:S(2)}) collective-permute-start(f32[144,128]{1,0:T(8,128)S(1)} %copy-done.16), channel_id=1, source_target_pairs={{0,256},{256,0},{1,257},{257,1},{2,258},{258,2},{3,259},{259,3},{4... | collective-permute-start | bytes 221192 | tf_op jit(solution)/shard_map/ppermute | solution.py:361
  137.6 10.1 %copy-start.1 = (f32[4,144,128]{2,1,0:T(8,128)}, f32[4,144,128]{2,1,0:T(8,128)S(1)}, u32[]{:S(2)}) copy-start(f32[4,144,128]{2,1,0:T(8,128)S(1)} %all-to-all-done.5.refs_0_) | copy-start | bytes 884740
  164.4 4.1 %collective-permute-start.6 = (f32[144,128]{1,0:T(8,128)}, f32[144,128]{1,0:T(8,128)S(1)}, u32[]{:S(2)}, u32[]{:S(2)}) collective-permute-start(f32[144,128]{1,0:T(8,128)} %get-tuple-element.38), channel_id=1, source_target_pairs={{0,4},{4,8},{8,12},{12,16},{16,20},{20,24},{24,28},{28,32},{32,36}... | collective-permute-start | bytes 221192 | tf_op jit(solution)/shard_map/ppermute | solution.py:383
  166.9 7.0 %collective-permute-start.7 = (f32[144,128]{1,0:T(8,128)}, f32[144,128]{1,0:T(8,128)S(1)}, u32[]{:S(2)}, u32[]{:S(2)}) collective-permute-start(f32[144,128]{1,0:T(8,128)} %get-tuple-element.39), channel_id=1, source_target_pairs={{4,0},{8,4},{12,8},{16,12},{20,16},{24,20},{28,24},{32,28},{36,32}... | collective-permute-start | bytes 221192 | tf_op jit(solution)/shard_map/ppermute | solution.py:384
  168.6 5.3 %copy-start.11 = (f32[144,128]{1,0:T(8,128)}, f32[144,128]{1,0:T(8,128)S(1)}, u32[]{:S(2)}) copy-start(f32[144,128]{1,0:T(8,128)S(1)} %collective-permute-done.6.refs_2_) | copy-start | bytes 221188
  173.9 0.6 copy-start.12

commit v3 on v2

--- a/solution.py
+++ b/solution.py
@@ -26,11 +26,18 @@
 
 
 def call(kernel, outs, scratch=()):
-    return pl.pallas_call(
-        kernel,
-        out_shape=[jax.ShapeDtypeStruct(s, F32) for s in outs],
-        scratch_shapes=[pltpu.VMEM(s, F32) for s in scratch],
-    )
+    vmem = pl.BlockSpec(memory_space=pltpu.VMEM)
+
+    def run(*args):
+        return pl.pallas_call(
+            kernel,
+            out_shape=[pltpu.VMEM(s, F32) for s in outs],
+            in_specs=[vmem] * len(args),
+            out_specs=[vmem] * len(outs),
+            scratch_shapes=[pltpu.VMEM(s, F32) for s in scratch],
+        )(*[pltpu.with_memory_space_constraint(a, pltpu.VMEM) for a in args])
+
+    return run
 
 
 def faces(e, other):
@@ -40,13 +47,21 @@
 def coupling_kernel(nk, *refs):
     first = nk > NK
     if first:
-        (near, far, load, e0, em, ep, partner, variable, weight, out, us, mx, fx, fy, fz) = refs
+        (u, load, e0, em, ep, partner, variable, weight, out, us, mx, fx, fy, fz) = refs
     else:
-        (near, far, e0, em, ep, partner, variable, weight, out, us, mx, fx, fy, fz) = refs
+        (u, e0, em, ep, partner, variable, weight, out, us, mx, fx, fy, fz) = refs
     for g in range(NG):
-        for yc in range(NY * 3):
-            half = near if g < NG // 2 else far
-            us[yc, g * NM : (g + 1) * NM, :] = half[g % (NG // 2), yc * NM : (yc + 1) * NM, :]
+        half, x = divmod(g, NG // 2)
+        for y in range(NY):
+            for c in range(3):
+                yc = y * 3 + c
+                if first:
+                    at = (half * NY * 3 + yc) * NM
+                    us[yc, g * NM : (g + 1) * NM, :] = u[x, at : at + NM, :]
+                    continue
+                for d in range(QUAD):
+                    at, to = half * SLAB + y * ROWS + c * TRI, g * NM + d * TRI
+                    us[yc, to : to + TRI, :] = u[x * QUAD + d, at : at + TRI, :]
     lane = lax.broadcasted_iota(jnp.int32, (16, NG * NM), 1)
     pr, vr, wr = partner[...], variable[...], weight[...]
     links = NL + 1 if first else NL
@@ -315,16 +330,11 @@
             out[s, rows, :] = change
 
 
-def merge_kernel(q, out, copies):
-    for y in range(NY):
-        for c in range(3):
-            for d in range(QUAD):
-                at = y * ROWS + c * TRI
-                piece = q[d, at : at + TRI, :]
-                to = (y * 3 + c) * NM + d * TRI
-                out[to : to + TRI, :] = piece
-                for g in range(NG // 2):
-                    copies[g, to : to + TRI, :] = piece
+def fan_kernel(blocks, near, far, out):
+    for d in range(blocks):
+        both = jnp.concatenate([near[d], far[d]], axis=0)
+        for x in range(NG // 2):
+            out[x * blocks + d] = both
 
 
 def packed(field):
@@ -332,15 +342,15 @@
 
 
 def shards(load_modes, first_guess, kl_fields, region_labels, partner, variable, weight):
+    mine = packed(first_guess)
+    mine, kl_fields, region_labels = lax.optimization_barrier((mine, kl_fields, region_labels))
     mean = jnp.where(region_labels == 0, 1.3, jnp.where(region_labels == 1, 1.0, 0.6)).astype(F32)
     varying = jnp.where(region_labels[None] == 1, kl_fields, 0.0)
-    moduli = jnp.concatenate([varying, mean[None]], 0).reshape((NK + 1) * NY, NZ)
-    e0 = moduli
+    e0 = jnp.concatenate([varying, mean[None]], 0).reshape((NK + 1) * NY, NZ)
     em = lax.ppermute(e0, SLABS, line(64, 1))
     ep = lax.ppermute(e0, SLABS, line(64, -1))
     load = packed(load_modes)
-    mine = packed(first_guess)
-    copies = jnp.broadcast_to(mine[None], (NG // 2,) + mine.shape)
+    swap = [(0, 1), (1, 0)]
 
     half = lax.axis_index("zh") * (NG // 2 * NM)
     offset = half + lax.axis_index("x") * NM
@@ -358,11 +368,14 @@
     for sweep in range(2):
         first = sweep == 0
         nk = NK + 1 if first else NK
-        far = lax.ppermute(mine, "zh", [(0, 1), (1, 0)])
-        near = lax.all_to_all(copies, "x", 0, 0, tiled=True)
-        far = jnp.broadcast_to(far[None], (NG // 2,) + far.shape)
-        far = lax.all_to_all(far, "x", 0, 0, tiled=True)
-        fields = (near, far, load, e0, em, ep) if first else (near, far, e0, em, ep)
+        blocks = 1 if first else QUAD
+        mine = mine.reshape((blocks, -1, NZ))
+        far = lax.ppermute(mine, "zh", swap)
+        (copies,) = call(
+            functools.partial(fan_kernel, blocks), [(NG // 2 * blocks, 2 * mine.shape[1], NZ)]
+        )(mine, far)
+        u = lax.all_to_all(copies, ("x",) if first else ("x",) + WITHIN, 0, 0, tiled=True)
+        fields = (u, load, e0, em, ep) if first else (u, e0, em, ep)
         face_rows = ((NK + 1) * NY, NZ)
         (sent,) = call(
             functools.partial(coupling_kernel, nk),
@@ -401,10 +414,8 @@
             (change,) = call(functools.partial(update_kernel, False), [chunk])(
                 mom, v0, v1, v2, change
             )
-        by_slab = lax.all_to_all(change, WITHIN, 0, 0, tiled=True)
-        if first:
-            rows = (NY * 3 * NM, NZ)
-            mine, copies = call(merge_kernel, [rows, (NG // 2,) + rows])(by_slab)
+        mine = change
+    by_slab = lax.all_to_all(change, WITHIN, 0, 0, tiled=True)
     total = by_slab.reshape(QUAD, NY, 3, TRI, NZ).transpose(0, 3, 2, 1, 4)
     return first_guess + total.reshape(NM, 3, 1, NY, NZ)
 

time: 216 us -> 187 us (0.87)
  Pallas kernels: 19.9 us -> 6.02 us
  starting transfers between devices: 47 us -> 40.3 us
  local copies, waits for them, and re-layouts: 6.58 us -> 4.24 us
    pallas_call x9 -> x10, Pallas kernels: 19.9 us -> 6.02 us  [run(): pl.pallas_call(kernel, out_shape=[pltpu.VMEM(s, F32) for s in outs], in_s...]
    all_to_all x2 -> x1, blocking collectives: 21.4 us -> 9.45 us  [shards(): by_slab = lax.all_to_all(change, WITHIN, 0, 0, tiled=True)]
    all_to_all x1, blocking collectives: 10.1 us -> 21.8 us  [shards(): lax.all_to_all(copies, ('x',) if first else ('x',) + WITHIN, 0, 0, tiled=...]
    all_to_all x3 -> x1, starting transfers between devices: 11 us -> 3.48 us  [shards(): lax.all_to_all(copies, ('x',) if first else ('x',) + WITHIN, 0, 0, tiled=...]
    all_to_all x2, blocking collectives: 22.7 us -> 17.6 us  [shards(): q = lax.all_to_all(sent, WITHIN, 0, 0, tiled=True)]
    all_to_all x2, blocking collectives: 51.2 us -> 54.1 us  [shards(): mom = lax.all_to_all(mom, CHUNKS, 0, 0, tiled=True)]
    all_to_all x3 -> x1, waiting for transfers between devices: 9.46 us -> 7.51 us  [shards(): lax.all_to_all(copies, ('x',) if first else ('x',) + WITHIN, 0, 0, tiled=...]
  transfers between devices with their start and end apart: 11 -> 9, of which waited for: 7 -> 7; matrix products, arithmetic and copies ran while one was open for 2% -> 0% of each run, Pallas kernels for 0% -> 0%
where the time goes in v3:
time: 187 us; the launch traced here: 186 us
  blocking collectives  103 us (55%)
  starting transfers between devices  40.3 us (22%)
  waiting for transfers between devices  31.9 us (17%)
  Pallas kernels  6.02 us (3%)
  local copies, waits for them, and re-layouts  4.24 us (2%)
    all_to_all x2, blocking collectives, shards(): mom = lax.all_to_all(mom, CHUNKS, 0, 0, tiled=True)  54.1 us
    all_to_all x1, blocking collectives, shards(): lax.all_to_all(copies, ('x',) if first else ('x',) + WITHIN, 0, 0, tiled=...  21.8 us
    all_to_all x2, blocking collectives, shards(): q = lax.all_to_all(sent, WITHIN, 0, 0, tiled=True)  17.6 us
    ppermute x2, starting transfers between devices, shards(): far = lax.ppermute(mine, 'zh', swap)  17 us
    ppermute x2, waiting for transfers between devices, shards(): high = lax.ppermute(down, CHUNKS, line(16, -1))  14 us
    ppermute x2, waiting for transfers between devices, shards(): far = lax.ppermute(mine, 'zh', swap)  10.1 us
    all_to_all x1, blocking collectives, shards(): by_slab = lax.all_to_all(change, WITHIN, 0, 0, tiled=True)  9.45 us
    ppermute x1, starting transfers between devices, shards(): ep = lax.ppermute(e0, SLABS, line(64, -1))  8.79 us
  transfers between devices with their start and end apart: 9, of which 7 were waited for; matrix products, arithmetic and copies ran while one was open for 0% of the time, Pallas kernels for 0%

profile of v3, /device:TPU:1, one launch (start us, length us, event | category | flops | bytes accessed | tf_op | source)
XLA Modules:
  0.0 186.4 jit_solution(2381379290806259647)
XLA Ops:
  0.0 0.0 copy-start
  0.0 0.9 copy.29
  0.9 0.0 copy-start.4
  0.9 0.0 copy-start.3
  1.0 0.6 copy-done.4
  1.6 0.0 copy-done.3
  1.7 8.8 %collective-permute-start.2 = (f32[36,128]{1,0:T(8,128)S(1)}, f32[36,128]{1,0:T(8,128)S(1)}, u32[]{:S(2)}, u32[]{:S(2)}) collective-permute-start(f32[36,128]{1,0:T(8,128)S(1)} %reshape.44.refs_2_.refs_1_), channel_id=1, source_target_pairs={{1,0},{2,1},{3,2},{4,3},{5,4},{6,5},{7,6},{8,7},{9,8},{10,9},{11,1... | collective-permute-start | bytes 55304 | tf_op jit(solution)/shard_map/ppermute | solution.py:351
  10.5 1.9 %collective-permute-start.1 = (f32[36,128]{1,0:T(8,128)S(1)}, f32[36,128]{1,0:T(8,128)S(1)}, u32[]{:S(2)}, u32[]{:S(2)}) collective-permute-start(f32[36,128]{1,0:T(8,128)S(1)} %reshape.44.refs_2_.refs_1_), channel_id=1, source_target_pairs={{0,1},{1,2},{2,3},{3,4},{4,5},{5,6},{6,7},{7,8},{8,9},{9,10},{10,1... | collective-permute-start | bytes 55304 | tf_op jit(solution)/shard_map/ppermute | solution.py:350
  12.4 11.1 %collective-permute-start = (f32[1,144,128]{2,1,0:T(8,128)S(1)}, f32[1,144,128]{2,1,0:T(8,128)S(1)}, u32[]{:S(2)}, u32[]{:S(2)}) collective-permute-start(f32[1,144,128]{2,1,0:T(8,128)S(1)} %bitcast.27), channel_id=1, source_target_pairs={{0,256},{256,0},{1,257},{257,1},{2,258},{258,2},{3,259},{259,3},{4... | collective-permute-start | bytes 221192 | tf_op jit(solution)/shard_map/ppermute | solution.py:373
  23.6 0.0 copy-done
  23.6 0.1 constant_dynamic-slice_fusion
  23.6 0.0 copy-start.5
  23.6 0.0 copy-start.6
  23.6 0.1 copy.42
  23.7 0.6 copy-done.5
  24.3 0.0 copy-done.6
  24.3 0.1 constant_dynamic-slice_fusion.1
  24.4 0.1 copy.40
  24.5 2.0 %collective-permute-done.far = f32[1,144,128]{2,1,0:T(8,128)S(1)} collective-permute-done((f32[1,144,128]{2,1,0:T(8,128)S(1)}, f32[1,144,128]{2,1,0:T(8,128)S(1)}, u32[]{:S(2)}, u32[]{:S(2)}) %collective-permute-start) | collective-permute-done | bytes 73760 | tf_op jit(solution)/shard_map/ppermute | solution.py:373
  26.6 0.9 shard_map.73
  27.4 3.5 %all-to-all-start = ((f32[4,288,128]{2,1,0:T(8,128)}), f32[4,288,128]{2,1,0:T(8,128)S(1)}, u32[]{:S(2)}, u32[]{:S(2)}) async-start(f32[4,288,128]{2,1,0:T(8,128)} %shard_map.73), calls=%async_computation | async-start | bytes 1179648 | tf_op jit(solution)/shard_map/all_to_all | solution.py:377
  30.9 0.0 copy-start.2
  30.9 0.1 pad_add_fusion
  31.0 0.1 copy.41
  31.1 0.7 copy-done.2
  31.8 0.0 collective-permute-done.2.refs_4_.refs_3_
  31.8 0.0 collective-permute-done.1.refs_3_.refs_2_
  31.8 7.5 %all-to-all-done.refs_0_ = f32[4,288,128]{2,1,0:T(8,128)S(1)} async-done(((f32[4,288,128]{2,1,0:T(8,128)}), f32[4,288,128]{2,1,0:T(8,128)S(1)}, u32[]{:S(2)}, u32[]{:S(2)}) %all-to-all-start) | async-done | bytes 589856 | tf_op jit(solution)/shard_map/all_to_all | solution.py:377
  39.4 1.4 shard_map.74
  40.8 10.0 %all_to_all.47.refs_0_ = f32[4,112,128]{2,1,0:T(8,128)S(1)} all-to-all(f32[4,112,128]{2,1,0:T(8,128)S(1)} %shard_map.74), channel_id=1, replica_groups=mesh['zh'=2,'x'=4,'y'=4,'zp'=4,'zq'=2,'c'=2] {'zq','c'}, dimensions={0} | all-to-all | bytes 458752 | tf_op jit(solution)/shard_map/all_to_all | solution.py:391
  50.9 5.1 %collective-permute-start.3 = (f32[160,128]{1,0:T(8,128)S(1)}, f32[160,128]{1,0:T(8,128)S(1)}, u32[]{:S(2)}, u32[]{:S(2)}) collective-permute-start(f32[160,128]{1,0:T(8,128)S(1)} %get-tuple-element.30), channel_id=1, source_target_pairs={{0,4},{4,8},{8,12},{12,16},{16,20},{20,24},{24,28},{28,32},{32,36}... | collective-permute-start | bytes 245768 | tf_op jit(solution)/shard_map/ppermute | solution.py:396
  56.0 1.3 collective-permute-start.4
  57.3 0.2 collective-permute-done.3.refs_2_
  57.5 8.6 %collective-permute-done.4.refs_3_ = f32[160,128]{1,0:T(8,128)S(1)} collective-permute-done((f32[160,128]{1,0:T(8,128)S(1)}, f32[160,128]{1,0:T(8,128)S(1)}, u32[]{:S(2)}, u32[]{:S(2)}) %collective-permute-start.4) | collective-permute-done | bytes 81952 | tf_op jit(solution)/shard_map/ppermute | solution.py:397
  66.1 0.7 shard_map.76
  66.8 28.2 %all_to_all.48 = f32[16,1,128]{2,1,0:T(1,128)S(1)} all-to-all(f32[16,1,128]{2,1,0:T(1,128)S(1)} %bitcast.31), channel_id=1, replica_groups=mesh['zh'=2,'x'=4,'y'=4,'zp'=4,'zq'=2,'c'=2] {'y','zp'}, dimensions={0} | all-to-all | bytes 16384 | tf_op jit(solution)/shard_map/all_to_all | solution.py:408
  94.9 0.2 shard_map.77
  95.2 5.9 %collective-permute-start.5 = (f32[4,36,128]{2,1,0:T(8,128)S(1)}, f32[4,36,128]{2,1,0:T(8,128)S(1)}, u32[]{:S(2)}, u32[]{:S(2)}) collective-permute-start(f32[4,36,128]{2,1,0:T(8,128)S(1)} %get-tuple-element.37.near.refs_4_), channel_id=1, source_target_pairs={{0,256},{256,0},{1,257},{257,1},{2,258},{258,2},{3,259},{259,3},{4... | collective-permute-start | bytes 221192 | tf_op jit(solution)/shard_map/ppermute | solution.py:373
  101.1 8.0 %collective-permute-done.5.far = f32[4,36,128]{2,1,0:T(8,128)S(1)} collective-permute-done((f32[4,36,128]{2,1,0:T(8,128)S(1)}, f32[4,36,128]{2,1,0:T(8,128)S(1)}, u32[]{:S(2)}, u32[]{:S(2)}) %collective-permute-start.5) | collective-permute-done | bytes 73760 | tf_op jit(solution)/shard_map/ppermute | solution.py:373
  109.1 21.8 %all_to_all.49.refs_0_ = f32[16,72,128]{2,1,0:T(8,128)S(1)} all-to-all(f32[16,72,128]{2,1,0:T(8,128)S(1)} %shard_map.78), channel_id=1, replica_groups=mesh['zh'=2,'x'=4,'y'=4,'zp'=4,'zq'=2,'c'=2] {'x','zq','c'}, dimensions={0} | all-to-all | bytes 1179648 | tf_op jit(solution)/shard_map/all_to_all | solution.py:377
  130.9 1.3 shard_map.79
  132.3 7.6 %all_to_all.50.refs_0_ = f32[4,112,128]{2,1,0:T(8,128)S(1)} all-to-all(f32[4,112,128]{2,1,0:T(8,128)S(1)} %shard_map.79), channel_id=1, replica_groups=mesh['zh'=2,'x'=4,'y'=4,'zp'=4,'zq'=2,'c'=2] {'zq','c'}, dimensions={0} | all-to-all | bytes 458752 | tf_op jit(solution)/shard_map/all_to_all | solution.py:391
  139.8 1.4 collective-permute-start.6
  141.2 1.3 collective-permute-start.7
  142.5 0.1 collective-permute-done.6.refs_2_
  142.6 5.4 %collective-permute-done.7.refs_3_ = f32[144,128]{1,0:T(8,128)S(1)} collective-permute-done((f32[144,128]{1,0:T(8,128)S(1)}, f32[144,128]{1,0:T(8,128)S(1)}, u32[]{:S(2)}, u32[]{:S(2)}) %collective-permute-start.7) | collective-permute-done | bytes 73760 | tf_op jit(solution)/shard_map/ppermute | solution.py:397
  148.0 1.2 shard_map.81
  149.3 25.9 %all_to_all.51 = f32[16,1,128]{2,1,0:T(1,128)S(1)} all-to-all(f32[16,1,128]{2,1,0:T(1,128)S(1)} %bitcast.32), channel_id=1, replica_groups=mesh['zh'=2,'x'=4,'y'=4,'zp'=4,'zq'=2,'c'=2] {'y','zp'}, dimensions={0} | all-to-all | bytes 16384 | tf_op jit(solution)/shard_map/all_to_all | solution.py:408
  175.2 0.2 shard_map.82
  175.4 9.4 %all_to_all.52 = f32[4,36,128]{2,1,0:T(8,128)S(1)} all-to-all(f32[4,36,128]{2,1,0:T(8,128)S(1)} %shard_map.82), channel_id=1, replica_groups=mesh['zh'=2,'x'=4,'y'=4,'zp'=4,'zq'=2,'c'=2] {'zq','c'}, dimensions={0} | all-to-all | bytes 147456 | tf_op jit(solution)/shard_map/all_to_all | solution.py:418
  184.9 0.0 copy-start.1
  184.9 0.8 copy-done.1
  185.8 0.7 bitcast_add_fusion
  (18 shorter events, 0.2 us)
Async XLA Ops:
  0.0 23.6 %copy-start = (f32[96,8]{0,1:T(8,128)S(1)}, f32[96,8]{0,1:T(8,128)}, u32[]{:S(2)}) copy-start(f32[96,8]{0,1:T(8,128)} %param.13) | copy-start | bytes 9220
  0.9 0.7 copy-start.4
  0.9 0.7 copy-start.3
  1.7 30.1 %collective-permute-start.2 = (f32[36,128]{1,0:T(8,128)S(1)}, f32[36,128]{1,0:T(8,128)S(1)}, u32[]{:S(2)}, u32[]{:S(2)}) collective-permute-start(f32[36,128]{1,0:T(8,128)S(1)} %reshape.44.refs_2_.refs_1_), channel_id=1, source_target_pairs={{1,0},{2,1},{3,2},{4,3},{5,4},{6,5},{7,6},{8,7},{9,8},{10,9},{11,1... | collective-permute-start | bytes 55304 | tf_op jit(solution)/shard_map/ppermute | solution.py:351
  10.5 21.4 %collective-permute-start.1 = (f32[36,128]{1,0:T(8,128)S(1)}, f32[36,128]{1,0:T(8,128)S(1)}, u32[]{:S(2)}, u32[]{:S(2)}) collective-permute-start(f32[36,128]{1,0:T(8,128)S(1)} %reshape.44.refs_2_.refs_1_), channel_id=1, source_target_pairs={{0,1},{1,2},{2,3},{3,4},{4,5},{5,6},{6,7},{7,8},{8,9},{9,10},{10,1... | collective-permute-start | bytes 55304 | tf_op jit(solution)/shard_map/ppermute | solution.py:350
  12.4 14.1 %collective-permute-start = (f32[1,144,128]{2,1,0:T(8,128)S(1)}, f32[1,144,128]{2,1,0:T(8,128)S(1)}, u32[]{:S(2)}, u32[]{:S(2)}) collective-permute-start(f32[1,144,128]{2,1,0:T(8,128)S(1)} %bitcast.27), channel_id=1, source_target_pairs={{0,256},{256,0},{1,257},{257,1},{2,258},{258,2},{3,259},{259,3},{4... | collective-permute-start | bytes 221192 | tf_op jit(solution)/shard_map/ppermute | solution.py:373
  23.6 0.7 copy-start.5
  23.6 0.7 copy-start.6
  27.4 12.0 %all-to-all-start = ((f32[4,288,128]{2,1,0:T(8,128)}), f32[4,288,128]{2,1,0:T(8,128)S(1)}, u32[]{:S(2)}, u32[]{:S(2)}) async-start(f32[4,288,128]{2,1,0:T(8,128)} %shard_map.73), calls=%async_computation | async-start | bytes 1179648 | tf_op jit(solution)/shard_map/all_to_all | solution.py:377
  30.9 0.9 copy-start.2
  50.9 6.6 %collective-permute-start.3 = (f32[160,128]{1,0:T(8,128)S(1)}, f32[160,128]{1,0:T(8,128)S(1)}, u32[]{:S(2)}, u32[]{:S(2)}) collective-permute-start(f32[160,128]{1,0:T(8,128)S(1)} %get-tuple-element.30), channel_id=1, source_target_pairs={{0,4},{4,8},{8,12},{12,16},{16,20},{20,24},{24,28},{28,32},{32,36}... | collective-permute-start | bytes 245768 | tf_op jit(solution)/shard_map/ppermute | solution.py:396
  56.0 10.1 %collective-permute-start.4 = (f32[160,128]{1,0:T(8,128)S(1)}, f32[160,128]{1,0:T(8,128)S(1)}, u32[]{:S(2)}, u32[]{:S(2)}) collective-permute-start(f32[160,128]{1,0:T(8,128)S(1)} %get-tuple-element.31), channel_id=1, source_target_pairs={{4,0},{8,4},{12,8},{16,12},{20,16},{24,20},{28,24},{32,28},{36,32}... | collective-permute-start | bytes 245768 | tf_op jit(solution)/shard_map/ppermute | solution.py:397
  95.2 13.9 %collective-permute-start.5 = (f32[4,36,128]{2,1,0:T(8,128)S(1)}, f32[4,36,128]{2,1,0:T(8,128)S(1)}, u32[]{:S(2)}, u32[]{:S(2)}) collective-permute-start(f32[4,36,128]{2,1,0:T(8,128)S(1)} %get-tuple-element.37.near.refs_4_), channel_id=1, source_target_pairs={{0,256},{256,0},{1,257},{257,1},{2,258},{258,2},{3,259},{259,3},{4... | collective-permute-start | bytes 221192 | tf_op jit(solution)/shard_map/ppermute | solution.py:373
  139.8 2.8 %collective-permute-start.6 = (f32[144,128]{1,0:T(8,128)S(1)}, f32[144,128]{1,0:T(8,128)S(1)}, u32[]{:S(2)}, u32[]{:S(2)}) collective-permute-start(f32[144,128]{1,0:T(8,128)S(1)} %get-tuple-element.40), channel_id=1, source_target_pairs={{0,4},{4,8},{8,12},{12,16},{16,20},{20,24},{24,28},{28,32},{32,36}... | collective-permute-start | bytes 221192 | tf_op jit(solution)/shard_map/ppermute | solution.py:396
  141.2 6.8 %collective-permute-start.7 = (f32[144,128]{1,0:T(8,128)S(1)}, f32[144,128]{1,0:T(8,128)S(1)}, u32[]{:S(2)}, u32[]{:S(2)}) collective-permute-start(f32[144,128]{1,0:T(8,128)S(1)} %get-tuple-element.41), channel_id=1, source_target_pairs={{4,0},{8,4},{12,8},{16,12},{20,16},{24,20},{28,24},{32,28},{36,32}... | collective-permute-start | bytes 221192 | tf_op jit(solution)/shard_map/ppermute | solution.py:397
  184.9 0.9 copy-start.1

commit v4 on v3

--- a/solution.py
+++ b/solution.py
@@ -8,9 +8,11 @@
 from jax.sharding import Mesh
 from jax.sharding import PartitionSpec as P
 
-AXES = ("zh", "x", "y", "zp", "zq", "c")
-SLABS = ("y", "zp", "zq", "c")
-CHUNKS = ("y", "zp")
+AXES = ("zh", "x", "y1", "y0", "zp", "zq", "c")
+SWAP = [(0, 0), (1, 2), (2, 1), (3, 3)]
+GROUPS = ("y0", "x")
+SLABS = ("zh", "y1", "zp", "zq", "c")
+CHUNKS = ("zh", "y1", "zp")
 WITHIN = ("zq", "c")
 NG, NM, NL, NK = 8, 12, 8, 8
 NY, NZ, SHIFT = 4, 128, 4.0
@@ -21,8 +23,13 @@
 F32 = jnp.float32
 
 
-def line(count, step):
-    return [(i, i + step) for i in range(count) if 0 <= i + step < count]
+def line(inner, step):
+    def place(i):
+        y1, zh, low = i // (2 * inner), i // inner % 2, i % inner
+        return (zh * 2 + y1) * inner + low
+
+    count = 4 * inner
+    return [(place(i), place(i + step)) for i in range(count) if 0 <= i + step < count]
 
 
 def call(kernel, outs, scratch=()):
@@ -51,17 +58,8 @@
     else:
         (u, e0, em, ep, partner, variable, weight, out, us, mx, fx, fy, fz) = refs
     for g in range(NG):
-        half, x = divmod(g, NG // 2)
-        for y in range(NY):
-            for c in range(3):
-                yc = y * 3 + c
-                if first:
-                    at = (half * NY * 3 + yc) * NM
-                    us[yc, g * NM : (g + 1) * NM, :] = u[x, at : at + NM, :]
-                    continue
-                for d in range(QUAD):
-                    at, to = half * SLAB + y * ROWS + c * TRI, g * NM + d * TRI
-                    us[yc, to : to + TRI, :] = u[x * QUAD + d, at : at + TRI, :]
+        for yc in range(NY * 3):
+            us[yc, g * NM : (g + 1) * NM, :] = u[g, yc * NM : (yc + 1) * NM, :]
     lane = lax.broadcasted_iota(jnp.int32, (16, NG * NM), 1)
     pr, vr, wr = partner[...], variable[...], weight[...]
     links = NL + 1 if first else NL
@@ -330,11 +328,23 @@
             out[s, rows, :] = change
 
 
-def fan_kernel(blocks, near, far, out):
-    for d in range(blocks):
-        both = jnp.concatenate([near[d], far[d]], axis=0)
-        for x in range(NG // 2):
-            out[x * blocks + d] = both
+def fan_kernel(field, out):
+    own = field[: NY * 3 * NM, :]
+    for g in range(NG):
+        out[g] = own
+
+
+def merge_kernel(q, out):
+    for y in range(NY):
+        for c in range(3):
+            pieces = []
+            for d in range(QUAD):
+                at = y * ROWS + c * TRI
+                pieces.append(q[d, at : at + TRI, :])
+            own = jnp.concatenate(pieces, axis=0)
+            to = (y * 3 + c) * NM
+            for g in range(NG):
+                out[g, to : to + NM, :] = own
 
 
 def packed(field):
@@ -342,22 +352,20 @@
 
 
 def shards(load_modes, first_guess, kl_fields, region_labels, partner, variable, weight):
-    mine = packed(first_guess)
-    mine, kl_fields, region_labels = lax.optimization_barrier((mine, kl_fields, region_labels))
     mean = jnp.where(region_labels == 0, 1.3, jnp.where(region_labels == 1, 1.0, 0.6)).astype(F32)
     varying = jnp.where(region_labels[None] == 1, kl_fields, 0.0)
-    e0 = jnp.concatenate([varying, mean[None]], 0).reshape((NK + 1) * NY, NZ)
-    em = lax.ppermute(e0, SLABS, line(64, 1))
-    ep = lax.ppermute(e0, SLABS, line(64, -1))
-    load = packed(load_modes)
-    swap = [(0, 1), (1, 0)]
-
-    half = lax.axis_index("zh") * (NG // 2 * NM)
-    offset = half + lax.axis_index("x") * NM
-    modes = NG * NM
-    own = offset - half + jnp.arange(NM, dtype=jnp.int32)[:, None]
+    moduli = jnp.concatenate([varying, mean[None]], 0).reshape((NK + 1) * NY, NZ)
+    guess = jnp.concatenate([packed(first_guess), moduli], 0)
+    guess = lax.ppermute(guess, ("zh", "y0"), SWAP)
+    load = lax.ppermute(packed(load_modes), ("zh", "y0"), SWAP)
+    e0 = guess[NY * 3 * NM :]
+    em = lax.ppermute(e0, SLABS, line(16, 1))
+    ep = lax.ppermute(e0, SLABS, line(16, -1))
+
+    offset = (lax.axis_index("y0") * 4 + lax.axis_index("x")) * NM
+    own = offset + jnp.arange(NM, dtype=jnp.int32)[:, None]
     pad = ((0, 16 - NM), (0, 0))
-    rows_partner = (lax.dynamic_slice_in_dim(partner, offset, NM, 0) + modes - half) % modes
+    rows_partner = lax.dynamic_slice_in_dim(partner, offset, NM, 0)
     rows_partner = jnp.pad(jnp.concatenate([rows_partner, own], 1), pad, constant_values=-1)
     rows_variable = jnp.pad(lax.dynamic_slice_in_dim(variable, offset, NM, 0), pad)
     rows_weight = lax.dynamic_slice_in_dim(weight, offset, NM, 0)
@@ -368,13 +376,9 @@
     for sweep in range(2):
         first = sweep == 0
         nk = NK + 1 if first else NK
-        blocks = 1 if first else QUAD
-        mine = mine.reshape((blocks, -1, NZ))
-        far = lax.ppermute(mine, "zh", swap)
-        (copies,) = call(
-            functools.partial(fan_kernel, blocks), [(NG // 2 * blocks, 2 * mine.shape[1], NZ)]
-        )(mine, far)
-        u = lax.all_to_all(copies, ("x",) if first else ("x",) + WITHIN, 0, 0, tiled=True)
+        kernel = fan_kernel if first else merge_kernel
+        (copies,) = call(kernel, [(NG, NY * 3 * NM, NZ)])(guess if first else by_slab)
+        u = lax.all_to_all(copies, GROUPS, 0, 0, tiled=True)
         fields = (u, load, e0, em, ep) if first else (u, e0, em, ep)
         face_rows = ((NK + 1) * NY, NZ)
         (sent,) = call(
@@ -393,8 +397,8 @@
         chunk_r, up, down = call(functools.partial(edges_kernel, first), [chunk, edge, edge])(
             *((q,) if first else (q, rest))
         )
-        low = lax.ppermute(up, CHUNKS, line(16, 1))
-        high = lax.ppermute(down, CHUNKS, line(16, -1))
+        low = lax.ppermute(up, CHUNKS, line(4, 1))
+        high = lax.ppermute(down, CHUNKS, line(4, -1))
         scratch = [(10 * NY, ROWS, NZ)] * 4
         outs = [cells] * 4 + [(16, NZ)]
         if first:
@@ -414,15 +418,15 @@
             (change,) = call(functools.partial(update_kernel, False), [chunk])(
                 mom, v0, v1, v2, change
             )
-        mine = change
-    by_slab = lax.all_to_all(change, WITHIN, 0, 0, tiled=True)
-    total = by_slab.reshape(QUAD, NY, 3, TRI, NZ).transpose(0, 3, 2, 1, 4)
+        by_slab = lax.all_to_all(change, WITHIN, 0, 0, tiled=True)
+    total = lax.ppermute(by_slab, ("zh", "y0"), SWAP)
+    total = total.reshape(QUAD, NY, 3, TRI, NZ).transpose(0, 3, 2, 1, 4)
     return first_guess + total.reshape(NM, 3, 1, NY, NZ)
 
 
 def solution(mesh):
-    split = Mesh(mesh.devices.reshape(2, 4, 4, 4, 2, 2), AXES)
-    mode, space = ("zh", "x"), SLABS
+    split = Mesh(mesh.devices.reshape(2, 4, 2, 2, 4, 2, 2), AXES)
+    mode, space = ("zh", "x"), ("y1", "y0", "zp", "zq", "c")
     return jax.shard_map(
         shards,
         mesh=split,

time: 187 us -> 191 us (1.021)
  the two profiles are of different devices: /device:TPU:1 before, /device:TPU:41 now
where the time goes in v4:
time: 191 us; the launch traced here: 190 us
  blocking collectives  102 us (53%)
  starting transfers between devices  49.4 us (26%)
  waiting for transfers between devices  28.4 us (15%)
  Pallas kernels  6.01 us (3%)
  other arithmetic  2.25 us (1%)
    all_to_all x2, blocking collectives, shards(): mom = lax.all_to_all(mom, CHUNKS, 0, 0, tiled=True)  51.2 us
    all_to_all x2, blocking collectives, shards(): by_slab = lax.all_to_all(change, WITHIN, 0, 0, tiled=True)  19.7 us
    all_to_all x2, blocking collectives, shards(): q = lax.all_to_all(sent, WITHIN, 0, 0, tiled=True)  18 us
    ppermute x1, waiting for transfers between devices, shards(): total = lax.ppermute(by_slab, ('zh', 'y0'), SWAP)  17.3 us
    ppermute x1, starting transfers between devices, shards(): ep = lax.ppermute(e0, SLABS, line(16, -1))  14.5 us
    ppermute x1, starting transfers between devices, shards(): guess = lax.ppermute(guess, ('zh', 'y0'), SWAP)  14.4 us
    all_to_all x1, blocking collectives, shards(): u = lax.all_to_all(copies, GROUPS, 0, 0, tiled=True)  13.5 us
    ppermute x2, waiting for transfers between devices, shards(): high = lax.ppermute(down, CHUNKS, line(4, -1))  9.43 us
  transfers between devices with their start and end apart: 10, of which 7 were waited for; matrix products, arithmetic and copies ran while one was open for 0% of the time, Pallas kernels for 0%

profile of v4, /device:TPU:41, one launch (start us, length us, event | category | flops | bytes accessed | tf_op | source)
XLA Modules:
  0.0 189.7 jit_solution(1465091843607807058)
XLA Ops:
  0.0 0.0 copy-start
  0.0 0.0 copy-start.3
  0.0 0.0 copy-start.1
  0.0 0.8 fusion
  0.8 0.0 copy-done.3
  0.8 0.7 broadcast_select_fusion
  1.5 0.0 copy-done.1
  1.6 0.0 copy-start.2
  1.6 14.4 %collective-permute-start = (f32[180,128]{1,0:T(8,128)S(1)}, f32[180,128]{1,0:T(8,128)S(1)}, u32[]{:S(2)}, u32[]{:S(2)}) collective-permute-start(f32[180,128]{1,0:T(8,128)S(1)} %pad_maximum_fusion), channel_id=1, source_target_pairs={{0,0},{16,256},{256,16},{272,272},{1,1},{17,257},{257,17},{273,273... | collective-permute-start | bytes 276488 | tf_op jit(solution)/shard_map/ppermute | solution.py:359
  16.0 0.0 copy-done.2
  16.1 1.9 %collective-permute-start.1 = (f32[144,128]{1,0:T(8,128)S(1)}, f32[144,128]{1,0:T(8,128)S(1)}, u32[]{:S(2)}, u32[]{:S(2)}) collective-permute-start(f32[144,128]{1,0:T(8,128)S(1)} %reshape.40), channel_id=1, source_target_pairs={{0,0},{16,256},{256,16},{272,272},{1,1},{17,257},{257,17},{273,273... | collective-permute-start | bytes 221192 | tf_op jit(solution)/shard_map/ppermute | solution.py:360
  18.0 0.4 collective-permute-done.field
  18.5 0.9 shard_map.73
  19.3 5.2 %all-to-all-start = ((f32[8,144,128]{2,1,0:T(8,128)}), f32[8,144,128]{2,1,0:T(8,128)S(1)}, u32[]{:S(2)}, u32[]{:S(2)}) async-start(f32[8,144,128]{2,1,0:T(8,128)} %shard_map.73), calls=%async_computation | async-start | bytes 1179648 | tf_op jit(solution)/shard_map/all_to_all | solution.py:381
  24.5 0.0 copy-done
  24.5 0.1 constant_dynamic-slice_fusion
  24.6 0.0 copy-start.4
  24.6 0.0 copy-start.5
  24.6 0.1 copy.42
  24.7 0.6 copy-done.4
  25.3 0.0 copy-done.5
  25.3 0.1 constant_dynamic-slice_fusion.1
  25.4 0.1 copy.40
  25.5 14.5 %collective-permute-start.3 = (f32[36,128]{1,0:T(8,128)S(1)}, f32[36,128]{1,0:T(8,128)S(1)}, u32[]{:S(2)}, u32[]{:S(2)}) collective-permute-start(f32[36,128]{1,0:T(8,128)S(1)} %slice.4.refs_2_.refs_1_), channel_id=1, source_target_pairs={{1,0},{2,1},{3,2},{4,3},{5,4},{6,5},{7,6},{8,7},{9,8},{10,9},{11,1... | collective-permute-start | bytes 55304 | tf_op jit(solution)/shard_map/ppermute | solution.py:363
  40.0 1.9 %collective-permute-start.2 = (f32[36,128]{1,0:T(8,128)S(1)}, f32[36,128]{1,0:T(8,128)S(1)}, u32[]{:S(2)}, u32[]{:S(2)}) collective-permute-start(f32[36,128]{1,0:T(8,128)S(1)} %slice.4.refs_2_.refs_1_), channel_id=1, source_target_pairs={{0,1},{1,2},{2,3},{3,4},{4,5},{5,6},{6,7},{7,8},{8,9},{9,10},{10,1... | collective-permute-start | bytes 55304 | tf_op jit(solution)/shard_map/ppermute | solution.py:362
  41.9 0.1 pad_add_fusion
  42.0 0.1 copy.41
  42.1 0.0 collective-permute-done.1.refs_1_
  42.1 0.0 collective-permute-done.3.refs_4_.refs_3_
  42.1 1.0 collective-permute-done.2.refs_3_.refs_2_
  43.1 0.0 all-to-all-done.refs_0_
  43.1 1.4 shard_map.74
  44.5 8.6 %all_to_all.52.refs_0_ = f32[4,112,128]{2,1,0:T(8,128)S(1)} all-to-all(f32[4,112,128]{2,1,0:T(8,128)S(1)} %shard_map.74), channel_id=1, replica_groups=mesh['zh'=2,'x'=4,'y1'=2,'y0'=2,'zp'=4,'zq'=2,'c'=2] {'zq','c'}, dimensions={0} | all-to-all | bytes 458752 | tf_op jit(solution)/shard_map/all_to_all | solution.py:395
  53.1 2.7 %collective-permute-start.4 = (f32[160,128]{1,0:T(8,128)S(1)}, f32[160,128]{1,0:T(8,128)S(1)}, u32[]{:S(2)}, u32[]{:S(2)}) collective-permute-start(f32[160,128]{1,0:T(8,128)S(1)} %get-tuple-element.24), channel_id=1, source_target_pairs={{0,4},{4,8},{8,12},{12,256},{256,260},{260,264},{264,268},{268,32}... | collective-permute-start | bytes 245768 | tf_op jit(solution)/shard_map/ppermute | solution.py:400
  55.9 1.3 collective-permute-start.5
  57.2 0.2 collective-permute-done.4.refs_2_
  57.3 4.7 %collective-permute-done.5.refs_3_ = f32[160,128]{1,0:T(8,128)S(1)} collective-permute-done((f32[160,128]{1,0:T(8,128)S(1)}, f32[160,128]{1,0:T(8,128)S(1)}, u32[]{:S(2)}, u32[]{:S(2)}) %collective-permute-start.5) | collective-permute-done | bytes 81952 | tf_op jit(solution)/shard_map/ppermute | solution.py:401
  62.1 0.7 shard_map.76
  62.7 29.5 %all_to_all.53 = f32[16,1,128]{2,1,0:T(1,128)S(1)} all-to-all(f32[16,1,128]{2,1,0:T(1,128)S(1)} %bitcast.28), channel_id=1, replica_groups=mesh['zh'=2,'x'=4,'y1'=2,'y0'=2,'zp'=4,'zq'=2,'c'=2] {'zh','y1','zp'}, dimensions={0} | all-to-all | bytes 16384 | tf_op jit(solution)/shard_map/all_to_all | solution.py:412
  92.2 0.2 shard_map.77
  92.5 9.8 %all_to_all.54.q = f32[4,36,128]{2,1,0:T(8,128)S(1)} all-to-all(f32[4,36,128]{2,1,0:T(8,128)S(1)} %get-tuple-element.31.refs_4_), channel_id=1, replica_groups=mesh['zh'=2,'x'=4,'y1'=2,'y0'=2,'zp'=4,'zq'=2,'c'=2] {'zq','c'}, dimensions={0} | all-to-all | bytes 147456 | tf_op jit(solution)/shard_map/all_to_all | solution.py:421
  102.2 0.1 shard_map.78
  102.3 13.5 %all_to_all.55.refs_0_ = f32[8,144,128]{2,1,0:T(8,128)S(1)} all-to-all(f32[8,144,128]{2,1,0:T(8,128)S(1)} %shard_map.78), channel_id=1, replica_groups=mesh['zh'=2,'x'=4,'y1'=2,'y0'=2,'zp'=4,'zq'=2,'c'=2] {'y0','x'}, dimensions={0} | all-to-all | bytes 1179648 | tf_op jit(solution)/shard_map/all_to_all | solution.py:381
  115.8 1.3 shard_map.79
  117.1 9.4 %all_to_all.56.refs_0_ = f32[4,112,128]{2,1,0:T(8,128)S(1)} all-to-all(f32[4,112,128]{2,1,0:T(8,128)S(1)} %shard_map.79), channel_id=1, replica_groups=mesh['zh'=2,'x'=4,'y1'=2,'y0'=2,'zp'=4,'zq'=2,'c'=2] {'zq','c'}, dimensions={0} | all-to-all | bytes 458752 | tf_op jit(solution)/shard_map/all_to_all | solution.py:395
  126.5 2.3 %collective-permute-start.6 = (f32[144,128]{1,0:T(8,128)S(1)}, f32[144,128]{1,0:T(8,128)S(1)}, u32[]{:S(2)}, u32[]{:S(2)}) collective-permute-start(f32[144,128]{1,0:T(8,128)S(1)} %get-tuple-element.34), channel_id=1, source_target_pairs={{0,4},{4,8},{8,12},{12,256},{256,260},{260,264},{264,268},{268,32}... | collective-permute-start | bytes 221192 | tf_op jit(solution)/shard_map/ppermute | solution.py:400
  128.8 1.3 collective-permute-start.7
  130.1 0.1 collective-permute-done.6.refs_2_
  130.2 4.7 %collective-permute-done.7.refs_3_ = f32[144,128]{1,0:T(8,128)S(1)} collective-permute-done((f32[144,128]{1,0:T(8,128)S(1)}, f32[144,128]{1,0:T(8,128)S(1)}, u32[]{:S(2)}, u32[]{:S(2)}) %collective-permute-start.7) | collective-permute-done | bytes 73760 | tf_op jit(solution)/shard_map/ppermute | solution.py:401
  134.9 1.2 shard_map.81
  136.1 21.7 %all_to_all.57 = f32[16,1,128]{2,1,0:T(1,128)S(1)} all-to-all(f32[16,1,128]{2,1,0:T(1,128)S(1)} %bitcast.29), channel_id=1, replica_groups=mesh['zh'=2,'x'=4,'y1'=2,'y0'=2,'zp'=4,'zq'=2,'c'=2] {'zh','y1','zp'}, dimensions={0} | all-to-all | bytes 16384 | tf_op jit(solution)/shard_map/all_to_all | solution.py:412
  157.8 0.2 shard_map.82
  158.0 9.9 %all_to_all.58 = f32[4,36,128]{2,1,0:T(8,128)S(1)} all-to-all(f32[4,36,128]{2,1,0:T(8,128)S(1)} %shard_map.82), channel_id=1, replica_groups=mesh['zh'=2,'x'=4,'y1'=2,'y0'=2,'zp'=4,'zq'=2,'c'=2] {'zq','c'}, dimensions={0} | all-to-all | bytes 147456 | tf_op jit(solution)/shard_map/all_to_all | solution.py:421
  167.9 3.8 %collective-permute-start.8 = (f32[4,36,128]{2,1,0:T(8,128)S(1)}, f32[4,36,128]{2,1,0:T(8,128)S(1)}, u32[]{:S(2)}, u32[]{:S(2)}) collective-permute-start(f32[4,36,128]{2,1,0:T(8,128)S(1)} %all_to_all.58), channel_id=1, source_target_pairs={{0,0},{16,256},{256,16},{272,272},{1,1},{17,257},{257,17},{273,273... | collective-permute-start | bytes 221192 | tf_op jit(solution)/shard_map/ppermute | solution.py:422
  171.7 17.3 %collective-permute-done.8 = f32[4,36,128]{2,1,0:T(8,128)S(1)} collective-permute-done((f32[4,36,128]{2,1,0:T(8,128)S(1)}, f32[4,36,128]{2,1,0:T(8,128)S(1)}, u32[]{:S(2)}, u32[]{:S(2)}) %collective-permute-start.8) | collective-permute-done | bytes 73760 | tf_op jit(solution)/shard_map/ppermute | solution.py:422
  189.1 0.7 bitcast_add_fusion
  (17 shorter events, 0.2 us)
Async XLA Ops:
  0.0 24.5 %copy-start = (f32[96,8]{0,1:T(8,128)S(1)}, f32[96,8]{0,1:T(8,128)}, u32[]{:S(2)}) copy-start(f32[96,8]{0,1:T(8,128)} %param.13) | copy-start | bytes 9220
  0.0 0.8 copy-start.3
  0.0 1.5 copy-start.1
  1.6 14.5 %copy-start.2 = (f32[12,3,1,4,128]{4,3,2,1,0:T(4,128)S(1)}, f32[12,3,1,4,128]{4,3,2,1,0:T(4,128)}, u32[]{:S(2)}) copy-start(f32[12,3,1,4,128]{4,3,2,1,0:T(4,128)} %param.7) | copy-start | bytes 221188
  1.6 16.9 %collective-permute-start = (f32[180,128]{1,0:T(8,128)S(1)}, f32[180,128]{1,0:T(8,128)S(1)}, u32[]{:S(2)}, u32[]{:S(2)}) collective-permute-start(f32[180,128]{1,0:T(8,128)S(1)} %pad_maximum_fusion), channel_id=1, source_target_pairs={{0,0},{16,256},{256,16},{272,272},{1,1},{17,257},{257,17},{273,273... | collective-permute-start | bytes 276488 | tf_op jit(solution)/shard_map/ppermute | solution.py:359
  16.1 26.0 %collective-permute-start.1 = (f32[144,128]{1,0:T(8,128)S(1)}, f32[144,128]{1,0:T(8,128)S(1)}, u32[]{:S(2)}, u32[]{:S(2)}) collective-permute-start(f32[144,128]{1,0:T(8,128)S(1)} %reshape.40), channel_id=1, source_target_pairs={{0,0},{16,256},{256,16},{272,272},{1,1},{17,257},{257,17},{273,273... | collective-permute-start | bytes 221192 | tf_op jit(solution)/shard_map/ppermute | solution.py:360
  19.3 23.8 %all-to-all-start = ((f32[8,144,128]{2,1,0:T(8,128)}), f32[8,144,128]{2,1,0:T(8,128)S(1)}, u32[]{:S(2)}, u32[]{:S(2)}) async-start(f32[8,144,128]{2,1,0:T(8,128)} %shard_map.73), calls=%async_computation | async-start | bytes 1179648 | tf_op jit(solution)/shard_map/all_to_all | solution.py:381
  24.6 0.7 copy-start.4
  24.6 0.7 copy-start.5
  25.5 16.7 %collective-permute-start.3 = (f32[36,128]{1,0:T(8,128)S(1)}, f32[36,128]{1,0:T(8,128)S(1)}, u32[]{:S(2)}, u32[]{:S(2)}) collective-permute-start(f32[36,128]{1,0:T(8,128)S(1)} %slice.4.refs_2_.refs_1_), channel_id=1, source_target_pairs={{1,0},{2,1},{3,2},{4,3},{5,4},{6,5},{7,6},{8,7},{9,8},{10,9},{11,1... | collective-permute-start | bytes 55304 | tf_op jit(solution)/shard_map/ppermute | solution.py:363
  40.0 3.1 %collective-permute-start.2 = (f32[36,128]{1,0:T(8,128)S(1)}, f32[36,128]{1,0:T(8,128)S(1)}, u32[]{:S(2)}, u32[]{:S(2)}) collective-permute-start(f32[36,128]{1,0:T(8,128)S(1)} %slice.4.refs_2_.refs_1_), channel_id=1, source_target_pairs={{0,1},{1,2},{2,3},{3,4},{4,5},{5,6},{6,7},{7,8},{8,9},{9,10},{10,1... | collective-permute-start | bytes 55304 | tf_op jit(solution)/shard_map/ppermute | solution.py:362
  53.1 4.2 %collective-permute-start.4 = (f32[160,128]{1,0:T(8,128)S(1)}, f32[160,128]{1,0:T(8,128)S(1)}, u32[]{:S(2)}, u32[]{:S(2)}) collective-permute-start(f32[160,128]{1,0:T(8,128)S(1)} %get-tuple-element.24), channel_id=1, source_target_pairs={{0,4},{4,8},{8,12},{12,256},{256,260},{260,264},{264,268},{268,32}... | collective-permute-start | bytes 245768 | tf_op jit(solution)/shard_map/ppermute | solution.py:400
  55.9 6.2 %collective-permute-start.5 = (f32[160,128]{1,0:T(8,128)S(1)}, f32[160,128]{1,0:T(8,128)S(1)}, u32[]{:S(2)}, u32[]{:S(2)}) collective-permute-start(f32[160,128]{1,0:T(8,128)S(1)} %get-tuple-element.25), channel_id=1, source_target_pairs={{4,0},{8,4},{12,8},{256,12},{260,256},{264,260},{268,264},{32,268}... | collective-permute-start | bytes 245768 | tf_op jit(solution)/shard_map/ppermute | solution.py:401
  126.5 3.7 %collective-permute-start.6 = (f32[144,128]{1,0:T(8,128)S(1)}, f32[144,128]{1,0:T(8,128)S(1)}, u32[]{:S(2)}, u32[]{:S(2)}) collective-permute-start(f32[144,128]{1,0:T(8,128)S(1)} %get-tuple-element.34), channel_id=1, source_target_pairs={{0,4},{4,8},{8,12},{12,256},{256,260},{260,264},{264,268},{268,32}... | collective-permute-start | bytes 221192 | tf_op jit(solution)/shard_map/ppermute | solution.py:400
  128.8 6.1 %collective-permute-start.7 = (f32[144,128]{1,0:T(8,128)S(1)}, f32[144,128]{1,0:T(8,128)S(1)}, u32[]{:S(2)}, u32[]{:S(2)}) collective-permute-start(f32[144,128]{1,0:T(8,128)S(1)} %get-tuple-element.35), channel_id=1, source_target_pairs={{4,0},{8,4},{12,8},{256,12},{260,256},{264,260},{268,264},{32,268}... | collective-permute-start | bytes 221192 | tf_op jit(solution)/shard_map/ppermute | solution.py:401
  167.9 21.1 %collective-permute-start.8 = (f32[4,36,128]{2,1,0:T(8,128)S(1)}, f32[4,36,128]{2,1,0:T(8,128)S(1)}, u32[]{:S(2)}, u32[]{:S(2)}) collective-permute-start(f32[4,36,128]{2,1,0:T(8,128)S(1)} %all_to_all.58), channel_id=1, source_target_pairs={{0,0},{16,256},{256,16},{272,272},{1,1},{17,257},{257,17},{273,273... | collective-permute-start | bytes 221192 | tf_op jit(solution)/shard_map/ppermute | solution.py:422

commit v5 on v4

--- a/solution.py
+++ b/solution.py
@@ -11,7 +11,8 @@
 AXES = ("zh", "x", "y1", "y0", "zp", "zq", "c")
 SWAP = [(0, 0), (1, 2), (2, 1), (3, 3)]
 GROUPS = ("y0", "x")
-SLABS = ("zh", "y1", "zp", "zq", "c")
+SLABS = ("zh", "y1", "y0", "zp", "zq", "c")
+LINES = ("zh", "y1", "y0", "zp")
 CHUNKS = ("zh", "y1", "zp")
 WITHIN = ("zq", "c")
 NG, NM, NL, NK = 8, 12, 8, 8
@@ -23,10 +24,11 @@
 F32 = jnp.float32
 
 
-def line(inner, step):
+def line(inner, step, held=False):
     def place(i):
         y1, zh, low = i // (2 * inner), i // inner % 2, i % inner
-        return (zh * 2 + y1) * inner + low
+        first = zh * 2 + y1
+        return ((first * 2 + zh) if held else first) * inner + low
 
     count = 4 * inner
     return [(place(i), place(i + step)) for i in range(count) if 0 <= i + step < count]
@@ -173,10 +175,18 @@
         for s in range(QUAD):
             ec[(3 + s) * NY : (4 + s) * NY, :] = q[s, 3 * SLAB : 3 * SLAB + NY, :]
     else:
-        q, own, low, high, ec, v0, v1, v2, v3, mom, w0, w1, w2, dg = refs
+        q, own, low, high, ec, before, stack, mom, w0, w1, w2, dg = refs
+        v0 = v1 = v2 = v3 = None
+        stack[3] = before[...]
 
     def rows(ref, at, y):
         return ref[at + y * ROWS : at + (y + 1) * ROWS, :]
+
+    def keep(k, s, y, val):
+        if first:
+            (v0, v1, v2, v3)[k][s * NY + y] = val
+        elif k < 3:
+            stack[k, s, y * ROWS : (y + 1) * ROWS, :] = val
 
     rid = lax.broadcasted_iota(jnp.int32, (ROWS, NZ), 0)
     wx = jnp.where(rid < TRI, 2.0, 1.0)
@@ -206,7 +216,7 @@
             if s == QUAD - 1:
                 r = r + rows(high, 3 * SLAB, y)
             w0[(3 + s) * NY + y] = r
-            v0[s * NY + y] = r
+            keep(0, s, y, r)
 
     def face(p, y):
         e = em[p][y]
@@ -248,19 +258,19 @@
             t = apply(w0, p, y)
             w1[p * NY + y] = t
             if 3 <= p <= 6:
-                v1[(p - 3) * NY + y] = t
+                keep(1, p - 3, y, t)
     for p in range(2, 8):
         for y in range(NY):
             t = apply(w1, p, y)
             w2[p * NY + y] = t
             if 3 <= p <= 6:
-                v2[(p - 3) * NY + y] = t
+                keep(2, p - 3, y, t)
     sums = [None] * 6
     for p in range(3, 7):
         for y in range(NY):
             a, b, d = w0[p * NY + y], w1[p * NY + y], w2[p * NY + y]
             t = apply(w2, p, y)
-            v3[(p - 3) * NY + y] = t
+            keep(3, p - 3, y, t)
             for j, val in enumerate((a * a, a * b, b * b, b * d, d * d, d * t)):
                 sums[j] = val if sums[j] is None else sums[j] + val
     lane = lax.broadcasted_iota(jnp.int32, (ROWS, NZ), 1)
@@ -306,8 +316,9 @@
     if first:
         mom, v0, v1, v2, v3, out, rest = refs
     else:
-        mom, v0, v1, v2, before, out = refs
-    total = jnp.sum(mom[...], axis=0, keepdims=True)
+        mom, kept, stack, out = refs
+    shares = mom[...] if first else jnp.where(kept[...] > 0.0, mom[...], 0.0)
+    total = jnp.sum(shares, axis=0, keepdims=True)
     rid = lax.broadcasted_iota(jnp.int32, (ROWS, NZ), 0)
     lane = lax.broadcasted_iota(jnp.int32, (ROWS, NZ), 1)
     spot = lane - 8 * (rid % TRI)
@@ -319,12 +330,12 @@
         for y in range(NY):
             at = s * NY + y
             rows = slice(y * ROWS, (y + 1) * ROWS)
-            a, b, d = v0[at], v1[at], v2[at]
+            a, b, d = (v0[at], v1[at], v2[at]) if first else (stack[k, s, rows, :] for k in range(3))
             change = x[0] * a + x[1] * b + x[2] * d
             if first:
                 rest[s, rows, :] = r[0] * a + r[1] * b + r[2] * d + r[3] * v3[at]
             else:
-                change = change + before[s, rows, :]
+                change = change + stack[3, s, rows, :]
             out[s, rows, :] = change
 
 
@@ -355,12 +366,18 @@
     mean = jnp.where(region_labels == 0, 1.3, jnp.where(region_labels == 1, 1.0, 0.6)).astype(F32)
     varying = jnp.where(region_labels[None] == 1, kl_fields, 0.0)
     moduli = jnp.concatenate([varying, mean[None]], 0).reshape((NK + 1) * NY, NZ)
-    guess = jnp.concatenate([packed(first_guess), moduli], 0)
-    guess = lax.ppermute(guess, ("zh", "y0"), SWAP)
-    load = lax.ppermute(packed(load_modes), ("zh", "y0"), SWAP)
-    e0 = guess[NY * 3 * NM :]
-    em = lax.ppermute(e0, SLABS, line(16, 1))
-    ep = lax.ppermute(e0, SLABS, line(16, -1))
+    swapped = ("zh", "y0")
+    guess = packed(lax.ppermute(first_guess, swapped, SWAP))
+    load = packed(lax.ppermute(load_modes, swapped, SWAP))
+    em = lax.ppermute(moduli, SLABS, line(16, 1, True))
+    ep = lax.ppermute(moduli, SLABS, line(16, -1, True))
+    held = lax.axis_index("zh") == lax.axis_index("y0")
+    three = jnp.concatenate([moduli, em, ep], 0)
+    three = jnp.where(held, three, lax.ppermute(three, swapped, [(0, 1), (3, 2)]))
+    count = moduli.shape[0]
+    e0, em, ep = three[:count], three[count : 2 * count], three[2 * count :]
+    source = jnp.arange(32, dtype=jnp.int32)[:, None] // 4 % 2
+    kept = jnp.broadcast_to((source == lax.axis_index("zh")).astype(F32), (32, NZ))
 
     offset = (lax.axis_index("y0") * 4 + lax.axis_index("x")) * NM
     own = offset + jnp.arange(NM, dtype=jnp.int32)[:, None]
@@ -400,27 +417,25 @@
         low = lax.ppermute(up, CHUNKS, line(4, 1))
         high = lax.ppermute(down, CHUNKS, line(4, -1))
         scratch = [(10 * NY, ROWS, NZ)] * 4
-        outs = [cells] * 4 + [(16, NZ)]
         if first:
             v0, v1, v2, v3, mom, ec = call(
-                functools.partial(powers_kernel, True), outs + [(10 * NY, NZ)], scratch
+                functools.partial(powers_kernel, True),
+                [cells] * 4 + [(16, NZ), (10 * NY, NZ)],
+                scratch,
             )(q, chunk_r, low, high)
-        else:
-            v0, v1, v2, v3, mom = call(functools.partial(powers_kernel, False), outs, scratch)(
-                q, chunk_r, low, high, ec
-            )
-        mom = lax.all_to_all(mom, CHUNKS, 0, 0, tiled=True)
-        if first:
+            mom = lax.all_to_all(mom, CHUNKS, 0, 0, tiled=True)
             change, rest = call(functools.partial(update_kernel, True), [chunk, chunk])(
                 mom, v0, v1, v2, v3
             )
         else:
-            (change,) = call(functools.partial(update_kernel, False), [chunk])(
-                mom, v0, v1, v2, change
-            )
+            stack, mom = call(
+                functools.partial(powers_kernel, False), [(4,) + chunk, (32, NZ)], scratch
+            )(q, chunk_r, low, high, ec, change)
+            stack = lax.ppermute(stack, swapped, SWAP)
+            mom = lax.all_to_all(mom, LINES, 0, 0, tiled=True)
+            (change,) = call(functools.partial(update_kernel, False), [chunk])(mom, kept, stack)
         by_slab = lax.all_to_all(change, WITHIN, 0, 0, tiled=True)
-    total = lax.ppermute(by_slab, ("zh", "y0"), SWAP)
-    total = total.reshape(QUAD, NY, 3, TRI, NZ).transpose(0, 3, 2, 1, 4)
+    total = by_slab.reshape(QUAD, NY, 3, TRI, NZ).transpose(0, 3, 2, 1, 4)
     return first_guess + total.reshape(NM, 3, 1, NY, NZ)
 
 

time: 191 us -> 190 us (level)
  the two profiles are of different devices: /device:TPU:41 before, /device:TPU:8 now
where the time goes in v5:
time: 190 us; the launch traced here: 189 us
  blocking collectives  77.9 us (41%)
  starting transfers between devices  53.5 us (28%)
  waiting for transfers between devices  48.2 us (25%)
  Pallas kernels  6.08 us (3%)
  other arithmetic  2.27 us (1%)
    all_to_all x1, blocking collectives, shards(): mom = lax.all_to_all(mom, CHUNKS, 0, 0, tiled=True)  31.7 us
    all_to_all x1, waiting for transfers between devices, shards(): mom = lax.all_to_all(mom, LINES, 0, 0, tiled=True)  25.1 us
    all_to_all x2, blocking collectives, shards(): q = lax.all_to_all(sent, WITHIN, 0, 0, tiled=True)  19.1 us
    ppermute x1, starting transfers between devices, shards(): guess = packed(lax.ppermute(first_guess, swapped, SWAP))  15.6 us
    all_to_all x1, blocking collectives, shards(): u = lax.all_to_all(copies, GROUPS, 0, 0, tiled=True)  13.9 us
    all_to_all x1, starting transfers between devices, shards(): mom = lax.all_to_all(mom, LINES, 0, 0, tiled=True)  13.9 us
    all_to_all x2, blocking collectives, shards(): by_slab = lax.all_to_all(change, WITHIN, 0, 0, tiled=True)  13.2 us
    ppermute x2, waiting for transfers between devices, shards(): high = lax.ppermute(down, CHUNKS, line(4, -1))  11.7 us
  transfers between devices with their start and end apart: 12, of which 7 were waited for; matrix products, arithmetic and copies ran while one was open for 0% of the time, Pallas kernels for 0%

profile of v5, /device:TPU:8, one launch (start us, length us, event | category | flops | bytes accessed | tf_op | source)
XLA Modules:
  0.0 189.4 jit_solution(5219188974713106858)
XLA Ops:
  0.0 0.0 copy-start
  0.0 0.0 copy-start.2
  0.0 0.0 copy-start.1
  0.0 0.8 fusion
  0.8 0.0 copy-done.2
  0.8 0.7 broadcast_select_fusion.1
  1.5 0.7 collective-permute-start.2
  2.2 0.7 collective-permute-start.3
  2.9 0.0 copy-done.1
  2.9 15.6 %collective-permute-start = (f32[12,3,1,4,128]{4,3,2,1,0:T(4,128)S(1)}, f32[12,3,1,4,128]{4,3,2,1,0:T(4,128)S(1)}, u32[]{:S(2)}, u32[]{:S(2)}) collective-permute-start(f32[12,3,1,4,128]{4,3,2,1,0:T(4,128)S(1)} %copy-done.1), channel_id=1, source_target_pairs={{0,0},{16,256},{256,16},{272,272},{1,1},{17,257},{257,17},{273,273... | collective-permute-start | bytes 221192 | tf_op jit(solution)/shard_map/ppermute | solution.py:370
  18.5 1.9 %collective-permute-start.1 = (f32[12,3,1,4,128]{4,3,2,1,0:T(4,128)}, f32[12,3,1,4,128]{4,3,2,1,0:T(4,128)S(1)}, u32[]{:S(2)}, u32[]{:S(2)}) collective-permute-start(f32[12,3,1,4,128]{4,3,2,1,0:T(4,128)} %param.7), channel_id=1, source_target_pairs={{0,0},{16,256},{256,16},{272,272},{1,1},{17,257},{257,17},{273,273... | collective-permute-start | bytes 221192 | tf_op jit(solution)/shard_map/ppermute | solution.py:371
  20.4 0.0 copy-done
  20.5 0.1 constant_dynamic-slice_fusion
  20.5 0.1 copy.42
  20.6 0.0 copy-start.3
  20.6 0.0 copy-start.4
  20.6 0.7 copy-done.3
  21.3 0.0 copy-done.4
  21.3 0.1 constant_dynamic-slice_fusion.1
  21.4 0.1 copy.40
  21.5 0.0 collective-permute-done.2
  21.5 0.0 collective-permute-done.3
  21.5 1.3 collective-permute-start.4
  22.8 0.0 collective-permute-done
  22.8 0.9 shard_map.73
  23.7 6.9 %all-to-all-start = ((f32[8,144,128]{2,1,0:T(8,128)}), f32[8,144,128]{2,1,0:T(8,128)S(1)}, u32[]{:S(2)}, u32[]{:S(2)}) async-start(f32[8,144,128]{2,1,0:T(8,128)} %shard_map.73), calls=%async_computation | async-start | bytes 1179648 | tf_op jit(solution)/shard_map/all_to_all | solution.py:398
  30.7 0.1 pad_add_fusion
  30.7 0.1 copy.41
  30.8 4.5 %collective-permute-done.1 = f32[12,3,1,4,128]{4,3,2,1,0:T(4,128)S(1)} collective-permute-done((f32[12,3,1,4,128]{4,3,2,1,0:T(4,128)}, f32[12,3,1,4,128]{4,3,2,1,0:T(4,128)S(1)}, u32[]{:S(2)}, u32[]{:S(2)}) %collective-permute-start.1) | collective-permute-done | bytes 73760 | tf_op jit(solution)/shard_map/ppermute | solution.py:371
  35.4 0.0 collective-permute-done.4
  35.4 4.1 %all-to-all-done.refs_0_ = f32[8,144,128]{2,1,0:T(8,128)S(1)} async-done(((f32[8,144,128]{2,1,0:T(8,128)}), f32[8,144,128]{2,1,0:T(8,128)S(1)}, u32[]{:S(2)}, u32[]{:S(2)}) %all-to-all-start) | async-done | bytes 589856 | tf_op jit(solution)/shard_map/all_to_all | solution.py:398
  39.5 1.4 shard_map.74
  41.0 11.0 %all_to_all.52.refs_0_ = f32[4,112,128]{2,1,0:T(8,128)S(1)} all-to-all(f32[4,112,128]{2,1,0:T(8,128)S(1)} %shard_map.74), channel_id=1, replica_groups=mesh['zh'=2,'x'=4,'y1'=2,'y0'=2,'zp'=4,'zq'=2,'c'=2] {'zq','c'}, dimensions={0} | all-to-all | bytes 458752 | tf_op jit(solution)/shard_map/all_to_all | solution.py:412
  52.0 1.3 collective-permute-start.5
  53.3 1.3 collective-permute-start.6
  54.6 0.7 collective-permute-done.5.refs_2_
  55.4 7.1 %collective-permute-done.6.refs_3_ = f32[160,128]{1,0:T(8,128)S(1)} collective-permute-done((f32[160,128]{1,0:T(8,128)S(1)}, f32[160,128]{1,0:T(8,128)S(1)}, u32[]{:S(2)}, u32[]{:S(2)}) %collective-permute-start.6) | collective-permute-done | bytes 81952 | tf_op jit(solution)/shard_map/ppermute | solution.py:418
  62.4 0.7 shard_map.76
  63.1 31.7 %all_to_all.53 = f32[16,1,128]{2,1,0:T(1,128)S(1)} all-to-all(f32[16,1,128]{2,1,0:T(1,128)S(1)} %bitcast.28), channel_id=1, replica_groups=mesh['zh'=2,'x'=4,'y1'=2,'y0'=2,'zp'=4,'zq'=2,'c'=2] {'zh','y1','zp'}, dimensions={0} | all-to-all | bytes 16384 | tf_op jit(solution)/shard_map/all_to_all | solution.py:426
  94.8 0.2 shard_map.77
  95.0 6.6 %all_to_all.54.q = f32[4,36,128]{2,1,0:T(8,128)S(1)} all-to-all(f32[4,36,128]{2,1,0:T(8,128)S(1)} %get-tuple-element.29.refs_5_), channel_id=1, replica_groups=mesh['zh'=2,'x'=4,'y1'=2,'y0'=2,'zp'=4,'zq'=2,'c'=2] {'zq','c'}, dimensions={0} | all-to-all | bytes 147456 | tf_op jit(solution)/shard_map/all_to_all | solution.py:437
  101.6 0.1 shard_map.78
  101.7 13.9 %all_to_all.55.refs_0_ = f32[8,144,128]{2,1,0:T(8,128)S(1)} all-to-all(f32[8,144,128]{2,1,0:T(8,128)S(1)} %shard_map.78), channel_id=1, replica_groups=mesh['zh'=2,'x'=4,'y1'=2,'y0'=2,'zp'=4,'zq'=2,'c'=2] {'y0','x'}, dimensions={0} | all-to-all | bytes 1179648 | tf_op jit(solution)/shard_map/all_to_all | solution.py:398
  115.6 1.3 shard_map.79
  116.9 8.1 %all_to_all.56.refs_0_ = f32[4,112,128]{2,1,0:T(8,128)S(1)} all-to-all(f32[4,112,128]{2,1,0:T(8,128)S(1)} %shard_map.79), channel_id=1, replica_groups=mesh['zh'=2,'x'=4,'y1'=2,'y0'=2,'zp'=4,'zq'=2,'c'=2] {'zq','c'}, dimensions={0} | all-to-all | bytes 458752 | tf_op jit(solution)/shard_map/all_to_all | solution.py:412
  125.0 2.5 %collective-permute-start.7 = (f32[144,128]{1,0:T(8,128)S(1)}, f32[144,128]{1,0:T(8,128)S(1)}, u32[]{:S(2)}, u32[]{:S(2)}) collective-permute-start(f32[144,128]{1,0:T(8,128)S(1)} %get-tuple-element.32), channel_id=1, source_target_pairs={{0,4},{4,8},{8,12},{12,256},{256,260},{260,264},{264,268},{268,32}... | collective-permute-start | bytes 221192 | tf_op jit(solution)/shard_map/ppermute | solution.py:417
  127.5 1.3 collective-permute-start.8
  128.8 2.0 %collective-permute-done.7.refs_2_ = f32[144,128]{1,0:T(8,128)S(1)} collective-permute-done((f32[144,128]{1,0:T(8,128)S(1)}, f32[144,128]{1,0:T(8,128)S(1)}, u32[]{:S(2)}, u32[]{:S(2)}) %collective-permute-start.7) | collective-permute-done | bytes 73760 | tf_op jit(solution)/shard_map/ppermute | solution.py:417
  130.8 4.6 %collective-permute-done.8.refs_3_ = f32[144,128]{1,0:T(8,128)S(1)} collective-permute-done((f32[144,128]{1,0:T(8,128)S(1)}, f32[144,128]{1,0:T(8,128)S(1)}, u32[]{:S(2)}, u32[]{:S(2)}) %collective-permute-start.8) | collective-permute-done | bytes 73760 | tf_op jit(solution)/shard_map/ppermute | solution.py:418
  135.4 1.3 shard_map.81
  136.7 6.1 %collective-permute-start.9 = (f32[4,4,36,128]{3,2,1,0:T(8,128)S(1)}, f32[4,4,36,128]{3,2,1,0:T(8,128)S(1)}, u32[]{:S(2)}, u32[]{:S(2)}) collective-permute-start(f32[4,4,36,128]{3,2,1,0:T(8,128)S(1)} %get-tuple-element.36), channel_id=1, source_target_pairs={{0,0},{16,256},{256,16},{272,272},{1,1},{17,257},{257,17},{273,273... | collective-permute-start | bytes 884744 | tf_op jit(solution)/shard_map/ppermute | solution.py:434
  142.8 13.9 %all-to-all-start.6 = ((f32[32,1,128]{2,1,0:T(1,128)}), f32[32,1,128]{2,1,0:T(1,128)S(1)}, u32[]{:S(2)}, u32[]{:S(2)}) async-start(f32[32,1,128]{2,1,0:T(1,128)} %bitcast.11), calls=%async_computation.6 | async-start | bytes 32768 | tf_op jit(solution)/shard_map/all_to_all | solution.py:435
  156.7 25.1 %all-to-all-done.6 = f32[32,1,128]{2,1,0:T(1,128)S(1)} async-done(((f32[32,1,128]{2,1,0:T(1,128)}), f32[32,1,128]{2,1,0:T(1,128)S(1)}, u32[]{:S(2)}, u32[]{:S(2)}) %all-to-all-start.6) | async-done | bytes 16416 | tf_op jit(solution)/shard_map/all_to_all | solution.py:435
  181.9 0.0 collective-permute-done.9.refs_2_
  181.9 0.1 broadcast_in_dim.41.refs_1_
  182.0 0.2 shard_map.82
  182.2 6.6 %all_to_all.57 = f32[4,36,128]{2,1,0:T(8,128)S(1)} all-to-all(f32[4,36,128]{2,1,0:T(8,128)S(1)} %shard_map.82), channel_id=1, replica_groups=mesh['zh'=2,'x'=4,'y1'=2,'y0'=2,'zp'=4,'zq'=2,'c'=2] {'zq','c'}, dimensions={0} | all-to-all | bytes 147456 | tf_op jit(solution)/shard_map/all_to_all | solution.py:437
  188.8 0.7 bitcast_add_fusion
  (19 shorter events, 0.2 us)
Async XLA Ops:
  0.0 20.4 %copy-start = (f32[96,8]{0,1:T(8,128)S(1)}, f32[96,8]{0,1:T(8,128)}, u32[]{:S(2)}) copy-start(f32[96,8]{0,1:T(8,128)} %param.13) | copy-start | bytes 9220
  0.0 0.8 copy-start.2
  0.0 2.9 %copy-start.1 = (f32[12,3,1,4,128]{4,3,2,1,0:T(4,128)S(1)}, f32[12,3,1,4,128]{4,3,2,1,0:T(4,128)}, u32[]{:S(2)}) copy-start(f32[12,3,1,4,128]{4,3,2,1,0:T(4,128)} %param.8) | copy-start | bytes 221188
  1.5 20.0 %collective-permute-start.2 = (f32[36,128]{1,0:T(8,128)S(1)}, f32[36,128]{1,0:T(8,128)S(1)}, u32[]{:S(2)}, u32[]{:S(2)}) collective-permute-start(f32[36,128]{1,0:T(8,128)S(1)} %reshape.98), channel_id=1, source_target_pairs={{0,1},{1,2},{2,3},{3,4},{4,5},{5,6},{6,7},{7,8},{8,9},{9,10},{10,1... | collective-permute-start | bytes 55304 | tf_op jit(solution)/shard_map/ppermute | solution.py:372
  2.2 19.3 %collective-permute-start.3 = (f32[36,128]{1,0:T(8,128)S(1)}, f32[36,128]{1,0:T(8,128)S(1)}, u32[]{:S(2)}, u32[]{:S(2)}) collective-permute-start(f32[36,128]{1,0:T(8,128)S(1)} %reshape.98), channel_id=1, source_target_pairs={{1,0},{2,1},{3,2},{4,3},{5,4},{6,5},{7,6},{8,7},{9,8},{10,9},{11,1... | collective-permute-start | bytes 55304 | tf_op jit(solution)/shard_map/ppermute | solution.py:373
  2.9 19.9 %collective-permute-start = (f32[12,3,1,4,128]{4,3,2,1,0:T(4,128)S(1)}, f32[12,3,1,4,128]{4,3,2,1,0:T(4,128)S(1)}, u32[]{:S(2)}, u32[]{:S(2)}) collective-permute-start(f32[12,3,1,4,128]{4,3,2,1,0:T(4,128)S(1)} %copy-done.1), channel_id=1, source_target_pairs={{0,0},{16,256},{256,16},{272,272},{1,1},{17,257},{257,17},{273,273... | collective-permute-start | bytes 221192 | tf_op jit(solution)/shard_map/ppermute | solution.py:370
  18.5 16.8 %collective-permute-start.1 = (f32[12,3,1,4,128]{4,3,2,1,0:T(4,128)}, f32[12,3,1,4,128]{4,3,2,1,0:T(4,128)S(1)}, u32[]{:S(2)}, u32[]{:S(2)}) collective-permute-start(f32[12,3,1,4,128]{4,3,2,1,0:T(4,128)} %param.7), channel_id=1, source_target_pairs={{0,0},{16,256},{256,16},{272,272},{1,1},{17,257},{257,17},{273,273... | collective-permute-start | bytes 221192 | tf_op jit(solution)/shard_map/ppermute | solution.py:371
  20.6 0.7 copy-start.3
  20.6 0.7 copy-start.4
  21.5 13.9 %collective-permute-start.4 = (f32[108,128]{1,0:T(8,128)S(1)}, f32[108,128]{1,0:T(8,128)S(1)}, u32[]{:S(2)}, u32[]{:S(2)}) collective-permute-start(f32[108,128]{1,0:T(8,128)S(1)} %pad_maximum_fusion), channel_id=1, source_target_pairs={{0,16},{272,256},{1,17},{273,257},{2,18},{274,258},{3,19},{275,259... | collective-permute-start | bytes 165896 | tf_op jit(solution)/shard_map/ppermute | solution.py:376
  23.7 15.8 %all-to-all-start = ((f32[8,144,128]{2,1,0:T(8,128)}), f32[8,144,128]{2,1,0:T(8,128)S(1)}, u32[]{:S(2)}, u32[]{:S(2)}) async-start(f32[8,144,128]{2,1,0:T(8,128)} %shard_map.73), calls=%async_computation | async-start | bytes 1179648 | tf_op jit(solution)/shard_map/all_to_all | solution.py:398
  52.0 3.3 %collective-permute-start.5 = (f32[160,128]{1,0:T(8,128)S(1)}, f32[160,128]{1,0:T(8,128)S(1)}, u32[]{:S(2)}, u32[]{:S(2)}) collective-permute-start(f32[160,128]{1,0:T(8,128)S(1)} %get-tuple-element.22), channel_id=1, source_target_pairs={{0,4},{4,8},{8,12},{12,256},{256,260},{260,264},{264,268},{268,32}... | collective-permute-start | bytes 245768 | tf_op jit(solution)/shard_map/ppermute | solution.py:417
  53.3 9.1 %collective-permute-start.6 = (f32[160,128]{1,0:T(8,128)S(1)}, f32[160,128]{1,0:T(8,128)S(1)}, u32[]{:S(2)}, u32[]{:S(2)}) collective-permute-start(f32[160,128]{1,0:T(8,128)S(1)} %get-tuple-element.23), channel_id=1, source_target_pairs={{4,0},{8,4},{12,8},{256,12},{260,256},{264,260},{268,264},{32,268}... | collective-permute-start | bytes 245768 | tf_op jit(solution)/shard_map/ppermute | solution.py:418
  125.0 5.8 %collective-permute-start.7 = (f32[144,128]{1,0:T(8,128)S(1)}, f32[144,128]{1,0:T(8,128)S(1)}, u32[]{:S(2)}, u32[]{:S(2)}) collective-permute-start(f32[144,128]{1,0:T(8,128)S(1)} %get-tuple-element.32), channel_id=1, source_target_pairs={{0,4},{4,8},{8,12},{12,256},{256,260},{260,264},{264,268},{268,32}... | collective-permute-start | bytes 221192 | tf_op jit(solution)/shard_map/ppermute | solution.py:417
  127.5 7.9 %collective-permute-start.8 = (f32[144,128]{1,0:T(8,128)S(1)}, f32[144,128]{1,0:T(8,128)S(1)}, u32[]{:S(2)}, u32[]{:S(2)}) collective-permute-start(f32[144,128]{1,0:T(8,128)S(1)} %get-tuple-element.33), channel_id=1, source_target_pairs={{4,0},{8,4},{12,8},{256,12},{260,256},{264,260},{268,264},{32,268}... | collective-permute-start | bytes 221192 | tf_op jit(solution)/shard_map/ppermute | solution.py:418
  136.7 45.2 %collective-permute-start.9 = (f32[4,4,36,128]{3,2,1,0:T(8,128)S(1)}, f32[4,4,36,128]{3,2,1,0:T(8,128)S(1)}, u32[]{:S(2)}, u32[]{:S(2)}) collective-permute-start(f32[4,4,36,128]{3,2,1,0:T(8,128)S(1)} %get-tuple-element.36), channel_id=1, source_target_pairs={{0,0},{16,256},{256,16},{272,272},{1,1},{17,257},{257,17},{273,273... | collective-permute-start | bytes 884744 | tf_op jit(solution)/shard_map/ppermute | solution.py:434
  142.8 39.1 %all-to-all-start.6 = ((f32[32,1,128]{2,1,0:T(1,128)}), f32[32,1,128]{2,1,0:T(1,128)S(1)}, u32[]{:S(2)}, u32[]{:S(2)}) async-start(f32[32,1,128]{2,1,0:T(1,128)} %bitcast.11), calls=%async_computation.6 | async-start | bytes 32768 | tf_op jit(solution)/shard_map/all_to_all | solution.py:435

commit v6 on v4

--- a/solution.py
+++ b/solution.py
@@ -11,7 +11,7 @@
 AXES = ("zh", "x", "y1", "y0", "zp", "zq", "c")
 SWAP = [(0, 0), (1, 2), (2, 1), (3, 3)]
 GROUPS = ("y0", "x")
-SLABS = ("zh", "y1", "zp", "zq", "c")
+SLABS = ("zh", "y1", "y0", "zp", "zq", "c")
 CHUNKS = ("zh", "y1", "zp")
 WITHIN = ("zq", "c")
 NG, NM, NL, NK = 8, 12, 8, 8
@@ -23,10 +23,11 @@
 F32 = jnp.float32
 
 
-def line(inner, step):
+def line(inner, step, held=False):
     def place(i):
         y1, zh, low = i // (2 * inner), i // inner % 2, i % inner
-        return (zh * 2 + y1) * inner + low
+        first = zh * 2 + y1
+        return ((first * 2 + zh) if held else first) * inner + low
 
     count = 4 * inner
     return [(place(i), place(i + step)) for i in range(count) if 0 <= i + step < count]
@@ -355,12 +356,16 @@
     mean = jnp.where(region_labels == 0, 1.3, jnp.where(region_labels == 1, 1.0, 0.6)).astype(F32)
     varying = jnp.where(region_labels[None] == 1, kl_fields, 0.0)
     moduli = jnp.concatenate([varying, mean[None]], 0).reshape((NK + 1) * NY, NZ)
-    guess = jnp.concatenate([packed(first_guess), moduli], 0)
-    guess = lax.ppermute(guess, ("zh", "y0"), SWAP)
-    load = lax.ppermute(packed(load_modes), ("zh", "y0"), SWAP)
-    e0 = guess[NY * 3 * NM :]
-    em = lax.ppermute(e0, SLABS, line(16, 1))
-    ep = lax.ppermute(e0, SLABS, line(16, -1))
+    swapped = ("zh", "y0")
+    guess = packed(lax.ppermute(first_guess, swapped, SWAP))
+    load = packed(lax.ppermute(load_modes, swapped, SWAP))
+    em = lax.ppermute(moduli, SLABS, line(16, 1, True))
+    ep = lax.ppermute(moduli, SLABS, line(16, -1, True))
+    held = lax.axis_index("zh") == lax.axis_index("y0")
+    three = jnp.concatenate([moduli, em, ep], 0)
+    three = jnp.where(held, three, lax.ppermute(three, swapped, [(0, 1), (3, 2)]))
+    count = moduli.shape[0]
+    e0, em, ep = three[:count], three[count : 2 * count], three[2 * count :]
 
     offset = (lax.axis_index("y0") * 4 + lax.axis_index("x")) * NM
     own = offset + jnp.arange(NM, dtype=jnp.int32)[:, None]
@@ -419,7 +424,7 @@
                 mom, v0, v1, v2, change
             )
         by_slab = lax.all_to_all(change, WITHIN, 0, 0, tiled=True)
-    total = lax.ppermute(by_slab, ("zh", "y0"), SWAP)
+    total = lax.ppermute(by_slab, swapped, SWAP)
     total = total.reshape(QUAD, NY, 3, TRI, NZ).transpose(0, 3, 2, 1, 4)
     return first_guess + total.reshape(NM, 3, 1, NY, NZ)
 

time: 191 us -> 191 us (level)
  waiting for transfers between devices: 28.4 us -> 43.9 us
  starting transfers between devices: 49.4 us -> 34.3 us
    ppermute x5 -> x6, starting transfers between devices: 36.6 us -> 22.7 us  [the longest x1 14.4 us: shards(): load = packed(lax.ppermute(load_modes, swapped, SWAP))]
    ppermute x5 -> x6, waiting for transfers between devices: 18.7 us -> 27.7 us  [the longest x1 17.3 us: shards(): total = lax.ppermute(by_slab, swapped, SWAP)]
    all_to_all x1, waiting for transfers between devices: 0.01 us -> 6.44 us  [shards(): u = lax.all_to_all(copies, GROUPS, 0, 0, tiled=True)]
    all_to_all x2, blocking collectives: 18 us -> 22.6 us  [shards(): q = lax.all_to_all(sent, WITHIN, 0, 0, tiled=True)]
    all_to_all x2, blocking collectives: 51.2 us -> 46.8 us  [shards(): mom = lax.all_to_all(mom, CHUNKS, 0, 0, tiled=True)]
  transfers between devices with their start and end apart: 10 -> 11, of which waited for: 7 -> 7; matrix products, arithmetic and copies ran while one was open for 0% -> 0% of each run, Pallas kernels for 0% -> 0%
where the time goes in v6:
time: 191 us; the launch traced here: 190 us
  blocking collectives  102 us (53%)
  waiting for transfers between devices  43.9 us (23%)
  starting transfers between devices  34.3 us (18%)
  Pallas kernels  6.03 us (3%)
  other arithmetic  2.26 us (1%)
    all_to_all x2, blocking collectives, shards(): mom = lax.all_to_all(mom, CHUNKS, 0, 0, tiled=True)  46.8 us
    all_to_all x2, blocking collectives, shards(): q = lax.all_to_all(sent, WITHIN, 0, 0, tiled=True)  22.6 us
    all_to_all x2, blocking collectives, shards(): by_slab = lax.all_to_all(change, WITHIN, 0, 0, tiled=True)  18.8 us
    ppermute x1, waiting for transfers between devices, shards(): total = lax.ppermute(by_slab, swapped, SWAP)  17.3 us
    ppermute x1, starting transfers between devices, shards(): load = packed(lax.ppermute(load_modes, swapped, SWAP))  14.4 us
    all_to_all x1, blocking collectives, shards(): u = lax.all_to_all(copies, GROUPS, 0, 0, tiled=True)  13.8 us
    ppermute x1, waiting for transfers between devices, shards(): guess = packed(lax.ppermute(first_guess, swapped, SWAP))  10.4 us
    ppermute x2, waiting for transfers between devices, shards(): high = lax.ppermute(down, CHUNKS, line(4, -1))  9.43 us
  transfers between devices with their start and end apart: 11, of which 7 were waited for; matrix products, arithmetic and copies ran while one was open for 0% of the time, Pallas kernels for 0%

profile of v6, /device:TPU:41, one launch (start us, length us, event | category | flops | bytes accessed | tf_op | source)
XLA Modules:
  0.0 189.8 jit_solution(14678374375541005549)
XLA Ops:
  0.0 0.0 copy-start
  0.0 0.0 copy-start.2
  0.0 0.0 copy-start.1
  0.0 0.8 fusion
  0.8 0.0 copy-done.2
  0.8 0.7 broadcast_select_fusion.1
  1.5 0.7 collective-permute-start.3
  2.2 0.7 collective-permute-start.2
  2.9 14.4 %collective-permute-start.1 = (f32[12,3,1,4,128]{4,3,2,1,0:T(4,128)}, f32[12,3,1,4,128]{4,3,2,1,0:T(4,128)S(1)}, u32[]{:S(2)}, u32[]{:S(2)}) collective-permute-start(f32[12,3,1,4,128]{4,3,2,1,0:T(4,128)} %param.7), channel_id=1, source_target_pairs={{0,0},{16,256},{256,16},{272,272},{1,1},{17,257},{257,17},{273,273... | collective-permute-start | bytes 221192 | tf_op jit(solution)/shard_map/ppermute | solution.py:361
  17.3 0.0 copy-done.1
  17.3 1.9 %collective-permute-start = (f32[12,3,1,4,128]{4,3,2,1,0:T(4,128)S(1)}, f32[12,3,1,4,128]{4,3,2,1,0:T(4,128)S(1)}, u32[]{:S(2)}, u32[]{:S(2)}) collective-permute-start(f32[12,3,1,4,128]{4,3,2,1,0:T(4,128)S(1)} %copy-done.1), channel_id=1, source_target_pairs={{0,0},{16,256},{256,16},{272,272},{1,1},{17,257},{257,17},{273,273... | collective-permute-start | bytes 221192 | tf_op jit(solution)/shard_map/ppermute | solution.py:360
  19.3 0.0 copy-done
  19.3 0.1 constant_dynamic-slice_fusion
  19.4 0.1 copy.42
  19.4 0.0 copy-start.3
  19.4 0.0 copy-start.4
  19.5 0.7 copy-done.3
  20.1 0.0 copy-done.4
  20.1 0.1 constant_dynamic-slice_fusion.1
  20.2 0.1 copy.40
  20.3 0.0 collective-permute-done.3
  20.3 0.0 collective-permute-done.2
  20.3 1.3 collective-permute-start.4
  21.6 10.4 %collective-permute-done = f32[12,3,1,4,128]{4,3,2,1,0:T(4,128)S(1)} collective-permute-done((f32[12,3,1,4,128]{4,3,2,1,0:T(4,128)S(1)}, f32[12,3,1,4,128]{4,3,2,1,0:T(4,128)S(1)}, u32[]{:S(2)}, u32[]{:S(2)}) %collective-permute-start) | collective-permute-done | bytes 73760 | tf_op jit(solution)/shard_map/ppermute | solution.py:360
  32.1 0.9 shard_map.73
  32.9 5.2 %all-to-all-start = ((f32[8,144,128]{2,1,0:T(8,128)}), f32[8,144,128]{2,1,0:T(8,128)S(1)}, u32[]{:S(2)}, u32[]{:S(2)}) async-start(f32[8,144,128]{2,1,0:T(8,128)} %shard_map.73), calls=%async_computation | async-start | bytes 1179648 | tf_op jit(solution)/shard_map/all_to_all | solution.py:386
  38.1 0.1 pad_add_fusion
  38.2 0.1 copy.41
  38.3 0.0 collective-permute-done.1
  38.4 0.0 collective-permute-done.4
  38.4 6.4 %all-to-all-done.refs_0_ = f32[8,144,128]{2,1,0:T(8,128)S(1)} async-done(((f32[8,144,128]{2,1,0:T(8,128)}), f32[8,144,128]{2,1,0:T(8,128)S(1)}, u32[]{:S(2)}, u32[]{:S(2)}) %all-to-all-start) | async-done | bytes 589856 | tf_op jit(solution)/shard_map/all_to_all | solution.py:386
  44.8 1.4 shard_map.74
  46.3 14.3 %all_to_all.52.refs_0_ = f32[4,112,128]{2,1,0:T(8,128)S(1)} all-to-all(f32[4,112,128]{2,1,0:T(8,128)S(1)} %shard_map.74), channel_id=1, replica_groups=mesh['zh'=2,'x'=4,'y1'=2,'y0'=2,'zp'=4,'zq'=2,'c'=2] {'zq','c'}, dimensions={0} | all-to-all | bytes 458752 | tf_op jit(solution)/shard_map/all_to_all | solution.py:400
  60.6 1.5 collective-permute-start.5
  62.1 1.3 collective-permute-start.6
  63.4 0.2 collective-permute-done.5.refs_2_
  63.6 4.7 %collective-permute-done.6.refs_3_ = f32[160,128]{1,0:T(8,128)S(1)} collective-permute-done((f32[160,128]{1,0:T(8,128)S(1)}, f32[160,128]{1,0:T(8,128)S(1)}, u32[]{:S(2)}, u32[]{:S(2)}) %collective-permute-start.6) | collective-permute-done | bytes 81952 | tf_op jit(solution)/shard_map/ppermute | solution.py:406
  68.3 0.7 shard_map.76
  69.0 25.7 %all_to_all.53 = f32[16,1,128]{2,1,0:T(1,128)S(1)} all-to-all(f32[16,1,128]{2,1,0:T(1,128)S(1)} %bitcast.28), channel_id=1, replica_groups=mesh['zh'=2,'x'=4,'y1'=2,'y0'=2,'zp'=4,'zq'=2,'c'=2] {'zh','y1','zp'}, dimensions={0} | all-to-all | bytes 16384 | tf_op jit(solution)/shard_map/all_to_all | solution.py:417
  94.7 0.2 shard_map.77
  94.9 8.8 %all_to_all.54.q = f32[4,36,128]{2,1,0:T(8,128)S(1)} all-to-all(f32[4,36,128]{2,1,0:T(8,128)S(1)} %get-tuple-element.31.refs_4_), channel_id=1, replica_groups=mesh['zh'=2,'x'=4,'y1'=2,'y0'=2,'zp'=4,'zq'=2,'c'=2] {'zq','c'}, dimensions={0} | all-to-all | bytes 147456 | tf_op jit(solution)/shard_map/all_to_all | solution.py:426
  103.8 0.1 shard_map.78
  103.8 13.8 %all_to_all.55.refs_0_ = f32[8,144,128]{2,1,0:T(8,128)S(1)} all-to-all(f32[8,144,128]{2,1,0:T(8,128)S(1)} %shard_map.78), channel_id=1, replica_groups=mesh['zh'=2,'x'=4,'y1'=2,'y0'=2,'zp'=4,'zq'=2,'c'=2] {'y0','x'}, dimensions={0} | all-to-all | bytes 1179648 | tf_op jit(solution)/shard_map/all_to_all | solution.py:386
  117.6 1.3 shard_map.79
  118.9 8.3 %all_to_all.56.refs_0_ = f32[4,112,128]{2,1,0:T(8,128)S(1)} all-to-all(f32[4,112,128]{2,1,0:T(8,128)S(1)} %shard_map.79), channel_id=1, replica_groups=mesh['zh'=2,'x'=4,'y1'=2,'y0'=2,'zp'=4,'zq'=2,'c'=2] {'zq','c'}, dimensions={0} | all-to-all | bytes 458752 | tf_op jit(solution)/shard_map/all_to_all | solution.py:400
  127.3 2.2 %collective-permute-start.7 = (f32[144,128]{1,0:T(8,128)S(1)}, f32[144,128]{1,0:T(8,128)S(1)}, u32[]{:S(2)}, u32[]{:S(2)}) collective-permute-start(f32[144,128]{1,0:T(8,128)S(1)} %get-tuple-element.34), channel_id=1, source_target_pairs={{0,4},{4,8},{8,12},{12,256},{256,260},{260,264},{264,268},{268,32}... | collective-permute-start | bytes 221192 | tf_op jit(solution)/shard_map/ppermute | solution.py:405
  129.5 1.3 collective-permute-start.8
  130.8 0.1 collective-permute-done.7.refs_2_
  130.9 4.7 %collective-permute-done.8.refs_3_ = f32[144,128]{1,0:T(8,128)S(1)} collective-permute-done((f32[144,128]{1,0:T(8,128)S(1)}, f32[144,128]{1,0:T(8,128)S(1)}, u32[]{:S(2)}, u32[]{:S(2)}) %collective-permute-start.8) | collective-permute-done | bytes 73760 | tf_op jit(solution)/shard_map/ppermute | solution.py:406
  135.6 1.2 shard_map.81
  136.8 21.1 %all_to_all.57 = f32[16,1,128]{2,1,0:T(1,128)S(1)} all-to-all(f32[16,1,128]{2,1,0:T(1,128)S(1)} %bitcast.29), channel_id=1, replica_groups=mesh['zh'=2,'x'=4,'y1'=2,'y0'=2,'zp'=4,'zq'=2,'c'=2] {'zh','y1','zp'}, dimensions={0} | all-to-all | bytes 16384 | tf_op jit(solution)/shard_map/all_to_all | solution.py:417
  157.9 0.2 shard_map.82
  158.1 9.9 %all_to_all.58 = f32[4,36,128]{2,1,0:T(8,128)S(1)} all-to-all(f32[4,36,128]{2,1,0:T(8,128)S(1)} %shard_map.82), channel_id=1, replica_groups=mesh['zh'=2,'x'=4,'y1'=2,'y0'=2,'zp'=4,'zq'=2,'c'=2] {'zq','c'}, dimensions={0} | all-to-all | bytes 147456 | tf_op jit(solution)/shard_map/all_to_all | solution.py:426
  168.0 3.8 %collective-permute-start.9 = (f32[4,36,128]{2,1,0:T(8,128)S(1)}, f32[4,36,128]{2,1,0:T(8,128)S(1)}, u32[]{:S(2)}, u32[]{:S(2)}) collective-permute-start(f32[4,36,128]{2,1,0:T(8,128)S(1)} %all_to_all.58), channel_id=1, source_target_pairs={{0,0},{16,256},{256,16},{272,272},{1,1},{17,257},{257,17},{273,273... | collective-permute-start | bytes 221192 | tf_op jit(solution)/shard_map/ppermute | solution.py:427
  171.8 17.3 %collective-permute-done.9 = f32[4,36,128]{2,1,0:T(8,128)S(1)} collective-permute-done((f32[4,36,128]{2,1,0:T(8,128)S(1)}, f32[4,36,128]{2,1,0:T(8,128)S(1)}, u32[]{:S(2)}, u32[]{:S(2)}) %collective-permute-start.9) | collective-permute-done | bytes 73760 | tf_op jit(solution)/shard_map/ppermute | solution.py:427
  189.2 0.7 bitcast_add_fusion
  (18 shorter events, 0.2 us)
Async XLA Ops:
  0.0 19.3 %copy-start = (f32[96,8]{0,1:T(8,128)S(1)}, f32[96,8]{0,1:T(8,128)}, u32[]{:S(2)}) copy-start(f32[96,8]{0,1:T(8,128)} %param.13) | copy-start | bytes 9220
  0.0 0.8 copy-start.2
  0.0 17.3 %copy-start.1 = (f32[12,3,1,4,128]{4,3,2,1,0:T(4,128)S(1)}, f32[12,3,1,4,128]{4,3,2,1,0:T(4,128)}, u32[]{:S(2)}) copy-start(f32[12,3,1,4,128]{4,3,2,1,0:T(4,128)} %param.8) | copy-start | bytes 221188
  1.5 18.8 %collective-permute-start.3 = (f32[36,128]{1,0:T(8,128)S(1)}, f32[36,128]{1,0:T(8,128)S(1)}, u32[]{:S(2)}, u32[]{:S(2)}) collective-permute-start(f32[36,128]{1,0:T(8,128)S(1)} %reshape.40), channel_id=1, source_target_pairs={{1,0},{2,1},{3,2},{4,3},{5,4},{6,5},{7,6},{8,7},{9,8},{10,9},{11,1... | collective-permute-start | bytes 55304 | tf_op jit(solution)/shard_map/ppermute | solution.py:363
  2.2 18.1 %collective-permute-start.2 = (f32[36,128]{1,0:T(8,128)S(1)}, f32[36,128]{1,0:T(8,128)S(1)}, u32[]{:S(2)}, u32[]{:S(2)}) collective-permute-start(f32[36,128]{1,0:T(8,128)S(1)} %reshape.40), channel_id=1, source_target_pairs={{0,1},{1,2},{2,3},{3,4},{4,5},{5,6},{6,7},{7,8},{8,9},{9,10},{10,1... | collective-permute-start | bytes 55304 | tf_op jit(solution)/shard_map/ppermute | solution.py:362
  2.9 35.4 %collective-permute-start.1 = (f32[12,3,1,4,128]{4,3,2,1,0:T(4,128)}, f32[12,3,1,4,128]{4,3,2,1,0:T(4,128)S(1)}, u32[]{:S(2)}, u32[]{:S(2)}) collective-permute-start(f32[12,3,1,4,128]{4,3,2,1,0:T(4,128)} %param.7), channel_id=1, source_target_pairs={{0,0},{16,256},{256,16},{272,272},{1,1},{17,257},{257,17},{273,273... | collective-permute-start | bytes 221192 | tf_op jit(solution)/shard_map/ppermute | solution.py:361
  17.3 14.7 %collective-permute-start = (f32[12,3,1,4,128]{4,3,2,1,0:T(4,128)S(1)}, f32[12,3,1,4,128]{4,3,2,1,0:T(4,128)S(1)}, u32[]{:S(2)}, u32[]{:S(2)}) collective-permute-start(f32[12,3,1,4,128]{4,3,2,1,0:T(4,128)S(1)} %copy-done.1), channel_id=1, source_target_pairs={{0,0},{16,256},{256,16},{272,272},{1,1},{17,257},{257,17},{273,273... | collective-permute-start | bytes 221192 | tf_op jit(solution)/shard_map/ppermute | solution.py:360
  19.4 0.7 copy-start.3
  19.4 0.7 copy-start.4
  20.3 18.0 %collective-permute-start.4 = (f32[108,128]{1,0:T(8,128)S(1)}, f32[108,128]{1,0:T(8,128)S(1)}, u32[]{:S(2)}, u32[]{:S(2)}) collective-permute-start(f32[108,128]{1,0:T(8,128)S(1)} %pad_maximum_fusion), channel_id=1, source_target_pairs={{0,16},{272,256},{1,17},{273,257},{2,18},{274,258},{3,19},{275,259... | collective-permute-start | bytes 165896 | tf_op jit(solution)/shard_map/ppermute | solution.py:366
  32.9 11.9 %all-to-all-start = ((f32[8,144,128]{2,1,0:T(8,128)}), f32[8,144,128]{2,1,0:T(8,128)S(1)}, u32[]{:S(2)}, u32[]{:S(2)}) async-start(f32[8,144,128]{2,1,0:T(8,128)} %shard_map.73), calls=%async_computation | async-start | bytes 1179648 | tf_op jit(solution)/shard_map/all_to_all | solution.py:386
  60.6 3.0 %collective-permute-start.5 = (f32[160,128]{1,0:T(8,128)S(1)}, f32[160,128]{1,0:T(8,128)S(1)}, u32[]{:S(2)}, u32[]{:S(2)}) collective-permute-start(f32[160,128]{1,0:T(8,128)S(1)} %get-tuple-element.24), channel_id=1, source_target_pairs={{0,4},{4,8},{8,12},{12,256},{256,260},{260,264},{264,268},{268,32}... | collective-permute-start | bytes 245768 | tf_op jit(solution)/shard_map/ppermute | solution.py:405
  62.1 6.2 %collective-permute-start.6 = (f32[160,128]{1,0:T(8,128)S(1)}, f32[160,128]{1,0:T(8,128)S(1)}, u32[]{:S(2)}, u32[]{:S(2)}) collective-permute-start(f32[160,128]{1,0:T(8,128)S(1)} %get-tuple-element.25), channel_id=1, source_target_pairs={{4,0},{8,4},{12,8},{256,12},{260,256},{264,260},{268,264},{32,268}... | collective-permute-start | bytes 245768 | tf_op jit(solution)/shard_map/ppermute | solution.py:406
  127.3 3.6 %collective-permute-start.7 = (f32[144,128]{1,0:T(8,128)S(1)}, f32[144,128]{1,0:T(8,128)S(1)}, u32[]{:S(2)}, u32[]{:S(2)}) collective-permute-start(f32[144,128]{1,0:T(8,128)S(1)} %get-tuple-element.34), channel_id=1, source_target_pairs={{0,4},{4,8},{8,12},{12,256},{256,260},{260,264},{264,268},{268,32}... | collective-permute-start | bytes 221192 | tf_op jit(solution)/shard_map/ppermute | solution.py:405
  129.5 6.1 %collective-permute-start.8 = (f32[144,128]{1,0:T(8,128)S(1)}, f32[144,128]{1,0:T(8,128)S(1)}, u32[]{:S(2)}, u32[]{:S(2)}) collective-permute-start(f32[144,128]{1,0:T(8,128)S(1)} %get-tuple-element.35), channel_id=1, source_target_pairs={{4,0},{8,4},{12,8},{256,12},{260,256},{264,260},{268,264},{32,268}... | collective-permute-start | bytes 221192 | tf_op jit(solution)/shard_map/ppermute | solution.py:406
  168.0 21.1 %collective-permute-start.9 = (f32[4,36,128]{2,1,0:T(8,128)S(1)}, f32[4,36,128]{2,1,0:T(8,128)S(1)}, u32[]{:S(2)}, u32[]{:S(2)}) collective-permute-start(f32[4,36,128]{2,1,0:T(8,128)S(1)} %all_to_all.58), channel_id=1, source_target_pairs={{0,0},{16,256},{256,16},{272,272},{1,1},{17,257},{257,17},{273,273... | collective-permute-start | bytes 221192 | tf_op jit(solution)/shard_map/ppermute | solution.py:427

commit v7 on v6

--- a/solution.py
+++ b/solution.py
@@ -358,9 +358,10 @@
     moduli = jnp.concatenate([varying, mean[None]], 0).reshape((NK + 1) * NY, NZ)
     swapped = ("zh", "y0")
     guess = packed(lax.ppermute(first_guess, swapped, SWAP))
-    load = packed(lax.ppermute(load_modes, swapped, SWAP))
     em = lax.ppermute(moduli, SLABS, line(16, 1, True))
     ep = lax.ppermute(moduli, SLABS, line(16, -1, True))
+    em, ep, later = lax.optimization_barrier((em, ep, load_modes))
+    load = packed(lax.ppermute(later, swapped, SWAP))
     held = lax.axis_index("zh") == lax.axis_index("y0")
     three = jnp.concatenate([moduli, em, ep], 0)
     three = jnp.where(held, three, lax.ppermute(three, swapped, [(0, 1), (3, 2)]))

time: 191 us -> 193 us (1.010)
  waiting for transfers between devices: 43.9 us -> 33.9 us
  starting transfers between devices: 34.3 us -> 43.7 us
  blocking collectives: 102 us -> 104 us
    ppermute x1, starting transfers between devices: 1.92 us -> 14.4 us  [shards(): guess = packed(lax.ppermute(first_guess, swapped, SWAP))]
    ppermute x1, waiting for transfers between devices: 10.4 us -> 0.01 us  [shards(): guess = packed(lax.ppermute(first_guess, swapped, SWAP))]
    all_to_all x1, waiting for transfers between devices: 6.44 us -> 0.01 us  [shards(): u = lax.all_to_all(copies, GROUPS, 0, 0, tiled=True)]
    ppermute x1, waiting for transfers between devices: 0.01 us -> 4.43 us  [shards(): load = packed(lax.ppermute(later, swapped, SWAP))]
    ppermute x1, starting transfers between devices: 14.4 us -> 10.2 us  [shards(): load = packed(lax.ppermute(later, swapped, SWAP))]
    all_to_all x1, blocking collectives: 13.8 us -> 17.3 us  [shards(): u = lax.all_to_all(copies, GROUPS, 0, 0, tiled=True)]
    ppermute x2, waiting for transfers between devices: 9.43 us -> 11.9 us  [shards(): high = lax.ppermute(down, CHUNKS, line(4, -1))]
    all_to_all x2, blocking collectives: 46.8 us -> 44.7 us  [shards(): mom = lax.all_to_all(mom, CHUNKS, 0, 0, tiled=True)]
  transfers between devices with their start and end apart: 11 -> 11, of which waited for: 7 -> 6; matrix products, arithmetic and copies ran while one was open for 0% -> 0% of each run, Pallas kernels for 0% -> 0%
where the time goes in v7:
time: 193 us; the launch traced here: 192 us
  blocking collectives  104 us (54%)
  starting transfers between devices  43.7 us (23%)
  waiting for transfers between devices  33.9 us (18%)
  Pallas kernels  6.01 us (3%)
  other arithmetic  2.26 us (1%)
  local copies, waits for them, and re-layouts  1.93 us (1%)
    all_to_all x2, blocking collectives, shards(): mom = lax.all_to_all(mom, CHUNKS, 0, 0, tiled=True)  44.7 us
    all_to_all x2, blocking collectives, shards(): q = lax.all_to_all(sent, WITHIN, 0, 0, tiled=True)  21.9 us
    all_to_all x2, blocking collectives, shards(): by_slab = lax.all_to_all(change, WITHIN, 0, 0, tiled=True)  20 us
    all_to_all x1, blocking collectives, shards(): u = lax.all_to_all(copies, GROUPS, 0, 0, tiled=True)  17.3 us
    ppermute x1, waiting for transfers between devices, shards(): total = lax.ppermute(by_slab, swapped, SWAP)  17.3 us
    ppermute x1, starting transfers between devices, shards(): guess = packed(lax.ppermute(first_guess, swapped, SWAP))  14.4 us
    ppermute x2, waiting for transfers between devices, shards(): high = lax.ppermute(down, CHUNKS, line(4, -1))  11.9 us
    ppermute x1, starting transfers between devices, shards(): load = packed(lax.ppermute(later, swapped, SWAP))  10.2 us
  transfers between devices with their start and end apart: 11, of which 6 were waited for; matrix products, arithmetic and copies ran while one was open for 0% of the time, Pallas kernels for 0%

profile of v7, /device:TPU:41, one launch (start us, length us, event | category | flops | bytes accessed | tf_op | source)
XLA Modules:
  0.0 192.0 jit_solution(18351699828342201318)
XLA Ops:
  0.0 0.0 copy-start
  0.0 0.0 copy-start.2
  0.0 0.0 copy-start.1
  0.0 0.8 fusion
  0.8 0.0 copy-done.2
  0.8 0.7 broadcast_select_fusion.1
  1.5 0.7 collective-permute-start.2
  2.2 0.7 collective-permute-start.1
  2.9 0.0 copy-done.1
  2.9 14.4 %collective-permute-start = (f32[12,3,1,4,128]{4,3,2,1,0:T(4,128)S(1)}, f32[12,3,1,4,128]{4,3,2,1,0:T(4,128)S(1)}, u32[]{:S(2)}, u32[]{:S(2)}) collective-permute-start(f32[12,3,1,4,128]{4,3,2,1,0:T(4,128)S(1)} %copy-done.1), channel_id=1, source_target_pairs={{0,0},{16,256},{256,16},{272,272},{1,1},{17,257},{257,17},{273,273... | collective-permute-start | bytes 221192 | tf_op jit(solution)/shard_map/ppermute | solution.py:360
  17.3 0.0 copy-done
  17.3 0.1 constant_dynamic-slice_fusion
  17.4 0.1 copy.42
  17.5 0.0 copy-start.3
  17.5 0.0 copy-start.4
  17.5 0.7 copy-done.3
  18.2 0.0 copy-done.4
  18.2 0.1 constant_dynamic-slice_fusion.1
  18.3 0.1 copy.40
  18.4 0.0 collective-permute-done.2
  18.4 0.0 collective-permute-done.1
  18.4 1.3 collective-permute-start.4
  19.7 0.0 collective-permute-done
  19.7 0.9 shard_map.73
  20.6 6.1 %all-to-all-start = ((f32[8,144,128]{2,1,0:T(8,128)}), f32[8,144,128]{2,1,0:T(8,128)S(1)}, u32[]{:S(2)}, u32[]{:S(2)}) async-start(f32[8,144,128]{2,1,0:T(8,128)} %shard_map.73), calls=%async_computation | async-start | bytes 1179648 | tf_op jit(solution)/shard_map/all_to_all | solution.py:387
  26.7 0.0 copy-start.5
  26.7 0.1 pad_add_fusion
  26.8 0.1 copy.41
  26.9 0.7 copy-done.5
  27.6 10.2 %collective-permute-start.3 = (f32[12,3,1,4,128]{4,3,2,1,0:T(4,128)S(1)}, f32[12,3,1,4,128]{4,3,2,1,0:T(4,128)S(1)}, u32[]{:S(2)}, u32[]{:S(2)}) collective-permute-start(f32[12,3,1,4,128]{4,3,2,1,0:T(4,128)S(1)} %copy-done.5), channel_id=1, source_target_pairs={{0,0},{16,256},{256,16},{272,272},{1,1},{17,257},{257,17},{273,273... | collective-permute-start | bytes 221192 | tf_op jit(solution)/shard_map/ppermute | solution.py:364
  37.8 0.0 collective-permute-done.4
  37.9 4.4 %collective-permute-done.3 = f32[12,3,1,4,128]{4,3,2,1,0:T(4,128)S(1)} collective-permute-done((f32[12,3,1,4,128]{4,3,2,1,0:T(4,128)S(1)}, f32[12,3,1,4,128]{4,3,2,1,0:T(4,128)S(1)}, u32[]{:S(2)}, u32[]{:S(2)}) %collective-permute-start.3) | collective-permute-done | bytes 73760 | tf_op jit(solution)/shard_map/ppermute | solution.py:364
  42.3 0.0 all-to-all-done.refs_0_
  42.3 1.4 shard_map.74
  43.8 12.5 %all_to_all.52.refs_0_ = f32[4,112,128]{2,1,0:T(8,128)S(1)} all-to-all(f32[4,112,128]{2,1,0:T(8,128)S(1)} %shard_map.74), channel_id=1, replica_groups=mesh['zh'=2,'x'=4,'y1'=2,'y0'=2,'zp'=4,'zq'=2,'c'=2] {'zq','c'}, dimensions={0} | all-to-all | bytes 458752 | tf_op jit(solution)/shard_map/all_to_all | solution.py:401
  56.3 1.8 collective-permute-start.5
  58.1 1.3 collective-permute-start.6
  59.4 0.2 collective-permute-done.5.refs_2_
  59.6 7.2 %collective-permute-done.6.refs_3_ = f32[160,128]{1,0:T(8,128)S(1)} collective-permute-done((f32[160,128]{1,0:T(8,128)S(1)}, f32[160,128]{1,0:T(8,128)S(1)}, u32[]{:S(2)}, u32[]{:S(2)}) %collective-permute-start.6) | collective-permute-done | bytes 81952 | tf_op jit(solution)/shard_map/ppermute | solution.py:407
  66.8 0.7 shard_map.76
  67.4 23.6 %all_to_all.53 = f32[16,1,128]{2,1,0:T(1,128)S(1)} all-to-all(f32[16,1,128]{2,1,0:T(1,128)S(1)} %bitcast.28), channel_id=1, replica_groups=mesh['zh'=2,'x'=4,'y1'=2,'y0'=2,'zp'=4,'zq'=2,'c'=2] {'zh','y1','zp'}, dimensions={0} | all-to-all | bytes 16384 | tf_op jit(solution)/shard_map/all_to_all | solution.py:418
  91.0 0.2 shard_map.77
  91.2 10.1 %all_to_all.54.q = f32[4,36,128]{2,1,0:T(8,128)S(1)} all-to-all(f32[4,36,128]{2,1,0:T(8,128)S(1)} %get-tuple-element.37.refs_4_), channel_id=1, replica_groups=mesh['zh'=2,'x'=4,'y1'=2,'y0'=2,'zp'=4,'zq'=2,'c'=2] {'zq','c'}, dimensions={0} | all-to-all | bytes 147456 | tf_op jit(solution)/shard_map/all_to_all | solution.py:427
  101.3 0.1 shard_map.78
  101.4 17.3 %all_to_all.55.refs_0_ = f32[8,144,128]{2,1,0:T(8,128)S(1)} all-to-all(f32[8,144,128]{2,1,0:T(8,128)S(1)} %shard_map.78), channel_id=1, replica_groups=mesh['zh'=2,'x'=4,'y1'=2,'y0'=2,'zp'=4,'zq'=2,'c'=2] {'y0','x'}, dimensions={0} | all-to-all | bytes 1179648 | tf_op jit(solution)/shard_map/all_to_all | solution.py:387
  118.7 1.3 shard_map.79
  120.0 9.4 %all_to_all.56.refs_0_ = f32[4,112,128]{2,1,0:T(8,128)S(1)} all-to-all(f32[4,112,128]{2,1,0:T(8,128)S(1)} %shard_map.79), channel_id=1, replica_groups=mesh['zh'=2,'x'=4,'y1'=2,'y0'=2,'zp'=4,'zq'=2,'c'=2] {'zq','c'}, dimensions={0} | all-to-all | bytes 458752 | tf_op jit(solution)/shard_map/all_to_all | solution.py:401
  129.5 2.2 %collective-permute-start.7 = (f32[144,128]{1,0:T(8,128)S(1)}, f32[144,128]{1,0:T(8,128)S(1)}, u32[]{:S(2)}, u32[]{:S(2)}) collective-permute-start(f32[144,128]{1,0:T(8,128)S(1)} %get-tuple-element.40), channel_id=1, source_target_pairs={{0,4},{4,8},{8,12},{12,256},{256,260},{260,264},{264,268},{268,32}... | collective-permute-start | bytes 221192 | tf_op jit(solution)/shard_map/ppermute | solution.py:406
  131.7 1.3 collective-permute-start.8
  133.0 0.1 collective-permute-done.7.refs_2_
  133.1 4.7 %collective-permute-done.8.refs_3_ = f32[144,128]{1,0:T(8,128)S(1)} collective-permute-done((f32[144,128]{1,0:T(8,128)S(1)}, f32[144,128]{1,0:T(8,128)S(1)}, u32[]{:S(2)}, u32[]{:S(2)}) %collective-permute-start.8) | collective-permute-done | bytes 73760 | tf_op jit(solution)/shard_map/ppermute | solution.py:407
  137.8 1.2 shard_map.81
  139.0 21.1 %all_to_all.57 = f32[16,1,128]{2,1,0:T(1,128)S(1)} all-to-all(f32[16,1,128]{2,1,0:T(1,128)S(1)} %bitcast.29), channel_id=1, replica_groups=mesh['zh'=2,'x'=4,'y1'=2,'y0'=2,'zp'=4,'zq'=2,'c'=2] {'zh','y1','zp'}, dimensions={0} | all-to-all | bytes 16384 | tf_op jit(solution)/shard_map/all_to_all | solution.py:418
  160.1 0.2 shard_map.82
  160.3 9.9 %all_to_all.58 = f32[4,36,128]{2,1,0:T(8,128)S(1)} all-to-all(f32[4,36,128]{2,1,0:T(8,128)S(1)} %shard_map.82), channel_id=1, replica_groups=mesh['zh'=2,'x'=4,'y1'=2,'y0'=2,'zp'=4,'zq'=2,'c'=2] {'zq','c'}, dimensions={0} | all-to-all | bytes 147456 | tf_op jit(solution)/shard_map/all_to_all | solution.py:427
  170.2 3.8 %collective-permute-start.9 = (f32[4,36,128]{2,1,0:T(8,128)S(1)}, f32[4,36,128]{2,1,0:T(8,128)S(1)}, u32[]{:S(2)}, u32[]{:S(2)}) collective-permute-start(f32[4,36,128]{2,1,0:T(8,128)S(1)} %all_to_all.58), channel_id=1, source_target_pairs={{0,0},{16,256},{256,16},{272,272},{1,1},{17,257},{257,17},{273,273... | collective-permute-start | bytes 221192 | tf_op jit(solution)/shard_map/ppermute | solution.py:428
  174.0 17.3 %collective-permute-done.9 = f32[4,36,128]{2,1,0:T(8,128)S(1)} collective-permute-done((f32[4,36,128]{2,1,0:T(8,128)S(1)}, f32[4,36,128]{2,1,0:T(8,128)S(1)}, u32[]{:S(2)}, u32[]{:S(2)}) %collective-permute-start.9) | collective-permute-done | bytes 73760 | tf_op jit(solution)/shard_map/ppermute | solution.py:428
  191.4 0.7 bitcast_add_fusion
  (18 shorter events, 0.2 us)
Async XLA Ops:
  0.0 17.3 %copy-start = (f32[96,8]{0,1:T(8,128)S(1)}, f32[96,8]{0,1:T(8,128)}, u32[]{:S(2)}) copy-start(f32[96,8]{0,1:T(8,128)} %param.13) | copy-start | bytes 9220
  0.0 0.8 copy-start.2
  0.0 2.9 %copy-start.1 = (f32[12,3,1,4,128]{4,3,2,1,0:T(4,128)S(1)}, f32[12,3,1,4,128]{4,3,2,1,0:T(4,128)}, u32[]{:S(2)}) copy-start(f32[12,3,1,4,128]{4,3,2,1,0:T(4,128)} %param.8) | copy-start | bytes 221188
  1.5 16.9 %collective-permute-start.2 = (f32[36,128]{1,0:T(8,128)S(1)}, f32[36,128]{1,0:T(8,128)S(1)}, u32[]{:S(2)}, u32[]{:S(2)}) collective-permute-start(f32[36,128]{1,0:T(8,128)S(1)} %reshape.39), channel_id=1, source_target_pairs={{1,0},{2,1},{3,2},{4,3},{5,4},{6,5},{7,6},{8,7},{9,8},{10,9},{11,1... | collective-permute-start | bytes 55304 | tf_op jit(solution)/shard_map/ppermute | solution.py:362
  2.2 16.2 %collective-permute-start.1 = (f32[36,128]{1,0:T(8,128)S(1)}, f32[36,128]{1,0:T(8,128)S(1)}, u32[]{:S(2)}, u32[]{:S(2)}) collective-permute-start(f32[36,128]{1,0:T(8,128)S(1)} %reshape.39), channel_id=1, source_target_pairs={{0,1},{1,2},{2,3},{3,4},{4,5},{5,6},{6,7},{7,8},{8,9},{9,10},{10,1... | collective-permute-start | bytes 55304 | tf_op jit(solution)/shard_map/ppermute | solution.py:361
  2.9 16.8 %collective-permute-start = (f32[12,3,1,4,128]{4,3,2,1,0:T(4,128)S(1)}, f32[12,3,1,4,128]{4,3,2,1,0:T(4,128)S(1)}, u32[]{:S(2)}, u32[]{:S(2)}) collective-permute-start(f32[12,3,1,4,128]{4,3,2,1,0:T(4,128)S(1)} %copy-done.1), channel_id=1, source_target_pairs={{0,0},{16,256},{256,16},{272,272},{1,1},{17,257},{257,17},{273,273... | collective-permute-start | bytes 221192 | tf_op jit(solution)/shard_map/ppermute | solution.py:360
  17.5 0.7 copy-start.3
  17.5 0.7 copy-start.4
  18.4 19.4 %collective-permute-start.4 = (f32[108,128]{1,0:T(8,128)S(1)}, f32[108,128]{1,0:T(8,128)S(1)}, u32[]{:S(2)}, u32[]{:S(2)}) collective-permute-start(f32[108,128]{1,0:T(8,128)S(1)} %pad_maximum_fusion), channel_id=1, source_target_pairs={{0,16},{272,256},{1,17},{273,257},{2,18},{274,258},{3,19},{275,259... | collective-permute-start | bytes 165896 | tf_op jit(solution)/shard_map/ppermute | solution.py:367
  20.6 21.7 %all-to-all-start = ((f32[8,144,128]{2,1,0:T(8,128)}), f32[8,144,128]{2,1,0:T(8,128)S(1)}, u32[]{:S(2)}, u32[]{:S(2)}) async-start(f32[8,144,128]{2,1,0:T(8,128)} %shard_map.73), calls=%async_computation | async-start | bytes 1179648 | tf_op jit(solution)/shard_map/all_to_all | solution.py:387
  26.7 0.9 copy-start.5
  27.6 14.7 %collective-permute-start.3 = (f32[12,3,1,4,128]{4,3,2,1,0:T(4,128)S(1)}, f32[12,3,1,4,128]{4,3,2,1,0:T(4,128)S(1)}, u32[]{:S(2)}, u32[]{:S(2)}) collective-permute-start(f32[12,3,1,4,128]{4,3,2,1,0:T(4,128)S(1)} %copy-done.5), channel_id=1, source_target_pairs={{0,0},{16,256},{256,16},{272,272},{1,1},{17,257},{257,17},{273,273... | collective-permute-start | bytes 221192 | tf_op jit(solution)/shard_map/ppermute | solution.py:364
  56.3 3.3 %collective-permute-start.5 = (f32[160,128]{1,0:T(8,128)S(1)}, f32[160,128]{1,0:T(8,128)S(1)}, u32[]{:S(2)}, u32[]{:S(2)}) collective-permute-start(f32[160,128]{1,0:T(8,128)S(1)} %get-tuple-element.30), channel_id=1, source_target_pairs={{0,4},{4,8},{8,12},{12,256},{256,260},{260,264},{264,268},{268,32}... | collective-permute-start | bytes 245768 | tf_op jit(solution)/shard_map/ppermute | solution.py:406
  58.1 8.7 %collective-permute-start.6 = (f32[160,128]{1,0:T(8,128)S(1)}, f32[160,128]{1,0:T(8,128)S(1)}, u32[]{:S(2)}, u32[]{:S(2)}) collective-permute-start(f32[160,128]{1,0:T(8,128)S(1)} %get-tuple-element.31), channel_id=1, source_target_pairs={{4,0},{8,4},{12,8},{256,12},{260,256},{264,260},{268,264},{32,268}... | collective-permute-start | bytes 245768 | tf_op jit(solution)/shard_map/ppermute | solution.py:407
  129.5 3.6 %collective-permute-start.7 = (f32[144,128]{1,0:T(8,128)S(1)}, f32[144,128]{1,0:T(8,128)S(1)}, u32[]{:S(2)}, u32[]{:S(2)}) collective-permute-start(f32[144,128]{1,0:T(8,128)S(1)} %get-tuple-element.40), channel_id=1, source_target_pairs={{0,4},{4,8},{8,12},{12,256},{256,260},{260,264},{264,268},{268,32}... | collective-permute-start | bytes 221192 | tf_op jit(solution)/shard_map/ppermute | solution.py:406
  131.7 6.1 %collective-permute-start.8 = (f32[144,128]{1,0:T(8,128)S(1)}, f32[144,128]{1,0:T(8,128)S(1)}, u32[]{:S(2)}, u32[]{:S(2)}) collective-permute-start(f32[144,128]{1,0:T(8,128)S(1)} %get-tuple-element.41), channel_id=1, source_target_pairs={{4,0},{8,4},{12,8},{256,12},{260,256},{264,260},{268,264},{32,268}... | collective-permute-start | bytes 221192 | tf_op jit(solution)/shard_map/ppermute | solution.py:407
  170.2 21.1 %collective-permute-start.9 = (f32[4,36,128]{2,1,0:T(8,128)S(1)}, f32[4,36,128]{2,1,0:T(8,128)S(1)}, u32[]{:S(2)}, u32[]{:S(2)}) collective-permute-start(f32[4,36,128]{2,1,0:T(8,128)S(1)} %all_to_all.58), channel_id=1, source_target_pairs={{0,0},{16,256},{256,16},{272,272},{1,1},{17,257},{257,17},{273,273... | collective-permute-start | bytes 221192 | tf_op jit(solution)/shard_map/ppermute | solution.py:428

commit v8 on v3

--- a/solution.py
+++ b/solution.py
@@ -9,20 +9,32 @@
 from jax.sharding import PartitionSpec as P
 
 AXES = ("zh", "x", "y", "zp", "zq", "c")
-SLABS = ("y", "zp", "zq", "c")
+SLABS = ("zh", "y", "zp", "zq", "c")
+CHAIN = ("zh", "y", "zp")
 CHUNKS = ("y", "zp")
 WITHIN = ("zq", "c")
-NG, NM, NL, NK = 8, 12, 8, 8
+NX, NM, NT, NL, NK = 4, 12, 24, 8, 8
+MODES = 2 * NX * NM
 NY, NZ, SHIFT = 4, 128, 4.0
 QUAD = 4
 TRI = NM // QUAD
-ROWS = 3 * TRI
+SIX = 2 * TRI
+ROWS = 3 * SIX
 SLAB = NY * ROWS
+SENT = 3 * SLAB + 8
 F32 = jnp.float32
 
 
-def line(count, step):
-    return [(i, i + step) for i in range(count) if 0 <= i + step < count]
+def line(inner, step):
+    count = 4 * inner
+    pairs = []
+    for zh in range(2):
+        for i in range(count):
+            j = i + step
+            if 0 <= j < count:
+                other = zh ^ (i // inner != j // inner)
+                pairs.append((zh * count + i, other * count + j))
+    return pairs
 
 
 def call(kernel, outs, scratch=()):
@@ -50,8 +62,8 @@
         (u, load, e0, em, ep, partner, variable, weight, out, us, mx, fx, fy, fz) = refs
     else:
         (u, e0, em, ep, partner, variable, weight, out, us, mx, fx, fy, fz) = refs
-    for g in range(NG):
-        half, x = divmod(g, NG // 2)
+    for g in range(2 * NX):
+        half, x = divmod(g, NX)
         for y in range(NY):
             for c in range(3):
                 yc = y * 3 + c
@@ -60,9 +72,9 @@
                     us[yc, g * NM : (g + 1) * NM, :] = u[x, at : at + NM, :]
                     continue
                 for d in range(QUAD):
-                    at, to = half * SLAB + y * ROWS + c * TRI, g * NM + d * TRI
+                    at, to = y * ROWS + c * SIX + half * TRI, g * NM + d * TRI
                     us[yc, to : to + TRI, :] = u[x * QUAD + d, at : at + TRI, :]
-    lane = lax.broadcasted_iota(jnp.int32, (16, NG * NM), 1)
+    lane = lax.broadcasted_iota(jnp.int32, (NT, MODES), 1)
     pr, vr, wr = partner[...], variable[...], weight[...]
     links = NL + 1 if first else NL
     hit = [jnp.where(lane == pr[:, l : l + 1], wr[:, l : l + 1], 0.0) for l in range(links)]
@@ -108,7 +120,7 @@
             own = up = down = None
             for k in range(nk):
                 r = slice(k * NY + y, k * NY + y + 1)
-                rows = slice(k * 16, k * 16 + 16)
+                rows = slice(k * NT, (k + 1) * NT)
                 m = mx[y * 3 + c, rows, :]
                 t = fz[2 + c, r, :] * m
                 side = None
@@ -125,14 +137,15 @@
             if c == 0:
                 up, down = 2.0 * up, 2.0 * down
             yc = y * 3 + c
-            own = load[yc * NM : (yc + 1) * NM, :] - own[:NM] if first else -own[:NM]
+            own = load[yc * NT : (yc + 1) * NT, :] - own if first else -own
             for kind, val in enumerate((own, up, down)):
-                at = (kind * NY + y) * ROWS + c * TRI
+                at = (kind * NY + y) * ROWS + c * SIX
                 for d in range(QUAD):
-                    out[d, at : at + TRI, :] = val[d * TRI : (d + 1) * TRI]
-    tail = e[NK * NY : NK * NY + NY] if first else jnp.zeros((NY, NZ), F32)
+                    out[d, at : at + SIX, :] = val[d * SIX : (d + 1) * SIX]
+    zeros = jnp.zeros((NY, NZ), F32)
+    tail = jnp.concatenate([e[NK * NY : NK * NY + NY] if first else zeros, zeros], axis=0)
     for d in range(QUAD):
-        out[d, 3 * SLAB : 3 * SLAB + NY, :] = tail
+        out[d, 3 * SLAB : SENT, :] = tail
 
 
 def edges_kernel(first, *refs):
@@ -181,9 +194,9 @@
         return ref[at + y * ROWS : at + (y + 1) * ROWS, :]
 
     rid = lax.broadcasted_iota(jnp.int32, (ROWS, NZ), 0)
-    wx = jnp.where(rid < TRI, 2.0, 1.0)
-    wy = jnp.where((rid >= TRI) & (rid < 2 * TRI), 2.0, 1.0)
-    wz = jnp.where(rid >= 2 * TRI, 2.0, 1.0)
+    wx = jnp.where(rid < SIX, 2.0, 1.0)
+    wy = jnp.where((rid >= SIX) & (rid < 2 * SIX), 2.0, 1.0)
+    wz = jnp.where(rid >= 2 * SIX, 2.0, 1.0)
     lane1 = lax.broadcasted_iota(jnp.int32, (1, NZ), 1)
     em = [[ec[p * NY + y : p * NY + y + 1, :] for y in range(NY)] for p in range(10)]
     zero = jnp.zeros((1, NZ), F32)
@@ -266,7 +279,7 @@
             for j, val in enumerate((a * a, a * b, b * b, b * d, d * d, d * t)):
                 sums[j] = val if sums[j] is None else sums[j] + val
     lane = lax.broadcasted_iota(jnp.int32, (ROWS, NZ), 1)
-    spot = lane - 8 * (rid % TRI)
+    spot = lane - 8 * (rid % SIX)
     packed = jnp.zeros((ROWS, NZ), F32)
     for j in range(6):
         packed = jnp.where(spot == j, jnp.sum(sums[j], axis=1, keepdims=True), packed)
@@ -308,11 +321,12 @@
     if first:
         mom, v0, v1, v2, v3, out, rest = refs
     else:
-        mom, v0, v1, v2, before, out = refs
+        mom, half, v0, v1, v2, before, out = refs
+        upper = half[...] > 0.0
     total = jnp.sum(mom[...], axis=0, keepdims=True)
     rid = lax.broadcasted_iota(jnp.int32, (ROWS, NZ), 0)
     lane = lax.broadcasted_iota(jnp.int32, (ROWS, NZ), 1)
-    spot = lane - 8 * (rid % TRI)
+    spot = lane - 8 * (rid % SIX)
     picked = [jnp.sum(jnp.where(spot == j, total, 0.0), axis=1, keepdims=True) for j in range(6)]
     x, r = step_coefficients(picked)
     x = [jnp.broadcast_to(s, (ROWS, NZ)) for s in x]
@@ -327,41 +341,56 @@
                 rest[s, rows, :] = r[0] * a + r[1] * b + r[2] * d + r[3] * v3[at]
             else:
                 change = change + before[s, rows, :]
+                for c in range(3):
+                    at = c * SIX
+                    pick = jnp.where(upper, change[at + TRI : at + SIX], change[at : at + TRI])
+                    to = (y * 3 + c) * TRI
+                    out[s, to : to + TRI, :] = pick
+                continue
             out[s, rows, :] = change
 
 
-def fan_kernel(blocks, near, far, out):
+def fan_kernel(blocks, field, out):
     for d in range(blocks):
-        both = jnp.concatenate([near[d], far[d]], axis=0)
-        for x in range(NG // 2):
-            out[x * blocks + d] = both
+        own = field[d]
+        for x in range(NX):
+            out[x * blocks + d] = own
 
 
 def packed(field):
-    return field[:, :, 0].transpose(2, 1, 0, 3).reshape(NY * 3 * NM, NZ)
+    return field.transpose(0, 3, 2, 1, 4).reshape(1, 2 * NY * 3 * NM, NZ)
+
+
+def by_target(field):
+    field = field.reshape(2, QUAD, TRI, 3, NY, NZ)
+    return field.transpose(4, 3, 1, 0, 2, 5).reshape(NY * 3 * NT, NZ)
+
+
+def rows_of(table, x):
+    table = lax.dynamic_index_in_dim(table.reshape(2, NX, QUAD, TRI, -1), x, 1, keepdims=False)
+    return table.transpose(1, 0, 2, 3).reshape(NT, -1)
 
 
 def shards(load_modes, first_guess, kl_fields, region_labels, partner, variable, weight):
-    mine = packed(first_guess)
-    mine, kl_fields, region_labels = lax.optimization_barrier((mine, kl_fields, region_labels))
     mean = jnp.where(region_labels == 0, 1.3, jnp.where(region_labels == 1, 1.0, 0.6)).astype(F32)
     varying = jnp.where(region_labels[None] == 1, kl_fields, 0.0)
-    e0 = jnp.concatenate([varying, mean[None]], 0).reshape((NK + 1) * NY, NZ)
-    em = lax.ppermute(e0, SLABS, line(64, 1))
-    ep = lax.ppermute(e0, SLABS, line(64, -1))
-    load = packed(load_modes)
-    swap = [(0, 1), (1, 0)]
-
-    half = lax.axis_index("zh") * (NG // 2 * NM)
-    offset = half + lax.axis_index("x") * NM
-    modes = NG * NM
-    own = offset - half + jnp.arange(NM, dtype=jnp.int32)[:, None]
-    pad = ((0, 16 - NM), (0, 0))
-    rows_partner = (lax.dynamic_slice_in_dim(partner, offset, NM, 0) + modes - half) % modes
-    rows_partner = jnp.pad(jnp.concatenate([rows_partner, own], 1), pad, constant_values=-1)
-    rows_variable = jnp.pad(lax.dynamic_slice_in_dim(variable, offset, NM, 0), pad)
-    rows_weight = lax.dynamic_slice_in_dim(weight, offset, NM, 0)
-    rows_weight = jnp.pad(jnp.concatenate([rows_weight, jnp.ones((NM, 1), F32)], 1), pad)
+    moduli = jnp.concatenate([varying, mean[None]], 0).reshape((NK + 1) * NY, NZ)
+    em = lax.ppermute(moduli, SLABS, line(16, 1))
+    ep = lax.ppermute(moduli, SLABS, line(16, -1))
+    e0 = moduli
+    mine = jnp.concatenate([first_guess, load_modes], 0)
+    far = lax.ppermute(mine, "zh", [(0, 1), (1, 0)])
+    zh, x = lax.axis_index("zh"), lax.axis_index("x")
+    lower = zh == 0
+    both = jnp.stack([jnp.where(lower, mine, far), jnp.where(lower, far, mine)])
+    both = both.reshape(2, 2, NM, 3, NY, NZ)
+    guess, load = packed(both[:, 0]), by_target(both[:, 1])
+    half = jnp.broadcast_to(zh.astype(F32), (TRI, NZ))
+
+    own = rows_of(jnp.arange(MODES, dtype=jnp.int32), x)
+    rows_partner = jnp.concatenate([rows_of(partner, x), own], 1)
+    rows_variable = rows_of(variable, x)
+    rows_weight = jnp.concatenate([rows_of(weight, x), jnp.ones((NT, 1), F32)], 1)
     links = (rows_partner, rows_variable, rows_weight)
 
     chunk, cells = (QUAD, SLAB, NZ), (QUAD * NY, ROWS, NZ)
@@ -369,20 +398,19 @@
         first = sweep == 0
         nk = NK + 1 if first else NK
         blocks = 1 if first else QUAD
-        mine = mine.reshape((blocks, -1, NZ))
-        far = lax.ppermute(mine, "zh", swap)
+        field = guess if first else change
         (copies,) = call(
-            functools.partial(fan_kernel, blocks), [(NG // 2 * blocks, 2 * mine.shape[1], NZ)]
-        )(mine, far)
+            functools.partial(fan_kernel, blocks), [(NX * blocks,) + field.shape[1:]]
+        )(field)
         u = lax.all_to_all(copies, ("x",) if first else ("x",) + WITHIN, 0, 0, tiled=True)
         fields = (u, load, e0, em, ep) if first else (u, e0, em, ep)
         face_rows = ((NK + 1) * NY, NZ)
         (sent,) = call(
             functools.partial(coupling_kernel, nk),
-            [(QUAD, 3 * SLAB + NY, NZ)],
+            [(QUAD, SENT, NZ)],
             [
-                (NY * 3, NG * NM, NZ),
-                (NY * 3, nk * 16, NZ),
+                (NY * 3, MODES, NZ),
+                (NY * 3, nk * NT, NZ),
                 (2,) + face_rows,
                 (2,) + face_rows,
                 (5,) + face_rows,
@@ -393,8 +421,8 @@
         chunk_r, up, down = call(functools.partial(edges_kernel, first), [chunk, edge, edge])(
             *((q,) if first else (q, rest))
         )
-        low = lax.ppermute(up, CHUNKS, line(16, 1))
-        high = lax.ppermute(down, CHUNKS, line(16, -1))
+        low = lax.ppermute(up, CHAIN, line(4, 1))
+        high = lax.ppermute(down, CHAIN, line(4, -1))
         scratch = [(10 * NY, ROWS, NZ)] * 4
         outs = [cells] * 4 + [(16, NZ)]
         if first:
@@ -411,18 +439,17 @@
                 mom, v0, v1, v2, v3
             )
         else:
-            (change,) = call(functools.partial(update_kernel, False), [chunk])(
-                mom, v0, v1, v2, change
-            )
-        mine = change
-    by_slab = lax.all_to_all(change, WITHIN, 0, 0, tiled=True)
-    total = by_slab.reshape(QUAD, NY, 3, TRI, NZ).transpose(0, 3, 2, 1, 4)
+            (total,) = call(
+                functools.partial(update_kernel, False), [(QUAD, NY * 3 * TRI, NZ)]
+            )(mom, half, v0, v1, v2, change)
+    total = lax.all_to_all(total, WITHIN, 0, 0, tiled=True)
+    total = total.reshape(QUAD, NY, 3, TRI, NZ).transpose(0, 3, 2, 1, 4)
     return first_guess + total.reshape(NM, 3, 1, NY, NZ)
 
 
 def solution(mesh):
     split = Mesh(mesh.devices.reshape(2, 4, 4, 4, 2, 2), AXES)
-    mode, space = ("zh", "x"), SLABS
+    mode, space = ("zh", "x"), ("y", "zp", "zq", "c")
     return jax.shard_map(
         shards,
         mesh=split,

time: 187 us -> 172 us (0.920)
  blocking collectives: 103 us -> 79.7 us
  waiting for transfers between devices: 31.9 us -> 40.4 us
  starting transfers between devices: 40.3 us -> 36.4 us
  Pallas kernels: 6.02 us -> 8.68 us
    all_to_all x2 -> x1, blocking collectives: 54.1 us -> 25.1 us  [shards(): mom = lax.all_to_all(mom, CHUNKS, 0, 0, tiled=True)]
    all_to_all x0 -> x1, waiting for transfers between devices: none -> 10.6 us  [shards(): mom = lax.all_to_all(mom, CHUNKS, 0, 0, tiled=True)]
    ppermute x8 -> x7, starting transfers between devices: 36.8 us -> 27.7 us  [the longest x1 16.3 us: shards(): far = lax.ppermute(mine, 'zh', [(0, 1), (1, 0)])]
    all_to_all x2, blocking collectives: 17.6 us -> 26.5 us  [shards(): q = lax.all_to_all(sent, WITHIN, 0, 0, tiled=True)]
    all_to_all x0 -> x1, starting transfers between devices: none -> 4.68 us  [shards(): mom = lax.all_to_all(mom, CHUNKS, 0, 0, tiled=True)]
    all_to_all x1, blocking collectives: 21.8 us -> 17.9 us  [shards(): lax.all_to_all(copies, ('x',) if first else ('x',) + WITHIN, 0, 0, tiled=...]
    pallas_call x10, Pallas kernels: 6.02 us -> 8.68 us  [run(): pl.pallas_call(kernel, out_shape=[pltpu.VMEM(s, F32) for s in outs], in_s...]
    ppermute x8 -> x7, waiting for transfers between devices: 24.4 us -> 22.5 us  [the longest x2 18.5 us: shards(): high = lax.ppermute(down, CHAIN, line(4, -1))]
  transfers between devices with their start and end apart: 9 -> 9, of which waited for: 7 -> 7; matrix products, arithmetic and copies ran while one was open for 0% -> 1% of each run, Pallas kernels for 0% -> 1%
where the time goes in v8:
time: 172 us; the launch traced here: 171 us
  blocking collectives  79.7 us (46%)
  waiting for transfers between devices  40.4 us (23%)
  starting transfers between devices  36.4 us (21%)
  Pallas kernels  8.68 us (5%)
  local copies, waits for them, and re-layouts  4.55 us (3%)
    all_to_all x2, blocking collectives, shards(): q = lax.all_to_all(sent, WITHIN, 0, 0, tiled=True)  26.5 us
    all_to_all x1, blocking collectives, shards(): mom = lax.all_to_all(mom, CHUNKS, 0, 0, tiled=True)  25.1 us
    ppermute x2, waiting for transfers between devices, shards(): high = lax.ppermute(down, CHAIN, line(4, -1))  18.5 us
    all_to_all x1, blocking collectives, shards(): lax.all_to_all(copies, ('x',) if first else ('x',) + WITHIN, 0, 0, tiled=...  17.9 us
    ppermute x1, starting transfers between devices, shards(): far = lax.ppermute(mine, 'zh', [(0, 1), (1, 0)])  16.3 us
    all_to_all x1, waiting for transfers between devices, shards(): mom = lax.all_to_all(mom, CHUNKS, 0, 0, tiled=True)  10.6 us
    all_to_all x1, blocking collectives, shards(): total = lax.all_to_all(total, WITHIN, 0, 0, tiled=True)  10.1 us
    pallas_call x10, Pallas kernels, run(): pl.pallas_call(kernel, out_shape=[pltpu.VMEM(s, F32) for s in outs], in_s...  8.68 us
  transfers between devices with their start and end apart: 9, of which 7 were waited for; matrix products, arithmetic and copies ran while one was open for 1% of the time, Pallas kernels for 1%

profile of v8, /device:TPU:1, one launch (start us, length us, event | category | flops | bytes accessed | tf_op | source)
XLA Modules:
  0.0 171.1 jit_solution(9269950011827055308)
XLA Ops:
  0.0 0.0 copy-start.1
  0.0 0.9 constant_dynamic-update-slice_fusion.1
  0.9 0.0 copy-done.1
  0.9 0.0 copy-start.3
  0.9 0.0 copy-start.2
  1.0 16.3 %collective-permute-start = (f32[24,3,1,4,128]{4,3,2,1,0:T(4,128)S(1)}, f32[24,3,1,4,128]{4,3,2,1,0:T(4,128)S(1)}, u32[]{:S(2)}, u32[]{:S(2)}) collective-permute-start(f32[24,3,1,4,128]{4,3,2,1,0:T(4,128)S(1)} %constant_dynamic-update-slice_fusion), channel_id=1, source_target_pairs={{0,256},{256,0},{1,257},{257,1},{2,258},{258,2},{3,259},{259,3},{4... | collective-permute-start | bytes 442376 | tf_op jit(solution)/shard_map/ppermute | solution.py:382
  17.3 0.0 copy-done.3
  17.3 0.0 copy-done.2
  17.4 3.5 %collective-permute-start.1 = (f32[36,128]{1,0:T(8,128)S(1)}, f32[36,128]{1,0:T(8,128)S(1)}, u32[]{:S(2)}, u32[]{:S(2)}) collective-permute-start(f32[36,128]{1,0:T(8,128)S(1)} %reshape.117.refs_2_.refs_1_), channel_id=1, source_target_pairs={{0,1},{1,2},{2,3},{3,4},{4,5},{5,6},{6,7},{7,8},{8,9},{9,10},{10,1... | collective-permute-start | bytes 55304 | tf_op jit(solution)/shard_map/ppermute | solution.py:378
  20.8 1.9 %collective-permute-start.2 = (f32[36,128]{1,0:T(8,128)S(1)}, f32[36,128]{1,0:T(8,128)S(1)}, u32[]{:S(2)}, u32[]{:S(2)}) collective-permute-start(f32[36,128]{1,0:T(8,128)S(1)} %reshape.117.refs_2_.refs_1_), channel_id=1, source_target_pairs={{1,0},{2,1},{3,2},{4,3},{5,4},{6,5},{7,6},{8,7},{9,8},{10,9},{11,1... | collective-permute-start | bytes 55304 | tf_op jit(solution)/shard_map/ppermute | solution.py:379
  22.8 0.0 copy-start.4
  22.8 0.7 copy-done.4
  23.5 0.1 copy.49
  23.6 0.0 copy-start.5
  23.6 0.7 copy-done.5
  24.2 0.1 copy.54
  24.4 0.0 collective-permute-done
  24.4 0.1 broadcast_select_fusion
  24.4 0.1 pad_maximum_fusion
  24.6 0.9 shard_map.73
  25.5 4.0 %all-to-all-start = ((f32[4,288,128]{2,1,0:T(8,128)}), f32[4,288,128]{2,1,0:T(8,128)S(1)}, u32[]{:S(2)}, u32[]{:S(2)}) async-start(f32[4,288,128]{2,1,0:T(8,128)} %shard_map.73), calls=%async_computation | async-start | bytes 1179648 | tf_op jit(solution)/shard_map/all_to_all | solution.py:405
  29.5 0.1 copy.52
  29.6 0.0 copy-start.6
  29.6 0.1 reshape.136
  29.7 0.6 copy-done.6
  30.3 0.1 copy.57
  30.4 0.1 pad_add_fusion.refs_5_.refs_4_
  30.6 0.1 copy.48
  30.6 0.1 reshape.116.refs_1_
  30.7 0.0 collective-permute-done.1.refs_3_.refs_2_
  30.7 1.3 collective-permute-done.2.refs_4_.refs_3_
  32.1 7.4 %all-to-all-done.refs_0_ = f32[4,288,128]{2,1,0:T(8,128)S(1)} async-done(((f32[4,288,128]{2,1,0:T(8,128)}), f32[4,288,128]{2,1,0:T(8,128)S(1)}, u32[]{:S(2)}, u32[]{:S(2)}) %all-to-all-start) | async-done | bytes 589856 | tf_op jit(solution)/shard_map/all_to_all | solution.py:405
  39.5 2.9 %shard_map.74 = f32[4,224,128]{2,1,0:T(8,128)S(1)} custom-call(f32[4,288,128]{2,1,0:T(8,128)S(1)} %all-to-all-done.refs_0_, f32[288,128]{1,0:T(8,128)S(1)} %reshape.116.refs_1_, f32[36,128]{1,0:T(8,128)S(1)} %reshape.117.refs_2_.refs_1_, f32[36,128]{1,0:T(8,128)S(1)} %collective-permute-done.1.refs_3_.refs_2_, ...), custom_call_target="tpu_custom_call" | custom-call | tf_op jit(solution)/shard_map/pallas_call | solution.py:44
  42.4 16.3 %all_to_all.47.refs_0_ = f32[4,224,128]{2,1,0:T(8,128)S(1)} all-to-all(f32[4,224,128]{2,1,0:T(8,128)S(1)} %shard_map.74), channel_id=1, replica_groups=mesh['zh'=2,'x'=4,'y'=4,'zp'=4,'zq'=2,'c'=2] {'zq','c'}, dimensions={0} | all-to-all | bytes 917504 | tf_op jit(solution)/shard_map/all_to_all | solution.py:419
  58.8 1.3 collective-permute-start.3
  60.1 1.3 collective-permute-start.4
  61.4 1.4 collective-permute-done.3.refs_2_
  62.8 9.6 %collective-permute-done.4.refs_3_ = f32[304,128]{1,0:T(8,128)S(1)} collective-permute-done((f32[304,128]{1,0:T(8,128)S(1)}, f32[304,128]{1,0:T(8,128)S(1)}, u32[]{:S(2)}, u32[]{:S(2)}) %collective-permute-start.4) | collective-permute-done | bytes 155680 | tf_op jit(solution)/shard_map/ppermute | solution.py:425
  72.4 0.9 shard_map.76
  73.3 25.1 %all_to_all.48 = f32[16,1,128]{2,1,0:T(1,128)S(1)} all-to-all(f32[16,1,128]{2,1,0:T(1,128)S(1)} %bitcast.53), channel_id=1, replica_groups=mesh['zh'=2,'x'=4,'y'=4,'zp'=4,'zq'=2,'c'=2] {'y','zp'}, dimensions={0} | all-to-all | bytes 16384 | tf_op jit(solution)/shard_map/all_to_all | solution.py:436
  98.4 0.2 shard_map.77
  98.7 17.9 %all_to_all.49.refs_0_ = f32[16,72,128]{2,1,0:T(8,128)S(1)} all-to-all(f32[16,72,128]{2,1,0:T(8,128)S(1)} %shard_map.78), channel_id=1, replica_groups=mesh['zh'=2,'x'=4,'y'=4,'zp'=4,'zq'=2,'c'=2] {'x','zq','c'}, dimensions={0} | all-to-all | bytes 1179648 | tf_op jit(solution)/shard_map/all_to_all | solution.py:405
  116.6 1.9 %shard_map.79 = f32[4,224,128]{2,1,0:T(8,128)S(1)} custom-call(f32[16,72,128]{2,1,0:T(8,128)S(1)} %all_to_all.49.refs_0_, f32[36,128]{1,0:T(8,128)S(1)} %reshape.117.refs_2_.refs_1_, f32[36,128]{1,0:T(8,128)S(1)} %collective-permute-done.1.refs_3_.refs_2_, f32[36,128]{1,0:T(8,128)S(1)} %collective-permute-done.2.refs_4_.refs_3_, ...), custom_call_target="tpu_custom_call" | custom-call | tf_op jit(solution)/shard_map/pallas_call | solution.py:44
  118.6 10.2 %all_to_all.50.refs_0_ = f32[4,224,128]{2,1,0:T(8,128)S(1)} all-to-all(f32[4,224,128]{2,1,0:T(8,128)S(1)} %shard_map.79), channel_id=1, replica_groups=mesh['zh'=2,'x'=4,'y'=4,'zp'=4,'zq'=2,'c'=2] {'zq','c'}, dimensions={0} | all-to-all | bytes 917504 | tf_op jit(solution)/shard_map/all_to_all | solution.py:419
  128.8 2.2 %collective-permute-start.5 = (f32[288,128]{1,0:T(8,128)S(1)}, f32[288,128]{1,0:T(8,128)S(1)}, u32[]{:S(2)}, u32[]{:S(2)}) collective-permute-start(f32[288,128]{1,0:T(8,128)S(1)} %get-tuple-element.34), channel_id=1, source_target_pairs={{0,4},{4,8},{8,12},{12,272},{16,20},{20,24},{24,28},{28,288},{32,3... | collective-permute-start | bytes 442376 | tf_op jit(solution)/shard_map/ppermute | solution.py:424
  131.0 1.3 collective-permute-start.6
  132.3 1.2 collective-permute-done.5.refs_2_
  133.5 8.9 %collective-permute-done.6.refs_3_ = f32[288,128]{1,0:T(8,128)S(1)} collective-permute-done((f32[288,128]{1,0:T(8,128)S(1)}, f32[288,128]{1,0:T(8,128)S(1)}, u32[]{:S(2)}, u32[]{:S(2)}) %collective-permute-start.6) | collective-permute-done | bytes 147488 | tf_op jit(solution)/shard_map/ppermute | solution.py:425
  142.4 1.5 shard_map.81
  143.9 4.7 %all-to-all-start.5 = ((f32[16,1,128]{2,1,0:T(1,128)}), f32[16,1,128]{2,1,0:T(1,128)S(1)}, u32[]{:S(2)}, u32[]{:S(2)}) async-start(f32[16,1,128]{2,1,0:T(1,128)} %bitcast.26), calls=%async_computation.5 | async-start | bytes 16384 | tf_op jit(solution)/shard_map/all_to_all | solution.py:436
  148.6 10.6 %all-to-all-done.5 = f32[16,1,128]{2,1,0:T(1,128)S(1)} async-done(((f32[16,1,128]{2,1,0:T(1,128)}), f32[16,1,128]{2,1,0:T(1,128)S(1)}, u32[]{:S(2)}, u32[]{:S(2)}) %all-to-all-start.5) | async-done | bytes 8224 | tf_op jit(solution)/shard_map/all_to_all | solution.py:436
  159.1 0.2 shard_map.82
  159.4 10.1 %all_to_all.51 = f32[4,36,128]{2,1,0:T(8,128)S(1)} all-to-all(f32[4,36,128]{2,1,0:T(8,128)S(1)} %shard_map.82), channel_id=1, replica_groups=mesh['zh'=2,'x'=4,'y'=4,'zp'=4,'zq'=2,'c'=2] {'zq','c'}, dimensions={0} | all-to-all | bytes 147456 | tf_op jit(solution)/shard_map/all_to_all | solution.py:445
  169.5 0.0 copy-start
  169.6 0.8 copy-done
  170.4 0.7 bitcast_add_fusion
  (27 shorter events, 0.4 us)
Async XLA Ops:
  0.0 0.9 copy-start.1
  0.9 16.3 %copy-start.3 = (s32[1,4,128]{2,1,0:T(4,128)S(1)}, s32[1,4,128]{2,1,0:T(4,128)}, u32[]{:S(2)}) copy-start(s32[1,4,128]{2,1,0:T(4,128)} %param.10) | copy-start | bytes 6148
  0.9 16.3 %copy-start.2 = (f32[8,1,4,128]{3,2,1,0:T(4,128)S(1)}, f32[8,1,4,128]{3,2,1,0:T(4,128)}, u32[]{:S(2)}) copy-start(f32[8,1,4,128]{3,2,1,0:T(4,128)} %param.9) | copy-start | bytes 49156
  1.0 23.4 %collective-permute-start = (f32[24,3,1,4,128]{4,3,2,1,0:T(4,128)S(1)}, f32[24,3,1,4,128]{4,3,2,1,0:T(4,128)S(1)}, u32[]{:S(2)}, u32[]{:S(2)}) collective-permute-start(f32[24,3,1,4,128]{4,3,2,1,0:T(4,128)S(1)} %constant_dynamic-update-slice_fusion), channel_id=1, source_target_pairs={{0,256},{256,0},{1,257},{257,1},{2,258},{258,2},{3,259},{259,3},{4... | collective-permute-start | bytes 442376 | tf_op jit(solution)/shard_map/ppermute | solution.py:382
  17.4 13.4 %collective-permute-start.1 = (f32[36,128]{1,0:T(8,128)S(1)}, f32[36,128]{1,0:T(8,128)S(1)}, u32[]{:S(2)}, u32[]{:S(2)}) collective-permute-start(f32[36,128]{1,0:T(8,128)S(1)} %reshape.117.refs_2_.refs_1_), channel_id=1, source_target_pairs={{0,1},{1,2},{2,3},{3,4},{4,5},{5,6},{6,7},{7,8},{8,9},{9,10},{10,1... | collective-permute-start | bytes 55304 | tf_op jit(solution)/shard_map/ppermute | solution.py:378
  20.8 11.2 %collective-permute-start.2 = (f32[36,128]{1,0:T(8,128)S(1)}, f32[36,128]{1,0:T(8,128)S(1)}, u32[]{:S(2)}, u32[]{:S(2)}) collective-permute-start(f32[36,128]{1,0:T(8,128)S(1)} %reshape.117.refs_2_.refs_1_), channel_id=1, source_target_pairs={{1,0},{2,1},{3,2},{4,3},{5,4},{6,5},{7,6},{8,7},{9,8},{10,9},{11,1... | collective-permute-start | bytes 55304 | tf_op jit(solution)/shard_map/ppermute | solution.py:379
  22.8 0.7 copy-start.4
  23.6 0.7 copy-start.5
  25.5 14.0 %all-to-all-start = ((f32[4,288,128]{2,1,0:T(8,128)}), f32[4,288,128]{2,1,0:T(8,128)S(1)}, u32[]{:S(2)}, u32[]{:S(2)}) async-start(f32[4,288,128]{2,1,0:T(8,128)} %shard_map.73), calls=%async_computation | async-start | bytes 1179648 | tf_op jit(solution)/shard_map/all_to_all | solution.py:405
  29.6 0.7 copy-start.6
  58.8 4.0 %collective-permute-start.3 = (f32[304,128]{1,0:T(8,128)S(1)}, f32[304,128]{1,0:T(8,128)S(1)}, u32[]{:S(2)}, u32[]{:S(2)}) collective-permute-start(f32[304,128]{1,0:T(8,128)S(1)} %get-tuple-element.24), channel_id=1, source_target_pairs={{0,4},{4,8},{8,12},{12,272},{16,20},{20,24},{24,28},{28,288},{32,3... | collective-permute-start | bytes 466952 | tf_op jit(solution)/shard_map/ppermute | solution.py:424
  60.1 12.3 %collective-permute-start.4 = (f32[304,128]{1,0:T(8,128)S(1)}, f32[304,128]{1,0:T(8,128)S(1)}, u32[]{:S(2)}, u32[]{:S(2)}) collective-permute-start(f32[304,128]{1,0:T(8,128)S(1)} %get-tuple-element.25), channel_id=1, source_target_pairs={{4,0},{8,4},{12,8},{16,268},{20,16},{24,20},{28,24},{32,284},{36,3... | collective-permute-start | bytes 466952 | tf_op jit(solution)/shard_map/ppermute | solution.py:425
  128.8 4.7 %collective-permute-start.5 = (f32[288,128]{1,0:T(8,128)S(1)}, f32[288,128]{1,0:T(8,128)S(1)}, u32[]{:S(2)}, u32[]{:S(2)}) collective-permute-start(f32[288,128]{1,0:T(8,128)S(1)} %get-tuple-element.34), channel_id=1, source_target_pairs={{0,4},{4,8},{8,12},{12,272},{16,20},{20,24},{24,28},{28,288},{32,3... | collective-permute-start | bytes 442376 | tf_op jit(solution)/shard_map/ppermute | solution.py:424
  131.0 11.4 %collective-permute-start.6 = (f32[288,128]{1,0:T(8,128)S(1)}, f32[288,128]{1,0:T(8,128)S(1)}, u32[]{:S(2)}, u32[]{:S(2)}) collective-permute-start(f32[288,128]{1,0:T(8,128)S(1)} %get-tuple-element.35), channel_id=1, source_target_pairs={{4,0},{8,4},{12,8},{16,268},{20,16},{24,20},{28,24},{32,284},{36,3... | collective-permute-start | bytes 442376 | tf_op jit(solution)/shard_map/ppermute | solution.py:425
  143.9 15.2 %all-to-all-start.5 = ((f32[16,1,128]{2,1,0:T(1,128)}), f32[16,1,128]{2,1,0:T(1,128)S(1)}, u32[]{:S(2)}, u32[]{:S(2)}) async-start(f32[16,1,128]{2,1,0:T(1,128)} %bitcast.26), calls=%async_computation.5 | async-start | bytes 16384 | tf_op jit(solution)/shard_map/all_to_all | solution.py:436
  169.5 0.9 copy-start

commit v9 on v8

--- a/solution.py
+++ b/solution.py
@@ -378,13 +378,16 @@
     em = lax.ppermute(moduli, SLABS, line(16, 1))
     ep = lax.ppermute(moduli, SLABS, line(16, -1))
     e0 = moduli
-    mine = jnp.concatenate([first_guess, load_modes], 0)
-    far = lax.ppermute(mine, "zh", [(0, 1), (1, 0)])
+    swap = [(0, 1), (1, 0)]
     zh, x = lax.axis_index("zh"), lax.axis_index("x")
     lower = zh == 0
-    both = jnp.stack([jnp.where(lower, mine, far), jnp.where(lower, far, mine)])
-    both = both.reshape(2, 2, NM, 3, NY, NZ)
-    guess, load = packed(both[:, 0]), by_target(both[:, 1])
+
+    def halves(mine):
+        far = lax.ppermute(mine, "zh", swap)
+        both = jnp.stack([jnp.where(lower, mine, far), jnp.where(lower, far, mine)])
+        return both.reshape(2, NM, 3, NY, NZ)
+
+    guess, load = packed(halves(first_guess)), by_target(halves(load_modes))
     half = jnp.broadcast_to(zh.astype(F32), (TRI, NZ))
 
     own = rows_of(jnp.arange(MODES, dtype=jnp.int32), x)

time: 172 us -> 173 us (level)
  starting transfers between devices: 36.4 us -> 38.6 us
    ppermute x1 -> x2, waiting for transfers between devices: 0.01 us -> 5.79 us  [halves(): far = lax.ppermute(mine, 'zh', swap)]
    all_to_all x1, blocking collectives: 25.1 us -> 30 us  [shards(): mom = lax.all_to_all(mom, CHUNKS, 0, 0, tiled=True)]
    all_to_all x1, waiting for transfers between devices: 7.39 us -> 3.33 us  [shards(): lax.all_to_all(copies, ('x',) if first else ('x',) + WITHIN, 0, 0, tiled=...]
    ppermute x1, starting transfers between devices: 1.92 us -> 5.14 us  [shards(): ep = lax.ppermute(moduli, SLABS, line(16, -1))]
    all_to_all x2, blocking collectives: 26.5 us -> 23.9 us  [shards(): q = lax.all_to_all(sent, WITHIN, 0, 0, tiled=True)]
    ppermute x1 -> x2, starting transfers between devices: 16.3 us -> 14 us  [halves(): far = lax.ppermute(mine, 'zh', swap)]
    all_to_all x1, blocking collectives: 10.1 us -> 8.37 us  [shards(): total = lax.all_to_all(total, WITHIN, 0, 0, tiled=True)]
    unnamed x18 -> x15, local copies, waits for them, and re-layouts: 4.01 us -> 2.3 us
  transfers between devices with their start and end apart: 9 -> 10, of which waited for: 7 -> 7; matrix products, arithmetic and copies ran while one was open for 1% -> 1% of each run, Pallas kernels for 1% -> 1%
where the time goes in v9:
time: 173 us; the launch traced here: 172 us
  blocking collectives  79 us (46%)
  waiting for transfers between devices  40.2 us (23%)
  starting transfers between devices  38.6 us (22%)
  Pallas kernels  8.67 us (5%)
  local copies, waits for them, and re-layouts  2.84 us (2%)
  other arithmetic  2.38 us (1%)
    all_to_all x1, blocking collectives, shards(): mom = lax.all_to_all(mom, CHUNKS, 0, 0, tiled=True)  30 us
    all_to_all x2, blocking collectives, shards(): q = lax.all_to_all(sent, WITHIN, 0, 0, tiled=True)  23.9 us
    ppermute x2, waiting for transfers between devices, shards(): high = lax.ppermute(down, CHAIN, line(4, -1))  17.9 us
    all_to_all x1, blocking collectives, shards(): lax.all_to_all(copies, ('x',) if first else ('x',) + WITHIN, 0, 0, tiled=...  16.8 us
    ppermute x2, starting transfers between devices, halves(): far = lax.ppermute(mine, 'zh', swap)  14 us
    all_to_all x1, waiting for transfers between devices, shards(): mom = lax.all_to_all(mom, CHUNKS, 0, 0, tiled=True)  10.5 us
    pallas_call x10, Pallas kernels, run(): pl.pallas_call(kernel, out_shape=[pltpu.VMEM(s, F32) for s in outs], in_s...  8.67 us
    all_to_all x1, blocking collectives, shards(): total = lax.all_to_all(total, WITHIN, 0, 0, tiled=True)  8.37 us
  transfers between devices with their start and end apart: 10, of which 7 were waited for; matrix products, arithmetic and copies ran while one was open for 1% of the time, Pallas kernels for 1%

profile of v9, /device:TPU:1, one launch (start us, length us, event | category | flops | bytes accessed | tf_op | source)
XLA Modules:
  0.0 172.0 jit_solution(13677429751178094890)
XLA Ops:
  0.0 0.0 copy-start.2
  0.0 0.0 copy-start
  0.0 0.8 fusion.4
  0.8 0.0 copy-done.2
  0.8 0.7 broadcast_select_fusion.2
  1.5 4.9 %collective-permute-start.2 = (f32[36,128]{1,0:T(8,128)S(1)}, f32[36,128]{1,0:T(8,128)S(1)}, u32[]{:S(2)}, u32[]{:S(2)}) collective-permute-start(f32[36,128]{1,0:T(8,128)S(1)} %reshape.120.refs_2_.refs_1_), channel_id=1, source_target_pairs={{0,1},{1,2},{2,3},{3,4},{4,5},{5,6},{6,7},{7,8},{8,9},{9,10},{10,1... | collective-permute-start | bytes 55304 | tf_op jit(solution)/shard_map/ppermute | solution.py:378
  6.5 5.1 %collective-permute-start.3 = (f32[36,128]{1,0:T(8,128)S(1)}, f32[36,128]{1,0:T(8,128)S(1)}, u32[]{:S(2)}, u32[]{:S(2)}) collective-permute-start(f32[36,128]{1,0:T(8,128)S(1)} %reshape.120.refs_2_.refs_1_), channel_id=1, source_target_pairs={{1,0},{2,1},{3,2},{4,3},{5,4},{6,5},{7,6},{8,7},{9,8},{10,9},{11,1... | collective-permute-start | bytes 55304 | tf_op jit(solution)/shard_map/ppermute | solution.py:379
  11.6 0.0 copy-done
  11.6 11.3 %collective-permute-start = (f32[12,3,1,4,128]{4,3,1,0,2:T(4,128)S(1)}, f32[12,3,1,4,128]{4,3,1,0,2:T(4,128)S(1)}, u32[]{:S(2)}, u32[]{:S(2)}) collective-permute-start(f32[12,3,1,4,128]{4,3,1,0,2:T(4,128)S(1)} %bitcast.63), channel_id=1, source_target_pairs={{0,256},{256,0},{1,257},{257,1},{2,258},{258,2},{3,259},{259,3},{4... | collective-permute-start | bytes 221192 | tf_op jit(solution)/shard_map/ppermute | solution.py:386
  23.0 2.7 %collective-permute-start.1 = (f32[12,3,1,4,128]{4,3,1,0,2:T(4,128)}, f32[12,3,1,4,128]{4,3,1,0,2:T(4,128)S(1)}, u32[]{:S(2)}, u32[]{:S(2)}) collective-permute-start(f32[12,3,1,4,128]{4,3,1,0,2:T(4,128)} %bitcast.67), channel_id=1, source_target_pairs={{0,256},{256,0},{1,257},{257,1},{2,258},{258,2},{3,259},{259,3},{4... | collective-permute-start | bytes 221192 | tf_op jit(solution)/shard_map/ppermute | solution.py:386
  25.6 0.0 copy-start.3
  25.7 0.7 copy-done.3
  26.3 0.1 copy.75
  26.4 0.0 copy-start.4
  26.5 0.7 copy-done.4
  27.1 0.1 copy.80
  27.3 0.1 copy.78
  27.4 0.1 reshape.139
  27.5 0.0 copy-start.5
  27.5 0.7 copy-done.5
  28.2 0.1 copy.83
  28.4 0.0 collective-permute-done
  28.5 0.9 shard_map.73
  29.4 0.0 copy-start.1
  29.4 5.0 %all-to-all-start = ((f32[4,288,128]{2,1,0:T(8,128)}), f32[4,288,128]{2,1,0:T(8,128)S(1)}, u32[]{:S(2)}, u32[]{:S(2)}) async-start(f32[4,288,128]{2,1,0:T(8,128)} %shard_map.73), calls=%async_computation | async-start | bytes 1179648 | tf_op jit(solution)/shard_map/all_to_all | solution.py:408
  34.4 0.1 pad_add_fusion.refs_5_.refs_4_
  34.4 5.8 %collective-permute-done.1 = f32[12,3,1,4,128]{4,3,1,0,2:T(4,128)S(1)} collective-permute-done((f32[12,3,1,4,128]{4,3,1,0,2:T(4,128)}, f32[12,3,1,4,128]{4,3,1,0,2:T(4,128)S(1)}, u32[]{:S(2)}, u32[]{:S(2)}) %collective-permute-start.1) | collective-permute-done | bytes 73760 | tf_op jit(solution)/shard_map/ppermute | solution.py:386
  40.2 0.0 copy-done.1
  40.4 0.1 reshape.119.refs_1_
  40.5 0.0 collective-permute-done.2.refs_3_.refs_2_
  40.5 0.0 collective-permute-done.3.refs_4_.refs_3_
  40.5 3.3 %all-to-all-done.refs_0_ = f32[4,288,128]{2,1,0:T(8,128)S(1)} async-done(((f32[4,288,128]{2,1,0:T(8,128)}), f32[4,288,128]{2,1,0:T(8,128)S(1)}, u32[]{:S(2)}, u32[]{:S(2)}) %all-to-all-start) | async-done | bytes 589856 | tf_op jit(solution)/shard_map/all_to_all | solution.py:408
  43.8 2.9 %shard_map.74 = f32[4,224,128]{2,1,0:T(8,128)S(1)} custom-call(f32[4,288,128]{2,1,0:T(8,128)S(1)} %all-to-all-done.refs_0_, f32[288,128]{1,0:T(8,128)S(1)} %reshape.119.refs_1_, f32[36,128]{1,0:T(8,128)S(1)} %reshape.120.refs_2_.refs_1_, f32[36,128]{1,0:T(8,128)S(1)} %collective-permute-done.2.refs_3_.refs_2_, ...), custom_call_target="tpu_custom_call" | custom-call | tf_op jit(solution)/shard_map/pallas_call | solution.py:44
  46.8 13.7 %all_to_all.47.refs_0_ = f32[4,224,128]{2,1,0:T(8,128)S(1)} all-to-all(f32[4,224,128]{2,1,0:T(8,128)S(1)} %shard_map.74), channel_id=1, replica_groups=mesh['zh'=2,'x'=4,'y'=4,'zp'=4,'zq'=2,'c'=2] {'zq','c'}, dimensions={0} | all-to-all | bytes 917504 | tf_op jit(solution)/shard_map/all_to_all | solution.py:422
  60.5 1.3 collective-permute-start.4
  61.8 1.3 collective-permute-start.5
  63.1 1.4 collective-permute-done.4.refs_2_
  64.5 9.0 %collective-permute-done.5.refs_3_ = f32[304,128]{1,0:T(8,128)S(1)} collective-permute-done((f32[304,128]{1,0:T(8,128)S(1)}, f32[304,128]{1,0:T(8,128)S(1)}, u32[]{:S(2)}, u32[]{:S(2)}) %collective-permute-start.5) | collective-permute-done | bytes 155680 | tf_op jit(solution)/shard_map/ppermute | solution.py:428
  73.6 0.9 shard_map.76
  74.4 30.0 %all_to_all.48 = f32[16,1,128]{2,1,0:T(1,128)S(1)} all-to-all(f32[16,1,128]{2,1,0:T(1,128)S(1)} %bitcast.62), channel_id=1, replica_groups=mesh['zh'=2,'x'=4,'y'=4,'zp'=4,'zq'=2,'c'=2] {'y','zp'}, dimensions={0} | all-to-all | bytes 16384 | tf_op jit(solution)/shard_map/all_to_all | solution.py:439
  104.4 0.2 shard_map.77
  104.7 16.8 %all_to_all.49.refs_0_ = f32[16,72,128]{2,1,0:T(8,128)S(1)} all-to-all(f32[16,72,128]{2,1,0:T(8,128)S(1)} %shard_map.78), channel_id=1, replica_groups=mesh['zh'=2,'x'=4,'y'=4,'zp'=4,'zq'=2,'c'=2] {'x','zq','c'}, dimensions={0} | all-to-all | bytes 1179648 | tf_op jit(solution)/shard_map/all_to_all | solution.py:408
  121.5 1.9 %shard_map.79 = f32[4,224,128]{2,1,0:T(8,128)S(1)} custom-call(f32[16,72,128]{2,1,0:T(8,128)S(1)} %all_to_all.49.refs_0_, f32[36,128]{1,0:T(8,128)S(1)} %reshape.120.refs_2_.refs_1_, f32[36,128]{1,0:T(8,128)S(1)} %collective-permute-done.2.refs_3_.refs_2_, f32[36,128]{1,0:T(8,128)S(1)} %collective-permute-done.3.refs_4_.refs_3_, ...), custom_call_target="tpu_custom_call" | custom-call | tf_op jit(solution)/shard_map/pallas_call | solution.py:44
  123.4 10.2 %all_to_all.50.refs_0_ = f32[4,224,128]{2,1,0:T(8,128)S(1)} all-to-all(f32[4,224,128]{2,1,0:T(8,128)S(1)} %shard_map.79), channel_id=1, replica_groups=mesh['zh'=2,'x'=4,'y'=4,'zp'=4,'zq'=2,'c'=2] {'zq','c'}, dimensions={0} | all-to-all | bytes 917504 | tf_op jit(solution)/shard_map/all_to_all | solution.py:422
  133.7 2.2 %collective-permute-start.6 = (f32[288,128]{1,0:T(8,128)S(1)}, f32[288,128]{1,0:T(8,128)S(1)}, u32[]{:S(2)}, u32[]{:S(2)}) collective-permute-start(f32[288,128]{1,0:T(8,128)S(1)} %get-tuple-element.34), channel_id=1, source_target_pairs={{0,4},{4,8},{8,12},{12,272},{16,20},{20,24},{24,28},{28,288},{32,3... | collective-permute-start | bytes 442376 | tf_op jit(solution)/shard_map/ppermute | solution.py:427
  135.8 1.3 collective-permute-start.7
  137.1 1.2 collective-permute-done.6.refs_2_
  138.3 8.9 %collective-permute-done.7.refs_3_ = f32[288,128]{1,0:T(8,128)S(1)} collective-permute-done((f32[288,128]{1,0:T(8,128)S(1)}, f32[288,128]{1,0:T(8,128)S(1)}, u32[]{:S(2)}, u32[]{:S(2)}) %collective-permute-start.7) | collective-permute-done | bytes 147488 | tf_op jit(solution)/shard_map/ppermute | solution.py:428
  147.2 1.5 shard_map.81
  148.7 3.5 %all-to-all-start.5 = ((f32[16,1,128]{2,1,0:T(1,128)}), f32[16,1,128]{2,1,0:T(1,128)S(1)}, u32[]{:S(2)}, u32[]{:S(2)}) async-start(f32[16,1,128]{2,1,0:T(1,128)} %bitcast.28), calls=%async_computation.5 | async-start | bytes 16384 | tf_op jit(solution)/shard_map/all_to_all | solution.py:439
  152.2 10.5 %all-to-all-done.5 = f32[16,1,128]{2,1,0:T(1,128)S(1)} async-done(((f32[16,1,128]{2,1,0:T(1,128)}), f32[16,1,128]{2,1,0:T(1,128)S(1)}, u32[]{:S(2)}, u32[]{:S(2)}) %all-to-all-start.5) | async-done | bytes 8224 | tf_op jit(solution)/shard_map/all_to_all | solution.py:439
  162.7 0.2 shard_map.82
  162.9 8.4 %all_to_all.51 = f32[4,36,128]{2,1,0:T(8,128)S(1)} all-to-all(f32[4,36,128]{2,1,0:T(8,128)S(1)} %shard_map.82), channel_id=1, replica_groups=mesh['zh'=2,'x'=4,'y'=4,'zp'=4,'zq'=2,'c'=2] {'zq','c'}, dimensions={0} | all-to-all | bytes 147456 | tf_op jit(solution)/shard_map/all_to_all | solution.py:448
  171.4 0.7 bitcast_add_fusion
  (31 shorter events, 0.6 us)
Async XLA Ops:
  0.0 0.8 copy-start.2
  0.0 11.6 %copy-start = (f32[12,3,1,4,128]{4,3,2,1,0:T(4,128)S(1)}, f32[12,3,1,4,128]{4,3,2,1,0:T(4,128)}, u32[]{:S(2)}) copy-start(f32[12,3,1,4,128]{4,3,2,1,0:T(4,128)} %param.8) | copy-start | bytes 221188
  1.5 39.0 %collective-permute-start.2 = (f32[36,128]{1,0:T(8,128)S(1)}, f32[36,128]{1,0:T(8,128)S(1)}, u32[]{:S(2)}, u32[]{:S(2)}) collective-permute-start(f32[36,128]{1,0:T(8,128)S(1)} %reshape.120.refs_2_.refs_1_), channel_id=1, source_target_pairs={{0,1},{1,2},{2,3},{3,4},{4,5},{5,6},{6,7},{7,8},{8,9},{9,10},{10,1... | collective-permute-start | bytes 55304 | tf_op jit(solution)/shard_map/ppermute | solution.py:378
  6.5 34.0 %collective-permute-start.3 = (f32[36,128]{1,0:T(8,128)S(1)}, f32[36,128]{1,0:T(8,128)S(1)}, u32[]{:S(2)}, u32[]{:S(2)}) collective-permute-start(f32[36,128]{1,0:T(8,128)S(1)} %reshape.120.refs_2_.refs_1_), channel_id=1, source_target_pairs={{1,0},{2,1},{3,2},{4,3},{5,4},{6,5},{7,6},{8,7},{9,8},{10,9},{11,1... | collective-permute-start | bytes 55304 | tf_op jit(solution)/shard_map/ppermute | solution.py:379
  11.6 16.7 %collective-permute-start = (f32[12,3,1,4,128]{4,3,1,0,2:T(4,128)S(1)}, f32[12,3,1,4,128]{4,3,1,0,2:T(4,128)S(1)}, u32[]{:S(2)}, u32[]{:S(2)}) collective-permute-start(f32[12,3,1,4,128]{4,3,1,0,2:T(4,128)S(1)} %bitcast.63), channel_id=1, source_target_pairs={{0,256},{256,0},{1,257},{257,1},{2,258},{258,2},{3,259},{259,3},{4... | collective-permute-start | bytes 221192 | tf_op jit(solution)/shard_map/ppermute | solution.py:386
  23.0 17.3 %collective-permute-start.1 = (f32[12,3,1,4,128]{4,3,1,0,2:T(4,128)}, f32[12,3,1,4,128]{4,3,1,0,2:T(4,128)S(1)}, u32[]{:S(2)}, u32[]{:S(2)}) collective-permute-start(f32[12,3,1,4,128]{4,3,1,0,2:T(4,128)} %bitcast.67), channel_id=1, source_target_pairs={{0,256},{256,0},{1,257},{257,1},{2,258},{258,2},{3,259},{259,3},{4... | collective-permute-start | bytes 221192 | tf_op jit(solution)/shard_map/ppermute | solution.py:386
  25.6 0.7 copy-start.3
  26.4 0.7 copy-start.4
  27.5 0.7 copy-start.5
  29.4 10.8 %copy-start.1 = (f32[12,3,1,4,128]{4,3,2,1,0:T(4,128)S(1)}, f32[12,3,1,4,128]{4,3,2,1,0:T(4,128)}, u32[]{:S(2)}) copy-start(f32[12,3,1,4,128]{4,3,2,1,0:T(4,128)} %param.7) | copy-start | bytes 221188
  29.4 14.4 %all-to-all-start = ((f32[4,288,128]{2,1,0:T(8,128)}), f32[4,288,128]{2,1,0:T(8,128)S(1)}, u32[]{:S(2)}, u32[]{:S(2)}) async-start(f32[4,288,128]{2,1,0:T(8,128)} %shard_map.73), calls=%async_computation | async-start | bytes 1179648 | tf_op jit(solution)/shard_map/all_to_all | solution.py:408
  60.5 4.0 %collective-permute-start.4 = (f32[304,128]{1,0:T(8,128)S(1)}, f32[304,128]{1,0:T(8,128)S(1)}, u32[]{:S(2)}, u32[]{:S(2)}) collective-permute-start(f32[304,128]{1,0:T(8,128)S(1)} %get-tuple-element.24), channel_id=1, source_target_pairs={{0,4},{4,8},{8,12},{12,272},{16,20},{20,24},{24,28},{28,288},{32,3... | collective-permute-start | bytes 466952 | tf_op jit(solution)/shard_map/ppermute | solution.py:427
  61.8 11.8 %collective-permute-start.5 = (f32[304,128]{1,0:T(8,128)S(1)}, f32[304,128]{1,0:T(8,128)S(1)}, u32[]{:S(2)}, u32[]{:S(2)}) collective-permute-start(f32[304,128]{1,0:T(8,128)S(1)} %get-tuple-element.25), channel_id=1, source_target_pairs={{4,0},{8,4},{12,8},{16,268},{20,16},{24,20},{28,24},{32,284},{36,3... | collective-permute-start | bytes 466952 | tf_op jit(solution)/shard_map/ppermute | solution.py:428
  133.7 4.7 %collective-permute-start.6 = (f32[288,128]{1,0:T(8,128)S(1)}, f32[288,128]{1,0:T(8,128)S(1)}, u32[]{:S(2)}, u32[]{:S(2)}) collective-permute-start(f32[288,128]{1,0:T(8,128)S(1)} %get-tuple-element.34), channel_id=1, source_target_pairs={{0,4},{4,8},{8,12},{12,272},{16,20},{20,24},{24,28},{28,288},{32,3... | collective-permute-start | bytes 442376 | tf_op jit(solution)/shard_map/ppermute | solution.py:427
  135.8 11.4 %collective-permute-start.7 = (f32[288,128]{1,0:T(8,128)S(1)}, f32[288,128]{1,0:T(8,128)S(1)}, u32[]{:S(2)}, u32[]{:S(2)}) collective-permute-start(f32[288,128]{1,0:T(8,128)S(1)} %get-tuple-element.35), channel_id=1, source_target_pairs={{4,0},{8,4},{12,8},{16,268},{20,16},{24,20},{28,24},{32,284},{36,3... | collective-permute-start | bytes 442376 | tf_op jit(solution)/shard_map/ppermute | solution.py:428
  148.7 14.0 %all-to-all-start.5 = ((f32[16,1,128]{2,1,0:T(1,128)}), f32[16,1,128]{2,1,0:T(1,128)S(1)}, u32[]{:S(2)}, u32[]{:S(2)}) async-start(f32[16,1,128]{2,1,0:T(1,128)} %bitcast.28), calls=%async_computation.5 | async-start | bytes 16384 | tf_op jit(solution)/shard_map/all_to_all | solution.py:439

commit v10 on v9

--- a/solution.py
+++ b/solution.py
@@ -372,22 +372,25 @@
 
 
 def shards(load_modes, first_guess, kl_fields, region_labels, partner, variable, weight):
-    mean = jnp.where(region_labels == 0, 1.3, jnp.where(region_labels == 1, 1.0, 0.6)).astype(F32)
-    varying = jnp.where(region_labels[None] == 1, kl_fields, 0.0)
-    moduli = jnp.concatenate([varying, mean[None]], 0).reshape((NK + 1) * NY, NZ)
-    em = lax.ppermute(moduli, SLABS, line(16, 1))
-    ep = lax.ppermute(moduli, SLABS, line(16, -1))
-    e0 = moduli
     swap = [(0, 1), (1, 0)]
     zh, x = lax.axis_index("zh"), lax.axis_index("x")
     lower = zh == 0
 
-    def halves(mine):
-        far = lax.ppermute(mine, "zh", swap)
+    def halves(mine, far):
         both = jnp.stack([jnp.where(lower, mine, far), jnp.where(lower, far, mine)])
         return both.reshape(2, NM, 3, NY, NZ)
 
-    guess, load = packed(halves(first_guess)), by_target(halves(load_modes))
+    far = lax.ppermute(first_guess, "zh", swap)
+    load = by_target(halves(load_modes, lax.ppermute(load_modes, "zh", swap)))
+    far, kl_fields, region_labels, partner, variable, weight = lax.optimization_barrier(
+        (far, kl_fields, region_labels, partner, variable, weight)
+    )
+    guess = packed(halves(first_guess, far))
+    mean = jnp.where(region_labels == 0, 1.3, jnp.where(region_labels == 1, 1.0, 0.6)).astype(F32)
+    varying = jnp.where(region_labels[None] == 1, kl_fields, 0.0)
+    e0 = jnp.concatenate([varying, mean[None]], 0).reshape((NK + 1) * NY, NZ)
+    em = lax.ppermute(e0, SLABS, line(16, 1))
+    ep = lax.ppermute(e0, SLABS, line(16, -1))
     half = jnp.broadcast_to(zh.astype(F32), (TRI, NZ))
 
     own = rows_of(jnp.arange(MODES, dtype=jnp.int32), x)

time: 173 us -> 174 us (level)
  starting transfers between devices: 38.6 us -> 46.5 us
  waiting for transfers between devices: 40.2 us -> 37.1 us
  blocking collectives: 79 us -> 76.2 us
    ppermute x4, starting transfers between devices: 24.1 us -> 32.8 us  [the longest x1 16.3 us: shards(): far = lax.ppermute(first_guess, 'zh', swap)]
    ppermute x4, waiting for transfers between devices: 5.8 us -> 0.02 us  [the longest x1 0.02 us: shards(): far = lax.ppermute(first_guess, 'zh', swap)]
    all_to_all x1, blocking collectives: 30 us -> 24.9 us  [shards(): mom = lax.all_to_all(mom, CHUNKS, 0, 0, tiled=True)]
    all_to_all x1, blocking collectives: 16.8 us -> 19.9 us  [shards(): lax.all_to_all(copies, ('x',) if first else ('x',) + WITHIN, 0, 0, tiled=...]
    all_to_all x1, waiting for transfers between devices: 3.33 us -> 6.02 us  [shards(): lax.all_to_all(copies, ('x',) if first else ('x',) + WITHIN, 0, 0, tiled=...]
  transfers between devices with their start and end apart: 10 -> 10, of which waited for: 7 -> 6; matrix products, arithmetic and copies ran while one was open for 1% -> 1% of each run, Pallas kernels for 1% -> 1%
where the time goes in v10:
time: 174 us; the launch traced here: 173 us
  blocking collectives  76.2 us (44%)
  starting transfers between devices  46.5 us (27%)
  waiting for transfers between devices  37.1 us (21%)
  Pallas kernels  8.68 us (5%)
  local copies, waits for them, and re-layouts  3.29 us (2%)
    all_to_all x1, blocking collectives, shards(): mom = lax.all_to_all(mom, CHUNKS, 0, 0, tiled=True)  24.9 us
    all_to_all x2, blocking collectives, shards(): q = lax.all_to_all(sent, WITHIN, 0, 0, tiled=True)  22.9 us
    all_to_all x1, blocking collectives, shards(): lax.all_to_all(copies, ('x',) if first else ('x',) + WITHIN, 0, 0, tiled=...  19.9 us
    ppermute x2, waiting for transfers between devices, shards(): high = lax.ppermute(down, CHAIN, line(4, -1))  17.7 us
    ppermute x1, starting transfers between devices, shards(): far = lax.ppermute(first_guess, 'zh', swap)  16.3 us
    ppermute x1, starting transfers between devices, shards(): em = lax.ppermute(e0, SLABS, line(16, 1))  12.7 us
    all_to_all x1, waiting for transfers between devices, shards(): mom = lax.all_to_all(mom, CHUNKS, 0, 0, tiled=True)  10.5 us
    pallas_call x10, Pallas kernels, run(): pl.pallas_call(kernel, out_shape=[pltpu.VMEM(s, F32) for s in outs], in_s...  8.68 us
  transfers between devices with their start and end apart: 10, of which 6 were waited for; matrix products, arithmetic and copies ran while one was open for 1% of the time, Pallas kernels for 1%

profile of v10, /device:TPU:1, one launch (start us, length us, event | category | flops | bytes accessed | tf_op | source)
XLA Modules:
  0.0 173.1 jit_solution(8922134907828269546)
XLA Ops:
  0.0 16.3 %collective-permute-start = (f32[12,3,1,4,128]{4,3,1,0,2:T(4,128)}, f32[12,3,1,4,128]{4,3,1,0,2:T(4,128)S(1)}, u32[]{:S(2)}, u32[]{:S(2)}) collective-permute-start(f32[12,3,1,4,128]{4,3,1,0,2:T(4,128)} %bitcast.63), channel_id=1, source_target_pairs={{0,256},{256,0},{1,257},{257,1},{2,258},{258,2},{3,259},{259,3},{4... | collective-permute-start | bytes 221192 | tf_op jit(solution)/shard_map/ppermute | solution.py:383
  16.3 1.9 %collective-permute-start.1 = (f32[12,3,1,4,128]{4,3,1,0,2:T(4,128)}, f32[12,3,1,4,128]{4,3,1,0,2:T(4,128)S(1)}, u32[]{:S(2)}, u32[]{:S(2)}) collective-permute-start(f32[12,3,1,4,128]{4,3,1,0,2:T(4,128)} %bitcast.67), channel_id=1, source_target_pairs={{0,256},{256,0},{1,257},{257,1},{2,258},{258,2},{3,259},{259,3},{4... | collective-permute-start | bytes 221192 | tf_op jit(solution)/shard_map/ppermute | solution.py:384
  18.2 0.0 copy-start.3
  18.2 0.0 copy-start.2
  18.2 0.0 copy-start
  18.3 0.1 copy.78
  18.4 0.1 reshape.139
  18.4 0.0 collective-permute-done
  18.4 0.4 copy-done.3
  18.9 0.0 copy-done.2
  19.0 12.7 %collective-permute-start.2 = (f32[36,128]{1,0:T(8,128)S(1)}, f32[36,128]{1,0:T(8,128)S(1)}, u32[]{:S(2)}, u32[]{:S(2)}) collective-permute-start(f32[36,128]{1,0:T(8,128)S(1)} %reshape.120.refs_2_.refs_1_), channel_id=1, source_target_pairs={{0,1},{1,2},{2,3},{3,4},{4,5},{5,6},{6,7},{7,8},{8,9},{9,10},{10,1... | collective-permute-start | bytes 55304 | tf_op jit(solution)/shard_map/ppermute | solution.py:392
  31.7 1.9 %collective-permute-start.3 = (f32[36,128]{1,0:T(8,128)S(1)}, f32[36,128]{1,0:T(8,128)S(1)}, u32[]{:S(2)}, u32[]{:S(2)}) collective-permute-start(f32[36,128]{1,0:T(8,128)S(1)} %reshape.120.refs_2_.refs_1_), channel_id=1, source_target_pairs={{1,0},{2,1},{3,2},{4,3},{5,4},{6,5},{7,6},{8,7},{9,8},{10,9},{11,1... | collective-permute-start | bytes 55304 | tf_op jit(solution)/shard_map/ppermute | solution.py:393
  33.6 0.0 copy-done
  33.6 0.0 copy-start.4
  33.7 0.6 copy-done.4
  34.3 0.1 copy.75
  34.4 0.0 copy-start.5
  34.5 0.7 copy-done.5
  35.1 0.1 copy.80
  35.3 0.9 shard_map.73
  36.2 0.0 copy-start.1
  36.2 4.1 %all-to-all-start = ((f32[4,288,128]{2,1,0:T(8,128)}), f32[4,288,128]{2,1,0:T(8,128)S(1)}, u32[]{:S(2)}, u32[]{:S(2)}) async-start(f32[4,288,128]{2,1,0:T(8,128)} %shard_map.73), calls=%async_computation | async-start | bytes 1179648 | tf_op jit(solution)/shard_map/all_to_all | solution.py:411
  40.4 0.0 collective-permute-done.1
  40.4 0.0 copy-done.1
  40.4 0.0 copy-start.6
  40.5 0.7 copy-done.6
  41.1 0.1 copy.83
  41.4 0.1 pad_add_fusion.refs_5_.refs_4_
  41.5 0.1 reshape.119.refs_1_
  41.6 0.0 collective-permute-done.2.refs_3_.refs_2_
  41.6 0.0 collective-permute-done.3.refs_4_.refs_3_
  41.6 6.0 %all-to-all-done.refs_0_ = f32[4,288,128]{2,1,0:T(8,128)S(1)} async-done(((f32[4,288,128]{2,1,0:T(8,128)}), f32[4,288,128]{2,1,0:T(8,128)S(1)}, u32[]{:S(2)}, u32[]{:S(2)}) %all-to-all-start) | async-done | bytes 589856 | tf_op jit(solution)/shard_map/all_to_all | solution.py:411
  47.6 2.9 %shard_map.74 = f32[4,224,128]{2,1,0:T(8,128)S(1)} custom-call(f32[4,288,128]{2,1,0:T(8,128)S(1)} %all-to-all-done.refs_0_, f32[288,128]{1,0:T(8,128)S(1)} %reshape.119.refs_1_, f32[36,128]{1,0:T(8,128)S(1)} %reshape.120.refs_2_.refs_1_, f32[36,128]{1,0:T(8,128)S(1)} %collective-permute-done.2.refs_3_.refs_2_, ...), custom_call_target="tpu_custom_call" | custom-call | tf_op jit(solution)/shard_map/pallas_call | solution.py:44
  50.6 12.7 %all_to_all.47.refs_0_ = f32[4,224,128]{2,1,0:T(8,128)S(1)} all-to-all(f32[4,224,128]{2,1,0:T(8,128)S(1)} %shard_map.74), channel_id=1, replica_groups=mesh['zh'=2,'x'=4,'y'=4,'zp'=4,'zq'=2,'c'=2] {'zq','c'}, dimensions={0} | all-to-all | bytes 917504 | tf_op jit(solution)/shard_map/all_to_all | solution.py:425
  63.3 1.3 collective-permute-start.4
  64.6 1.3 collective-permute-start.5
  65.9 1.6 collective-permute-done.4.refs_2_
  67.6 8.8 %collective-permute-done.5.refs_3_ = f32[304,128]{1,0:T(8,128)S(1)} collective-permute-done((f32[304,128]{1,0:T(8,128)S(1)}, f32[304,128]{1,0:T(8,128)S(1)}, u32[]{:S(2)}, u32[]{:S(2)}) %collective-permute-start.5) | collective-permute-done | bytes 155680 | tf_op jit(solution)/shard_map/ppermute | solution.py:431
  76.4 0.9 shard_map.76
  77.3 24.9 %all_to_all.48 = f32[16,1,128]{2,1,0:T(1,128)S(1)} all-to-all(f32[16,1,128]{2,1,0:T(1,128)S(1)} %bitcast.62), channel_id=1, replica_groups=mesh['zh'=2,'x'=4,'y'=4,'zp'=4,'zq'=2,'c'=2] {'y','zp'}, dimensions={0} | all-to-all | bytes 16384 | tf_op jit(solution)/shard_map/all_to_all | solution.py:442
  102.2 0.2 shard_map.77
  102.5 19.9 %all_to_all.49.refs_0_ = f32[16,72,128]{2,1,0:T(8,128)S(1)} all-to-all(f32[16,72,128]{2,1,0:T(8,128)S(1)} %shard_map.78), channel_id=1, replica_groups=mesh['zh'=2,'x'=4,'y'=4,'zp'=4,'zq'=2,'c'=2] {'x','zq','c'}, dimensions={0} | all-to-all | bytes 1179648 | tf_op jit(solution)/shard_map/all_to_all | solution.py:411
  122.4 1.9 %shard_map.79 = f32[4,224,128]{2,1,0:T(8,128)S(1)} custom-call(f32[16,72,128]{2,1,0:T(8,128)S(1)} %all_to_all.49.refs_0_, f32[36,128]{1,0:T(8,128)S(1)} %reshape.120.refs_2_.refs_1_, f32[36,128]{1,0:T(8,128)S(1)} %collective-permute-done.2.refs_3_.refs_2_, f32[36,128]{1,0:T(8,128)S(1)} %collective-permute-done.3.refs_4_.refs_3_, ...), custom_call_target="tpu_custom_call" | custom-call | tf_op jit(solution)/shard_map/pallas_call | solution.py:44
  124.4 10.2 %all_to_all.50.refs_0_ = f32[4,224,128]{2,1,0:T(8,128)S(1)} all-to-all(f32[4,224,128]{2,1,0:T(8,128)S(1)} %shard_map.79), channel_id=1, replica_groups=mesh['zh'=2,'x'=4,'y'=4,'zp'=4,'zq'=2,'c'=2] {'zq','c'}, dimensions={0} | all-to-all | bytes 917504 | tf_op jit(solution)/shard_map/all_to_all | solution.py:425
  134.6 2.2 %collective-permute-start.6 = (f32[288,128]{1,0:T(8,128)S(1)}, f32[288,128]{1,0:T(8,128)S(1)}, u32[]{:S(2)}, u32[]{:S(2)}) collective-permute-start(f32[288,128]{1,0:T(8,128)S(1)} %get-tuple-element.46), channel_id=1, source_target_pairs={{0,4},{4,8},{8,12},{12,272},{16,20},{20,24},{24,28},{28,288},{32,3... | collective-permute-start | bytes 442376 | tf_op jit(solution)/shard_map/ppermute | solution.py:430
  136.8 1.3 collective-permute-start.7
  138.1 1.2 collective-permute-done.6.refs_2_
  139.3 8.9 %collective-permute-done.7.refs_3_ = f32[288,128]{1,0:T(8,128)S(1)} collective-permute-done((f32[288,128]{1,0:T(8,128)S(1)}, f32[288,128]{1,0:T(8,128)S(1)}, u32[]{:S(2)}, u32[]{:S(2)}) %collective-permute-start.7) | collective-permute-done | bytes 147488 | tf_op jit(solution)/shard_map/ppermute | solution.py:431
  148.2 1.5 shard_map.81
  149.7 3.5 %all-to-all-start.5 = ((f32[16,1,128]{2,1,0:T(1,128)}), f32[16,1,128]{2,1,0:T(1,128)S(1)}, u32[]{:S(2)}, u32[]{:S(2)}) async-start(f32[16,1,128]{2,1,0:T(1,128)} %bitcast.28), calls=%async_computation.5 | async-start | bytes 16384 | tf_op jit(solution)/shard_map/all_to_all | solution.py:442
  153.2 10.5 %all-to-all-done.5 = f32[16,1,128]{2,1,0:T(1,128)S(1)} async-done(((f32[16,1,128]{2,1,0:T(1,128)}), f32[16,1,128]{2,1,0:T(1,128)S(1)}, u32[]{:S(2)}, u32[]{:S(2)}) %all-to-all-start.5) | async-done | bytes 8224 | tf_op jit(solution)/shard_map/all_to_all | solution.py:442
  163.7 0.2 shard_map.82
  163.9 8.4 %all_to_all.51 = f32[4,36,128]{2,1,0:T(8,128)S(1)} all-to-all(f32[4,36,128]{2,1,0:T(8,128)S(1)} %shard_map.82), channel_id=1, replica_groups=mesh['zh'=2,'x'=4,'y'=4,'zp'=4,'zq'=2,'c'=2] {'zq','c'}, dimensions={0} | all-to-all | bytes 147456 | tf_op jit(solution)/shard_map/all_to_all | solution.py:451
  172.4 0.7 bitcast_add_fusion
  (33 shorter events, 0.6 us)
Async XLA Ops:
  0.0 18.4 %collective-permute-start = (f32[12,3,1,4,128]{4,3,1,0,2:T(4,128)}, f32[12,3,1,4,128]{4,3,1,0,2:T(4,128)S(1)}, u32[]{:S(2)}, u32[]{:S(2)}) collective-permute-start(f32[12,3,1,4,128]{4,3,1,0,2:T(4,128)} %bitcast.63), channel_id=1, source_target_pairs={{0,256},{256,0},{1,257},{257,1},{2,258},{258,2},{3,259},{259,3},{4... | collective-permute-start | bytes 221192 | tf_op jit(solution)/shard_map/ppermute | solution.py:383
  16.3 24.1 %collective-permute-start.1 = (f32[12,3,1,4,128]{4,3,1,0,2:T(4,128)}, f32[12,3,1,4,128]{4,3,1,0,2:T(4,128)S(1)}, u32[]{:S(2)}, u32[]{:S(2)}) collective-permute-start(f32[12,3,1,4,128]{4,3,1,0,2:T(4,128)} %bitcast.67), channel_id=1, source_target_pairs={{0,256},{256,0},{1,257},{257,1},{2,258},{258,2},{3,259},{259,3},{4... | collective-permute-start | bytes 221192 | tf_op jit(solution)/shard_map/ppermute | solution.py:384
  18.2 0.7 copy-start.3
  18.2 0.7 copy-start.2
  18.2 15.4 %copy-start = (f32[12,3,1,4,128]{4,3,2,1,0:T(4,128)S(1)}, f32[12,3,1,4,128]{4,3,2,1,0:T(4,128)}, u32[]{:S(2)}) copy-start(f32[12,3,1,4,128]{4,3,2,1,0:T(4,128)} %param.8) | copy-start | bytes 221188
  19.0 22.6 %collective-permute-start.2 = (f32[36,128]{1,0:T(8,128)S(1)}, f32[36,128]{1,0:T(8,128)S(1)}, u32[]{:S(2)}, u32[]{:S(2)}) collective-permute-start(f32[36,128]{1,0:T(8,128)S(1)} %reshape.120.refs_2_.refs_1_), channel_id=1, source_target_pairs={{0,1},{1,2},{2,3},{3,4},{4,5},{5,6},{6,7},{7,8},{8,9},{9,10},{10,1... | collective-permute-start | bytes 55304 | tf_op jit(solution)/shard_map/ppermute | solution.py:392
  31.7 9.9 %collective-permute-start.3 = (f32[36,128]{1,0:T(8,128)S(1)}, f32[36,128]{1,0:T(8,128)S(1)}, u32[]{:S(2)}, u32[]{:S(2)}) collective-permute-start(f32[36,128]{1,0:T(8,128)S(1)} %reshape.120.refs_2_.refs_1_), channel_id=1, source_target_pairs={{1,0},{2,1},{3,2},{4,3},{5,4},{6,5},{7,6},{8,7},{9,8},{10,9},{11,1... | collective-permute-start | bytes 55304 | tf_op jit(solution)/shard_map/ppermute | solution.py:393
  33.6 0.7 copy-start.4
  34.4 0.7 copy-start.5
  36.2 4.2 %copy-start.1 = (f32[12,3,1,4,128]{4,3,2,1,0:T(4,128)S(1)}, f32[12,3,1,4,128]{4,3,2,1,0:T(4,128)}, u32[]{:S(2)}) copy-start(f32[12,3,1,4,128]{4,3,2,1,0:T(4,128)} %param.7) | copy-start | bytes 221188
  36.2 11.4 %all-to-all-start = ((f32[4,288,128]{2,1,0:T(8,128)}), f32[4,288,128]{2,1,0:T(8,128)S(1)}, u32[]{:S(2)}, u32[]{:S(2)}) async-start(f32[4,288,128]{2,1,0:T(8,128)} %shard_map.73), calls=%async_computation | async-start | bytes 1179648 | tf_op jit(solution)/shard_map/all_to_all | solution.py:411
  40.4 0.7 copy-start.6
  63.3 4.3 %collective-permute-start.4 = (f32[304,128]{1,0:T(8,128)S(1)}, f32[304,128]{1,0:T(8,128)S(1)}, u32[]{:S(2)}, u32[]{:S(2)}) collective-permute-start(f32[304,128]{1,0:T(8,128)S(1)} %get-tuple-element.36), channel_id=1, source_target_pairs={{0,4},{4,8},{8,12},{12,272},{16,20},{20,24},{24,28},{28,288},{32,3... | collective-permute-start | bytes 466952 | tf_op jit(solution)/shard_map/ppermute | solution.py:430
  64.6 11.8 %collective-permute-start.5 = (f32[304,128]{1,0:T(8,128)S(1)}, f32[304,128]{1,0:T(8,128)S(1)}, u32[]{:S(2)}, u32[]{:S(2)}) collective-permute-start(f32[304,128]{1,0:T(8,128)S(1)} %get-tuple-element.37), channel_id=1, source_target_pairs={{4,0},{8,4},{12,8},{16,268},{20,16},{24,20},{28,24},{32,284},{36,3... | collective-permute-start | bytes 466952 | tf_op jit(solution)/shard_map/ppermute | solution.py:431
  134.6 4.7 %collective-permute-start.6 = (f32[288,128]{1,0:T(8,128)S(1)}, f32[288,128]{1,0:T(8,128)S(1)}, u32[]{:S(2)}, u32[]{:S(2)}) collective-permute-start(f32[288,128]{1,0:T(8,128)S(1)} %get-tuple-element.46), channel_id=1, source_target_pairs={{0,4},{4,8},{8,12},{12,272},{16,20},{20,24},{24,28},{28,288},{32,3... | collective-permute-start | bytes 442376 | tf_op jit(solution)/shard_map/ppermute | solution.py:430
  136.8 11.4 %collective-permute-start.7 = (f32[288,128]{1,0:T(8,128)S(1)}, f32[288,128]{1,0:T(8,128)S(1)}, u32[]{:S(2)}, u32[]{:S(2)}) collective-permute-start(f32[288,128]{1,0:T(8,128)S(1)} %get-tuple-element.47), channel_id=1, source_target_pairs={{4,0},{8,4},{12,8},{16,268},{20,16},{24,20},{28,24},{32,284},{36,3... | collective-permute-start | bytes 442376 | tf_op jit(solution)/shard_map/ppermute | solution.py:431
  149.7 14.0 %all-to-all-start.5 = ((f32[16,1,128]{2,1,0:T(1,128)}), f32[16,1,128]{2,1,0:T(1,128)S(1)}, u32[]{:S(2)}, u32[]{:S(2)}) async-start(f32[16,1,128]{2,1,0:T(1,128)} %bitcast.28), calls=%async_computation.5 | async-start | bytes 16384 | tf_op jit(solution)/shard_map/all_to_all | solution.py:442

commit v11 on v10

--- a/solution.py
+++ b/solution.py
@@ -382,10 +382,12 @@
 
     far = lax.ppermute(first_guess, "zh", swap)
     load = by_target(halves(load_modes, lax.ppermute(load_modes, "zh", swap)))
-    far, kl_fields, region_labels, partner, variable, weight = lax.optimization_barrier(
-        (far, kl_fields, region_labels, partner, variable, weight)
+    guess = packed(halves(first_guess, far))
+    fan = functools.partial(fan_kernel, 1)
+    (copies,) = call(fan, [(NX,) + guess.shape[1:]])(guess)
+    copies, kl_fields, region_labels, partner, variable, weight = lax.optimization_barrier(
+        (copies, kl_fields, region_labels, partner, variable, weight)
     )
-    guess = packed(halves(first_guess, far))
     mean = jnp.where(region_labels == 0, 1.3, jnp.where(region_labels == 1, 1.0, 0.6)).astype(F32)
     varying = jnp.where(region_labels[None] == 1, kl_fields, 0.0)
     e0 = jnp.concatenate([varying, mean[None]], 0).reshape((NK + 1) * NY, NZ)
@@ -403,11 +405,9 @@
     for sweep in range(2):
         first = sweep == 0
         nk = NK + 1 if first else NK
-        blocks = 1 if first else QUAD
-        field = guess if first else change
-        (copies,) = call(
-            functools.partial(fan_kernel, blocks), [(NX * blocks,) + field.shape[1:]]
-        )(field)
+        if not first:
+            fan = functools.partial(fan_kernel, QUAD)
+            (copies,) = call(fan, [(NX * QUAD,) + change.shape[1:]])(change)
         u = lax.all_to_all(copies, ("x",) if first else ("x",) + WITHIN, 0, 0, tiled=True)
         fields = (u, load, e0, em, ep) if first else (u, e0, em, ep)
         face_rows = ((NK + 1) * NY, NZ)

time: 174 us -> 174 us (level)
  no operation moved by 1% of the time
where the time goes in v11:
time: 174 us; the launch traced here: 173 us
  blocking collectives  76.2 us (44%)
  starting transfers between devices  46.9 us (27%)
  waiting for transfers between devices  37.1 us (21%)
  Pallas kernels  8.68 us (5%)
  local copies, waits for them, and re-layouts  2.17 us (1%)
  other arithmetic  1.83 us (1%)
    all_to_all x1, blocking collectives, shards(): mom = lax.all_to_all(mom, CHUNKS, 0, 0, tiled=True)  24.9 us
    all_to_all x2, blocking collectives, shards(): q = lax.all_to_all(sent, WITHIN, 0, 0, tiled=True)  22.9 us
    all_to_all x1, blocking collectives, shards(): lax.all_to_all(copies, ('x',) if first else ('x',) + WITHIN, 0, 0, tiled=...  19.9 us
    ppermute x2, waiting for transfers between devices, shards(): high = lax.ppermute(down, CHAIN, line(4, -1))  17.7 us
    ppermute x1, starting transfers between devices, shards(): far = lax.ppermute(first_guess, 'zh', swap)  16.3 us
    ppermute x1, starting transfers between devices, shards(): em = lax.ppermute(e0, SLABS, line(16, 1))  13.1 us
    all_to_all x1, waiting for transfers between devices, shards(): mom = lax.all_to_all(mom, CHUNKS, 0, 0, tiled=True)  10.5 us
    pallas_call x10, Pallas kernels, run(): pl.pallas_call(kernel, out_shape=[pltpu.VMEM(s, F32) for s in outs], in_s...  8.68 us
  transfers between devices with their start and end apart: 10, of which 6 were waited for; matrix products, arithmetic and copies ran while one was open for 1% of the time, Pallas kernels for 1%

profile of v11, /device:TPU:1, one launch (start us, length us, event | category | flops | bytes accessed | tf_op | source)
XLA Modules:
  0.0 173.3 jit_solution(3301480598000382288)
XLA Ops:
  0.0 16.3 %collective-permute-start = (f32[12,3,1,4,128]{4,3,1,0,2:T(4,128)}, f32[12,3,1,4,128]{4,3,1,0,2:T(4,128)S(1)}, u32[]{:S(2)}, u32[]{:S(2)}) collective-permute-start(f32[12,3,1,4,128]{4,3,1,0,2:T(4,128)} %bitcast.63), channel_id=1, source_target_pairs={{0,256},{256,0},{1,257},{257,1},{2,258},{258,2},{3,259},{259,3},{4... | collective-permute-start | bytes 221192 | tf_op jit(solution)/shard_map/ppermute | solution.py:383
  16.3 1.9 %collective-permute-start.1 = (f32[12,3,1,4,128]{4,3,1,0,2:T(4,128)}, f32[12,3,1,4,128]{4,3,1,0,2:T(4,128)S(1)}, u32[]{:S(2)}, u32[]{:S(2)}) collective-permute-start(f32[12,3,1,4,128]{4,3,1,0,2:T(4,128)} %bitcast.67), channel_id=1, source_target_pairs={{0,256},{256,0},{1,257},{257,1},{2,258},{258,2},{3,259},{259,3},{4... | collective-permute-start | bytes 221192 | tf_op jit(solution)/shard_map/ppermute | solution.py:384
  18.2 0.1 copy.78
  18.3 0.1 reshape.139
  18.4 0.0 copy-start
  18.4 0.0 collective-permute-done
  18.4 0.9 fusion
  19.4 0.0 copy-done
  19.5 0.0 copy-start.3
  19.5 0.0 copy-start.2
  19.5 0.9 shard_map.73
  20.4 0.0 copy-done.3
  20.4 0.0 copy-done.2
  20.5 0.0 copy-start.4
  20.5 13.1 %collective-permute-start.2 = (f32[36,128]{1,0:T(8,128)S(1)}, f32[36,128]{1,0:T(8,128)S(1)}, u32[]{:S(2)}, u32[]{:S(2)}) collective-permute-start(f32[36,128]{1,0:T(8,128)S(1)} %reshape.120.refs_2_.refs_1_), channel_id=1, source_target_pairs={{0,1},{1,2},{2,3},{3,4},{4,5},{5,6},{6,7},{7,8},{8,9},{9,10},{10,1... | collective-permute-start | bytes 55304 | tf_op jit(solution)/shard_map/ppermute | solution.py:394
  33.6 1.9 %collective-permute-start.3 = (f32[36,128]{1,0:T(8,128)S(1)}, f32[36,128]{1,0:T(8,128)S(1)}, u32[]{:S(2)}, u32[]{:S(2)}) collective-permute-start(f32[36,128]{1,0:T(8,128)S(1)} %reshape.120.refs_2_.refs_1_), channel_id=1, source_target_pairs={{1,0},{2,1},{3,2},{4,3},{5,4},{6,5},{7,6},{8,7},{9,8},{10,9},{11,1... | collective-permute-start | bytes 55304 | tf_op jit(solution)/shard_map/ppermute | solution.py:395
  35.6 0.0 copy-done.4
  35.6 0.1 copy.75
  35.7 0.0 copy-start.5
  35.7 0.7 copy-done.5
  36.4 0.1 copy.80
  36.5 0.0 copy-start.1
  36.5 4.2 %all-to-all-start = ((f32[4,288,128]{2,1,0:T(8,128)}), f32[4,288,128]{2,1,0:T(8,128)S(1)}, u32[]{:S(2)}, u32[]{:S(2)}) async-start(f32[4,288,128]{2,1,0:T(8,128)} %shard_map.73), calls=%async_computation | async-start | bytes 1179648 | tf_op jit(solution)/shard_map/all_to_all | solution.py:411
  40.6 0.0 collective-permute-done.1
  40.6 0.0 copy-done.1
  40.7 0.0 copy-start.6
  40.8 0.7 copy-done.6
  41.4 0.1 copy.83
  41.7 0.1 pad_add_fusion.refs_5_.refs_4_
  41.8 0.1 reshape.119.refs_1_
  41.9 0.0 collective-permute-done.2.refs_3_.refs_2_
  41.9 0.0 collective-permute-done.3.refs_4_.refs_3_
  41.9 6.0 %all-to-all-done.refs_0_ = f32[4,288,128]{2,1,0:T(8,128)S(1)} async-done(((f32[4,288,128]{2,1,0:T(8,128)}), f32[4,288,128]{2,1,0:T(8,128)S(1)}, u32[]{:S(2)}, u32[]{:S(2)}) %all-to-all-start) | async-done | bytes 589856 | tf_op jit(solution)/shard_map/all_to_all | solution.py:411
  47.9 2.9 %shard_map.74 = f32[4,224,128]{2,1,0:T(8,128)S(1)} custom-call(f32[4,288,128]{2,1,0:T(8,128)S(1)} %all-to-all-done.refs_0_, f32[288,128]{1,0:T(8,128)S(1)} %reshape.119.refs_1_, f32[36,128]{1,0:T(8,128)S(1)} %reshape.120.refs_2_.refs_1_, f32[36,128]{1,0:T(8,128)S(1)} %collective-permute-done.2.refs_3_.refs_2_, ...), custom_call_target="tpu_custom_call" | custom-call | tf_op jit(solution)/shard_map/pallas_call | solution.py:44
  50.9 12.7 %all_to_all.47.refs_0_ = f32[4,224,128]{2,1,0:T(8,128)S(1)} all-to-all(f32[4,224,128]{2,1,0:T(8,128)S(1)} %shard_map.74), channel_id=1, replica_groups=mesh['zh'=2,'x'=4,'y'=4,'zp'=4,'zq'=2,'c'=2] {'zq','c'}, dimensions={0} | all-to-all | bytes 917504 | tf_op jit(solution)/shard_map/all_to_all | solution.py:425
  63.6 1.3 collective-permute-start.4
  64.9 1.3 collective-permute-start.5
  66.2 1.6 collective-permute-done.4.refs_2_
  67.9 8.8 %collective-permute-done.5.refs_3_ = f32[304,128]{1,0:T(8,128)S(1)} collective-permute-done((f32[304,128]{1,0:T(8,128)S(1)}, f32[304,128]{1,0:T(8,128)S(1)}, u32[]{:S(2)}, u32[]{:S(2)}) %collective-permute-start.5) | collective-permute-done | bytes 155680 | tf_op jit(solution)/shard_map/ppermute | solution.py:431
  76.7 0.9 shard_map.76
  77.5 24.9 %all_to_all.48 = f32[16,1,128]{2,1,0:T(1,128)S(1)} all-to-all(f32[16,1,128]{2,1,0:T(1,128)S(1)} %bitcast.62), channel_id=1, replica_groups=mesh['zh'=2,'x'=4,'y'=4,'zp'=4,'zq'=2,'c'=2] {'y','zp'}, dimensions={0} | all-to-all | bytes 16384 | tf_op jit(solution)/shard_map/all_to_all | solution.py:442
  102.5 0.2 shard_map.77
  102.8 19.9 %all_to_all.49.refs_0_ = f32[16,72,128]{2,1,0:T(8,128)S(1)} all-to-all(f32[16,72,128]{2,1,0:T(8,128)S(1)} %shard_map.78), channel_id=1, replica_groups=mesh['zh'=2,'x'=4,'y'=4,'zp'=4,'zq'=2,'c'=2] {'x','zq','c'}, dimensions={0} | all-to-all | bytes 1179648 | tf_op jit(solution)/shard_map/all_to_all | solution.py:411
  122.7 1.9 %shard_map.79 = f32[4,224,128]{2,1,0:T(8,128)S(1)} custom-call(f32[16,72,128]{2,1,0:T(8,128)S(1)} %all_to_all.49.refs_0_, f32[36,128]{1,0:T(8,128)S(1)} %reshape.120.refs_2_.refs_1_, f32[36,128]{1,0:T(8,128)S(1)} %collective-permute-done.2.refs_3_.refs_2_, f32[36,128]{1,0:T(8,128)S(1)} %collective-permute-done.3.refs_4_.refs_3_, ...), custom_call_target="tpu_custom_call" | custom-call | tf_op jit(solution)/shard_map/pallas_call | solution.py:44
  124.7 10.2 %all_to_all.50.refs_0_ = f32[4,224,128]{2,1,0:T(8,128)S(1)} all-to-all(f32[4,224,128]{2,1,0:T(8,128)S(1)} %shard_map.79), channel_id=1, replica_groups=mesh['zh'=2,'x'=4,'y'=4,'zp'=4,'zq'=2,'c'=2] {'zq','c'}, dimensions={0} | all-to-all | bytes 917504 | tf_op jit(solution)/shard_map/all_to_all | solution.py:425
  134.9 2.2 %collective-permute-start.6 = (f32[288,128]{1,0:T(8,128)S(1)}, f32[288,128]{1,0:T(8,128)S(1)}, u32[]{:S(2)}, u32[]{:S(2)}) collective-permute-start(f32[288,128]{1,0:T(8,128)S(1)} %get-tuple-element.46), channel_id=1, source_target_pairs={{0,4},{4,8},{8,12},{12,272},{16,20},{20,24},{24,28},{28,288},{32,3... | collective-permute-start | bytes 442376 | tf_op jit(solution)/shard_map/ppermute | solution.py:430
  137.1 1.3 collective-permute-start.7
  138.4 1.2 collective-permute-done.6.refs_2_
  139.6 8.9 %collective-permute-done.7.refs_3_ = f32[288,128]{1,0:T(8,128)S(1)} collective-permute-done((f32[288,128]{1,0:T(8,128)S(1)}, f32[288,128]{1,0:T(8,128)S(1)}, u32[]{:S(2)}, u32[]{:S(2)}) %collective-permute-start.7) | collective-permute-done | bytes 147488 | tf_op jit(solution)/shard_map/ppermute | solution.py:431
  148.5 1.5 shard_map.81
  150.0 3.5 %all-to-all-start.5 = ((f32[16,1,128]{2,1,0:T(1,128)}), f32[16,1,128]{2,1,0:T(1,128)S(1)}, u32[]{:S(2)}, u32[]{:S(2)}) async-start(f32[16,1,128]{2,1,0:T(1,128)} %bitcast.28), calls=%async_computation.5 | async-start | bytes 16384 | tf_op jit(solution)/shard_map/all_to_all | solution.py:442
  153.5 10.5 %all-to-all-done.5 = f32[16,1,128]{2,1,0:T(1,128)S(1)} async-done(((f32[16,1,128]{2,1,0:T(1,128)}), f32[16,1,128]{2,1,0:T(1,128)S(1)}, u32[]{:S(2)}, u32[]{:S(2)}) %all-to-all-start.5) | async-done | bytes 8224 | tf_op jit(solution)/shard_map/all_to_all | solution.py:442
  164.0 0.2 shard_map.82
  164.2 8.4 %all_to_all.51 = f32[4,36,128]{2,1,0:T(8,128)S(1)} all-to-all(f32[4,36,128]{2,1,0:T(8,128)S(1)} %shard_map.82), channel_id=1, replica_groups=mesh['zh'=2,'x'=4,'y'=4,'zp'=4,'zq'=2,'c'=2] {'zq','c'}, dimensions={0} | all-to-all | bytes 147456 | tf_op jit(solution)/shard_map/all_to_all | solution.py:451
  172.7 0.7 bitcast_add_fusion
  (32 shorter events, 0.6 us)
Async XLA Ops:
  0.0 18.4 %collective-permute-start = (f32[12,3,1,4,128]{4,3,1,0,2:T(4,128)}, f32[12,3,1,4,128]{4,3,1,0,2:T(4,128)S(1)}, u32[]{:S(2)}, u32[]{:S(2)}) collective-permute-start(f32[12,3,1,4,128]{4,3,1,0,2:T(4,128)} %bitcast.63), channel_id=1, source_target_pairs={{0,256},{256,0},{1,257},{257,1},{2,258},{258,2},{3,259},{259,3},{4... | collective-permute-start | bytes 221192 | tf_op jit(solution)/shard_map/ppermute | solution.py:383
  16.3 24.4 %collective-permute-start.1 = (f32[12,3,1,4,128]{4,3,1,0,2:T(4,128)}, f32[12,3,1,4,128]{4,3,1,0,2:T(4,128)S(1)}, u32[]{:S(2)}, u32[]{:S(2)}) collective-permute-start(f32[12,3,1,4,128]{4,3,1,0,2:T(4,128)} %bitcast.67), channel_id=1, source_target_pairs={{0,256},{256,0},{1,257},{257,1},{2,258},{258,2},{3,259},{259,3},{4... | collective-permute-start | bytes 221192 | tf_op jit(solution)/shard_map/ppermute | solution.py:384
  18.4 1.0 copy-start
  19.5 0.9 copy-start.3
  19.5 0.9 copy-start.2
  20.5 15.1 %copy-start.4 = (s32[96,8]{0,1:T(8,128)S(1)}, s32[96,8]{0,1:T(8,128)}, u32[]{:S(2)}) copy-start(s32[96,8]{0,1:T(8,128)} %param.11) | copy-start | bytes 9220
  20.5 21.4 %collective-permute-start.2 = (f32[36,128]{1,0:T(8,128)S(1)}, f32[36,128]{1,0:T(8,128)S(1)}, u32[]{:S(2)}, u32[]{:S(2)}) collective-permute-start(f32[36,128]{1,0:T(8,128)S(1)} %reshape.120.refs_2_.refs_1_), channel_id=1, source_target_pairs={{0,1},{1,2},{2,3},{3,4},{4,5},{5,6},{6,7},{7,8},{8,9},{9,10},{10,1... | collective-permute-start | bytes 55304 | tf_op jit(solution)/shard_map/ppermute | solution.py:394
  33.6 8.3 %collective-permute-start.3 = (f32[36,128]{1,0:T(8,128)S(1)}, f32[36,128]{1,0:T(8,128)S(1)}, u32[]{:S(2)}, u32[]{:S(2)}) collective-permute-start(f32[36,128]{1,0:T(8,128)S(1)} %reshape.120.refs_2_.refs_1_), channel_id=1, source_target_pairs={{1,0},{2,1},{3,2},{4,3},{5,4},{6,5},{7,6},{8,7},{9,8},{10,9},{11,1... | collective-permute-start | bytes 55304 | tf_op jit(solution)/shard_map/ppermute | solution.py:395
  35.7 0.7 copy-start.5
  36.5 4.2 %copy-start.1 = (f32[12,3,1,4,128]{4,3,2,1,0:T(4,128)S(1)}, f32[12,3,1,4,128]{4,3,2,1,0:T(4,128)}, u32[]{:S(2)}) copy-start(f32[12,3,1,4,128]{4,3,2,1,0:T(4,128)} %param.7) | copy-start | bytes 221188
  36.5 11.4 %all-to-all-start = ((f32[4,288,128]{2,1,0:T(8,128)}), f32[4,288,128]{2,1,0:T(8,128)S(1)}, u32[]{:S(2)}, u32[]{:S(2)}) async-start(f32[4,288,128]{2,1,0:T(8,128)} %shard_map.73), calls=%async_computation | async-start | bytes 1179648 | tf_op jit(solution)/shard_map/all_to_all | solution.py:411
  40.7 0.7 copy-start.6
  63.6 4.3 %collective-permute-start.4 = (f32[304,128]{1,0:T(8,128)S(1)}, f32[304,128]{1,0:T(8,128)S(1)}, u32[]{:S(2)}, u32[]{:S(2)}) collective-permute-start(f32[304,128]{1,0:T(8,128)S(1)} %get-tuple-element.36), channel_id=1, source_target_pairs={{0,4},{4,8},{8,12},{12,272},{16,20},{20,24},{24,28},{28,288},{32,3... | collective-permute-start | bytes 466952 | tf_op jit(solution)/shard_map/ppermute | solution.py:430
  64.9 11.8 %collective-permute-start.5 = (f32[304,128]{1,0:T(8,128)S(1)}, f32[304,128]{1,0:T(8,128)S(1)}, u32[]{:S(2)}, u32[]{:S(2)}) collective-permute-start(f32[304,128]{1,0:T(8,128)S(1)} %get-tuple-element.37), channel_id=1, source_target_pairs={{4,0},{8,4},{12,8},{16,268},{20,16},{24,20},{28,24},{32,284},{36,3... | collective-permute-start | bytes 466952 | tf_op jit(solution)/shard_map/ppermute | solution.py:431
  134.9 4.7 %collective-permute-start.6 = (f32[288,128]{1,0:T(8,128)S(1)}, f32[288,128]{1,0:T(8,128)S(1)}, u32[]{:S(2)}, u32[]{:S(2)}) collective-permute-start(f32[288,128]{1,0:T(8,128)S(1)} %get-tuple-element.46), channel_id=1, source_target_pairs={{0,4},{4,8},{8,12},{12,272},{16,20},{20,24},{24,28},{28,288},{32,3... | collective-permute-start | bytes 442376 | tf_op jit(solution)/shard_map/ppermute | solution.py:430
  137.1 11.4 %collective-permute-start.7 = (f32[288,128]{1,0:T(8,128)S(1)}, f32[288,128]{1,0:T(8,128)S(1)}, u32[]{:S(2)}, u32[]{:S(2)}) collective-permute-start(f32[288,128]{1,0:T(8,128)S(1)} %get-tuple-element.47), channel_id=1, source_target_pairs={{4,0},{8,4},{12,8},{16,268},{20,16},{24,20},{28,24},{32,284},{36,3... | collective-permute-start | bytes 442376 | tf_op jit(solution)/shard_map/ppermute | solution.py:431
  150.0 14.0 %all-to-all-start.5 = ((f32[16,1,128]{2,1,0:T(1,128)}), f32[16,1,128]{2,1,0:T(1,128)S(1)}, u32[]{:S(2)}, u32[]{:S(2)}) async-start(f32[16,1,128]{2,1,0:T(1,128)} %bitcast.28), calls=%async_computation.5 | async-start | bytes 16384 | tf_op jit(solution)/shard_map/all_to_all | solution.py:442

commit v12 on v8

--- a/solution.py
+++ b/solution.py
@@ -62,6 +62,14 @@
         (u, load, e0, em, ep, partner, variable, weight, out, us, mx, fx, fy, fz) = refs
     else:
         (u, e0, em, ep, partner, variable, weight, out, us, mx, fx, fy, fz) = refs
+
+    def lanes(yc):
+        return slice(yc % 2 * NZ, (yc % 2 + 1) * NZ)
+
+    def mixed(y, c, rows):
+        yc = y * 3 + c
+        return mx[yc // 2, rows, lanes(yc)]
+
     for g in range(2 * NX):
         half, x = divmod(g, NX)
         for y in range(NY):
@@ -69,11 +77,11 @@
                 yc = y * 3 + c
                 if first:
                     at = (half * NY * 3 + yc) * NM
-                    us[yc, g * NM : (g + 1) * NM, :] = u[x, at : at + NM, :]
+                    us[yc // 2, g * NM : (g + 1) * NM, lanes(yc)] = u[x, at : at + NM, :]
                     continue
                 for d in range(QUAD):
                     at, to = y * ROWS + c * SIX + half * TRI, g * NM + d * TRI
-                    us[yc, to : to + TRI, :] = u[x * QUAD + d, at : at + TRI, :]
+                    us[yc // 2, to : to + TRI, lanes(yc)] = u[x * QUAD + d, at : at + TRI, :]
     lane = lax.broadcasted_iota(jnp.int32, (NT, MODES), 1)
     pr, vr, wr = partner[...], variable[...], weight[...]
     links = NL + 1 if first else NL
@@ -88,10 +96,10 @@
             acc = term if acc is None else acc + term
         blocks.append(acc)
     mix = jnp.concatenate(blocks, axis=0)
-    for yc in range(NY * 3):
-        mx[yc] = lax.dot_general(
+    for pair in range(NY * 3 // 2):
+        mx[pair] = lax.dot_general(
             mix,
-            us[yc],
+            us[pair],
             (((1,), (0,)), ((), ())),
             precision=lax.Precision.HIGHEST,
             preferred_element_type=F32,
@@ -121,13 +129,13 @@
             for k in range(nk):
                 r = slice(k * NY + y, k * NY + y + 1)
                 rows = slice(k * NT, (k + 1) * NT)
-                m = mx[y * 3 + c, rows, :]
+                m = mixed(y, c, rows)
                 t = fz[2 + c, r, :] * m
                 side = None
                 if y + 1 < NY:
-                    side = fy[0, r, :] * mx[(y + 1) * 3 + c, rows, :]
+                    side = fy[0, r, :] * mixed(y + 1, c, rows)
                 if y > 0:
-                    less = fy[1, r, :] * mx[(y - 1) * 3 + c, rows, :]
+                    less = fy[1, r, :] * mixed(y - 1, c, rows)
                     side = less if side is None else side + less
                 t = t - (2.0 * side if c == 1 else side)
                 side = fz[0, r, :] * pltpu.roll(m, NZ - 1, 1) + fz[1, r, :] * pltpu.roll(m, 1, 1)
@@ -378,7 +386,7 @@
     em = lax.ppermute(moduli, SLABS, line(16, 1))
     ep = lax.ppermute(moduli, SLABS, line(16, -1))
     e0 = moduli
-    mine = jnp.concatenate([first_guess, load_modes], 0)
+    mine = lax.optimization_barrier(jnp.concatenate([first_guess, load_modes], 0))
     far = lax.ppermute(mine, "zh", [(0, 1), (1, 0)])
     zh, x = lax.axis_index("zh"), lax.axis_index("x")
     lower = zh == 0
@@ -409,8 +417,8 @@
             functools.partial(coupling_kernel, nk),
             [(QUAD, SENT, NZ)],
             [
-                (NY * 3, MODES, NZ),
-                (NY * 3, nk * NT, NZ),
+                (NY * 3 // 2, MODES, 2 * NZ),
+                (NY * 3 // 2, nk * NT, 2 * NZ),
                 (2,) + face_rows,
                 (2,) + face_rows,
                 (5,) + face_rows,
@@ -444,7 +452,7 @@
             )(mom, half, v0, v1, v2, change)
     total = lax.all_to_all(total, WITHIN, 0, 0, tiled=True)
     total = total.reshape(QUAD, NY, 3, TRI, NZ).transpose(0, 3, 2, 1, 4)
-    return first_guess + total.reshape(NM, 3, 1, NY, NZ)
+    return mine[:NM] + total.reshape(NM, 3, 1, NY, NZ)
 
 
 def solution(mesh):

time: 172 us -> 170 us (0.988)
  local copies, waits for them, and re-layouts: 4.55 us -> 2.75 us
    unnamed x18 -> x13, local copies, waits for them, and re-layouts: 4.01 us -> 2.22 us
where the time goes in v12:
time: 170 us; the launch traced here: 169 us
  blocking collectives  79.7 us (47%)
  waiting for transfers between devices  40.4 us (24%)
  starting transfers between devices  36.4 us (21%)
  Pallas kernels  7.85 us (5%)
  local copies, waits for them, and re-layouts  2.75 us (2%)
  other arithmetic  1.87 us (1%)
    all_to_all x2, blocking collectives, shards(): q = lax.all_to_all(sent, WITHIN, 0, 0, tiled=True)  26.5 us
    all_to_all x1, blocking collectives, shards(): mom = lax.all_to_all(mom, CHUNKS, 0, 0, tiled=True)  25.1 us
    ppermute x2, waiting for transfers between devices, shards(): high = lax.ppermute(down, CHAIN, line(4, -1))  18.5 us
    all_to_all x1, blocking collectives, shards(): lax.all_to_all(copies, ('x',) if first else ('x',) + WITHIN, 0, 0, tiled=...  18 us
    ppermute x1, starting transfers between devices, shards(): far = lax.ppermute(mine, 'zh', [(0, 1), (1, 0)])  16.3 us
    all_to_all x1, waiting for transfers between devices, shards(): mom = lax.all_to_all(mom, CHUNKS, 0, 0, tiled=True)  10.6 us
    all_to_all x1, blocking collectives, shards(): total = lax.all_to_all(total, WITHIN, 0, 0, tiled=True)  10.1 us
    pallas_call x10, Pallas kernels, run(): pl.pallas_call(kernel, out_shape=[pltpu.VMEM(s, F32) for s in outs], in_s...  7.85 us
  transfers between devices with their start and end apart: 9, of which 7 were waited for; matrix products, arithmetic and copies ran while one was open for 1% of the time, Pallas kernels for 1%

profile of v12, /device:TPU:1, one launch (start us, length us, event | category | flops | bytes accessed | tf_op | source)
XLA Modules:
  0.0 169.4 jit_solution(16576402354182936234)
XLA Ops:
  0.0 0.0 copy-start.1
  0.0 0.0 copy-start
  0.0 1.0 pad_maximum_fusion.1
  1.0 16.3 %collective-permute-start = (f32[24,3,1,4,128]{4,3,1,0,2:T(4,128)S(1)}, f32[24,3,1,4,128]{4,3,1,0,2:T(4,128)S(1)}, u32[]{:S(2)}, u32[]{:S(2)}) collective-permute-start(f32[24,3,1,4,128]{4,3,1,0,2:T(4,128)S(1)} %pad_maximum_fusion.1), channel_id=1, source_target_pairs={{0,256},{256,0},{1,257},{257,1},{2,258},{258,2},{3,259},{259,3},{4... | collective-permute-start | bytes 442376 | tf_op jit(solution)/shard_map/ppermute | solution.py:390
  17.3 0.0 copy-done.1
  17.3 0.0 copy-done
  17.4 3.5 %collective-permute-start.1 = (f32[36,128]{1,0:T(8,128)S(1)}, f32[36,128]{1,0:T(8,128)S(1)}, u32[]{:S(2)}, u32[]{:S(2)}) collective-permute-start(f32[36,128]{1,0:T(8,128)S(1)} %reshape.117.refs_2_.refs_1_), channel_id=1, source_target_pairs={{0,1},{1,2},{2,3},{3,4},{4,5},{5,6},{6,7},{7,8},{8,9},{9,10},{10,1... | collective-permute-start | bytes 55304 | tf_op jit(solution)/shard_map/ppermute | solution.py:386
  20.9 1.9 %collective-permute-start.2 = (f32[36,128]{1,0:T(8,128)S(1)}, f32[36,128]{1,0:T(8,128)S(1)}, u32[]{:S(2)}, u32[]{:S(2)}) collective-permute-start(f32[36,128]{1,0:T(8,128)S(1)} %reshape.117.refs_2_.refs_1_), channel_id=1, source_target_pairs={{1,0},{2,1},{3,2},{4,3},{5,4},{6,5},{7,6},{8,7},{9,8},{10,9},{11,1... | collective-permute-start | bytes 55304 | tf_op jit(solution)/shard_map/ppermute | solution.py:387
  22.8 0.0 copy-start.2
  22.8 0.7 copy-done.2
  23.5 0.1 copy.52
  23.6 0.0 copy-start.3
  23.6 0.7 copy-done.3
  24.3 0.1 copy.57
  24.4 0.0 collective-permute-done
  24.4 0.1 broadcast_select_fusion
  24.5 0.1 pad_maximum_fusion
  24.6 0.9 shard_map.73
  25.5 4.0 %all-to-all-start = ((f32[4,288,128]{2,1,0:T(8,128)}), f32[4,288,128]{2,1,0:T(8,128)S(1)}, u32[]{:S(2)}, u32[]{:S(2)}) async-start(f32[4,288,128]{2,1,0:T(8,128)} %shard_map.73), calls=%async_computation | async-start | bytes 1179648 | tf_op jit(solution)/shard_map/all_to_all | solution.py:413
  29.5 0.1 copy.55
  29.6 0.0 copy-start.4
  29.6 0.1 reshape.136
  29.7 0.6 copy-done.4
  30.3 0.1 copy.60
  30.4 0.1 pad_add_fusion.refs_5_.refs_4_
  30.6 0.1 copy.51
  30.6 0.1 reshape.116.refs_1_
  30.7 0.0 collective-permute-done.1.refs_3_.refs_2_
  30.7 1.4 collective-permute-done.2.refs_4_.refs_3_
  32.1 7.4 %all-to-all-done.refs_0_ = f32[4,288,128]{2,1,0:T(8,128)S(1)} async-done(((f32[4,288,128]{2,1,0:T(8,128)}), f32[4,288,128]{2,1,0:T(8,128)S(1)}, u32[]{:S(2)}, u32[]{:S(2)}) %all-to-all-start) | async-done | bytes 589856 | tf_op jit(solution)/shard_map/all_to_all | solution.py:413
  39.5 2.1 %shard_map.74 = f32[4,224,128]{2,1,0:T(8,128)S(1)} custom-call(f32[4,288,128]{2,1,0:T(8,128)S(1)} %all-to-all-done.refs_0_, f32[288,128]{1,0:T(8,128)S(1)} %reshape.116.refs_1_, f32[36,128]{1,0:T(8,128)S(1)} %reshape.117.refs_2_.refs_1_, f32[36,128]{1,0:T(8,128)S(1)} %collective-permute-done.1.refs_3_.refs_2_, ...), custom_call_target="tpu_custom_call" | custom-call | tf_op jit(solution)/shard_map/pallas_call | solution.py:44
  41.6 16.3 %all_to_all.47.refs_0_ = f32[4,224,128]{2,1,0:T(8,128)S(1)} all-to-all(f32[4,224,128]{2,1,0:T(8,128)S(1)} %shard_map.74), channel_id=1, replica_groups=mesh['zh'=2,'x'=4,'y'=4,'zp'=4,'zq'=2,'c'=2] {'zq','c'}, dimensions={0} | all-to-all | bytes 917504 | tf_op jit(solution)/shard_map/all_to_all | solution.py:427
  57.9 1.3 collective-permute-start.3
  59.2 1.3 collective-permute-start.4
  60.5 1.4 collective-permute-done.3.refs_2_
  61.9 9.6 %collective-permute-done.4.refs_3_ = f32[304,128]{1,0:T(8,128)S(1)} collective-permute-done((f32[304,128]{1,0:T(8,128)S(1)}, f32[304,128]{1,0:T(8,128)S(1)}, u32[]{:S(2)}, u32[]{:S(2)}) %collective-permute-start.4) | collective-permute-done | bytes 155680 | tf_op jit(solution)/shard_map/ppermute | solution.py:433
  71.5 0.9 shard_map.76
  72.4 25.1 %all_to_all.48 = f32[16,1,128]{2,1,0:T(1,128)S(1)} all-to-all(f32[16,1,128]{2,1,0:T(1,128)S(1)} %bitcast.54), channel_id=1, replica_groups=mesh['zh'=2,'x'=4,'y'=4,'zp'=4,'zq'=2,'c'=2] {'y','zp'}, dimensions={0} | all-to-all | bytes 16384 | tf_op jit(solution)/shard_map/all_to_all | solution.py:444
  97.5 0.2 shard_map.77
  97.8 18.0 %all_to_all.49.refs_0_ = f32[16,72,128]{2,1,0:T(8,128)S(1)} all-to-all(f32[16,72,128]{2,1,0:T(8,128)S(1)} %shard_map.78), channel_id=1, replica_groups=mesh['zh'=2,'x'=4,'y'=4,'zp'=4,'zq'=2,'c'=2] {'x','zq','c'}, dimensions={0} | all-to-all | bytes 1179648 | tf_op jit(solution)/shard_map/all_to_all | solution.py:413
  115.8 2.0 %shard_map.79 = f32[4,224,128]{2,1,0:T(8,128)S(1)} custom-call(f32[16,72,128]{2,1,0:T(8,128)S(1)} %all_to_all.49.refs_0_, f32[36,128]{1,0:T(8,128)S(1)} %reshape.117.refs_2_.refs_1_, f32[36,128]{1,0:T(8,128)S(1)} %collective-permute-done.1.refs_3_.refs_2_, f32[36,128]{1,0:T(8,128)S(1)} %collective-permute-done.2.refs_4_.refs_3_, ...), custom_call_target="tpu_custom_call" | custom-call | tf_op jit(solution)/shard_map/pallas_call | solution.py:44
  117.8 10.2 %all_to_all.50.refs_0_ = f32[4,224,128]{2,1,0:T(8,128)S(1)} all-to-all(f32[4,224,128]{2,1,0:T(8,128)S(1)} %shard_map.79), channel_id=1, replica_groups=mesh['zh'=2,'x'=4,'y'=4,'zp'=4,'zq'=2,'c'=2] {'zq','c'}, dimensions={0} | all-to-all | bytes 917504 | tf_op jit(solution)/shard_map/all_to_all | solution.py:427
  128.0 2.2 %collective-permute-start.5 = (f32[288,128]{1,0:T(8,128)S(1)}, f32[288,128]{1,0:T(8,128)S(1)}, u32[]{:S(2)}, u32[]{:S(2)}) collective-permute-start(f32[288,128]{1,0:T(8,128)S(1)} %get-tuple-element.34), channel_id=1, source_target_pairs={{0,4},{4,8},{8,12},{12,272},{16,20},{20,24},{24,28},{28,288},{32,3... | collective-permute-start | bytes 442376 | tf_op jit(solution)/shard_map/ppermute | solution.py:432
  130.2 1.3 collective-permute-start.6
  131.5 1.2 collective-permute-done.5.refs_2_
  132.7 8.9 %collective-permute-done.6.refs_3_ = f32[288,128]{1,0:T(8,128)S(1)} collective-permute-done((f32[288,128]{1,0:T(8,128)S(1)}, f32[288,128]{1,0:T(8,128)S(1)}, u32[]{:S(2)}, u32[]{:S(2)}) %collective-permute-start.6) | collective-permute-done | bytes 147488 | tf_op jit(solution)/shard_map/ppermute | solution.py:433
  141.6 1.5 shard_map.81
  143.1 4.7 %all-to-all-start.5 = ((f32[16,1,128]{2,1,0:T(1,128)}), f32[16,1,128]{2,1,0:T(1,128)S(1)}, u32[]{:S(2)}, u32[]{:S(2)}) async-start(f32[16,1,128]{2,1,0:T(1,128)} %bitcast.27), calls=%async_computation.5 | async-start | bytes 16384 | tf_op jit(solution)/shard_map/all_to_all | solution.py:444
  147.8 10.6 %all-to-all-done.5 = f32[16,1,128]{2,1,0:T(1,128)S(1)} async-done(((f32[16,1,128]{2,1,0:T(1,128)}), f32[16,1,128]{2,1,0:T(1,128)S(1)}, u32[]{:S(2)}, u32[]{:S(2)}) %all-to-all-start.5) | async-done | bytes 8224 | tf_op jit(solution)/shard_map/all_to_all | solution.py:444
  158.3 0.2 shard_map.82
  158.6 10.1 %all_to_all.51 = f32[4,36,128]{2,1,0:T(8,128)S(1)} all-to-all(f32[4,36,128]{2,1,0:T(8,128)S(1)} %shard_map.82), channel_id=1, replica_groups=mesh['zh'=2,'x'=4,'y'=4,'zp'=4,'zq'=2,'c'=2] {'zq','c'}, dimensions={0} | all-to-all | bytes 147456 | tf_op jit(solution)/shard_map/all_to_all | solution.py:453
  168.7 0.7 fusion.2
  (26 shorter events, 0.4 us)
Async XLA Ops:
  0.0 17.3 %copy-start.1 = (s32[1,4,128]{2,1,0:T(4,128)S(1)}, s32[1,4,128]{2,1,0:T(4,128)}, u32[]{:S(2)}) copy-start(s32[1,4,128]{2,1,0:T(4,128)} %param.10) | copy-start | bytes 6148
  0.0 17.3 %copy-start = (f32[8,1,4,128]{3,2,1,0:T(4,128)S(1)}, f32[8,1,4,128]{3,2,1,0:T(4,128)}, u32[]{:S(2)}) copy-start(f32[8,1,4,128]{3,2,1,0:T(4,128)} %param.9) | copy-start | bytes 49156
  1.0 23.4 %collective-permute-start = (f32[24,3,1,4,128]{4,3,1,0,2:T(4,128)S(1)}, f32[24,3,1,4,128]{4,3,1,0,2:T(4,128)S(1)}, u32[]{:S(2)}, u32[]{:S(2)}) collective-permute-start(f32[24,3,1,4,128]{4,3,1,0,2:T(4,128)S(1)} %pad_maximum_fusion.1), channel_id=1, source_target_pairs={{0,256},{256,0},{1,257},{257,1},{2,258},{258,2},{3,259},{259,3},{4... | collective-permute-start | bytes 442376 | tf_op jit(solution)/shard_map/ppermute | solution.py:390
  17.4 13.4 %collective-permute-start.1 = (f32[36,128]{1,0:T(8,128)S(1)}, f32[36,128]{1,0:T(8,128)S(1)}, u32[]{:S(2)}, u32[]{:S(2)}) collective-permute-start(f32[36,128]{1,0:T(8,128)S(1)} %reshape.117.refs_2_.refs_1_), channel_id=1, source_target_pairs={{0,1},{1,2},{2,3},{3,4},{4,5},{5,6},{6,7},{7,8},{8,9},{9,10},{10,1... | collective-permute-start | bytes 55304 | tf_op jit(solution)/shard_map/ppermute | solution.py:386
  20.9 11.2 %collective-permute-start.2 = (f32[36,128]{1,0:T(8,128)S(1)}, f32[36,128]{1,0:T(8,128)S(1)}, u32[]{:S(2)}, u32[]{:S(2)}) collective-permute-start(f32[36,128]{1,0:T(8,128)S(1)} %reshape.117.refs_2_.refs_1_), channel_id=1, source_target_pairs={{1,0},{2,1},{3,2},{4,3},{5,4},{6,5},{7,6},{8,7},{9,8},{10,9},{11,1... | collective-permute-start | bytes 55304 | tf_op jit(solution)/shard_map/ppermute | solution.py:387
  22.8 0.7 copy-start.2
  23.6 0.7 copy-start.3
  25.5 14.0 %all-to-all-start = ((f32[4,288,128]{2,1,0:T(8,128)}), f32[4,288,128]{2,1,0:T(8,128)S(1)}, u32[]{:S(2)}, u32[]{:S(2)}) async-start(f32[4,288,128]{2,1,0:T(8,128)} %shard_map.73), calls=%async_computation | async-start | bytes 1179648 | tf_op jit(solution)/shard_map/all_to_all | solution.py:413
  29.6 0.7 copy-start.4
  57.9 4.0 %collective-permute-start.3 = (f32[304,128]{1,0:T(8,128)S(1)}, f32[304,128]{1,0:T(8,128)S(1)}, u32[]{:S(2)}, u32[]{:S(2)}) collective-permute-start(f32[304,128]{1,0:T(8,128)S(1)} %get-tuple-element.24), channel_id=1, source_target_pairs={{0,4},{4,8},{8,12},{12,272},{16,20},{20,24},{24,28},{28,288},{32,3... | collective-permute-start | bytes 466952 | tf_op jit(solution)/shard_map/ppermute | solution.py:432
  59.2 12.3 %collective-permute-start.4 = (f32[304,128]{1,0:T(8,128)S(1)}, f32[304,128]{1,0:T(8,128)S(1)}, u32[]{:S(2)}, u32[]{:S(2)}) collective-permute-start(f32[304,128]{1,0:T(8,128)S(1)} %get-tuple-element.25), channel_id=1, source_target_pairs={{4,0},{8,4},{12,8},{16,268},{20,16},{24,20},{28,24},{32,284},{36,3... | collective-permute-start | bytes 466952 | tf_op jit(solution)/shard_map/ppermute | solution.py:433
  128.0 4.7 %collective-permute-start.5 = (f32[288,128]{1,0:T(8,128)S(1)}, f32[288,128]{1,0:T(8,128)S(1)}, u32[]{:S(2)}, u32[]{:S(2)}) collective-permute-start(f32[288,128]{1,0:T(8,128)S(1)} %get-tuple-element.34), channel_id=1, source_target_pairs={{0,4},{4,8},{8,12},{12,272},{16,20},{20,24},{24,28},{28,288},{32,3... | collective-permute-start | bytes 442376 | tf_op jit(solution)/shard_map/ppermute | solution.py:432
  130.2 11.4 %collective-permute-start.6 = (f32[288,128]{1,0:T(8,128)S(1)}, f32[288,128]{1,0:T(8,128)S(1)}, u32[]{:S(2)}, u32[]{:S(2)}) collective-permute-start(f32[288,128]{1,0:T(8,128)S(1)} %get-tuple-element.35), channel_id=1, source_target_pairs={{4,0},{8,4},{12,8},{16,268},{20,16},{24,20},{28,24},{32,284},{36,3... | collective-permute-start | bytes 442376 | tf_op jit(solution)/shard_map/ppermute | solution.py:433
  143.1 15.2 %all-to-all-start.5 = ((f32[16,1,128]{2,1,0:T(1,128)}), f32[16,1,128]{2,1,0:T(1,128)S(1)}, u32[]{:S(2)}, u32[]{:S(2)}) async-start(f32[16,1,128]{2,1,0:T(1,128)} %bitcast.27), calls=%async_computation.5 | async-start | bytes 16384 | tf_op jit(solution)/shard_map/all_to_all | solution.py:444

commit v13 on v12

--- a/solution.py
+++ b/solution.py
@@ -387,10 +387,8 @@
     ep = lax.ppermute(moduli, SLABS, line(16, -1))
     e0 = moduli
     mine = lax.optimization_barrier(jnp.concatenate([first_guess, load_modes], 0))
-    far = lax.ppermute(mine, "zh", [(0, 1), (1, 0)])
     zh, x = lax.axis_index("zh"), lax.axis_index("x")
-    lower = zh == 0
-    both = jnp.stack([jnp.where(lower, mine, far), jnp.where(lower, far, mine)])
+    both = lax.all_to_all(jnp.stack([mine, mine]), "zh", 0, 0, tiled=True)
     both = both.reshape(2, 2, NM, 3, NY, NZ)
     guess, load = packed(both[:, 0]), by_target(both[:, 1])
     half = jnp.broadcast_to(zh.astype(F32), (TRI, NZ))

time: 170 us -> 178 us (1.047)
  starting transfers between devices: 36.4 us -> 41.4 us
  waiting for transfers between devices: 40.4 us -> 43.8 us
    ppermute x1 -> x0, starting transfers between devices: 16.3 us -> none  [shards(): far = lax.ppermute(mine, 'zh', [(0, 1), (1, 0)])]
    all_to_all x0 -> x1, starting transfers between devices: none -> 15.8 us  [shards(): both = lax.all_to_all(jnp.stack([mine, mine]), 'zh', 0, 0, tiled=True)]
    all_to_all x0 -> x1, waiting for transfers between devices: none -> 6.52 us  [shards(): both = lax.all_to_all(jnp.stack([mine, mine]), 'zh', 0, 0, tiled=True)]
    all_to_all x2, blocking collectives: 26.5 us -> 32.5 us  [shards(): q = lax.all_to_all(sent, WITHIN, 0, 0, tiled=True)]
    all_to_all x1, blocking collectives: 25.1 us -> 19.5 us  [shards(): mom = lax.all_to_all(mom, CHUNKS, 0, 0, tiled=True)]
    all_to_all x1, starting transfers between devices: 4.68 us -> 10.2 us  [shards(): mom = lax.all_to_all(mom, CHUNKS, 0, 0, tiled=True)]
  transfers between devices with their start and end apart: 9 -> 9, of which waited for: 7 -> 7; matrix products, arithmetic and copies ran while one was open for 1% -> 1% of each run, Pallas kernels for 1% -> 0%
where the time goes in v13:
time: 178 us; the launch traced here: 177 us
  blocking collectives  78.8 us (44%)
  waiting for transfers between devices  43.8 us (25%)
  starting transfers between devices  41.4 us (23%)
  Pallas kernels  7.86 us (4%)
  local copies, waits for them, and re-layouts  2.78 us (2%)
  other arithmetic  2.48 us (1%)
    all_to_all x2, blocking collectives, shards(): q = lax.all_to_all(sent, WITHIN, 0, 0, tiled=True)  32.5 us
    all_to_all x1, blocking collectives, shards(): mom = lax.all_to_all(mom, CHUNKS, 0, 0, tiled=True)  19.5 us
    ppermute x2, waiting for transfers between devices, shards(): high = lax.ppermute(down, CHAIN, line(4, -1))  17.7 us
    all_to_all x1, blocking collectives, shards(): lax.all_to_all(copies, ('x',) if first else ('x',) + WITHIN, 0, 0, tiled=...  16.7 us
    all_to_all x1, starting transfers between devices, shards(): both = lax.all_to_all(jnp.stack([mine, mine]), 'zh', 0, 0, tiled=True)  15.8 us
    all_to_all x1, waiting for transfers between devices, shards(): mom = lax.all_to_all(mom, CHUNKS, 0, 0, tiled=True)  10.6 us
    all_to_all x1, starting transfers between devices, shards(): mom = lax.all_to_all(mom, CHUNKS, 0, 0, tiled=True)  10.2 us
    all_to_all x1, blocking collectives, shards(): total = lax.all_to_all(total, WITHIN, 0, 0, tiled=True)  10.1 us
  transfers between devices with their start and end apart: 9, of which 7 were waited for; matrix products, arithmetic and copies ran while one was open for 1% of the time, Pallas kernels for 0%

profile of v13, /device:TPU:1, one launch (start us, length us, event | category | flops | bytes accessed | tf_op | source)
XLA Modules:
  0.0 177.5 jit_solution(8789798357390397805)
XLA Ops:
  0.0 1.0 pad_maximum_fusion.1
  1.0 0.8 pad_maximum_fusion
  1.7 0.0 copy-start.1
  1.7 0.0 copy-start
  1.7 15.8 %all-to-all-start = ((f32[2,24,3,1,4,128]{5,4,2,1,3,0:T(4,128)}), f32[2,24,3,1,4,128]{5,4,2,1,3,0:T(4,128)S(1)}, u32[]{:S(2)}, u32[]{:S(2)}) async-start(f32[2,24,3,1,4,128]{5,4,2,1,3,0:T(4,128)} %pad_maximum_fusion), calls=%async_computation | async-start | bytes 589824 | tf_op jit(solution)/shard_map/all_to_all | solution.py:391
  17.5 0.0 copy-done.1
  17.5 0.0 copy-done
  17.6 3.5 %collective-permute-start = (f32[36,128]{1,0:T(8,128)S(1)}, f32[36,128]{1,0:T(8,128)S(1)}, u32[]{:S(2)}, u32[]{:S(2)}) collective-permute-start(f32[36,128]{1,0:T(8,128)S(1)} %reshape.116.refs_2_.refs_1_), channel_id=1, source_target_pairs={{0,1},{1,2},{2,3},{3,4},{4,5},{5,6},{6,7},{7,8},{8,9},{9,10},{10,1... | collective-permute-start | bytes 55304 | tf_op jit(solution)/shard_map/ppermute | solution.py:386
  21.1 1.9 %collective-permute-start.1 = (f32[36,128]{1,0:T(8,128)S(1)}, f32[36,128]{1,0:T(8,128)S(1)}, u32[]{:S(2)}, u32[]{:S(2)}) collective-permute-start(f32[36,128]{1,0:T(8,128)S(1)} %reshape.116.refs_2_.refs_1_), channel_id=1, source_target_pairs={{1,0},{2,1},{3,2},{4,3},{5,4},{6,5},{7,6},{8,7},{9,8},{10,9},{11,1... | collective-permute-start | bytes 55304 | tf_op jit(solution)/shard_map/ppermute | solution.py:387
  23.0 0.0 copy-start.2
  23.0 0.7 copy-done.2
  23.7 0.1 copy.48
  23.8 0.0 copy-start.3
  23.8 0.7 copy-done.3
  24.5 0.1 copy.53
  24.6 6.5 %all-to-all-done = f32[2,24,3,1,4,128]{5,4,2,1,3,0:T(4,128)S(1)} async-done(((f32[2,24,3,1,4,128]{5,4,2,1,3,0:T(4,128)}), f32[2,24,3,1,4,128]{5,4,2,1,3,0:T(4,128)S(1)}, u32[]{:S(2)}, u32[]{:S(2)}) %all-to-all-start) | async-done | bytes 294944 | tf_op jit(solution)/shard_map/all_to_all | solution.py:391
  31.2 0.9 shard_map.73
  32.1 4.0 %all-to-all-start.1 = ((f32[4,288,128]{2,1,0:T(8,128)}), f32[4,288,128]{2,1,0:T(8,128)S(1)}, u32[]{:S(2)}, u32[]{:S(2)}) async-start(f32[4,288,128]{2,1,0:T(8,128)} %shard_map.73), calls=%async_computation.1 | async-start | bytes 1179648 | tf_op jit(solution)/shard_map/all_to_all | solution.py:411
  36.1 0.1 copy.51
  36.2 0.0 copy-start.4
  36.2 0.1 reshape.135
  36.3 0.6 copy-done.4
  36.9 0.1 copy.56
  37.0 0.1 pad_add_fusion.refs_5_.refs_4_
  37.2 0.1 copy.47
  37.2 0.1 reshape.115.refs_1_
  37.3 0.0 collective-permute-done.refs_3_.refs_2_
  37.3 0.0 collective-permute-done.1.refs_4_.refs_3_
  37.3 6.2 %all-to-all-done.1.refs_0_ = f32[4,288,128]{2,1,0:T(8,128)S(1)} async-done(((f32[4,288,128]{2,1,0:T(8,128)}), f32[4,288,128]{2,1,0:T(8,128)S(1)}, u32[]{:S(2)}, u32[]{:S(2)}) %all-to-all-start.1) | async-done | bytes 589856 | tf_op jit(solution)/shard_map/all_to_all | solution.py:411
  43.5 2.1 %shard_map.74 = f32[4,224,128]{2,1,0:T(8,128)S(1)} custom-call(f32[4,288,128]{2,1,0:T(8,128)S(1)} %all-to-all-done.1.refs_0_, f32[288,128]{1,0:T(8,128)S(1)} %reshape.115.refs_1_, f32[36,128]{1,0:T(8,128)S(1)} %reshape.116.refs_2_.refs_1_, f32[36,128]{1,0:T(8,128)S(1)} %collective-permute-done.refs_3_.refs_2_, ...), custom_call_target="tpu_custom_call" | custom-call | tf_op jit(solution)/shard_map/pallas_call | solution.py:44
  45.6 22.3 %all_to_all.52.refs_0_ = f32[4,224,128]{2,1,0:T(8,128)S(1)} all-to-all(f32[4,224,128]{2,1,0:T(8,128)S(1)} %shard_map.74), channel_id=1, replica_groups=mesh['zh'=2,'x'=4,'y'=4,'zp'=4,'zq'=2,'c'=2] {'zq','c'}, dimensions={0} | all-to-all | bytes 917504 | tf_op jit(solution)/shard_map/all_to_all | solution.py:425
  67.9 1.3 collective-permute-start.2
  69.2 1.3 collective-permute-start.3
  70.5 1.6 collective-permute-done.2.refs_2_
  72.2 8.8 %collective-permute-done.3.refs_3_ = f32[304,128]{1,0:T(8,128)S(1)} collective-permute-done((f32[304,128]{1,0:T(8,128)S(1)}, f32[304,128]{1,0:T(8,128)S(1)}, u32[]{:S(2)}, u32[]{:S(2)}) %collective-permute-start.3) | collective-permute-done | bytes 155680 | tf_op jit(solution)/shard_map/ppermute | solution.py:431
  81.0 0.9 shard_map.76
  81.9 19.5 %all_to_all.53 = f32[16,1,128]{2,1,0:T(1,128)S(1)} all-to-all(f32[16,1,128]{2,1,0:T(1,128)S(1)} %bitcast.53), channel_id=1, replica_groups=mesh['zh'=2,'x'=4,'y'=4,'zp'=4,'zq'=2,'c'=2] {'y','zp'}, dimensions={0} | all-to-all | bytes 16384 | tf_op jit(solution)/shard_map/all_to_all | solution.py:442
  101.3 0.2 shard_map.77
  101.7 16.7 %all_to_all.54.refs_0_ = f32[16,72,128]{2,1,0:T(8,128)S(1)} all-to-all(f32[16,72,128]{2,1,0:T(8,128)S(1)} %shard_map.78), channel_id=1, replica_groups=mesh['zh'=2,'x'=4,'y'=4,'zp'=4,'zq'=2,'c'=2] {'x','zq','c'}, dimensions={0} | all-to-all | bytes 1179648 | tf_op jit(solution)/shard_map/all_to_all | solution.py:411
  118.4 2.0 %shard_map.79 = f32[4,224,128]{2,1,0:T(8,128)S(1)} custom-call(f32[16,72,128]{2,1,0:T(8,128)S(1)} %all_to_all.54.refs_0_, f32[36,128]{1,0:T(8,128)S(1)} %reshape.116.refs_2_.refs_1_, f32[36,128]{1,0:T(8,128)S(1)} %collective-permute-done.refs_3_.refs_2_, f32[36,128]{1,0:T(8,128)S(1)} %collective-permute-done.1.refs_4_.refs_3_, ...), custom_call_target="tpu_custom_call" | custom-call | tf_op jit(solution)/shard_map/pallas_call | solution.py:44
  120.3 10.2 %all_to_all.55.refs_0_ = f32[4,224,128]{2,1,0:T(8,128)S(1)} all-to-all(f32[4,224,128]{2,1,0:T(8,128)S(1)} %shard_map.79), channel_id=1, replica_groups=mesh['zh'=2,'x'=4,'y'=4,'zp'=4,'zq'=2,'c'=2] {'zq','c'}, dimensions={0} | all-to-all | bytes 917504 | tf_op jit(solution)/shard_map/all_to_all | solution.py:425
  130.6 2.2 %collective-permute-start.4 = (f32[288,128]{1,0:T(8,128)S(1)}, f32[288,128]{1,0:T(8,128)S(1)}, u32[]{:S(2)}, u32[]{:S(2)}) collective-permute-start(f32[288,128]{1,0:T(8,128)S(1)} %get-tuple-element.34), channel_id=1, source_target_pairs={{0,4},{4,8},{8,12},{12,272},{16,20},{20,24},{24,28},{28,288},{32,3... | collective-permute-start | bytes 442376 | tf_op jit(solution)/shard_map/ppermute | solution.py:430
  132.8 1.3 collective-permute-start.5
  134.1 1.2 collective-permute-done.4.refs_2_
  135.3 8.9 %collective-permute-done.5.refs_3_ = f32[288,128]{1,0:T(8,128)S(1)} collective-permute-done((f32[288,128]{1,0:T(8,128)S(1)}, f32[288,128]{1,0:T(8,128)S(1)}, u32[]{:S(2)}, u32[]{:S(2)}) %collective-permute-start.5) | collective-permute-done | bytes 147488 | tf_op jit(solution)/shard_map/ppermute | solution.py:431
  144.2 1.5 shard_map.81
  145.6 10.2 %all-to-all-start.6 = ((f32[16,1,128]{2,1,0:T(1,128)}), f32[16,1,128]{2,1,0:T(1,128)S(1)}, u32[]{:S(2)}, u32[]{:S(2)}) async-start(f32[16,1,128]{2,1,0:T(1,128)} %bitcast.25), calls=%async_computation.6 | async-start | bytes 16384 | tf_op jit(solution)/shard_map/all_to_all | solution.py:442
  155.8 10.6 %all-to-all-done.6 = f32[16,1,128]{2,1,0:T(1,128)S(1)} async-done(((f32[16,1,128]{2,1,0:T(1,128)}), f32[16,1,128]{2,1,0:T(1,128)S(1)}, u32[]{:S(2)}, u32[]{:S(2)}) %all-to-all-start.6) | async-done | bytes 8224 | tf_op jit(solution)/shard_map/all_to_all | solution.py:442
  166.4 0.2 shard_map.82
  166.6 10.1 %all_to_all.56 = f32[4,36,128]{2,1,0:T(8,128)S(1)} all-to-all(f32[4,36,128]{2,1,0:T(8,128)S(1)} %shard_map.82), channel_id=1, replica_groups=mesh['zh'=2,'x'=4,'y'=4,'zp'=4,'zq'=2,'c'=2] {'zq','c'}, dimensions={0} | all-to-all | bytes 147456 | tf_op jit(solution)/shard_map/all_to_all | solution.py:451
  176.8 0.7 fusion
  (27 shorter events, 0.4 us)
Async XLA Ops:
  1.7 15.8 %copy-start.1 = (s32[1,4,128]{2,1,0:T(4,128)S(1)}, s32[1,4,128]{2,1,0:T(4,128)}, u32[]{:S(2)}) copy-start(s32[1,4,128]{2,1,0:T(4,128)} %param.10) | copy-start | bytes 6148
  1.7 15.8 %copy-start = (f32[8,1,4,128]{3,2,1,0:T(4,128)S(1)}, f32[8,1,4,128]{3,2,1,0:T(4,128)}, u32[]{:S(2)}) copy-start(f32[8,1,4,128]{3,2,1,0:T(4,128)} %param.9) | copy-start | bytes 49156
  1.7 29.4 %all-to-all-start = ((f32[2,24,3,1,4,128]{5,4,2,1,3,0:T(4,128)}), f32[2,24,3,1,4,128]{5,4,2,1,3,0:T(4,128)S(1)}, u32[]{:S(2)}, u32[]{:S(2)}) async-start(f32[2,24,3,1,4,128]{5,4,2,1,3,0:T(4,128)} %pad_maximum_fusion), calls=%async_computation | async-start | bytes 589824 | tf_op jit(solution)/shard_map/all_to_all | solution.py:391
  17.6 19.8 %collective-permute-start = (f32[36,128]{1,0:T(8,128)S(1)}, f32[36,128]{1,0:T(8,128)S(1)}, u32[]{:S(2)}, u32[]{:S(2)}) collective-permute-start(f32[36,128]{1,0:T(8,128)S(1)} %reshape.116.refs_2_.refs_1_), channel_id=1, source_target_pairs={{0,1},{1,2},{2,3},{3,4},{4,5},{5,6},{6,7},{7,8},{8,9},{9,10},{10,1... | collective-permute-start | bytes 55304 | tf_op jit(solution)/shard_map/ppermute | solution.py:386
  21.1 16.3 %collective-permute-start.1 = (f32[36,128]{1,0:T(8,128)S(1)}, f32[36,128]{1,0:T(8,128)S(1)}, u32[]{:S(2)}, u32[]{:S(2)}) collective-permute-start(f32[36,128]{1,0:T(8,128)S(1)} %reshape.116.refs_2_.refs_1_), channel_id=1, source_target_pairs={{1,0},{2,1},{3,2},{4,3},{5,4},{6,5},{7,6},{8,7},{9,8},{10,9},{11,1... | collective-permute-start | bytes 55304 | tf_op jit(solution)/shard_map/ppermute | solution.py:387
  23.0 0.7 copy-start.2
  23.8 0.7 copy-start.3
  32.1 11.5 %all-to-all-start.1 = ((f32[4,288,128]{2,1,0:T(8,128)}), f32[4,288,128]{2,1,0:T(8,128)S(1)}, u32[]{:S(2)}, u32[]{:S(2)}) async-start(f32[4,288,128]{2,1,0:T(8,128)} %shard_map.73), calls=%async_computation.1 | async-start | bytes 1179648 | tf_op jit(solution)/shard_map/all_to_all | solution.py:411
  36.2 0.7 copy-start.4
  67.9 4.3 %collective-permute-start.2 = (f32[304,128]{1,0:T(8,128)S(1)}, f32[304,128]{1,0:T(8,128)S(1)}, u32[]{:S(2)}, u32[]{:S(2)}) collective-permute-start(f32[304,128]{1,0:T(8,128)S(1)} %get-tuple-element.24), channel_id=1, source_target_pairs={{0,4},{4,8},{8,12},{12,272},{16,20},{20,24},{24,28},{28,288},{32,3... | collective-permute-start | bytes 466952 | tf_op jit(solution)/shard_map/ppermute | solution.py:430
  69.2 11.8 %collective-permute-start.3 = (f32[304,128]{1,0:T(8,128)S(1)}, f32[304,128]{1,0:T(8,128)S(1)}, u32[]{:S(2)}, u32[]{:S(2)}) collective-permute-start(f32[304,128]{1,0:T(8,128)S(1)} %get-tuple-element.25), channel_id=1, source_target_pairs={{4,0},{8,4},{12,8},{16,268},{20,16},{24,20},{28,24},{32,284},{36,3... | collective-permute-start | bytes 466952 | tf_op jit(solution)/shard_map/ppermute | solution.py:431
  130.6 4.7 %collective-permute-start.4 = (f32[288,128]{1,0:T(8,128)S(1)}, f32[288,128]{1,0:T(8,128)S(1)}, u32[]{:S(2)}, u32[]{:S(2)}) collective-permute-start(f32[288,128]{1,0:T(8,128)S(1)} %get-tuple-element.34), channel_id=1, source_target_pairs={{0,4},{4,8},{8,12},{12,272},{16,20},{20,24},{24,28},{28,288},{32,3... | collective-permute-start | bytes 442376 | tf_op jit(solution)/shard_map/ppermute | solution.py:430
  132.8 11.4 %collective-permute-start.5 = (f32[288,128]{1,0:T(8,128)S(1)}, f32[288,128]{1,0:T(8,128)S(1)}, u32[]{:S(2)}, u32[]{:S(2)}) collective-permute-start(f32[288,128]{1,0:T(8,128)S(1)} %get-tuple-element.35), channel_id=1, source_target_pairs={{4,0},{8,4},{12,8},{16,268},{20,16},{24,20},{28,24},{32,284},{36,3... | collective-permute-start | bytes 442376 | tf_op jit(solution)/shard_map/ppermute | solution.py:431
  145.6 20.8 %all-to-all-start.6 = ((f32[16,1,128]{2,1,0:T(1,128)}), f32[16,1,128]{2,1,0:T(1,128)S(1)}, u32[]{:S(2)}, u32[]{:S(2)}) async-start(f32[16,1,128]{2,1,0:T(1,128)} %bitcast.25), calls=%async_computation.6 | async-start | bytes 16384 | tf_op jit(solution)/shard_map/all_to_all | solution.py:442

commit v14 on v12

--- a/solution.py
+++ b/solution.py
@@ -327,7 +327,7 @@
 
 def update_kernel(first, *refs):
     if first:
-        mom, v0, v1, v2, v3, out, rest = refs
+        mom, v0, v1, v2, v3, out, rest, copies = refs
     else:
         mom, half, v0, v1, v2, before, out = refs
         upper = half[...] > 0.0
@@ -356,6 +356,8 @@
                     out[s, to : to + TRI, :] = pick
                 continue
             out[s, rows, :] = change
+            for place in range(NX):
+                copies[place * QUAD + s, rows, :] = change
 
 
 def fan_kernel(blocks, field, out):
@@ -405,11 +407,8 @@
     for sweep in range(2):
         first = sweep == 0
         nk = NK + 1 if first else NK
-        blocks = 1 if first else QUAD
-        field = guess if first else change
-        (copies,) = call(
-            functools.partial(fan_kernel, blocks), [(NX * blocks,) + field.shape[1:]]
-        )(field)
+        if first:
+            (copies,) = call(functools.partial(fan_kernel, 1), [(NX,) + guess.shape[1:]])(guess)
         u = lax.all_to_all(copies, ("x",) if first else ("x",) + WITHIN, 0, 0, tiled=True)
         fields = (u, load, e0, em, ep) if first else (u, e0, em, ep)
         face_rows = ((NK + 1) * NY, NZ)
@@ -443,7 +442,9 @@
             )
         mom = lax.all_to_all(mom, CHUNKS, 0, 0, tiled=True)
         if first:
-            change, rest = call(functools.partial(update_kernel, True), [chunk, chunk])(
+            change, rest, copies = call(
+                functools.partial(update_kernel, True), [chunk, chunk, (NX * QUAD, SLAB, NZ)]
+            )(
                 mom, v0, v1, v2, v3
             )
         else:

time: 170 us -> 170 us (level)
    pallas_call x10 -> x9, Pallas kernels: 7.85 us -> 7.84 us  [run(): pl.pallas_call(kernel, out_shape=[pltpu.VMEM(s, F32) for s in outs], in_s...]
where the time goes in v14:
time: 170 us; the launch traced here: 169 us
  blocking collectives  79.7 us (47%)
  waiting for transfers between devices  40.4 us (24%)
  starting transfers between devices  36.4 us (21%)
  Pallas kernels  7.84 us (5%)
  local copies, waits for them, and re-layouts  2.75 us (2%)
  other arithmetic  1.87 us (1%)
    all_to_all x2, blocking collectives, shards(): q = lax.all_to_all(sent, WITHIN, 0, 0, tiled=True)  26.5 us
    all_to_all x1, blocking collectives, shards(): mom = lax.all_to_all(mom, CHUNKS, 0, 0, tiled=True)  25.1 us
    ppermute x2, waiting for transfers between devices, shards(): high = lax.ppermute(down, CHAIN, line(4, -1))  18.5 us
    all_to_all x1, blocking collectives, shards(): lax.all_to_all(copies, ('x',) if first else ('x',) + WITHIN, 0, 0, tiled=...  18 us
    ppermute x1, starting transfers between devices, shards(): far = lax.ppermute(mine, 'zh', [(0, 1), (1, 0)])  16.3 us
    all_to_all x1, waiting for transfers between devices, shards(): mom = lax.all_to_all(mom, CHUNKS, 0, 0, tiled=True)  10.6 us
    all_to_all x1, blocking collectives, shards(): total = lax.all_to_all(total, WITHIN, 0, 0, tiled=True)  10.1 us
    pallas_call x9, Pallas kernels, run(): pl.pallas_call(kernel, out_shape=[pltpu.VMEM(s, F32) for s in outs], in_s...  7.84 us
  transfers between devices with their start and end apart: 9, of which 7 were waited for; matrix products, arithmetic and copies ran while one was open for 1% of the time, Pallas kernels for 1%

profile of v14, /device:TPU:1, one launch (start us, length us, event | category | flops | bytes accessed | tf_op | source)
XLA Modules:
  0.0 169.4 jit_solution(214121013846317596)
XLA Ops:
  0.0 0.0 copy-start.1
  0.0 0.0 copy-start
  0.0 1.0 pad_maximum_fusion.1
  1.0 16.3 %collective-permute-start = (f32[24,3,1,4,128]{4,3,1,0,2:T(4,128)S(1)}, f32[24,3,1,4,128]{4,3,1,0,2:T(4,128)S(1)}, u32[]{:S(2)}, u32[]{:S(2)}) collective-permute-start(f32[24,3,1,4,128]{4,3,1,0,2:T(4,128)S(1)} %pad_maximum_fusion.1), channel_id=1, source_target_pairs={{0,256},{256,0},{1,257},{257,1},{2,258},{258,2},{3,259},{259,3},{4... | collective-permute-start | bytes 442376 | tf_op jit(solution)/shard_map/ppermute | solution.py:392
  17.3 0.0 copy-done.1
  17.3 0.0 copy-done
  17.4 3.5 %collective-permute-start.1 = (f32[36,128]{1,0:T(8,128)S(1)}, f32[36,128]{1,0:T(8,128)S(1)}, u32[]{:S(2)}, u32[]{:S(2)}) collective-permute-start(f32[36,128]{1,0:T(8,128)S(1)} %reshape.117.refs_2_.refs_1_), channel_id=1, source_target_pairs={{0,1},{1,2},{2,3},{3,4},{4,5},{5,6},{6,7},{7,8},{8,9},{9,10},{10,1... | collective-permute-start | bytes 55304 | tf_op jit(solution)/shard_map/ppermute | solution.py:388
  20.9 1.9 %collective-permute-start.2 = (f32[36,128]{1,0:T(8,128)S(1)}, f32[36,128]{1,0:T(8,128)S(1)}, u32[]{:S(2)}, u32[]{:S(2)}) collective-permute-start(f32[36,128]{1,0:T(8,128)S(1)} %reshape.117.refs_2_.refs_1_), channel_id=1, source_target_pairs={{1,0},{2,1},{3,2},{4,3},{5,4},{6,5},{7,6},{8,7},{9,8},{10,9},{11,1... | collective-permute-start | bytes 55304 | tf_op jit(solution)/shard_map/ppermute | solution.py:389
  22.8 0.0 copy-start.2
  22.8 0.7 copy-done.2
  23.5 0.1 copy.52
  23.6 0.0 copy-start.3
  23.6 0.7 copy-done.3
  24.3 0.1 copy.57
  24.4 0.0 collective-permute-done
  24.4 0.1 broadcast_select_fusion
  24.5 0.1 pad_maximum_fusion
  24.6 0.9 shard_map.73
  25.5 4.0 %all-to-all-start = ((f32[4,288,128]{2,1,0:T(8,128)}), f32[4,288,128]{2,1,0:T(8,128)S(1)}, u32[]{:S(2)}, u32[]{:S(2)}) async-start(f32[4,288,128]{2,1,0:T(8,128)} %shard_map.73), calls=%async_computation | async-start | bytes 1179648 | tf_op jit(solution)/shard_map/all_to_all | solution.py:412
  29.5 0.1 copy.55
  29.6 0.0 copy-start.4
  29.6 0.1 reshape.136
  29.7 0.6 copy-done.4
  30.3 0.1 copy.60
  30.4 0.1 pad_add_fusion.refs_5_.refs_4_
  30.6 0.1 copy.51
  30.6 0.1 reshape.116.refs_1_
  30.7 0.0 collective-permute-done.1.refs_3_.refs_2_
  30.7 1.4 collective-permute-done.2.refs_4_.refs_3_
  32.1 7.4 %all-to-all-done.refs_0_ = f32[4,288,128]{2,1,0:T(8,128)S(1)} async-done(((f32[4,288,128]{2,1,0:T(8,128)}), f32[4,288,128]{2,1,0:T(8,128)S(1)}, u32[]{:S(2)}, u32[]{:S(2)}) %all-to-all-start) | async-done | bytes 589856 | tf_op jit(solution)/shard_map/all_to_all | solution.py:412
  39.5 2.1 %shard_map.74 = f32[4,224,128]{2,1,0:T(8,128)S(1)} custom-call(f32[4,288,128]{2,1,0:T(8,128)S(1)} %all-to-all-done.refs_0_, f32[288,128]{1,0:T(8,128)S(1)} %reshape.116.refs_1_, f32[36,128]{1,0:T(8,128)S(1)} %reshape.117.refs_2_.refs_1_, f32[36,128]{1,0:T(8,128)S(1)} %collective-permute-done.1.refs_3_.refs_2_, ...), custom_call_target="tpu_custom_call" | custom-call | tf_op jit(solution)/shard_map/pallas_call | solution.py:44
  41.6 16.3 %all_to_all.47.refs_0_ = f32[4,224,128]{2,1,0:T(8,128)S(1)} all-to-all(f32[4,224,128]{2,1,0:T(8,128)S(1)} %shard_map.74), channel_id=1, replica_groups=mesh['zh'=2,'x'=4,'y'=4,'zp'=4,'zq'=2,'c'=2] {'zq','c'}, dimensions={0} | all-to-all | bytes 917504 | tf_op jit(solution)/shard_map/all_to_all | solution.py:426
  57.9 1.3 collective-permute-start.3
  59.2 1.3 collective-permute-start.4
  60.5 1.4 collective-permute-done.3.refs_2_
  61.9 9.6 %collective-permute-done.4.refs_3_ = f32[304,128]{1,0:T(8,128)S(1)} collective-permute-done((f32[304,128]{1,0:T(8,128)S(1)}, f32[304,128]{1,0:T(8,128)S(1)}, u32[]{:S(2)}, u32[]{:S(2)}) %collective-permute-start.4) | collective-permute-done | bytes 155680 | tf_op jit(solution)/shard_map/ppermute | solution.py:432
  71.5 0.9 shard_map.76
  72.4 25.1 %all_to_all.48 = f32[16,1,128]{2,1,0:T(1,128)S(1)} all-to-all(f32[16,1,128]{2,1,0:T(1,128)S(1)} %bitcast.54), channel_id=1, replica_groups=mesh['zh'=2,'x'=4,'y'=4,'zp'=4,'zq'=2,'c'=2] {'y','zp'}, dimensions={0} | all-to-all | bytes 16384 | tf_op jit(solution)/shard_map/all_to_all | solution.py:443
  97.5 0.3 shard_map.77
  97.8 18.0 %all_to_all.49.refs_0_ = f32[16,72,128]{2,1,0:T(8,128)S(1)} all-to-all(f32[16,72,128]{2,1,0:T(8,128)S(1)} %get-tuple-element.32), channel_id=1, replica_groups=mesh['zh'=2,'x'=4,'y'=4,'zp'=4,'zq'=2,'c'=2] {'x','zq','c'}, dimensions={0} | all-to-all | bytes 1179648 | tf_op jit(solution)/shard_map/all_to_all | solution.py:412
  115.8 2.0 %shard_map.78 = f32[4,224,128]{2,1,0:T(8,128)S(1)} custom-call(f32[16,72,128]{2,1,0:T(8,128)S(1)} %all_to_all.49.refs_0_, f32[36,128]{1,0:T(8,128)S(1)} %reshape.117.refs_2_.refs_1_, f32[36,128]{1,0:T(8,128)S(1)} %collective-permute-done.1.refs_3_.refs_2_, f32[36,128]{1,0:T(8,128)S(1)} %collective-permute-done.2.refs_4_.refs_3_, ...), custom_call_target="tpu_custom_call" | custom-call | tf_op jit(solution)/shard_map/pallas_call | solution.py:44
  117.7 10.2 %all_to_all.50.refs_0_ = f32[4,224,128]{2,1,0:T(8,128)S(1)} all-to-all(f32[4,224,128]{2,1,0:T(8,128)S(1)} %shard_map.78), channel_id=1, replica_groups=mesh['zh'=2,'x'=4,'y'=4,'zp'=4,'zq'=2,'c'=2] {'zq','c'}, dimensions={0} | all-to-all | bytes 917504 | tf_op jit(solution)/shard_map/all_to_all | solution.py:426
  128.0 2.2 %collective-permute-start.5 = (f32[288,128]{1,0:T(8,128)S(1)}, f32[288,128]{1,0:T(8,128)S(1)}, u32[]{:S(2)}, u32[]{:S(2)}) collective-permute-start(f32[288,128]{1,0:T(8,128)S(1)} %get-tuple-element.35), channel_id=1, source_target_pairs={{0,4},{4,8},{8,12},{12,272},{16,20},{20,24},{24,28},{28,288},{32,3... | collective-permute-start | bytes 442376 | tf_op jit(solution)/shard_map/ppermute | solution.py:431
  130.2 1.3 collective-permute-start.6
  131.5 1.2 collective-permute-done.5.refs_2_
  132.7 8.9 %collective-permute-done.6.refs_3_ = f32[288,128]{1,0:T(8,128)S(1)} collective-permute-done((f32[288,128]{1,0:T(8,128)S(1)}, f32[288,128]{1,0:T(8,128)S(1)}, u32[]{:S(2)}, u32[]{:S(2)}) %collective-permute-start.6) | collective-permute-done | bytes 147488 | tf_op jit(solution)/shard_map/ppermute | solution.py:432
  141.6 1.5 shard_map.80
  143.1 4.7 %all-to-all-start.5 = ((f32[16,1,128]{2,1,0:T(1,128)}), f32[16,1,128]{2,1,0:T(1,128)S(1)}, u32[]{:S(2)}, u32[]{:S(2)}) async-start(f32[16,1,128]{2,1,0:T(1,128)} %bitcast.27), calls=%async_computation.5 | async-start | bytes 16384 | tf_op jit(solution)/shard_map/all_to_all | solution.py:443
  147.7 10.6 %all-to-all-done.5 = f32[16,1,128]{2,1,0:T(1,128)S(1)} async-done(((f32[16,1,128]{2,1,0:T(1,128)}), f32[16,1,128]{2,1,0:T(1,128)S(1)}, u32[]{:S(2)}, u32[]{:S(2)}) %all-to-all-start.5) | async-done | bytes 8224 | tf_op jit(solution)/shard_map/all_to_all | solution.py:443
  158.3 0.2 shard_map.81
  158.5 10.1 %all_to_all.51 = f32[4,36,128]{2,1,0:T(8,128)S(1)} all-to-all(f32[4,36,128]{2,1,0:T(8,128)S(1)} %shard_map.81), channel_id=1, replica_groups=mesh['zh'=2,'x'=4,'y'=4,'zp'=4,'zq'=2,'c'=2] {'zq','c'}, dimensions={0} | all-to-all | bytes 147456 | tf_op jit(solution)/shard_map/all_to_all | solution.py:454
  168.7 0.7 fusion.2
  (25 shorter events, 0.3 us)
Async XLA Ops:
  0.0 17.3 %copy-start.1 = (s32[1,4,128]{2,1,0:T(4,128)S(1)}, s32[1,4,128]{2,1,0:T(4,128)}, u32[]{:S(2)}) copy-start(s32[1,4,128]{2,1,0:T(4,128)} %param.10) | copy-start | bytes 6148
  0.0 17.3 %copy-start = (f32[8,1,4,128]{3,2,1,0:T(4,128)S(1)}, f32[8,1,4,128]{3,2,1,0:T(4,128)}, u32[]{:S(2)}) copy-start(f32[8,1,4,128]{3,2,1,0:T(4,128)} %param.9) | copy-start | bytes 49156
  1.0 23.4 %collective-permute-start = (f32[24,3,1,4,128]{4,3,1,0,2:T(4,128)S(1)}, f32[24,3,1,4,128]{4,3,1,0,2:T(4,128)S(1)}, u32[]{:S(2)}, u32[]{:S(2)}) collective-permute-start(f32[24,3,1,4,128]{4,3,1,0,2:T(4,128)S(1)} %pad_maximum_fusion.1), channel_id=1, source_target_pairs={{0,256},{256,0},{1,257},{257,1},{2,258},{258,2},{3,259},{259,3},{4... | collective-permute-start | bytes 442376 | tf_op jit(solution)/shard_map/ppermute | solution.py:392
  17.4 13.4 %collective-permute-start.1 = (f32[36,128]{1,0:T(8,128)S(1)}, f32[36,128]{1,0:T(8,128)S(1)}, u32[]{:S(2)}, u32[]{:S(2)}) collective-permute-start(f32[36,128]{1,0:T(8,128)S(1)} %reshape.117.refs_2_.refs_1_), channel_id=1, source_target_pairs={{0,1},{1,2},{2,3},{3,4},{4,5},{5,6},{6,7},{7,8},{8,9},{9,10},{10,1... | collective-permute-start | bytes 55304 | tf_op jit(solution)/shard_map/ppermute | solution.py:388
  20.9 11.2 %collective-permute-start.2 = (f32[36,128]{1,0:T(8,128)S(1)}, f32[36,128]{1,0:T(8,128)S(1)}, u32[]{:S(2)}, u32[]{:S(2)}) collective-permute-start(f32[36,128]{1,0:T(8,128)S(1)} %reshape.117.refs_2_.refs_1_), channel_id=1, source_target_pairs={{1,0},{2,1},{3,2},{4,3},{5,4},{6,5},{7,6},{8,7},{9,8},{10,9},{11,1... | collective-permute-start | bytes 55304 | tf_op jit(solution)/shard_map/ppermute | solution.py:389
  22.8 0.7 copy-start.2
  23.6 0.7 copy-start.3
  25.5 14.0 %all-to-all-start = ((f32[4,288,128]{2,1,0:T(8,128)}), f32[4,288,128]{2,1,0:T(8,128)S(1)}, u32[]{:S(2)}, u32[]{:S(2)}) async-start(f32[4,288,128]{2,1,0:T(8,128)} %shard_map.73), calls=%async_computation | async-start | bytes 1179648 | tf_op jit(solution)/shard_map/all_to_all | solution.py:412
  29.6 0.7 copy-start.4
  57.9 4.0 %collective-permute-start.3 = (f32[304,128]{1,0:T(8,128)S(1)}, f32[304,128]{1,0:T(8,128)S(1)}, u32[]{:S(2)}, u32[]{:S(2)}) collective-permute-start(f32[304,128]{1,0:T(8,128)S(1)} %get-tuple-element.25), channel_id=1, source_target_pairs={{0,4},{4,8},{8,12},{12,272},{16,20},{20,24},{24,28},{28,288},{32,3... | collective-permute-start | bytes 466952 | tf_op jit(solution)/shard_map/ppermute | solution.py:431
  59.2 12.3 %collective-permute-start.4 = (f32[304,128]{1,0:T(8,128)S(1)}, f32[304,128]{1,0:T(8,128)S(1)}, u32[]{:S(2)}, u32[]{:S(2)}) collective-permute-start(f32[304,128]{1,0:T(8,128)S(1)} %get-tuple-element.26), channel_id=1, source_target_pairs={{4,0},{8,4},{12,8},{16,268},{20,16},{24,20},{28,24},{32,284},{36,3... | collective-permute-start | bytes 466952 | tf_op jit(solution)/shard_map/ppermute | solution.py:432
  128.0 4.7 %collective-permute-start.5 = (f32[288,128]{1,0:T(8,128)S(1)}, f32[288,128]{1,0:T(8,128)S(1)}, u32[]{:S(2)}, u32[]{:S(2)}) collective-permute-start(f32[288,128]{1,0:T(8,128)S(1)} %get-tuple-element.35), channel_id=1, source_target_pairs={{0,4},{4,8},{8,12},{12,272},{16,20},{20,24},{24,28},{28,288},{32,3... | collective-permute-start | bytes 442376 | tf_op jit(solution)/shard_map/ppermute | solution.py:431
  130.2 11.4 %collective-permute-start.6 = (f32[288,128]{1,0:T(8,128)S(1)}, f32[288,128]{1,0:T(8,128)S(1)}, u32[]{:S(2)}, u32[]{:S(2)}) collective-permute-start(f32[288,128]{1,0:T(8,128)S(1)} %get-tuple-element.36), channel_id=1, source_target_pairs={{4,0},{8,4},{12,8},{16,268},{20,16},{24,20},{28,24},{32,284},{36,3... | collective-permute-start | bytes 442376 | tf_op jit(solution)/shard_map/ppermute | solution.py:432
  143.1 15.2 %all-to-all-start.5 = ((f32[16,1,128]{2,1,0:T(1,128)}), f32[16,1,128]{2,1,0:T(1,128)S(1)}, u32[]{:S(2)}, u32[]{:S(2)}) async-start(f32[16,1,128]{2,1,0:T(1,128)} %bitcast.27), calls=%async_computation.5 | async-start | bytes 16384 | tf_op jit(solution)/shard_map/all_to_all | solution.py:443

commit v15 on v14

--- a/solution.py
+++ b/solution.py
@@ -150,10 +150,10 @@
                 at = (kind * NY + y) * ROWS + c * SIX
                 for d in range(QUAD):
                     out[d, at : at + SIX, :] = val[d * SIX : (d + 1) * SIX]
-    zeros = jnp.zeros((NY, NZ), F32)
-    tail = jnp.concatenate([e[NK * NY : NK * NY + NY] if first else zeros, zeros], axis=0)
-    for d in range(QUAD):
-        out[d, 3 * SLAB : SENT, :] = tail
+    if first:
+        tail = jnp.concatenate([e[NK * NY : NK * NY + NY], jnp.zeros((NY, NZ), F32)], axis=0)
+        for d in range(QUAD):
+            out[d, 3 * SLAB : SENT, :] = tail
 
 
 def edges_kernel(first, *refs):
@@ -414,7 +414,7 @@
         face_rows = ((NK + 1) * NY, NZ)
         (sent,) = call(
             functools.partial(coupling_kernel, nk),
-            [(QUAD, SENT, NZ)],
+            [(QUAD, SENT if first else 3 * SLAB, NZ)],
             [
                 (NY * 3 // 2, MODES, 2 * NZ),
                 (NY * 3 // 2, nk * NT, 2 * NZ),

time: 170 us -> 169 us (level)
  no operation moved by 1% of the time
where the time goes in v15:
time: 169 us
  blocking collectives  78.7 us (47%)
  waiting for transfers between devices  40.5 us (24%)
  starting transfers between devices  36.6 us (22%)
  Pallas kernels  7.84 us (5%)
  local copies, waits for them, and re-layouts  2.75 us (2%)
  other arithmetic  1.87 us (1%)
    all_to_all x2, blocking collectives, shards(): q = lax.all_to_all(sent, WITHIN, 0, 0, tiled=True)  26.4 us
    all_to_all x1, blocking collectives, shards(): mom = lax.all_to_all(mom, CHUNKS, 0, 0, tiled=True)  25.1 us
    ppermute x2, waiting for transfers between devices, shards(): high = lax.ppermute(down, CHAIN, line(4, -1))  18.5 us
    all_to_all x1, blocking collectives, shards(): lax.all_to_all(copies, ('x',) if first else ('x',) + WITHIN, 0, 0, tiled=...  18 us
    ppermute x1, starting transfers between devices, shards(): far = lax.ppermute(mine, 'zh', [(0, 1), (1, 0)])  16.3 us
    all_to_all x1, waiting for transfers between devices, shards(): mom = lax.all_to_all(mom, CHUNKS, 0, 0, tiled=True)  10.6 us
    all_to_all x1, blocking collectives, shards(): total = lax.all_to_all(total, WITHIN, 0, 0, tiled=True)  9.18 us
    pallas_call x9, Pallas kernels, run(): pl.pallas_call(kernel, out_shape=[pltpu.VMEM(s, F32) for s in outs], in_s...  7.84 us
  transfers between devices with their start and end apart: 9, of which 7 were waited for; matrix products, arithmetic and copies ran while one was open for 1% of the time, Pallas kernels for 1%

profile of v15, /device:TPU:1, one launch (start us, length us, event | category | flops | bytes accessed | tf_op | source)
XLA Modules:
  0.0 168.6 jit_solution(1953479963312573850)
XLA Ops:
  0.0 0.0 copy-start.1
  0.0 0.0 copy-start
  0.0 1.0 pad_maximum_fusion.1
  1.0 16.3 %collective-permute-start = (f32[24,3,1,4,128]{4,3,1,0,2:T(4,128)S(1)}, f32[24,3,1,4,128]{4,3,1,0,2:T(4,128)S(1)}, u32[]{:S(2)}, u32[]{:S(2)}) collective-permute-start(f32[24,3,1,4,128]{4,3,1,0,2:T(4,128)S(1)} %pad_maximum_fusion.1), channel_id=1, source_target_pairs={{0,256},{256,0},{1,257},{257,1},{2,258},{258,2},{3,259},{259,3},{4... | collective-permute-start | bytes 442376 | tf_op jit(solution)/shard_map/ppermute | solution.py:392
  17.3 0.0 copy-done.1
  17.3 0.0 copy-done
  17.4 3.5 %collective-permute-start.1 = (f32[36,128]{1,0:T(8,128)S(1)}, f32[36,128]{1,0:T(8,128)S(1)}, u32[]{:S(2)}, u32[]{:S(2)}) collective-permute-start(f32[36,128]{1,0:T(8,128)S(1)} %reshape.117.refs_2_.refs_1_), channel_id=1, source_target_pairs={{0,1},{1,2},{2,3},{3,4},{4,5},{5,6},{6,7},{7,8},{8,9},{9,10},{10,1... | collective-permute-start | bytes 55304 | tf_op jit(solution)/shard_map/ppermute | solution.py:388
  20.9 1.9 %collective-permute-start.2 = (f32[36,128]{1,0:T(8,128)S(1)}, f32[36,128]{1,0:T(8,128)S(1)}, u32[]{:S(2)}, u32[]{:S(2)}) collective-permute-start(f32[36,128]{1,0:T(8,128)S(1)} %reshape.117.refs_2_.refs_1_), channel_id=1, source_target_pairs={{1,0},{2,1},{3,2},{4,3},{5,4},{6,5},{7,6},{8,7},{9,8},{10,9},{11,1... | collective-permute-start | bytes 55304 | tf_op jit(solution)/shard_map/ppermute | solution.py:389
  22.8 0.0 copy-start.2
  22.8 0.7 copy-done.2
  23.5 0.1 copy.52
  23.6 0.0 copy-start.3
  23.6 0.7 copy-done.3
  24.3 0.1 copy.57
  24.4 0.0 collective-permute-done
  24.4 0.1 broadcast_select_fusion
  24.5 0.1 pad_maximum_fusion
  24.6 0.9 shard_map.73
  25.5 4.0 %all-to-all-start = ((f32[4,288,128]{2,1,0:T(8,128)}), f32[4,288,128]{2,1,0:T(8,128)S(1)}, u32[]{:S(2)}, u32[]{:S(2)}) async-start(f32[4,288,128]{2,1,0:T(8,128)} %shard_map.73), calls=%async_computation | async-start | bytes 1179648 | tf_op jit(solution)/shard_map/all_to_all | solution.py:412
  29.5 0.1 copy.55
  29.6 0.0 copy-start.4
  29.6 0.1 reshape.136
  29.7 0.6 copy-done.4
  30.3 0.1 copy.60
  30.4 0.1 pad_add_fusion.refs_5_.refs_4_
  30.6 0.1 copy.51
  30.6 0.1 reshape.116.refs_1_
  30.7 0.0 collective-permute-done.1.refs_3_.refs_2_
  30.7 1.4 collective-permute-done.2.refs_4_.refs_3_
  32.1 7.4 %all-to-all-done.refs_0_ = f32[4,288,128]{2,1,0:T(8,128)S(1)} async-done(((f32[4,288,128]{2,1,0:T(8,128)}), f32[4,288,128]{2,1,0:T(8,128)S(1)}, u32[]{:S(2)}, u32[]{:S(2)}) %all-to-all-start) | async-done | bytes 589856 | tf_op jit(solution)/shard_map/all_to_all | solution.py:412
  39.5 2.1 %shard_map.74 = f32[4,224,128]{2,1,0:T(8,128)S(1)} custom-call(f32[4,288,128]{2,1,0:T(8,128)S(1)} %all-to-all-done.refs_0_, f32[288,128]{1,0:T(8,128)S(1)} %reshape.116.refs_1_, f32[36,128]{1,0:T(8,128)S(1)} %reshape.117.refs_2_.refs_1_, f32[36,128]{1,0:T(8,128)S(1)} %collective-permute-done.1.refs_3_.refs_2_, ...), custom_call_target="tpu_custom_call" | custom-call | tf_op jit(solution)/shard_map/pallas_call | solution.py:44
  41.6 16.3 %all_to_all.47.refs_0_ = f32[4,224,128]{2,1,0:T(8,128)S(1)} all-to-all(f32[4,224,128]{2,1,0:T(8,128)S(1)} %shard_map.74), channel_id=1, replica_groups=mesh['zh'=2,'x'=4,'y'=4,'zp'=4,'zq'=2,'c'=2] {'zq','c'}, dimensions={0} | all-to-all | bytes 917504 | tf_op jit(solution)/shard_map/all_to_all | solution.py:426
  57.9 1.3 collective-permute-start.3
  59.2 1.3 collective-permute-start.4
  60.5 1.4 collective-permute-done.3.refs_2_
  61.9 9.6 %collective-permute-done.4.refs_3_ = f32[304,128]{1,0:T(8,128)S(1)} collective-permute-done((f32[304,128]{1,0:T(8,128)S(1)}, f32[304,128]{1,0:T(8,128)S(1)}, u32[]{:S(2)}, u32[]{:S(2)}) %collective-permute-start.4) | collective-permute-done | bytes 155680 | tf_op jit(solution)/shard_map/ppermute | solution.py:432
  71.5 0.9 shard_map.76
  72.4 25.1 %all_to_all.48 = f32[16,1,128]{2,1,0:T(1,128)S(1)} all-to-all(f32[16,1,128]{2,1,0:T(1,128)S(1)} %bitcast.54), channel_id=1, replica_groups=mesh['zh'=2,'x'=4,'y'=4,'zp'=4,'zq'=2,'c'=2] {'y','zp'}, dimensions={0} | all-to-all | bytes 16384 | tf_op jit(solution)/shard_map/all_to_all | solution.py:443
  97.5 0.3 shard_map.77
  97.8 18.0 %all_to_all.49.refs_0_ = f32[16,72,128]{2,1,0:T(8,128)S(1)} all-to-all(f32[16,72,128]{2,1,0:T(8,128)S(1)} %get-tuple-element.32), channel_id=1, replica_groups=mesh['zh'=2,'x'=4,'y'=4,'zp'=4,'zq'=2,'c'=2] {'x','zq','c'}, dimensions={0} | all-to-all | bytes 1179648 | tf_op jit(solution)/shard_map/all_to_all | solution.py:412
  115.8 2.0 %shard_map.78 = f32[4,216,128]{2,1,0:T(8,128)S(1)} custom-call(f32[16,72,128]{2,1,0:T(8,128)S(1)} %all_to_all.49.refs_0_, f32[36,128]{1,0:T(8,128)S(1)} %reshape.117.refs_2_.refs_1_, f32[36,128]{1,0:T(8,128)S(1)} %collective-permute-done.1.refs_3_.refs_2_, f32[36,128]{1,0:T(8,128)S(1)} %collective-permute-done.2.refs_4_.refs_3_, ...), custom_call_target="tpu_custom_call" | custom-call | tf_op jit(solution)/shard_map/pallas_call | solution.py:44
  117.7 10.1 %all_to_all.50.refs_0_ = f32[4,216,128]{2,1,0:T(8,128)S(1)} all-to-all(f32[4,216,128]{2,1,0:T(8,128)S(1)} %shard_map.78), channel_id=1, replica_groups=mesh['zh'=2,'x'=4,'y'=4,'zp'=4,'zq'=2,'c'=2] {'zq','c'}, dimensions={0} | all-to-all | bytes 884736 | tf_op jit(solution)/shard_map/all_to_all | solution.py:426
  127.9 2.2 %collective-permute-start.5 = (f32[288,128]{1,0:T(8,128)S(1)}, f32[288,128]{1,0:T(8,128)S(1)}, u32[]{:S(2)}, u32[]{:S(2)}) collective-permute-start(f32[288,128]{1,0:T(8,128)S(1)} %get-tuple-element.35), channel_id=1, source_target_pairs={{0,4},{4,8},{8,12},{12,272},{16,20},{20,24},{24,28},{28,288},{32,3... | collective-permute-start | bytes 442376 | tf_op jit(solution)/shard_map/ppermute | solution.py:431
  130.1 1.3 collective-permute-start.6
  131.4 1.3 collective-permute-done.5.refs_2_
  132.7 8.9 %collective-permute-done.6.refs_3_ = f32[288,128]{1,0:T(8,128)S(1)} collective-permute-done((f32[288,128]{1,0:T(8,128)S(1)}, f32[288,128]{1,0:T(8,128)S(1)}, u32[]{:S(2)}, u32[]{:S(2)}) %collective-permute-start.6) | collective-permute-done | bytes 147488 | tf_op jit(solution)/shard_map/ppermute | solution.py:432
  141.6 1.5 shard_map.80
  143.0 4.8 %all-to-all-start.5 = ((f32[16,1,128]{2,1,0:T(1,128)}), f32[16,1,128]{2,1,0:T(1,128)S(1)}, u32[]{:S(2)}, u32[]{:S(2)}) async-start(f32[16,1,128]{2,1,0:T(1,128)} %bitcast.27), calls=%async_computation.5 | async-start | bytes 16384 | tf_op jit(solution)/shard_map/all_to_all | solution.py:443
  147.9 10.6 %all-to-all-done.5 = f32[16,1,128]{2,1,0:T(1,128)S(1)} async-done(((f32[16,1,128]{2,1,0:T(1,128)}), f32[16,1,128]{2,1,0:T(1,128)S(1)}, u32[]{:S(2)}, u32[]{:S(2)}) %all-to-all-start.5) | async-done | bytes 8224 | tf_op jit(solution)/shard_map/all_to_all | solution.py:443
  158.4 0.2 shard_map.81
  158.7 9.2 %all_to_all.51 = f32[4,36,128]{2,1,0:T(8,128)S(1)} all-to-all(f32[4,36,128]{2,1,0:T(8,128)S(1)} %shard_map.81), channel_id=1, replica_groups=mesh['zh'=2,'x'=4,'y'=4,'zp'=4,'zq'=2,'c'=2] {'zq','c'}, dimensions={0} | all-to-all | bytes 147456 | tf_op jit(solution)/shard_map/all_to_all | solution.py:454
  167.9 0.7 fusion.2
  (25 shorter events, 0.3 us)
Async XLA Ops:
  0.0 17.3 %copy-start.1 = (s32[1,4,128]{2,1,0:T(4,128)S(1)}, s32[1,4,128]{2,1,0:T(4,128)}, u32[]{:S(2)}) copy-start(s32[1,4,128]{2,1,0:T(4,128)} %param.10) | copy-start | bytes 6148
  0.0 17.3 %copy-start = (f32[8,1,4,128]{3,2,1,0:T(4,128)S(1)}, f32[8,1,4,128]{3,2,1,0:T(4,128)}, u32[]{:S(2)}) copy-start(f32[8,1,4,128]{3,2,1,0:T(4,128)} %param.9) | copy-start | bytes 49156
  1.0 23.4 %collective-permute-start = (f32[24,3,1,4,128]{4,3,1,0,2:T(4,128)S(1)}, f32[24,3,1,4,128]{4,3,1,0,2:T(4,128)S(1)}, u32[]{:S(2)}, u32[]{:S(2)}) collective-permute-start(f32[24,3,1,4,128]{4,3,1,0,2:T(4,128)S(1)} %pad_maximum_fusion.1), channel_id=1, source_target_pairs={{0,256},{256,0},{1,257},{257,1},{2,258},{258,2},{3,259},{259,3},{4... | collective-permute-start | bytes 442376 | tf_op jit(solution)/shard_map/ppermute | solution.py:392
  17.4 13.4 %collective-permute-start.1 = (f32[36,128]{1,0:T(8,128)S(1)}, f32[36,128]{1,0:T(8,128)S(1)}, u32[]{:S(2)}, u32[]{:S(2)}) collective-permute-start(f32[36,128]{1,0:T(8,128)S(1)} %reshape.117.refs_2_.refs_1_), channel_id=1, source_target_pairs={{0,1},{1,2},{2,3},{3,4},{4,5},{5,6},{6,7},{7,8},{8,9},{9,10},{10,1... | collective-permute-start | bytes 55304 | tf_op jit(solution)/shard_map/ppermute | solution.py:388
  20.9 11.2 %collective-permute-start.2 = (f32[36,128]{1,0:T(8,128)S(1)}, f32[36,128]{1,0:T(8,128)S(1)}, u32[]{:S(2)}, u32[]{:S(2)}) collective-permute-start(f32[36,128]{1,0:T(8,128)S(1)} %reshape.117.refs_2_.refs_1_), channel_id=1, source_target_pairs={{1,0},{2,1},{3,2},{4,3},{5,4},{6,5},{7,6},{8,7},{9,8},{10,9},{11,1... | collective-permute-start | bytes 55304 | tf_op jit(solution)/shard_map/ppermute | solution.py:389
  22.8 0.7 copy-start.2
  23.6 0.7 copy-start.3
  25.5 14.0 %all-to-all-start = ((f32[4,288,128]{2,1,0:T(8,128)}), f32[4,288,128]{2,1,0:T(8,128)S(1)}, u32[]{:S(2)}, u32[]{:S(2)}) async-start(f32[4,288,128]{2,1,0:T(8,128)} %shard_map.73), calls=%async_computation | async-start | bytes 1179648 | tf_op jit(solution)/shard_map/all_to_all | solution.py:412
  29.6 0.7 copy-start.4
  57.9 4.0 %collective-permute-start.3 = (f32[304,128]{1,0:T(8,128)S(1)}, f32[304,128]{1,0:T(8,128)S(1)}, u32[]{:S(2)}, u32[]{:S(2)}) collective-permute-start(f32[304,128]{1,0:T(8,128)S(1)} %get-tuple-element.25), channel_id=1, source_target_pairs={{0,4},{4,8},{8,12},{12,272},{16,20},{20,24},{24,28},{28,288},{32,3... | collective-permute-start | bytes 466952 | tf_op jit(solution)/shard_map/ppermute | solution.py:431
  59.2 12.3 %collective-permute-start.4 = (f32[304,128]{1,0:T(8,128)S(1)}, f32[304,128]{1,0:T(8,128)S(1)}, u32[]{:S(2)}, u32[]{:S(2)}) collective-permute-start(f32[304,128]{1,0:T(8,128)S(1)} %get-tuple-element.26), channel_id=1, source_target_pairs={{4,0},{8,4},{12,8},{16,268},{20,16},{24,20},{28,24},{32,284},{36,3... | collective-permute-start | bytes 466952 | tf_op jit(solution)/shard_map/ppermute | solution.py:432
  127.9 4.8 %collective-permute-start.5 = (f32[288,128]{1,0:T(8,128)S(1)}, f32[288,128]{1,0:T(8,128)S(1)}, u32[]{:S(2)}, u32[]{:S(2)}) collective-permute-start(f32[288,128]{1,0:T(8,128)S(1)} %get-tuple-element.35), channel_id=1, source_target_pairs={{0,4},{4,8},{8,12},{12,272},{16,20},{20,24},{24,28},{28,288},{32,3... | collective-permute-start | bytes 442376 | tf_op jit(solution)/shard_map/ppermute | solution.py:431
  130.1 11.5 %collective-permute-start.6 = (f32[288,128]{1,0:T(8,128)S(1)}, f32[288,128]{1,0:T(8,128)S(1)}, u32[]{:S(2)}, u32[]{:S(2)}) collective-permute-start(f32[288,128]{1,0:T(8,128)S(1)} %get-tuple-element.36), channel_id=1, source_target_pairs={{4,0},{8,4},{12,8},{16,268},{20,16},{24,20},{28,24},{32,284},{36,3... | collective-permute-start | bytes 442376 | tf_op jit(solution)/shard_map/ppermute | solution.py:432
  143.0 15.4 %all-to-all-start.5 = ((f32[16,1,128]{2,1,0:T(1,128)}), f32[16,1,128]{2,1,0:T(1,128)S(1)}, u32[]{:S(2)}, u32[]{:S(2)}) async-start(f32[16,1,128]{2,1,0:T(1,128)} %bitcast.27), calls=%async_computation.5 | async-start | bytes 16384 | tf_op jit(solution)/shard_map/all_to_all | solution.py:443
